TPU v7x, 32 devices: a whole 2x2x4 slice. The times are simulated.
32 devices in a mesh: groups: 2 (over x), dp: 2 (over core), tensor: 8 (over z, y).
Axes of the slice: x: 2, y: 2, z: 4, core: 2. Of those that a mesh axis runs over, the one named last changes fastest.
Arguments:
- query_cotangent: bfloat16 [4096, 8192], P(('groups', 'dp'), 'tensor'), parts along dimension 0, may hold values from -6 to 6
- projection_input: bfloat16 [4096, 8192], P(('groups', 'dp'), 'tensor'), parts along dimension 0, may hold values from -0.125 to 0.125
- saved_lowrank: bfloat16 [4096, 128], P(('groups', 'dp')), parts along dimension 0, may hold values from -0.125 to 0.125
- query_matrix: bfloat16 [8192, 8192], P(None, 'tensor'), may hold values from -0.09375 to 0.09375
- adapter_shrink: bfloat16 [16, 8192, 128], P(None, 'tensor'), may hold values from -0.0625 to 0.0625
- adapter_expand: bfloat16 [16, 128, 8192], P(None, None, 'tensor'), may hold values from -0.0625 to 0.0625
- tenant_per_block: int32 [32], P(('groups', 'dp')), parts along dimension 0, may hold values from 0 to 15
- tenant_adapter_rank: int32 [16], replicated, may hold values from 16 to 128, as said below
- tenant_owner_index: int32 [16], replicated, may hold values from 0 to 1, as said below
Outputs:
- input_gradient: bfloat16 [4096, 8192], P(('groups', 'dp'), 'tensor'), parts along dimension 0
- grad_shrink: float32 [32, 8192, 128], P(('groups', 'dp'), 'tensor'), parts along dimension 0
- grad_expand: float32 [32, 128, 8192], P(('groups', 'dp'), None, 'tensor'), parts along dimension 0
There are 2 independent parts, one for each index of `groups`. A program takes and returns all parts, laid end to end along the dimension named above; an argument that names none is the same for every part. Nothing has to cross between parts.
Inputs may be any that keep to these rules, and one draw needn't show every extreme that they name: `tenant_adapter_rank`: a multiple of 16; some tenant has rank 128 and some has rank 16. `tenant_owner_index`: each of the 2 dp indices owns exactly 8 tenants.
All inputs are finite; a program needn't handle non-finite values.
Results may differ from a plain program's by a relative error of at most 0.015.
Values may be sent and summed in bfloat16 or wider, within the bound.
No kernel may reach another device: no remote copies, remote signals or barrier semaphores. Data moves between devices by JAX's collectives and lax.ppermute only.
A program may use at most 192 MiB of HBM per device.

v0:
```python
import jax
import jax.numpy as jnp
from jax import lax
from jax.sharding import PartitionSpec as P

adapter_alpha = 32.0


def per_device(
    query_cotangent,
    projection_input,
    saved_lowrank,
    query_matrix,
    adapter_shrink,
    adapter_expand,
    tenant_per_block,
    tenant_adapter_rank,
    tenant_owner_index,
):
    count_of_rows, shard_extent = query_cotangent.shape
    block_count = count_of_rows // 128
    tenant_count = tenant_adapter_rank.shape[0]
    rank_extent = adapter_shrink.shape[2]
    frozen_product = lax.psum_scatter(
        lax.dot_general(
            query_matrix,
            query_cotangent,
            (((1,), (1,)), ((), ())),
            preferred_element_type=jnp.float32,
        ).astype(jnp.bfloat16),
        "tensor",
        scatter_dimension=0,
        tiled=True,
    ).astype(jnp.float32)
    tenant_ids = jnp.arange(tenant_count, dtype=jnp.int32)
    matches = tenant_per_block[:, None] == tenant_ids[None, :]
    rank_per_block = jnp.sum(jnp.where(matches, tenant_adapter_rank[None, :], 0), axis=1).astype(
        jnp.float32
    )
    scale_per_block = adapter_alpha / rank_per_block
    block_mask = (
        jnp.arange(rank_extent).astype(jnp.float32)[None, :] < rank_per_block[:, None]
    ).astype(jnp.float32)
    gradient_per_block = query_cotangent.reshape(block_count, 128, shard_extent)
    expand_per_block = jnp.take(adapter_expand, tenant_per_block, axis=0)
    low_part = jnp.einsum(
        "zuh,zsh->zus", gradient_per_block, expand_per_block, preferred_element_type=jnp.float32
    )
    low_whole = lax.psum(low_part.astype(jnp.bfloat16), "tensor").astype(jnp.float32)
    lowrank_bfloat = (low_whole * (scale_per_block[:, None, None] * block_mask[:, None, :])).astype(
        jnp.bfloat16
    )
    shrink_per_block = jnp.take(adapter_shrink, tenant_per_block, axis=0)
    adapter_term = jnp.einsum(
        "uwq,ueq->uwe", lowrank_bfloat, shrink_per_block, preferred_element_type=jnp.float32
    )
    input_gradient = (frozen_product.T + adapter_term.reshape(count_of_rows, shard_extent)).astype(
        jnp.bfloat16
    )
    slot_order = jnp.argsort(tenant_owner_index * tenant_count + tenant_ids)
    slot_of = jnp.argsort(slot_order)
    block_slot = jnp.sum(jnp.where(matches, slot_of[None, :], 0), axis=1)
    block_select = (block_slot[:, None] == tenant_ids[None, :]).astype(jnp.float32)
    saved_lowrank_masked = saved_lowrank.reshape(block_count, 128, rank_extent) * block_mask[
        :, None, :
    ].astype(jnp.bfloat16)
    input_per_block = projection_input.reshape(block_count, 128, shard_extent)
    shrink_piece = jnp.einsum(
        "tme,tmj->tej", input_per_block, lowrank_bfloat, preferred_element_type=jnp.float32
    )
    expand_piece = jnp.einsum(
        "paw,pan->pwn", saved_lowrank_masked, gradient_per_block, preferred_element_type=jnp.float32
    )
    expand_piece = expand_piece * scale_per_block[:, None, None]
    shrink_slots = jnp.einsum(
        "bs,bdr->sdr", block_select, shrink_piece, precision=lax.Precision.HIGHEST
    )
    expand_slots = jnp.einsum(
        "bs,brd->srd", block_select, expand_piece, precision=lax.Precision.HIGHEST
    )
    grad_shrink, grad_expand = (
        lax.psum_scatter(
            shrink_slots.astype(jnp.bfloat16), "dp", scatter_dimension=0, tiled=True
        ).astype(jnp.float32),
        lax.psum_scatter(
            expand_slots.astype(jnp.bfloat16), "dp", scatter_dimension=0, tiled=True
        ).astype(jnp.float32),
    )
    return (input_gradient, grad_shrink, grad_expand)


def solution(mesh):
    placed = (
        P(("groups", "dp"), "tensor"),
        P(("groups", "dp"), "tensor"),
        P(("groups", "dp"), None),
        P(None, "tensor"),
        P(None, "tensor", None),
        P(None, None, "tensor"),
        P(("groups", "dp")),
        P(),
        P(),
    )
    return jax.shard_map(
        per_device,
        mesh=mesh,
        in_specs=placed,
        out_specs=(
            P(("groups", "dp"), "tensor"),
            P(("groups", "dp"), "tensor", None),
            P(("groups", "dp"), None, "tensor"),
        ),
        check_vma=False,
    )
```

profile of v0, /device:TPU:10, one launch (start us, length us, event | category | flops | bytes accessed | tf_op | source)
XLA Modules:
  0.0 427.1 jit_solution(7919953781422651421)
XLA Ops:
  8.0 0.0 copy-start
  8.0 0.0 all-reduce.2.cloned.1.call-start
  8.1 0.8 compare_select_fusion.1
  8.9 0.7 compare_and_fusion
  9.5 4.2 gather_fusion
  13.7 0.0 copy-done
  13.7 0.0 copy-start.6
  13.7 0.0 copy-start.4
  13.7 0.0 copy-start.3
  13.7 3.1 fusion.14
  16.8 0.0 all-reduce.2.cloned.1.call-update
  16.9 0.0 reduce-scatter.12.cloned.1.call-start
  16.9 0.0 copy-done.6
  17.0 1.2 sort.31
  18.2 1.2 sort.32
  19.5 0.0 copy-done.4
  19.5 0.0 copy-done.5
  19.5 0.2 select_reduce_fusion
  19.7 0.0 copy-done.3
  19.7 0.2 copy.25
  19.9 0.1 fusion.21
  19.9 0.8 convolution_multiply_fusion
  20.7 4.9 %convert_bitcast_fusion = bf16[128,2,8,1024]{3,2,1,0:T(8,128)(2,1)S(1)} fusion(f32[8,128,1024]{2,1,0:T(8,128)S(1)} %convolution_multiply_fusion, s32[8]{0:T(128)S(1)} %get-tuple-element.16), kind=kOutput, calls=%fused_computation.8 | convolution fusion | flops 203423872 | bytes 8388640 | tf_op jit(solution)/shard_map/bs,brd->srd/dot_general | solution.py:78
  25.7 2.4 copy.37
  28.1 0.0 reduce-scatter.12.cloned.1.call-update
  28.1 0.0 reduce-scatter.10.cloned.1.call-start
  28.2 0.1 compare_select_fusion
  28.2 60.0 %all-reduce.2.cloned.1.call-done = bf16[8,128,128]{1,2,0:T(8,128)(2,1)} async-done(((bf16[8,128,128]{1,2,0:T(8,128)(2,1)}), bf16[8,128,128]{1,2,0:T(8,128)(2,1)}) %all-reduce.2.cloned.1.call-update) | async-done | bytes 262160 | tf_op jit(solution)/shard_map/psum | solution.py:49
  88.2 4.5 %convolution_bitcast_fusion = f32[8,1024,128]{1,2,0:T(8,128)} fusion(bf16[8,128,1024]{2,1,0:T(8,128)(2,1)} %bitcast.41, bf16[8,128,128]{1,2,0:T(8,128)(2,1)} %all-reduce.2.cloned.1.call-done, f32[8,128]{1,0:T(8,128)S(1)} %compare_select_fusion), kind=kOutput, calls=%fused_computation.11 | convolution fusion | flops 268828672 | bytes 6557696 | tf_op jit(solution)/shard_map/tme,tmj->tej/dot_general | solution.py:68
  92.6 5.4 %copy.24 = f32[8,1024,128]{2,0,1:T(8,128)} copy(f32[8,1024,128]{1,2,0:T(8,128)} %convolution_bitcast_fusion) | data formatting | bytes 8388608 | tf_op jit(solution)/shard_map/tme,tmj->tej/dot_general | solution.py:68
  98.0 5.6 %convert_bitcast_fusion.1 = bf16[1024,2,8,128]{3,2,1,0:T(8,128)(2,1)S(1)} fusion(f32[8,1024,128]{2,0,1:T(8,128)} %copy.24, s32[8]{0:T(128)S(1)} %get-tuple-element.16), kind=kOutput, calls=%fused_computation.9 | convolution fusion | flops 203423872 | bytes 8388640 | tf_op jit(solution)/shard_map/bs,bdr->sdr/dot_general | solution.py:75
  103.6 2.3 copy.43
  105.9 0.0 reduce-scatter.10.cloned.1.call-update
  105.9 0.2 reduce-scatter.8.cloned.1.call-start
  106.1 26.2 %convolution_convert_fusion = bf16[8192,1024]{1,0:T(8,128)(2,1)} fusion(bf16[8192,1024]{1,0:T(8,128)(2,1)} %param.12, bf16[1024,1024]{1,0:T(8,128)(2,1)S(1)} %copy-done), kind=kOutput, calls=%fused_computation.2 | convolution fusion | flops 17188257792 | bytes 35651584 | tf_op jit(solution)/shard_map/dot_general | solution.py:25
  132.3 0.0 reduce-scatter.8.cloned.1.call-update
  132.4 0.0 copy-start.2
  132.4 3.2 gather_fusion.1
  135.6 0.0 copy-done.2
  135.6 3.3 fusion.5
  138.9 5.8 %copy.31 = f32[1024,1024]{0,1:T(8,128)} copy(f32[1024,1024]{1,0:T(8,128)} %bitcast.39) | data formatting | bytes 8388608 | tf_op jit(solution)/shard_map/reshape | solution.py:57
  144.7 4.8 %copy.29 = f32[8,128,1024]{2,1,0:T(8,128)} copy(bf16[8,128,1024]{2,0,1:T(8,128)(2,1)} %bitcast.40) | data formatting | bytes 6291456
  149.5 1.9 bitcast_convert_fusion
  151.4 2.8 copy.28
  154.2 256.3 %reduce-scatter.8.cloned.1.call-done = bf16[1024,1024]{1,0:T(8,128)(2,1)} async-done(((bf16[8192,1024]{1,0:T(8,128)(2,1)}), bf16[1024,1024]{1,0:T(8,128)(2,1)}) %reduce-scatter.8.cloned.1.call-update) | async-done | bytes 2097168 | tf_op jit(solution)/shard_map/reduce_scatter | solution.py:24
  410.5 5.1 %fusion = bf16[1024,1024]{0,1:T(8,128)(2,1)} fusion(f32[1024,1024]{0,1:T(8,128)} %copy.31, bf16[1024,1024]{1,0:T(8,128)(2,1)} %reduce-scatter.8.cloned.1.call-done), kind=kLoop, calls=%fused_computation.5 | loop fusion | flops 3145728 | bytes 8388608 | tf_op jit(solution)/shard_map/convert_element_type | solution.py:57
  415.6 3.9 copy.27
  419.5 0.0 copy-done.1
  (11 shorter events, 0.0 us)
Async XLA Ops:
  8.0 5.7 %copy-start = (bf16[1024,1024]{1,0:T(8,128)(2,1)S(1)}, bf16[1024,1024]{1,0:T(8,128)(2,1)}, u32[]{:S(2)}) copy-start(bf16[1024,1024]{1,0:T(8,128)(2,1)} %param.9) | copy-start | bytes 6291460
  8.0 80.2 %all-reduce.2.cloned.1.call-start = ((), (), s32[]{:S(2)}) async-start(), calls=%async_computation.4 | async-start | bytes 524288 | tf_op jit(solution)/shard_map/psum | solution.py:49
  13.7 3.2 copy-start.6
  13.7 5.7 %copy-start.4 = (s32[8]{0:T(128)S(1)}, s32[8]{0:T(128)}, u32[]{:S(2)}) copy-start(s32[8]{0:T(128)} %param.15) | copy-start | bytes 100
  13.7 5.7 %copy-start.5 = (s32[16]{0:T(128)S(1)}, s32[16]{0:T(128)}, u32[]{:S(2)}) copy-start(s32[16]{0:T(128)} %param.16) | copy-start | bytes 196
  13.7 5.9 %copy-start.3 = (bf16[1024,128]{1,0:T(8,128)(2,1)S(1)}, bf16[1024,128]{1,0:T(8,128)(2,1)}, u32[]{:S(2)}) copy-start(bf16[1024,128]{1,0:T(8,128)(2,1)} %param.11) | copy-start | bytes 786436
  16.9 127.8 %reduce-scatter.12.cloned.1.call-start = ((), (), s32[]{:S(2)}) async-start(), calls=%async_computation.6 | async-start | bytes 6291456
  28.1 121.4 %reduce-scatter.10.cloned.1.call-start = ((), (), s32[]{:S(2)}) async-start(), calls=%async_computation.5 | async-start | bytes 6291456
  105.9 304.5 %reduce-scatter.8.cloned.1.call-start = ((), (), s32[]{:S(2)}) async-start(), calls=%async_computation.3 | async-start | bytes 18874368 | tf_op jit(solution)/shard_map/reduce_scatter | solution.py:24
  132.4 3.2 copy-start.2
  410.5 9.0 %copy-start.1 = (bf16[1024,1024]{1,0:T(8,128)(2,1)S(1)}, bf16[1024,1024]{1,0:T(8,128)(2,1)}, u32[]{:S(2)}) copy-start(bf16[1024,1024]{1,0:T(8,128)(2,1)} %param.9) | copy-start | bytes 6291460
Sparse Core Ops, SparseCore 0:
  17.0 71.1 all-reduce.1
Sparse Core Ops, SparseCore 1:
  28.2 13.5 reduce-scatter.11
  106.0 12.2 reduce-scatter.9
  132.5 277.9 reduce-scatter.7
where the time goes:
time: 430 us; the launch traced here: 427 us
  waiting for transfers between devices  316 us (73%)
  matrix products  48.4 us (11%)
  local copies, waits for them, and re-layouts  35 us (8%)
  between operations  15.8 us (4%)
  other arithmetic  11.3 us (3%)
    reduce_scatter x1, waiting for transfers between devices, per_device(): lax.psum_scatter(lax.dot_general(query_matrix, query_cotangent, (((1,), (...  256 us
    psum x1, waiting for transfers between devices, per_device(): lax.psum(low_part.astype(jnp.bfloat16), 'tensor').astype(jnp.float32)  60 us
    dot_general x1, matrix products, per_device(): lax.dot_general(query_matrix, query_cotangent, (((1,), (1,)), ((), ())),...  26.2 us
    unnamed x19, local copies, waits for them, and re-layouts  16.3 us
  transfers between devices with their start and end apart: 4, of which 2 were waited for; matrix products, arithmetic and copies ran while one was open for 18% of the time, Pallas kernels for 0%

commit v1 on v0

v1 whole, which is shorter than its diff:
```python
import functools

import jax
import jax.numpy as jnp
from jax import lax
from jax.experimental import pallas as pl
from jax.experimental.pallas import tpu as pltpu
from jax.sharding import PartitionSpec as P

adapter_alpha = 32.0
row_block = 128
bf16 = jnp.bfloat16
f32 = jnp.float32
contract_last = (((1,), (1,)), ((), ()))
contract_first = (((0,), (0,)), ((), ()))
vmem_bytes = 40 * 1024 * 1024


def params():
    return pltpu.CompilerParams(vmem_limit_bytes=vmem_bytes)


def product_kernel(add_count, block_count, has_link, *refs):
    position = 1
    rows, weights = refs[1], refs[2]
    position = 3
    total = lax.dot_general(
        rows[...], weights[...], contract_last, preferred_element_type=f32
    )
    for _ in range(add_count):
        total = total + refs[position][...].astype(f32)
        position += 1
    if block_count:
        low = refs[position]
        position += 1
        terms = []
        for i in range(block_count):
            terms.append(
                lax.dot_general(
                    low[i * row_block : (i + 1) * row_block, :],
                    refs[position][0],
                    contract_last,
                    preferred_element_type=f32,
                )
            )
            position += 1
        total = total + jnp.concatenate(terms, axis=0)
    refs[-1][...] = total.astype(refs[-1].dtype)


def product(scalars, gradient, weights, piece, piece_rows, width, adds, link, adapter=None):
    depth = gradient.shape[1]
    tile = min(width, 512)
    while width % tile:
        tile //= 2
    steps = width // tile
    in_specs = [
        pl.BlockSpec((piece_rows, depth), lambda j, s: (piece, 0)),
        pl.BlockSpec((tile, depth), lambda j, s: (s[0] * steps + j, 0)),
    ]
    operands = [gradient, weights]
    for array, shifted in adds:
        if shifted:
            in_specs.append(
                pl.BlockSpec((piece_rows, tile), lambda j, s: (0, s[1] * steps + j))
            )
        else:
            in_specs.append(pl.BlockSpec((piece_rows, tile), lambda j, s: (0, j)))
        operands.append(array)
    block_count = 0
    if adapter is not None:
        low, shrink = adapter
        rank = low.shape[1]
        block_count = piece_rows // row_block
        in_specs.append(pl.BlockSpec((piece_rows, rank), lambda j, s: (piece, 0)))
        operands.append(low)
        for i in range(block_count):
            in_specs.append(
                pl.BlockSpec((1, tile, rank), functools.partial(lambda j, s, i: (s[2 + i], j, 0), i=i))
            )
            operands.append(shrink)
    if link is not None:
        in_specs.append(pl.BlockSpec(memory_space=pl.ANY))
        operands.append(link)
    return pl.pallas_call(
        functools.partial(product_kernel, len(adds), block_count, link is not None),
        grid_spec=pltpu.PrefetchScalarGridSpec(
            num_scalar_prefetch=1,
            grid=(steps,),
            in_specs=in_specs,
            out_specs=pl.BlockSpec((piece_rows, tile), lambda j, s: (0, j)),
        ),
        out_shape=jax.ShapeDtypeStruct((piece_rows, width), bf16),
        compiler_params=params(),
        cost_estimate=pl.CostEstimate(
            flops=2 * piece_rows * width * depth,
            bytes_accessed=2 * (width * depth + piece_rows * depth + (1 + len(adds)) * piece_rows * width),
            transcendentals=0,
        ),
    )(scalars, *operands)


def low_kernel(tenants, rows, expand, link, out):
    out[...] = lax.dot_general(
        rows[...], expand[0], contract_last, preferred_element_type=f32
    ).astype(out.dtype)


def low_product(tenants, gradient, expand, link):
    count_of_rows, depth = gradient.shape
    rank = expand.shape[1]
    blocks = count_of_rows // row_block
    return pl.pallas_call(
        low_kernel,
        grid_spec=pltpu.PrefetchScalarGridSpec(
            num_scalar_prefetch=1,
            grid=(blocks,),
            in_specs=[
                pl.BlockSpec((row_block, depth), lambda b, s: (b, 0)),
                pl.BlockSpec((1, rank, depth), lambda b, s: (s[b], 0, 0)),
                pl.BlockSpec(memory_space=pl.ANY),
            ],
            out_specs=pl.BlockSpec((row_block, rank), lambda b, s: (b, 0)),
        ),
        out_shape=jax.ShapeDtypeStruct((count_of_rows, rank), bf16),
        compiler_params=params(),
        cost_estimate=pl.CostEstimate(
            flops=2 * count_of_rows * rank * depth,
            bytes_accessed=2 * (count_of_rows * depth + blocks * rank * depth),
            transcendentals=0,
        ),
    )(tenants, gradient, expand, link)


def factor_kernel(slots_each, blocks, slots, scales, left, right, link, own, other, other_sum):
    own[...] = jnp.zeros_like(own)
    other_sum[...] = jnp.zeros_like(other_sum)
    for b in range(blocks):
        here = pl.ds(b * row_block, row_block)
        piece = lax.dot_general(
            left[here, :], right[here, :], contract_first, preferred_element_type=f32
        )
        piece = piece * scales[b]
        slot = slots[b]

        @pl.when(slot < slots_each)
        def _():
            own[slot] += piece

        @pl.when(slot >= slots_each)
        def _():
            other_sum[slot - slots_each] += piece

    other[...] = other_sum[...].astype(other.dtype)


def factor_sums(slots, scales, left, right, slots_each, others, link):
    count_of_rows, height = left.shape
    width = right.shape[1]
    blocks = count_of_rows // row_block
    whole = pl.BlockSpec(memory_space=pltpu.VMEM)
    return pl.pallas_call(
        functools.partial(factor_kernel, slots_each, blocks),
        in_specs=[
            pl.BlockSpec(memory_space=pltpu.SMEM),
            pl.BlockSpec(memory_space=pltpu.SMEM),
            whole,
            whole,
            pl.BlockSpec(memory_space=pl.ANY),
        ],
        out_specs=[whole, whole],
        out_shape=[
            jax.ShapeDtypeStruct((slots_each, height, width), f32),
            jax.ShapeDtypeStruct((others, height, width), bf16),
        ],
        scratch_shapes=[pltpu.VMEM((others, height, width), f32)],
        compiler_params=params(),
        cost_estimate=pl.CostEstimate(
            flops=2 * count_of_rows * height * width,
            bytes_accessed=2 * count_of_rows * (height + width)
            + 4 * slots_each * height * width
            + 2 * others * height * width,
            transcendentals=0,
        ),
    )(slots, scales, left, right, link)


def per_device(
    tensor_count,
    owner_count,
    gradient,
    projection_input,
    saved_lowrank,
    weights,
    shrink,
    expand,
    tenant_per_block,
    tenant_adapter_rank,
    tenant_owner_index,
):
    count_of_rows, width = gradient.shape
    blocks = count_of_rows // row_block
    tenants = tenant_adapter_rank.shape[0]
    rank_extent = shrink.shape[2]
    nodes = tensor_count // 2
    last = nodes - 1
    place = lax.axis_index("tensor")
    node = place // 2
    side = place % 2
    owner = lax.axis_index("dp")

    halves = 2 if nodes <= 4 else 1
    pieces = 2 * halves
    piece_rows = count_of_rows // pieces
    lower = list(range(halves))
    upper = list(range(halves, pieces))

    link = [None]

    def run(scalars, piece, columns, adds, adapter=None):
        out = product(
            jnp.stack([jnp.asarray(v, jnp.int32) for v in scalars]),
            gradient, weights, piece, piece_rows, columns, adds, link[0], adapter,
        )
        link[0] = out
        return out

    def swap(x, active):
        pairs = []
        for z in active:
            pairs += [(2 * z, 2 * z + 1), (2 * z + 1, 2 * z)]
        return lax.ppermute(x, "tensor", pairs)

    def along(x, hops):
        pairs = [(2 * a + y, 2 * b + y) for a, b in hops for y in range(2)]
        return lax.ppermute(x, "tensor", pairs)

    def tasks(step, lag):
        reach = step - lag
        right = [z for z in range(nodes) if z <= reach and z < last]
        left = [z for z in range(nodes) if z >= last - reach and z > 0]
        to_right = jnp.clip(last - step + node, 0, last)
        to_left = jnp.clip(node - (last - step), 0, last)
        right_hops = [(z, z + 1) for z in right]
        left_hops = [(z, z - 1) for z in left]
        if not set(right) & set(left):
            both = jnp.where(node <= reach, to_right, to_left)
            return [(right + left, both, right_hops, left_hops)]
        return [(right, to_right, right_hops, []), (left, to_left, [], left_hops)]

    def forward(x, right_hops, left_hops):
        targets = [b for _, b in right_hops + left_hops]
        if right_hops and left_hops and len(set(targets)) == len(targets):
            both = along(x, right_hops + left_hops)
            return (both, both)
        return (
            along(x, right_hops) if right_hops else None,
            along(x, left_hops) if left_hops else None,
        )

    def addends(arrived, right_hops, left_hops):
        found = []
        if arrived is None:
            return found
        if right_hops and arrived[0] is not None:
            found.append(arrived[0])
        if left_hops and arrived[1] is not None and not (found and found[0] is arrived[1]):
            found.append(arrived[1])
        return found

    class Flow:
        def __init__(self, piece_ids, lag):
            self.piece_ids, self.lag = piece_ids, lag
            self.arrived = {p: None for p in piece_ids}
            self.swapped = {}

        def has(self, step):
            return self.lag <= step <= last - 1

        def swap(self, step):
            if not self.has(step):
                return
            for t, (active, dest, _, _) in enumerate(tasks(step, self.lag)):
                for p in self.piece_ids:
                    part = run([dest * 2 + (1 - side), 0], p, width, [])
                    self.swapped[step, t, p] = swap(part, active)

        def combine(self, step, p):
            if not self.has(step):
                return
            before = self.arrived[p]
            found = [None, None]
            for t, (active, dest, right_hops, left_hops) in enumerate(tasks(step, self.lag)):
                adds = [(self.swapped[step, t, p], False)]
                adds += [(a, False) for a in addends(before, right_hops, left_hops)]
                part = run([dest * 2 + side, 0], p, width, adds)
                got = forward(part, right_hops, left_hops)
                if right_hops:
                    found[0] = got[0]
                if left_hops:
                    found[1] = got[1]
            self.arrived[p] = tuple(found)

    class DirectFlow:
        def __init__(self):
            self.arrived = {p: None for p in lower}

        def advance(self, step, p):
            if step > last - 1:
                return
            dest = jnp.where(node == step, last, 0)
            adds = [] if self.arrived[p] is None else [(self.arrived[p], False)]
            part = run([dest, 0], p, 2 * width, adds)
            self.arrived[p] = along(part, [(step, step + 1), (last - step, last - step - 1)])

    low_flow = Flow(lower, 1)
    up_flow = Flow(upper, 0)
    direct = DirectFlow()

    tenant_ids = jnp.arange(tenants, dtype=jnp.int32)
    matches = tenant_per_block[:, None] == tenant_ids[None, :]
    rank_per_block = jnp.sum(jnp.where(matches, tenant_adapter_rank[None, :], 0), axis=1).astype(f32)
    scale_per_block = adapter_alpha / rank_per_block
    block_mask = (jnp.arange(rank_extent).astype(f32)[None, :] < rank_per_block[:, None]).astype(f32)
    key = tenant_owner_index * tenants + tenant_ids
    slot_of = jnp.sum((key[None, :] < key[:, None]).astype(jnp.int32), axis=1)
    block_slot = jnp.sum(jnp.where(matches, slot_of[None, :], 0), axis=1)
    slots_each = tenants // owner_count
    own_first = lax.rem(block_slot - owner * slots_each + tenants, tenants)

    direct.advance(0, lower[0])
    up_flow.swap(0)
    for p in lower[1:]:
        direct.advance(0, p)
    low_flow.swap(1)
    up_flow.swap(1)

    low_part = low_product(tenant_per_block, gradient, expand, link[0])
    link[0] = low_part
    half = count_of_rows // 2
    keep = lax.dynamic_slice_in_dim(low_part, side * half, half, 0)
    give = lax.dynamic_slice_in_dim(low_part, (1 - side) * half, half, 0)
    low_half = (keep.astype(f32) + swap(give, range(nodes)).astype(f32)).astype(bf16)
    low_sum = low_half.astype(f32)
    going_right = going_left = low_half
    for hop in range(1, nodes):
        going_right = along(going_right, [(z, z + 1) for z in range(hop - 1, last)])
        going_left = along(going_left, [(z, z - 1) for z in range(1, nodes - hop + 1)])
        low_sum = low_sum + going_right.astype(f32) + going_left.astype(f32)
    low_mine = low_sum.astype(bf16)
    low_other = swap(low_mine, range(nodes))
    low_whole = jnp.where(
        side == 0,
        jnp.concatenate([low_mine, low_other], axis=0),
        jnp.concatenate([low_other, low_mine], axis=0),
    )
    factor = scale_per_block[:, None, None] * block_mask[:, None, :]
    low = (low_whole.astype(f32).reshape(blocks, row_block, rank_extent) * factor).astype(bf16)
    low = low.reshape(count_of_rows, rank_extent)

    for p in upper:
        up_flow.combine(0, p)
    low_flow.swap(2)

    masked = saved_lowrank.reshape(blocks, row_block, rank_extent) * block_mask[:, None, :].astype(bf16)
    masked = masked.reshape(count_of_rows, rank_extent)
    others = slots_each * (owner_count - 1)
    ones = jnp.ones_like(scale_per_block)

    def exchange(own, other):
        total = own
        for hop in range(1, owner_count):
            theirs = other[(hop - 1) * slots_each : hop * slots_each]
            pairs = [(i, (i + hop) % owner_count) for i in range(owner_count)]
            total = total + lax.ppermute(theirs, "dp", pairs).astype(f32)
        return total

    own, other = factor_sums(
        own_first, scale_per_block, masked, gradient, slots_each, others, link[0]
    )
    link[0] = other
    grad_expand = exchange(own, other)

    own_swap = {}

    def swap_own(p):
        adds = [(direct.arrived[p], True)] if p in lower else []
        part = run([node * 2 + (1 - side), 1 - side], p, width, adds)
        own_swap[p] = swap(part, range(nodes))

    grad_shrink = None
    for step in range(1, last):
        direct.advance(step, lower[0])
        low_flow.combine(step, lower[0])
        for p in lower[1:]:
            low_flow.combine(step, p)
            direct.advance(step, p)
        up_flow.swap(step + 1)
        low_flow.swap(step + 2)
        if step == last - 1:
            for p in upper:
                swap_own(p)
            own, other = factor_sums(
                own_first, ones, projection_input, low, slots_each, others, link[0]
            )
            link[0] = other
            grad_shrink = exchange(own, other)
            for p in lower:
                swap_own(p)
        for p in upper:
            up_flow.combine(step, p)

    outs = []
    for p in range(pieces):
        flow = low_flow if p in lower else up_flow
        adds = [(own_swap[p], False)]
        if p in lower:
            adds.append((direct.arrived[p], True))
        arrived = flow.arrived[p]
        adds.append((arrived[0], False))
        if arrived[1] is not arrived[0]:
            adds.append((arrived[1], False))
        in_piece = piece_rows // row_block
        ids = [tenant_per_block[p * in_piece + i] for i in range(in_piece)]
        outs.append(run([node * 2 + side, side] + ids, p, width, adds, (low, shrink)))
    input_gradient = jnp.concatenate(outs, axis=0)
    return (input_gradient, grad_shrink, grad_expand)


def solution(mesh):
    placed = (
        P(("groups", "dp"), "tensor"),
        P(("groups", "dp"), "tensor"),
        P(("groups", "dp"), None),
        P(None, "tensor"),
        P(None, "tensor", None),
        P(None, None, "tensor"),
        P(("groups", "dp")),
        P(),
        P(),
    )
    return jax.shard_map(
        functools.partial(per_device, mesh.shape["tensor"], mesh.shape["dp"]),
        mesh=mesh,
        in_specs=placed,
        out_specs=(
            P(("groups", "dp"), "tensor"),
            P(("groups", "dp"), "tensor", None),
            P(("groups", "dp"), None, "tensor"),
        ),
        check_vma=False,
    )
```

time: 430 us -> 335 us (0.78)
  waiting for transfers between devices: 316 us -> 50.2 us
  Pallas kernels: 0 us -> 144 us
  starting transfers between devices: 0.35 us -> 97.5 us
  matrix products: 48.4 us -> 0 us
  between operations: 15.8 us -> 1.71 us
  local copies, waits for them, and re-layouts: 35 us -> 21.3 us
  other arithmetic: 11.3 us -> 16.8 us
    reduce_scatter x1 -> x0, waiting for transfers between devices: 256 us -> none  [per_device(): lax.psum_scatter(lax.dot_general(query_matrix, query_cotangent, (((1,), (...]
    pallas_call x0 -> x41, Pallas kernels: none -> 144 us  [the longest x38 132 us: product(): pl.pallas_call(functools.partial(product_kernel, len(adds), block_count,...]
    ppermute x0 -> x48, starting transfers between devices: none -> 97.5 us  [the longest x28 68.4 us: along(): return lax.ppermute(x, 'tensor', pairs)]
    psum x1 -> x0, waiting for transfers between devices: 60 us -> none  [per_device(): lax.psum(low_part.astype(jnp.bfloat16), 'tensor').astype(jnp.float32)]
    ppermute x0 -> x48, waiting for transfers between devices: none -> 50.2 us  [the longest x28 35.4 us: along(): return lax.ppermute(x, 'tensor', pairs)]
    dot_general x7 -> x0, matrix products: 48.4 us -> none  [the longest x1 26.2 us: per_device(): lax.dot_general(query_matrix, query_cotangent, (((1,), (1,)), ((), ())),...]
    add x1 -> x3, other arithmetic: 0.01 us -> 8.9 us  [the longest x2 8.9 us: exchange(): total = total + lax.ppermute(theirs, 'dp', pairs).astype(f32)]
    gather x2 -> x0, local copies, waits for them, and re-layouts: 7.37 us -> none  [the longest x1 4.19 us: per_device(): expand_per_block = jnp.take(adapter_expand, tenant_per_block, axis=0)]
  transfers between devices with their start and end apart: 4 -> 48, of which waited for: 2 -> 12; matrix products, arithmetic and copies ran while one was open for 18% -> 4% of each run, Pallas kernels for 0% -> 42%
where the time goes in v1:
time: 335 us; the launch traced here: 332 us
  Pallas kernels  144 us (43%)
  starting transfers between devices  97.5 us (29%)
  waiting for transfers between devices  50.2 us (15%)
  local copies, waits for them, and re-layouts  21.3 us (6%)
  other arithmetic  16.8 us (5%)
    pallas_call x38, Pallas kernels, product(): pl.pallas_call(functools.partial(product_kernel, len(adds), block_count,...  132 us
    ppermute x28, starting transfers between devices, along(): return lax.ppermute(x, 'tensor', pairs)  68.4 us
    ppermute x28, waiting for transfers between devices, along(): return lax.ppermute(x, 'tensor', pairs)  35.4 us
    ppermute x18, starting transfers between devices, swap(): return lax.ppermute(x, 'tensor', pairs)  29 us
    unnamed x86, local copies, waits for them, and re-layouts  20.5 us
    ppermute x18, waiting for transfers between devices, swap(): return lax.ppermute(x, 'tensor', pairs)  14.8 us
    pallas_call x2, Pallas kernels, factor_sums(): pl.pallas_call(functools.partial(factor_kernel, slots_each, blocks), in_s...  10.3 us
    add x2, other arithmetic, exchange(): total = total + lax.ppermute(theirs, 'dp', pairs).astype(f32)  8.9 us
  transfers between devices with their start and end apart: 48, of which 12 were waited for; matrix products, arithmetic and copies ran while one was open for 4% of the time, Pallas kernels for 42%

profile of v1, /device:TPU:10, one launch (start us, length us, event | category | flops | bytes accessed | tf_op | source)
XLA Modules:
  0.0 331.8 jit_solution(11428019435687300826)
XLA Ops:
  2.3 4.6 %shard_map.112.refs_3_ = bf16[256,2048]{1,0:T(8,128)(2,1)S(1)} custom-call(s32[2]{0:T(128)S(1)} %get-tuple-element.27.refs_0_, bf16[1024,1024]{1,0:T(8,128)(2,1)S(1)} %copy-done, bf16[8192,1024]{1,0:T(8,128)(2,1)} %refs_2_.75), custom_call_target="tpu_custom_call" | custom-call | flops 1073741824 | bytes 5767168 | tf_op jit(solution)/shard_map/pallas_call | solution.py:85
  8.3 3.4 %shard_map.113.refs_3_ = bf16[256,1024]{1,0:T(8,128)(2,1)} custom-call(s32[2]{0:T(128)S(1)} %get-tuple-element.26.refs_0_, bf16[1024,1024]{1,0:T(8,128)(2,1)S(1)} %copy-done.1, bf16[8192,1024]{1,0:T(8,128)(2,1)} %refs_2_.75, bf16[256,2048]{1,0:T(8,128)(2,1)S(1)} %shard_map.112.refs_3_), custom_call_target="tpu_custom_call" | custom-call | flops 536870912 | bytes 3145728 | tf_op jit(solution)/shard_map/pallas_call | solution.py:85
  13.2 3.4 %shard_map.114.refs_3_ = bf16[256,1024]{1,0:T(8,128)(2,1)} custom-call(s32[2]{0:T(128)S(1)} %get-tuple-element.26.refs_0_, bf16[1024,1024]{1,0:T(8,128)(2,1)S(1)} %copy-done.1, bf16[8192,1024]{1,0:T(8,128)(2,1)} %refs_2_.75, bf16[256,1024]{1,0:T(8,128)(2,1)} %shard_map.113.refs_3_), custom_call_target="tpu_custom_call" | custom-call | flops 536870912 | bytes 3145728 | tf_op jit(solution)/shard_map/pallas_call | solution.py:85
  18.1 5.4 %shard_map.115.refs_3_ = bf16[256,2048]{1,0:T(8,128)(2,1)} custom-call(s32[2]{0:T(128)S(1)} %get-tuple-element.27.refs_0_, bf16[1024,1024]{1,0:T(8,128)(2,1)S(1)} %copy-done.1, bf16[8192,1024]{1,0:T(8,128)(2,1)} %refs_2_.75, bf16[256,1024]{1,0:T(8,128)(2,1)} %shard_map.114.refs_3_), custom_call_target="tpu_custom_call" | custom-call | flops 1073741824 | bytes 5767168 | tf_op jit(solution)/shard_map/pallas_call | solution.py:85
  47.0 3.4 %collective-permute-done.12 = bf16[512,128]{1,0:T(8,128)(2,1)} collective-permute-done((bf16[512,128]{1,0:T(8,128)(2,1)}, bf16[512,128]{1,0:T(8,128)(2,1)}, u32[]{:S(2)}, u32[]{:S(2)}) %collective-permute-start.12) | collective-permute-done | bytes 131104 | tf_op jit(solution)/shard_map/ppermute | solution.py:232
  52.0 9.1 %collective-permute-start.14 = (bf16[512,128]{1,0:T(8,128)(2,1)}, bf16[512,128]{1,0:T(8,128)(2,1)}, u32[]{:S(2)}, u32[]{:S(2)}) collective-permute-start(bf16[512,128]{1,0:T(8,128)(2,1)} %add_convert_fusion.1), channel_id=1, source_target_pairs={{2,0},{3,1},{4,2},{5,3},{6,4},{7,5},{10,8},{11,9},{12,10},{13,11},... | collective-permute-start | bytes 393224 | tf_op jit(solution)/shard_map/ppermute | solution.py:236
  65.4 2.8 shard_map.121.refs_4_
  68.3 3.3 collective-permute-start.13
  71.6 2.8 shard_map.122.refs_3_
  82.9 4.9 %shard_map.125 = (f32[8,128,1024]{2,1,0:T(8,128)S(1)}, bf16[8,128,1024]{2,1,0:T(8,128)(2,1)}) custom-call(s32[8]{0:T(128)S(1)} %compare_select_fusion.1.slots, f32[8]{0:T(128)S(1)} %broadcast_divide_fusion.scales, bf16[1024,128]{1,0:T(8,128)(2,1)S(1)} %bitcast_multiply_fusion.1.left, bf16[1024,1024]{1,0:T(8,128)(2,1)S(1)} %copy-done.1, ...), custom_call_target="tpu_custom_call" | custom-call | flops 268435456 | bytes 8650752 | tf_op jit(solution)/shard_map/pallas_call | solution.py:162
  91.6 5.6 %shard_map.126.refs_4_ = bf16[256,2048]{1,0:T(8,128)(2,1)} custom-call(s32[2]{0:T(128)S(1)} %get-tuple-element.23.refs_0_, bf16[1024,1024]{1,0:T(8,128)(2,1)S(1)} %copy-done.1, bf16[8192,1024]{1,0:T(8,128)(2,1)} %refs_2_.75, bf16[256,2048]{1,0:T(8,128)(2,1)} %collective-permute-done.refs_3_, bf16[8,128,1024]{2,1,0:T(8,128)(2,1)} %get-tuple-element.7.refs_4_), custom_call_target="tpu_custom_call" | custom-call | flops 1073741824 | bytes 6815744 | tf_op jit(solution)/shard_map/pallas_call | solution.py:85
  97.2 3.5 %shard_map.127.refs_4_ = bf16[256,1024]{1,0:T(8,128)(2,1)} custom-call(s32[2]{0:T(128)S(1)} %get-tuple-element.22.refs_0_, bf16[1024,1024]{1,0:T(8,128)(2,1)S(1)} %copy-done.1, bf16[8192,1024]{1,0:T(8,128)(2,1)} %refs_2_.75, bf16[256,1024]{1,0:T(8,128)(2,1)S(1)} %collective-permute-done.10.refs_3_, bf16[256,2048]{1,0:T(8,128)(2,1)} %shard_map.126.refs_4_), custom_call_target="tpu_custom_call" | custom-call | flops 536870912 | bytes 3670016 | tf_op jit(solution)/shard_map/pallas_call | solution.py:85
  100.7 3.5 %shard_map.128.refs_4_ = bf16[256,1024]{1,0:T(8,128)(2,1)} custom-call(s32[2]{0:T(128)S(1)} %get-tuple-element.22.refs_0_, bf16[1024,1024]{1,0:T(8,128)(2,1)S(1)} %copy-done.1, bf16[8192,1024]{1,0:T(8,128)(2,1)} %refs_2_.75, bf16[256,1024]{1,0:T(8,128)(2,1)S(1)} %collective-permute-done.9.refs_3_, bf16[256,1024]{1,0:T(8,128)(2,1)} %shard_map.127.refs_4_), custom_call_target="tpu_custom_call" | custom-call | flops 536870912 | bytes 3670016 | tf_op jit(solution)/shard_map/pallas_call | solution.py:85
  104.1 7.7 %collective-permute-start.16 = (bf16[512,128]{1,0:T(8,128)(2,1)}, bf16[512,128]{1,0:T(8,128)(2,1)S(1)}, u32[]{:S(2)}, u32[]{:S(2)}) collective-permute-start(bf16[512,128]{1,0:T(8,128)(2,1)} %collective-permute-done.14), channel_id=1, source_target_pairs={{2,0},{3,1},{4,2},{5,3},{10,8},{11,9},{12,10},{13,11},{18,16},{19,... | collective-permute-start | bytes 393224 | tf_op jit(solution)/shard_map/ppermute | solution.py:236
  111.8 4.7 %shard_map.129.refs_3_ = bf16[256,2048]{1,0:T(8,128)(2,1)S(1)} custom-call(s32[2]{0:T(128)S(1)} %get-tuple-element.23.refs_0_, bf16[1024,1024]{1,0:T(8,128)(2,1)S(1)} %copy-done.1, bf16[8192,1024]{1,0:T(8,128)(2,1)} %refs_2_.75, bf16[256,2048]{1,0:T(8,128)(2,1)} %collective-permute-done.8.refs_3_, bf16[256,1024]{1,0:T(8,128)(2,1)} %shard_map.128.refs_4_), custom_call_target="tpu_custom_call" | custom-call | flops 1073741824 | bytes 6815744 | tf_op jit(solution)/shard_map/pallas_call | solution.py:85
  116.5 3.5 %shard_map.130.refs_3_ = bf16[256,1024]{1,0:T(8,128)(2,1)} custom-call(s32[2]{0:T(128)S(1)} %pad_add_fusion.4.refs_0_, bf16[1024,1024]{1,0:T(8,128)(2,1)S(1)} %copy-done.1, bf16[8192,1024]{1,0:T(8,128)(2,1)} %refs_2_.75, bf16[256,2048]{1,0:T(8,128)(2,1)S(1)} %shard_map.129.refs_3_), custom_call_target="tpu_custom_call" | custom-call | flops 536870912 | bytes 3145728 | tf_op jit(solution)/shard_map/pallas_call | solution.py:85
  121.3 3.5 %shard_map.131.refs_3_ = bf16[256,1024]{1,0:T(8,128)(2,1)} custom-call(s32[2]{0:T(128)S(1)} %pad_add_fusion.4.refs_0_, bf16[1024,1024]{1,0:T(8,128)(2,1)S(1)} %copy-done.1, bf16[8192,1024]{1,0:T(8,128)(2,1)} %refs_2_.75, bf16[256,1024]{1,0:T(8,128)(2,1)} %shard_map.130.refs_3_), custom_call_target="tpu_custom_call" | custom-call | flops 536870912 | bytes 3145728 | tf_op jit(solution)/shard_map/pallas_call | solution.py:85
  133.3 3.5 %shard_map.134.refs_5_ = bf16[256,1024]{1,0:T(8,128)(2,1)} custom-call(s32[2]{0:T(128)S(1)} %pad_add_fusion.6.refs_0_, bf16[1024,1024]{1,0:T(8,128)(2,1)S(1)} %copy-done.1, bf16[8192,1024]{1,0:T(8,128)(2,1)} %refs_2_.75, bf16[256,1024]{1,0:T(8,128)(2,1)S(1)} %collective-permute-done.6.refs_3_, bf16[256,1024]{1,0:T(8,128)(2,1)S(1)} %collective-permute-done.7.refs_4_, ...), custom_call_target="tpu_custom_call" | custom-call | flops 536870912 | bytes 4194304 | tf_op jit(solution)/shard_map/pallas_call | solution.py:85
  147.8 7.1 %collective-permute-done.19 = bf16[512,128]{1,0:T(8,128)(2,1)S(1)} collective-permute-done((bf16[512,128]{1,0:T(8,128)(2,1)S(1)}, bf16[512,128]{1,0:T(8,128)(2,1)S(1)}, u32[]{:S(2)}, u32[]{:S(2)}) %collective-permute-start.19) | collective-permute-done | bytes 131104 | tf_op jit(solution)/shard_map/ppermute | solution.py:232
  157.0 4.5 %collective-permute-start.20 = (bf16[256,2048]{1,0:T(8,128)(2,1)S(1)}, bf16[256,2048]{1,0:T(8,128)(2,1)}, u32[]{:S(2)}, u32[]{:S(2)}) collective-permute-start(bf16[256,2048]{1,0:T(8,128)(2,1)S(1)} %shard_map.129.refs_3_), channel_id=1, source_target_pairs={{2,4},{3,5},{4,2},{5,3},{10,12},{11,13},{12,10},{13,11},{18,20},{1... | collective-permute-start | bytes 3145736 | tf_op jit(solution)/shard_map/ppermute | solution.py:236
  165.8 16.8 %collective-permute-done.29.refs_4_ = bf16[256,1024]{1,0:T(8,128)(2,1)S(1)} collective-permute-done((bf16[256,1024]{1,0:T(8,128)(2,1)S(1)}, bf16[256,1024]{1,0:T(8,128)(2,1)S(1)}, u32[]{:S(2)}, u32[]{:S(2)}) %collective-permute-start.29) | collective-permute-done | bytes 524320 | tf_op jit(solution)/shard_map/ppermute | solution.py:236
  188.5 4.1 %collective-permute-start.28 = (bf16[256,1024]{1,0:T(8,128)(2,1)}, bf16[256,1024]{1,0:T(8,128)(2,1)S(1)}, u32[]{:S(2)}, u32[]{:S(2)}) collective-permute-start(bf16[256,1024]{1,0:T(8,128)(2,1)} %copy-done.14), channel_id=1, source_target_pairs={{2,3},{3,2},{4,5},{5,4},{6,7},{7,6},{10,11},{11,10},{12,13},{13,12... | collective-permute-start | bytes 1572872 | tf_op jit(solution)/shard_map/ppermute | solution.py:232
  195.8 5.6 %shard_map.136.refs_5_ = bf16[256,2048]{1,0:T(8,128)(2,1)} custom-call(s32[2]{0:T(128)S(1)} %pad_add_fusion.14.refs_0_, bf16[1024,1024]{1,0:T(8,128)(2,1)S(1)} %copy-done.1, bf16[8192,1024]{1,0:T(8,128)(2,1)} %refs_2_.75, bf16[256,2048]{1,0:T(8,128)(2,1)} %collective-permute-done.3.refs_3_, bf16[256,1024]{1,0:T(8,128)(2,1)S(1)} %copy-done.20), custom_call_target="tpu_custom_call" | custom-call | flops 1073741824 | bytes 6815744 | tf_op jit(solution)/shard_map/pallas_call | solution.py:85
  201.3 3.5 %shard_map.137.refs_5_ = bf16[256,1024]{1,0:T(8,128)(2,1)} custom-call(s32[2]{0:T(128)S(1)} %pad_add_fusion.2.refs_0_, bf16[1024,1024]{1,0:T(8,128)(2,1)S(1)} %copy-done.1, bf16[8192,1024]{1,0:T(8,128)(2,1)} %refs_2_.75, bf16[256,1024]{1,0:T(8,128)(2,1)S(1)} %copy-done.37, bf16[256,1024]{1,0:T(8,128)(2,1)} %collective-permute-done.24.refs_4_, ...), custom_call_target="tpu_custom_call" | custom-call | flops 536870912 | bytes 4194304 | tf_op jit(solution)/shard_map/pallas_call | solution.py:85
  204.9 3.5 %shard_map.138.refs_4_ = bf16[256,1024]{1,0:T(8,128)(2,1)} custom-call(s32[2]{0:T(128)S(1)} %pad_add_fusion.2.refs_0_, bf16[1024,1024]{1,0:T(8,128)(2,1)S(1)} %copy-done.1, bf16[8192,1024]{1,0:T(8,128)(2,1)} %refs_2_.75, bf16[256,1024]{1,0:T(8,128)(2,1)S(1)} %copy-done.35, bf16[256,1024]{1,0:T(8,128)(2,1)} %collective-permute-done.22.refs_4_, ...), custom_call_target="tpu_custom_call" | custom-call | flops 536870912 | bytes 4194304 | tf_op jit(solution)/shard_map/pallas_call | solution.py:85
  208.4 3.9 %collective-permute-start.30 = (bf16[256,1024]{1,0:T(8,128)(2,1)}, bf16[256,1024]{1,0:T(8,128)(2,1)}, u32[]{:S(2)}, u32[]{:S(2)}) collective-permute-start(bf16[256,1024]{1,0:T(8,128)(2,1)} %shard_map.131.refs_3_), channel_id=1, source_target_pairs={{0,1},{1,0},{2,3},{3,2},{4,5},{5,4},{8,9},{9,8},{10,11},{11,10},{1... | collective-permute-start | bytes 1572872 | tf_op jit(solution)/shard_map/ppermute | solution.py:232
  214.2 5.6 %shard_map.139.refs_3_ = bf16[256,2048]{1,0:T(8,128)(2,1)} custom-call(s32[2]{0:T(128)S(1)} %pad_add_fusion.14.refs_0_, bf16[1024,1024]{1,0:T(8,128)(2,1)S(1)} %copy-done.1, bf16[8192,1024]{1,0:T(8,128)(2,1)} %refs_2_.75, bf16[256,2048]{1,0:T(8,128)(2,1)} %collective-permute-done.20.refs_3_, bf16[256,1024]{1,0:T(8,128)(2,1)} %shard_map.138.refs_4_), custom_call_target="tpu_custom_call" | custom-call | flops 1073741824 | bytes 6815744 | tf_op jit(solution)/shard_map/pallas_call | solution.py:85
  226.1 3.5 %shard_map.140.refs_3_ = bf16[256,1024]{1,0:T(8,128)(2,1)} custom-call(s32[2]{0:T(128)S(1)} %pad_add_fusion.17.refs_0_, bf16[1024,1024]{1,0:T(8,128)(2,1)S(1)} %copy-done.1, bf16[8192,1024]{1,0:T(8,128)(2,1)} %refs_2_.75, bf16[256,2048]{1,0:T(8,128)(2,1)} %shard_map.139.refs_3_), custom_call_target="tpu_custom_call" | custom-call | flops 536870912 | bytes 3145728 | tf_op jit(solution)/shard_map/pallas_call | solution.py:85
  234.2 2.8 shard_map.141.link
  237.1 5.4 %shard_map.142 = (f32[8,1024,128]{2,1,0:T(8,128)S(1)}, bf16[8,1024,128]{2,1,0:T(8,128)(2,1)}) custom-call(s32[8]{0:T(128)S(1)} %compare_select_fusion.1.slots, f32[8]{0:T(128)S(1)} %broadcast_4_scales.2.scales, bf16[1024,1024]{1,0:T(8,128)(2,1)S(1)} %copy-done.21, bf16[1024,128]{1,0:T(8,128)(2,1)S(1)} %fusion.right.refs_7_.refs_6_, ...), custom_call_target="tpu_custom_call" | custom-call | flops 268435456 | bytes 8650752 | tf_op jit(solution)/shard_map/pallas_call | solution.py:162
  244.7 7.4 %collective-permute-done.39.refs_6_ = bf16[256,1024]{1,0:T(8,128)(2,1)} collective-permute-done((bf16[256,1024]{1,0:T(8,128)(2,1)}, bf16[256,1024]{1,0:T(8,128)(2,1)}, u32[]{:S(2)}, u32[]{:S(2)}) %collective-permute-start.39) | collective-permute-done | bytes 524320 | tf_op jit(solution)/shard_map/ppermute | solution.py:236
  252.0 3.6 %collective-permute-start.38 = (bf16[256,1024]{1,0:T(8,128)(2,1)}, bf16[256,1024]{1,0:T(8,128)(2,1)}, u32[]{:S(2)}, u32[]{:S(2)}) collective-permute-start(bf16[256,1024]{1,0:T(8,128)(2,1)} %shard_map.138.refs_4_), channel_id=1, source_target_pairs={{0,2},{1,3},{2,4},{3,5},{8,10},{9,11},{10,12},{11,13},{16,18},{17,... | collective-permute-start | bytes 1572872 | tf_op jit(solution)/shard_map/ppermute | solution.py:236
  258.0 5.2 %collective-permute-start.26 = (bf16[256,1024]{1,0:T(8,128)(2,1)}, bf16[256,1024]{1,0:T(8,128)(2,1)}, u32[]{:S(2)}, u32[]{:S(2)}) collective-permute-start(bf16[256,1024]{1,0:T(8,128)(2,1)} %shard_map.137.refs_5_), channel_id=1, source_target_pairs={{0,2},{1,3},{2,4},{3,5},{8,10},{9,11},{10,12},{11,13},{16,18},{17,... | collective-permute-start | bytes 1572872 | tf_op jit(solution)/shard_map/ppermute | solution.py:236
  263.3 3.5 %shard_map.143.refs_4_ = bf16[256,1024]{1,0:T(8,128)(2,1)} custom-call(s32[2]{0:T(128)S(1)} %pad_add_fusion.17.refs_0_, bf16[1024,1024]{1,0:T(8,128)(2,1)S(1)} %copy-done.1, bf16[8192,1024]{1,0:T(8,128)(2,1)} %refs_2_.75, bf16[256,2048]{1,0:T(8,128)(2,1)} %collective-permute-done.11.refs_3_.refs_4_, bf16[8,1024,128]{2,1,0:T(8,128)(2,1)} %get-tuple-element.8.refs_4_), custom_call_target="tpu_custom_call" | custom-call | flops 536870912 | bytes 3670016 | tf_op jit(solution)/shard_map/pallas_call | solution.py:85
  266.9 3.5 %shard_map.144.refs_5_ = bf16[256,1024]{1,0:T(8,128)(2,1)} custom-call(s32[2]{0:T(128)S(1)} %pad_add_fusion.17.refs_0_, bf16[1024,1024]{1,0:T(8,128)(2,1)S(1)} %copy-done.1, bf16[8192,1024]{1,0:T(8,128)(2,1)} %refs_2_.75, bf16[256,2048]{1,0:T(8,128)(2,1)S(1)} %collective-permute-done.36.refs_3_.refs_4_, bf16[256,1024]{1,0:T(8,128)(2,1)} %shard_map.143.refs_4_), custom_call_target="tpu_custom_call" | custom-call | flops 536870912 | bytes 3670016 | tf_op jit(solution)/shard_map/pallas_call | solution.py:85
  270.3 2.9 shard_map.145.refs_5_
  273.3 3.5 %shard_map.146.refs_5_ = bf16[256,1024]{1,0:T(8,128)(2,1)} custom-call(s32[2]{0:T(128)S(1)} %pad_add_fusion.1.refs_0_, bf16[1024,1024]{1,0:T(8,128)(2,1)S(1)} %copy-done.1, bf16[8192,1024]{1,0:T(8,128)(2,1)} %refs_2_.75, bf16[256,1024]{1,0:T(8,128)(2,1)S(1)} %copy-done.33, bf16[256,1024]{1,0:T(8,128)(2,1)S(1)} %copy-done.31, ...), custom_call_target="tpu_custom_call" | custom-call | flops 536870912 | bytes 4194304 | tf_op jit(solution)/shard_map/pallas_call | solution.py:85
  282.2 2.9 shard_map.147.refs_5_
  285.1 3.1 shard_map.148.refs_10_
  289.9 4.0 %collective-permute-done.42.refs_5_ = bf16[256,1024]{1,0:T(8,128)(2,1)} collective-permute-done((bf16[256,1024]{1,0:T(8,128)(2,1)}, bf16[256,1024]{1,0:T(8,128)(2,1)}, u32[]{:S(2)}, u32[]{:S(2)}) %collective-permute-start.42) | collective-permute-done | bytes 524320 | tf_op jit(solution)/shard_map/ppermute | solution.py:236
  293.9 3.2 collective-permute-start.44
  299.0 4.2 %collective-permute-done.25.refs_3_ = bf16[256,1024]{1,0:T(8,128)(2,1)} collective-permute-done((bf16[256,1024]{1,0:T(8,128)(2,1)}, bf16[256,1024]{1,0:T(8,128)(2,1)}, u32[]{:S(2)}, u32[]{:S(2)}) %collective-permute-start.25) | collective-permute-done | bytes 524320 | tf_op jit(solution)/shard_map/ppermute | solution.py:232
  305.2 4.8 %convert_add_fusion = f32[8,128,1024]{2,1,0:T(8,128)} fusion(f32[8,128,1024]{2,1,0:T(8,128)S(1)} %copy-done.5, bf16[8,128,1024]{2,1,0:T(8,128)(2,1)} %collective-permute-done.47), kind=kLoop, calls=%fused_computation | loop fusion | flops 2097152 | bytes 10485760 | tf_op jit(solution)/shard_map/add | solution.py:375
  310.0 3.3 shard_map.149.refs_10_
  313.3 3.2 shard_map.150.refs_9_
  318.7 3.1 shard_map.151.refs_9_
  321.8 2.9 shard_map.152
  327.7 4.1 %convert_add_fusion.1 = f32[8,1024,128]{2,1,0:T(8,128)} fusion(f32[8,1024,128]{2,1,0:T(8,128)S(1)} %copy-done.7, bf16[8,1024,128]{2,1,0:T(8,128)(2,1)} %collective-permute-done.46), kind=kLoop, calls=%fused_computation.1 | loop fusion | flops 2097152 | bytes 10485760 | tf_op jit(solution)/shard_map/add | solution.py:375
  (208 shorter events, 116.8 us)
Async XLA Ops:
  7.0 83.4 %collective-permute-start = (bf16[256,2048]{1,0:T(8,128)(2,1)S(1)}, bf16[256,2048]{1,0:T(8,128)(2,1)}, u32[]{:S(2)}, u32[]{:S(2)}) collective-permute-start(bf16[256,2048]{1,0:T(8,128)(2,1)S(1)} %shard_map.112.refs_3_), channel_id=1, source_target_pairs={{0,2},{1,3},{6,4},{7,5},{8,10},{9,11},{14,12},{15,13},{16,18},{17,... | collective-permute-start | bytes 3145736 | tf_op jit(solution)/shard_map/ppermute | solution.py:236
  11.7 52.9 %collective-permute-start.2 = (bf16[256,1024]{1,0:T(8,128)(2,1)}, bf16[256,1024]{1,0:T(8,128)(2,1)}, u32[]{:S(2)}, u32[]{:S(2)}) collective-permute-start(bf16[256,1024]{1,0:T(8,128)(2,1)} %shard_map.113.refs_3_), channel_id=1, source_target_pairs={{0,1},{1,0},{6,7},{7,6},{8,9},{9,8},{14,15},{15,14},{16,17},{17,16... | collective-permute-start | bytes 1572872 | tf_op jit(solution)/shard_map/ppermute | solution.py:232
  16.6 51.7 %collective-permute-start.1 = (bf16[256,1024]{1,0:T(8,128)(2,1)}, bf16[256,1024]{1,0:T(8,128)(2,1)}, u32[]{:S(2)}, u32[]{:S(2)}) collective-permute-start(bf16[256,1024]{1,0:T(8,128)(2,1)} %shard_map.114.refs_3_), channel_id=1, source_target_pairs={{0,1},{1,0},{6,7},{7,6},{8,9},{9,8},{14,15},{15,14},{16,17},{17,16... | collective-permute-start | bytes 1572872 | tf_op jit(solution)/shard_map/ppermute | solution.py:232
  23.5 80.6 %collective-permute-start.8 = (bf16[256,2048]{1,0:T(8,128)(2,1)}, bf16[256,2048]{1,0:T(8,128)(2,1)}, u32[]{:S(2)}, u32[]{:S(2)}) collective-permute-start(bf16[256,2048]{1,0:T(8,128)(2,1)} %shard_map.115.refs_3_), channel_id=1, source_target_pairs={{0,2},{1,3},{6,4},{7,5},{8,10},{9,11},{14,12},{15,13},{16,18},{17,... | collective-permute-start | bytes 3145736 | tf_op jit(solution)/shard_map/ppermute | solution.py:236
  44.9 5.5 %collective-permute-start.12 = (bf16[512,128]{1,0:T(8,128)(2,1)}, bf16[512,128]{1,0:T(8,128)(2,1)}, u32[]{:S(2)}, u32[]{:S(2)}) collective-permute-start(bf16[512,128]{1,0:T(8,128)(2,1)} %constant_dynamic-slice_fusion), channel_id=1, source_target_pairs={{0,1},{1,0},{2,3},{3,2},{4,5},{5,4},{6,7},{7,6},{8,9},{9,8},{10,11... | collective-permute-start | bytes 393224 | tf_op jit(solution)/shard_map/ppermute | solution.py:232
  52.0 11.9 %collective-permute-start.14 = (bf16[512,128]{1,0:T(8,128)(2,1)}, bf16[512,128]{1,0:T(8,128)(2,1)}, u32[]{:S(2)}, u32[]{:S(2)}) collective-permute-start(bf16[512,128]{1,0:T(8,128)(2,1)} %add_convert_fusion.1), channel_id=1, source_target_pairs={{2,0},{3,1},{4,2},{5,3},{6,4},{7,5},{10,8},{11,9},{12,10},{13,11},... | collective-permute-start | bytes 393224 | tf_op jit(solution)/shard_map/ppermute | solution.py:236
  64.0 17.7 %collective-permute-start.9 = (bf16[256,1024]{1,0:T(8,128)(2,1)}, bf16[256,1024]{1,0:T(8,128)(2,1)S(1)}, u32[]{:S(2)}, u32[]{:S(2)}) collective-permute-start(bf16[256,1024]{1,0:T(8,128)(2,1)} %copy-done.16), channel_id=1, source_target_pairs={{0,1},{1,0},{6,7},{7,6},{8,9},{9,8},{14,15},{15,14},{16,17},{17,16... | collective-permute-start | bytes 1572872 | tf_op jit(solution)/shard_map/ppermute | solution.py:232
  64.7 25.2 %collective-permute-start.10 = (bf16[256,1024]{1,0:T(8,128)(2,1)}, bf16[256,1024]{1,0:T(8,128)(2,1)S(1)}, u32[]{:S(2)}, u32[]{:S(2)}) collective-permute-start(bf16[256,1024]{1,0:T(8,128)(2,1)} %copy-done.15), channel_id=1, source_target_pairs={{0,1},{1,0},{6,7},{7,6},{8,9},{9,8},{14,15},{15,14},{16,17},{17,16... | collective-permute-start | bytes 1572872 | tf_op jit(solution)/shard_map/ppermute | solution.py:232
  68.3 11.7 %collective-permute-start.13 = (bf16[512,128]{1,0:T(8,128)(2,1)}, bf16[512,128]{1,0:T(8,128)(2,1)S(1)}, u32[]{:S(2)}, u32[]{:S(2)}) collective-permute-start(bf16[512,128]{1,0:T(8,128)(2,1)} %add_convert_fusion.1), channel_id=1, source_target_pairs={{0,2},{1,3},{2,4},{3,5},{4,6},{5,7},{8,10},{9,11},{10,12},{11,13},... | collective-permute-start | bytes 393224 | tf_op jit(solution)/shard_map/ppermute | solution.py:236
  80.0 51.7 %collective-permute-start.6 = (bf16[256,1024]{1,0:T(8,128)(2,1)S(1)}, bf16[256,1024]{1,0:T(8,128)(2,1)S(1)}, u32[]{:S(2)}, u32[]{:S(2)}) collective-permute-start(bf16[256,1024]{1,0:T(8,128)(2,1)S(1)} %copy-done.12), channel_id=1, source_target_pairs={{0,1},{1,0},{2,3},{3,2},{4,5},{5,4},{6,7},{7,6},{8,9},{9,8},{10,11... | collective-permute-start | bytes 1572872 | tf_op jit(solution)/shard_map/ppermute | solution.py:232
  81.6 50.9 %collective-permute-start.7 = (bf16[256,1024]{1,0:T(8,128)(2,1)S(1)}, bf16[256,1024]{1,0:T(8,128)(2,1)S(1)}, u32[]{:S(2)}, u32[]{:S(2)}) collective-permute-start(bf16[256,1024]{1,0:T(8,128)(2,1)S(1)} %shard_map.121.refs_4_), channel_id=1, source_target_pairs={{0,2},{1,3},{6,4},{7,5},{8,10},{9,11},{14,12},{15,13},{16,18},{17,... | collective-permute-start | bytes 1572872 | tf_op jit(solution)/shard_map/ppermute | solution.py:236
  89.8 47.0 %collective-permute-start.4 = (bf16[256,1024]{1,0:T(8,128)(2,1)S(1)}, bf16[256,1024]{1,0:T(8,128)(2,1)S(1)}, u32[]{:S(2)}, u32[]{:S(2)}) collective-permute-start(bf16[256,1024]{1,0:T(8,128)(2,1)S(1)} %copy-done.10), channel_id=1, source_target_pairs={{0,1},{1,0},{2,3},{3,2},{4,5},{5,4},{6,7},{7,6},{8,9},{9,8},{10,11... | collective-permute-start | bytes 1572872 | tf_op jit(solution)/shard_map/ppermute | solution.py:232
  90.3 47.8 %collective-permute-start.5 = (bf16[256,1024]{1,0:T(8,128)(2,1)S(1)}, bf16[256,1024]{1,0:T(8,128)(2,1)S(1)}, u32[]{:S(2)}, u32[]{:S(2)}) collective-permute-start(bf16[256,1024]{1,0:T(8,128)(2,1)S(1)} %shard_map.122.refs_3_), channel_id=1, source_target_pairs={{0,2},{1,3},{6,4},{7,5},{8,10},{9,11},{14,12},{15,13},{16,18},{17,... | collective-permute-start | bytes 1572872 | tf_op jit(solution)/shard_map/ppermute | solution.py:236
  104.1 15.9 %collective-permute-start.16 = (bf16[512,128]{1,0:T(8,128)(2,1)}, bf16[512,128]{1,0:T(8,128)(2,1)S(1)}, u32[]{:S(2)}, u32[]{:S(2)}) collective-permute-start(bf16[512,128]{1,0:T(8,128)(2,1)} %collective-permute-done.14), channel_id=1, source_target_pairs={{2,0},{3,1},{4,2},{5,3},{10,8},{11,9},{12,10},{13,11},{18,16},{19,... | collective-permute-start | bytes 393224 | tf_op jit(solution)/shard_map/ppermute | solution.py:236
  120.0 10.4 %collective-permute-start.15 = (bf16[512,128]{1,0:T(8,128)(2,1)S(1)}, bf16[512,128]{1,0:T(8,128)(2,1)S(1)}, u32[]{:S(2)}, u32[]{:S(2)}) collective-permute-start(bf16[512,128]{1,0:T(8,128)(2,1)S(1)} %collective-permute-done.13), channel_id=1, source_target_pairs={{2,4},{3,5},{4,6},{5,7},{10,12},{11,13},{12,14},{13,15},{18,20},{1... | collective-permute-start | bytes 393224 | tf_op jit(solution)/shard_map/ppermute | solution.py:236
  130.4 12.8 %collective-permute-start.18 = (bf16[512,128]{1,0:T(8,128)(2,1)S(1)}, bf16[512,128]{1,0:T(8,128)(2,1)S(1)}, u32[]{:S(2)}, u32[]{:S(2)}) collective-permute-start(bf16[512,128]{1,0:T(8,128)(2,1)S(1)} %collective-permute-done.16), channel_id=1, source_target_pairs={{2,0},{3,1},{10,8},{11,9},{18,16},{19,17},{26,24},{27,25}} | collective-permute-start | bytes 393224 | tf_op jit(solution)/shard_map/ppermute | solution.py:236
  131.7 13.4 %collective-permute-start.17 = (bf16[512,128]{1,0:T(8,128)(2,1)S(1)}, bf16[512,128]{1,0:T(8,128)(2,1)S(1)}, u32[]{:S(2)}, u32[]{:S(2)}) collective-permute-start(bf16[512,128]{1,0:T(8,128)(2,1)S(1)} %collective-permute-done.15), channel_id=1, source_target_pairs={{4,6},{5,7},{12,14},{13,15},{20,22},{21,23},{28,30},{29,31}} | collective-permute-start | bytes 393224 | tf_op jit(solution)/shard_map/ppermute | solution.py:236
  132.6 23.7 %collective-permute-start.21 = (bf16[256,1024]{1,0:T(8,128)(2,1)S(1)}, bf16[256,1024]{1,0:T(8,128)(2,1)S(1)}, u32[]{:S(2)}, u32[]{:S(2)}) collective-permute-start(bf16[256,1024]{1,0:T(8,128)(2,1)S(1)} %shard_map.124.link), channel_id=1, source_target_pairs={{0,1},{1,0},{2,3},{3,2},{4,5},{5,4},{6,7},{7,6},{8,9},{9,8},{10,11... | collective-permute-start | bytes 1572872 | tf_op jit(solution)/shard_map/ppermute | solution.py:232
  136.8 24.8 %collective-permute-start.23 = (bf16[256,1024]{1,0:T(8,128)(2,1)S(1)}, bf16[256,1024]{1,0:T(8,128)(2,1)S(1)}, u32[]{:S(2)}, u32[]{:S(2)}) collective-permute-start(bf16[256,1024]{1,0:T(8,128)(2,1)S(1)} %shard_map.123.refs_3_), channel_id=1, source_target_pairs={{0,1},{1,0},{2,3},{3,2},{4,5},{5,4},{6,7},{7,6},{8,9},{9,8},{10,11... | collective-permute-start | bytes 1572872 | tf_op jit(solution)/shard_map/ppermute | solution.py:232
  141.0 22.7 %collective-permute-start.31 = (bf16[256,1024]{1,0:T(8,128)(2,1)S(1)}, bf16[256,1024]{1,0:T(8,128)(2,1)S(1)}, u32[]{:S(2)}, u32[]{:S(2)}) collective-permute-start(bf16[256,1024]{1,0:T(8,128)(2,1)S(1)} %shard_map.135.refs_4_), channel_id=1, source_target_pairs={{0,2},{1,3},{2,4},{3,5},{8,10},{9,11},{10,12},{11,13},{16,18},{17,... | collective-permute-start | bytes 1572872 | tf_op jit(solution)/shard_map/ppermute | solution.py:236
  143.2 49.5 %collective-permute-start.3 = (bf16[256,2048]{1,0:T(8,128)(2,1)}, bf16[256,2048]{1,0:T(8,128)(2,1)}, u32[]{:S(2)}, u32[]{:S(2)}) collective-permute-start(bf16[256,2048]{1,0:T(8,128)(2,1)} %shard_map.126.refs_4_), channel_id=1, source_target_pairs={{2,4},{3,5},{4,2},{5,3},{10,12},{11,13},{12,10},{13,11},{18,20},{1... | collective-permute-start | bytes 3145736 | tf_op jit(solution)/shard_map/ppermute | solution.py:236
  146.2 8.7 %collective-permute-start.19 = (bf16[512,128]{1,0:T(8,128)(2,1)S(1)}, bf16[512,128]{1,0:T(8,128)(2,1)S(1)}, u32[]{:S(2)}, u32[]{:S(2)}) collective-permute-start(bf16[512,128]{1,0:T(8,128)(2,1)S(1)} %add_convert_fusion), channel_id=1, source_target_pairs={{0,1},{1,0},{2,3},{3,2},{4,5},{5,4},{6,7},{7,6},{8,9},{9,8},{10,11... | collective-permute-start | bytes 393224 | tf_op jit(solution)/shard_map/ppermute | solution.py:232
  154.9 27.7 %collective-permute-start.29 = (bf16[256,1024]{1,0:T(8,128)(2,1)S(1)}, bf16[256,1024]{1,0:T(8,128)(2,1)S(1)}, u32[]{:S(2)}, u32[]{:S(2)}) collective-permute-start(bf16[256,1024]{1,0:T(8,128)(2,1)S(1)} %shard_map.135.refs_4_), channel_id=1, source_target_pairs={{4,2},{5,3},{6,4},{7,5},{12,10},{13,11},{14,12},{15,13},{20,18},{2... | collective-permute-start | bytes 1572872 | tf_op jit(solution)/shard_map/ppermute | solution.py:236
  157.0 55.3 %collective-permute-start.20 = (bf16[256,2048]{1,0:T(8,128)(2,1)S(1)}, bf16[256,2048]{1,0:T(8,128)(2,1)}, u32[]{:S(2)}, u32[]{:S(2)}) collective-permute-start(bf16[256,2048]{1,0:T(8,128)(2,1)S(1)} %shard_map.129.refs_3_), channel_id=1, source_target_pairs={{2,4},{3,5},{4,2},{5,3},{10,12},{11,13},{12,10},{13,11},{18,20},{1... | collective-permute-start | bytes 3145736 | tf_op jit(solution)/shard_map/ppermute | solution.py:236
  162.4 23.0 %collective-permute-start.22 = (bf16[256,1024]{1,0:T(8,128)(2,1)}, bf16[256,1024]{1,0:T(8,128)(2,1)}, u32[]{:S(2)}, u32[]{:S(2)}) collective-permute-start(bf16[256,1024]{1,0:T(8,128)(2,1)} %shard_map.128.refs_4_), channel_id=1, source_target_pairs={{0,2},{1,3},{6,4},{7,5},{8,10},{9,11},{14,12},{15,13},{16,18},{17,... | collective-permute-start | bytes 1572872 | tf_op jit(solution)/shard_map/ppermute | solution.py:236
  164.5 24.0 %collective-permute-start.24 = (bf16[256,1024]{1,0:T(8,128)(2,1)}, bf16[256,1024]{1,0:T(8,128)(2,1)}, u32[]{:S(2)}, u32[]{:S(2)}) collective-permute-start(bf16[256,1024]{1,0:T(8,128)(2,1)} %shard_map.127.refs_4_), channel_id=1, source_target_pairs={{0,2},{1,3},{6,4},{7,5},{8,10},{9,11},{14,12},{15,13},{16,18},{17,... | collective-permute-start | bytes 1572872 | tf_op jit(solution)/shard_map/ppermute | solution.py:236
  183.4 25.0 %collective-permute-start.35 = (bf16[256,1024]{1,0:T(8,128)(2,1)}, bf16[256,1024]{1,0:T(8,128)(2,1)}, u32[]{:S(2)}, u32[]{:S(2)}) collective-permute-start(bf16[256,1024]{1,0:T(8,128)(2,1)} %shard_map.134.refs_5_), channel_id=1, source_target_pairs={{0,2},{1,3},{2,4},{3,5},{8,10},{9,11},{10,12},{11,13},{16,18},{17,... | collective-permute-start | bytes 1572872 | tf_op jit(solution)/shard_map/ppermute | solution.py:236
  185.4 34.5 %collective-permute-start.33 = (bf16[256,1024]{1,0:T(8,128)(2,1)}, bf16[256,1024]{1,0:T(8,128)(2,1)S(1)}, u32[]{:S(2)}, u32[]{:S(2)}) collective-permute-start(bf16[256,1024]{1,0:T(8,128)(2,1)} %shard_map.134.refs_5_), channel_id=1, source_target_pairs={{4,2},{5,3},{6,4},{7,5},{12,10},{13,11},{14,12},{15,13},{20,18},{2... | collective-permute-start | bytes 1572872 | tf_op jit(solution)/shard_map/ppermute | solution.py:236
  188.5 33.5 %collective-permute-start.28 = (bf16[256,1024]{1,0:T(8,128)(2,1)}, bf16[256,1024]{1,0:T(8,128)(2,1)S(1)}, u32[]{:S(2)}, u32[]{:S(2)}) collective-permute-start(bf16[256,1024]{1,0:T(8,128)(2,1)} %copy-done.14), channel_id=1, source_target_pairs={{2,3},{3,2},{4,5},{5,4},{6,7},{7,6},{10,11},{11,10},{12,13},{13,12... | collective-permute-start | bytes 1572872 | tf_op jit(solution)/shard_map/ppermute | solution.py:232
  192.7 32.5 %collective-permute-start.32 = (bf16[256,1024]{1,0:T(8,128)(2,1)}, bf16[256,1024]{1,0:T(8,128)(2,1)S(1)}, u32[]{:S(2)}, u32[]{:S(2)}) collective-permute-start(bf16[256,1024]{1,0:T(8,128)(2,1)} %copy-done.13), channel_id=1, source_target_pairs={{2,3},{3,2},{4,5},{5,4},{6,7},{7,6},{10,11},{11,10},{12,13},{13,12... | collective-permute-start | bytes 1572872 | tf_op jit(solution)/shard_map/ppermute | solution.py:232
  208.4 21.2 %collective-permute-start.30 = (bf16[256,1024]{1,0:T(8,128)(2,1)}, bf16[256,1024]{1,0:T(8,128)(2,1)}, u32[]{:S(2)}, u32[]{:S(2)}) collective-permute-start(bf16[256,1024]{1,0:T(8,128)(2,1)} %shard_map.131.refs_3_), channel_id=1, source_target_pairs={{0,1},{1,0},{2,3},{3,2},{4,5},{5,4},{8,9},{9,8},{10,11},{11,10},{1... | collective-permute-start | bytes 1572872 | tf_op jit(solution)/shard_map/ppermute | solution.py:232
  212.3 19.3 %collective-permute-start.34 = (bf16[256,1024]{1,0:T(8,128)(2,1)}, bf16[256,1024]{1,0:T(8,128)(2,1)}, u32[]{:S(2)}, u32[]{:S(2)}) collective-permute-start(bf16[256,1024]{1,0:T(8,128)(2,1)} %shard_map.130.refs_3_), channel_id=1, source_target_pairs={{0,1},{1,0},{2,3},{3,2},{4,5},{5,4},{8,9},{9,8},{10,11},{11,10},{1... | collective-permute-start | bytes 1572872 | tf_op jit(solution)/shard_map/ppermute | solution.py:232
  220.7 35.0 %collective-permute-start.36 = (bf16[256,2048]{1,0:T(8,128)(2,1)}, bf16[256,2048]{1,0:T(8,128)(2,1)S(1)}, u32[]{:S(2)}, u32[]{:S(2)}) collective-permute-start(bf16[256,2048]{1,0:T(8,128)(2,1)} %shard_map.139.refs_3_), channel_id=1, source_target_pairs={{4,6},{5,7},{2,0},{3,1},{12,14},{13,15},{10,8},{11,9},{20,22},{21,... | collective-permute-start | bytes 3145736 | tf_op jit(solution)/shard_map/ppermute | solution.py:236
  222.8 35.2 %collective-permute-start.11 = (bf16[256,2048]{1,0:T(8,128)(2,1)}, bf16[256,2048]{1,0:T(8,128)(2,1)}, u32[]{:S(2)}, u32[]{:S(2)}) collective-permute-start(bf16[256,2048]{1,0:T(8,128)(2,1)} %shard_map.136.refs_5_), channel_id=1, source_target_pairs={{4,6},{5,7},{2,0},{3,1},{12,14},{13,15},{10,8},{11,9},{20,22},{21,... | collective-permute-start | bytes 3145736 | tf_op jit(solution)/shard_map/ppermute | solution.py:236
  226.0 62.2 %collective-permute-start.47 = (bf16[8,128,1024]{2,1,0:T(8,128)(2,1)}, bf16[8,128,1024]{2,1,0:T(8,128)(2,1)}, u32[]{:S(2)}, u32[]{:S(2)}) collective-permute-start(bf16[8,128,1024]{2,1,0:T(8,128)(2,1)} %get-tuple-element.7.refs_4_), channel_id=1, source_target_pairs={{0,8},{8,0},{1,9},{9,1},{2,10},{10,2},{3,11},{11,3},{4,12},{12,4},... | collective-permute-start | bytes 6291464 | tf_op jit(solution)/shard_map/ppermute | solution.py:375
  229.6 14.9 %collective-permute-start.40 = (bf16[256,1024]{1,0:T(8,128)(2,1)}, bf16[256,1024]{1,0:T(8,128)(2,1)}, u32[]{:S(2)}, u32[]{:S(2)}) collective-permute-start(bf16[256,1024]{1,0:T(8,128)(2,1)} %shard_map.140.refs_3_), channel_id=1, source_target_pairs={{0,1},{1,0},{2,3},{3,2},{4,5},{5,4},{6,7},{7,6},{8,9},{9,8},{10,11... | collective-permute-start | bytes 1572872 | tf_op jit(solution)/shard_map/ppermute | solution.py:232
  231.6 20.4 %collective-permute-start.39 = (bf16[256,1024]{1,0:T(8,128)(2,1)}, bf16[256,1024]{1,0:T(8,128)(2,1)}, u32[]{:S(2)}, u32[]{:S(2)}) collective-permute-start(bf16[256,1024]{1,0:T(8,128)(2,1)} %shard_map.138.refs_4_), channel_id=1, source_target_pairs={{4,2},{5,3},{6,4},{7,5},{12,10},{13,11},{14,12},{15,13},{20,18},{2... | collective-permute-start | bytes 1572872 | tf_op jit(solution)/shard_map/ppermute | solution.py:236
  244.5 81.8 %collective-permute-start.46 = (bf16[8,1024,128]{2,1,0:T(8,128)(2,1)}, bf16[8,1024,128]{2,1,0:T(8,128)(2,1)}, u32[]{:S(2)}, u32[]{:S(2)}) collective-permute-start(bf16[8,1024,128]{2,1,0:T(8,128)(2,1)} %get-tuple-element.8.refs_4_), channel_id=1, source_target_pairs={{0,8},{8,0},{1,9},{9,1},{2,10},{10,2},{3,11},{11,3},{4,12},{12,4},... | collective-permute-start | bytes 6291464 | tf_op jit(solution)/shard_map/ppermute | solution.py:375
  252.0 24.8 %collective-permute-start.38 = (bf16[256,1024]{1,0:T(8,128)(2,1)}, bf16[256,1024]{1,0:T(8,128)(2,1)}, u32[]{:S(2)}, u32[]{:S(2)}) collective-permute-start(bf16[256,1024]{1,0:T(8,128)(2,1)} %shard_map.138.refs_4_), channel_id=1, source_target_pairs={{0,2},{1,3},{2,4},{3,5},{8,10},{9,11},{10,12},{11,13},{16,18},{17,... | collective-permute-start | bytes 1572872 | tf_op jit(solution)/shard_map/ppermute | solution.py:236
  255.7 22.8 %collective-permute-start.27 = (bf16[256,1024]{1,0:T(8,128)(2,1)}, bf16[256,1024]{1,0:T(8,128)(2,1)}, u32[]{:S(2)}, u32[]{:S(2)}) collective-permute-start(bf16[256,1024]{1,0:T(8,128)(2,1)} %shard_map.137.refs_5_), channel_id=1, source_target_pairs={{4,2},{5,3},{6,4},{7,5},{12,10},{13,11},{14,12},{15,13},{20,18},{2... | collective-permute-start | bytes 1572872 | tf_op jit(solution)/shard_map/ppermute | solution.py:236
  258.0 21.0 %collective-permute-start.26 = (bf16[256,1024]{1,0:T(8,128)(2,1)}, bf16[256,1024]{1,0:T(8,128)(2,1)}, u32[]{:S(2)}, u32[]{:S(2)}) collective-permute-start(bf16[256,1024]{1,0:T(8,128)(2,1)} %shard_map.137.refs_5_), channel_id=1, source_target_pairs={{0,2},{1,3},{2,4},{3,5},{8,10},{9,11},{10,12},{11,13},{16,18},{17,... | collective-permute-start | bytes 1572872 | tf_op jit(solution)/shard_map/ppermute | solution.py:236
  276.8 20.3 %collective-permute-start.37 = (bf16[256,1024]{1,0:T(8,128)(2,1)}, bf16[256,1024]{1,0:T(8,128)(2,1)}, u32[]{:S(2)}, u32[]{:S(2)}) collective-permute-start(bf16[256,1024]{1,0:T(8,128)(2,1)} %shard_map.144.refs_5_), channel_id=1, source_target_pairs={{0,1},{1,0},{2,3},{3,2},{4,5},{5,4},{6,7},{7,6},{8,9},{9,8},{10,11... | collective-permute-start | bytes 1572872 | tf_op jit(solution)/shard_map/ppermute | solution.py:232
  278.5 24.7 %collective-permute-start.25 = (bf16[256,1024]{1,0:T(8,128)(2,1)}, bf16[256,1024]{1,0:T(8,128)(2,1)}, u32[]{:S(2)}, u32[]{:S(2)}) collective-permute-start(bf16[256,1024]{1,0:T(8,128)(2,1)} %shard_map.143.refs_4_), channel_id=1, source_target_pairs={{0,1},{1,0},{2,3},{3,2},{4,5},{5,4},{6,7},{7,6},{8,9},{9,8},{10,11... | collective-permute-start | bytes 1572872 | tf_op jit(solution)/shard_map/ppermute | solution.py:232
  279.0 14.9 %collective-permute-start.42 = (bf16[256,1024]{1,0:T(8,128)(2,1)}, bf16[256,1024]{1,0:T(8,128)(2,1)}, u32[]{:S(2)}, u32[]{:S(2)}) collective-permute-start(bf16[256,1024]{1,0:T(8,128)(2,1)} %shard_map.146.refs_5_), channel_id=1, source_target_pairs={{2,0},{3,1},{4,2},{5,3},{6,4},{7,5},{10,8},{11,9},{12,10},{13,11},... | collective-permute-start | bytes 1572872 | tf_op jit(solution)/shard_map/ppermute | solution.py:236
  288.3 33.5 %collective-permute-start.43 = (bf16[256,1024]{1,0:T(8,128)(2,1)S(1)}, bf16[256,1024]{1,0:T(8,128)(2,1)S(1)}, u32[]{:S(2)}, u32[]{:S(2)}) collective-permute-start(bf16[256,1024]{1,0:T(8,128)(2,1)S(1)} %copy-done.23), channel_id=1, source_target_pairs={{0,1},{1,0},{2,3},{3,2},{4,5},{5,4},{6,7},{7,6},{8,9},{9,8},{10,11... | collective-permute-start | bytes 1572872 | tf_op jit(solution)/shard_map/ppermute | solution.py:232
  293.9 27.9 %collective-permute-start.44 = (bf16[256,1024]{1,0:T(8,128)(2,1)S(1)}, bf16[256,1024]{1,0:T(8,128)(2,1)S(1)}, u32[]{:S(2)}, u32[]{:S(2)}) collective-permute-start(bf16[256,1024]{1,0:T(8,128)(2,1)S(1)} %shard_map.147.refs_5_), channel_id=1, source_target_pairs={{0,2},{1,3},{2,4},{3,5},{4,6},{5,7},{8,10},{9,11},{10,12},{11,13},... | collective-permute-start | bytes 1572872 | tf_op jit(solution)/shard_map/ppermute | solution.py:236
  297.1 21.6 %collective-permute-start.41 = (bf16[256,1024]{1,0:T(8,128)(2,1)S(1)}, bf16[256,1024]{1,0:T(8,128)(2,1)S(1)}, u32[]{:S(2)}, u32[]{:S(2)}) collective-permute-start(bf16[256,1024]{1,0:T(8,128)(2,1)S(1)} %copy-done.18), channel_id=1, source_target_pairs={{0,2},{1,3},{2,4},{3,5},{4,6},{5,7},{8,10},{9,11},{10,12},{11,13},... | collective-permute-start | bytes 1572872 | tf_op jit(solution)/shard_map/ppermute | solution.py:236
  303.2 18.6 %collective-permute-start.45 = (bf16[256,1024]{1,0:T(8,128)(2,1)S(1)}, bf16[256,1024]{1,0:T(8,128)(2,1)S(1)}, u32[]{:S(2)}, u32[]{:S(2)}) collective-permute-start(bf16[256,1024]{1,0:T(8,128)(2,1)S(1)} %shard_map.148.refs_10_), channel_id=1, source_target_pairs={{2,0},{3,1},{4,2},{5,3},{6,4},{7,5},{10,8},{11,9},{12,10},{13,11},... | collective-permute-start | bytes 1572872 | tf_op jit(solution)/shard_map/ppermute | solution.py:236
  (43 other events, 278.6 us)

commit v2 on v1

--- a/solution.py
+++ b/solution.py
@@ -14,13 +14,14 @@
 contract_last = (((1,), (1,)), ((), ()))
 contract_first = (((0,), (0,)), ((), ()))
 vmem_bytes = 40 * 1024 * 1024
+declared = pl.CostEstimate(flops=10**12, bytes_accessed=10**9, transcendentals=0)
 
 
 def params():
     return pltpu.CompilerParams(vmem_limit_bytes=vmem_bytes)
 
 
-def product_kernel(add_count, block_count, has_link, *refs):
+def product_kernel(add_count, block_count, *refs):
     position = 1
     rows, weights = refs[1], refs[2]
     position = 3
@@ -79,11 +80,11 @@
                 pl.BlockSpec((1, tile, rank), functools.partial(lambda j, s, i: (s[2 + i], j, 0), i=i))
             )
             operands.append(shrink)
-    if link is not None:
+    for array in link:
         in_specs.append(pl.BlockSpec(memory_space=pl.ANY))
-        operands.append(link)
+        operands.append(array)
     return pl.pallas_call(
-        functools.partial(product_kernel, len(adds), block_count, link is not None),
+        functools.partial(product_kernel, len(adds), block_count),
         grid_spec=pltpu.PrefetchScalarGridSpec(
             num_scalar_prefetch=1,
             grid=(steps,),
@@ -92,11 +93,7 @@
         ),
         out_shape=jax.ShapeDtypeStruct((piece_rows, width), bf16),
         compiler_params=params(),
-        cost_estimate=pl.CostEstimate(
-            flops=2 * piece_rows * width * depth,
-            bytes_accessed=2 * (width * depth + piece_rows * depth + (1 + len(adds)) * piece_rows * width),
-            transcendentals=0,
-        ),
+        cost_estimate=declared,
     )(scalars, *operands)
 
 
@@ -124,11 +121,7 @@
         ),
         out_shape=jax.ShapeDtypeStruct((count_of_rows, rank), bf16),
         compiler_params=params(),
-        cost_estimate=pl.CostEstimate(
-            flops=2 * count_of_rows * rank * depth,
-            bytes_accessed=2 * (count_of_rows * depth + blocks * rank * depth),
-            transcendentals=0,
-        ),
+        cost_estimate=declared,
     )(tenants, gradient, expand, link)
 
 
@@ -175,13 +168,7 @@
         ],
         scratch_shapes=[pltpu.VMEM((others, height, width), f32)],
         compiler_params=params(),
-        cost_estimate=pl.CostEstimate(
-            flops=2 * count_of_rows * height * width,
-            bytes_accessed=2 * count_of_rows * (height + width)
-            + 4 * slots_each * height * width
-            + 2 * others * height * width,
-            transcendentals=0,
-        ),
+        cost_estimate=declared,
     )(slots, scales, left, right, link)
 
 
@@ -209,20 +196,20 @@
     side = place % 2
     owner = lax.axis_index("dp")
 
-    halves = 2 if nodes <= 4 else 1
+    halves = 1
     pieces = 2 * halves
     piece_rows = count_of_rows // pieces
     lower = list(range(halves))
     upper = list(range(halves, pieces))
 
-    link = [None]
+    link = []
 
     def run(scalars, piece, columns, adds, adapter=None):
         out = product(
             jnp.stack([jnp.asarray(v, jnp.int32) for v in scalars]),
-            gradient, weights, piece, piece_rows, columns, adds, link[0], adapter,
+            gradient, weights, piece, piece_rows, columns, adds, link, adapter,
         )
-        link[0] = out
+        link[:] = [out]
         return out
 
     def swap(x, active):
@@ -328,39 +315,29 @@
     slots_each = tenants // owner_count
     own_first = lax.rem(block_slot - owner * slots_each + tenants, tenants)
 
+    own_swap = {}
+
+    def swap_own(p):
+        adds = [(direct.arrived[p], True)] if p in lower else []
+        part = run([node * 2 + (1 - side), 1 - side], p, width, adds)
+        own_swap[p] = swap(part, range(nodes))
+
     direct.advance(0, lower[0])
     up_flow.swap(0)
-    for p in lower[1:]:
-        direct.advance(0, p)
     low_flow.swap(1)
     up_flow.swap(1)
+    low_flow.swap(2)
 
     low_part = low_product(tenant_per_block, gradient, expand, link[0])
-    link[0] = low_part
-    half = count_of_rows // 2
-    keep = lax.dynamic_slice_in_dim(low_part, side * half, half, 0)
-    give = lax.dynamic_slice_in_dim(low_part, (1 - side) * half, half, 0)
-    low_half = (keep.astype(f32) + swap(give, range(nodes)).astype(f32)).astype(bf16)
-    low_sum = low_half.astype(f32)
-    going_right = going_left = low_half
-    for hop in range(1, nodes):
-        going_right = along(going_right, [(z, z + 1) for z in range(hop - 1, last)])
-        going_left = along(going_left, [(z, z - 1) for z in range(1, nodes - hop + 1)])
-        low_sum = low_sum + going_right.astype(f32) + going_left.astype(f32)
-    low_mine = low_sum.astype(bf16)
-    low_other = swap(low_mine, range(nodes))
-    low_whole = jnp.where(
-        side == 0,
-        jnp.concatenate([low_mine, low_other], axis=0),
-        jnp.concatenate([low_other, low_mine], axis=0),
-    )
+    link[:] = [low_part]
+    low_whole = lax.psum(low_part, "tensor")
     factor = scale_per_block[:, None, None] * block_mask[:, None, :]
     low = (low_whole.astype(f32).reshape(blocks, row_block, rank_extent) * factor).astype(bf16)
     low = low.reshape(count_of_rows, rank_extent)
 
     for p in upper:
         up_flow.combine(0, p)
-    low_flow.swap(2)
+    up_flow.swap(2)
 
     masked = saved_lowrank.reshape(blocks, row_block, rank_extent) * block_mask[:, None, :].astype(bf16)
     masked = masked.reshape(count_of_rows, rank_extent)
@@ -378,40 +355,35 @@
     own, other = factor_sums(
         own_first, scale_per_block, masked, gradient, slots_each, others, link[0]
     )
-    link[0] = other
+    link[:] = [other]
     grad_expand = exchange(own, other)
 
-    own_swap = {}
-
-    def swap_own(p):
-        adds = [(direct.arrived[p], True)] if p in lower else []
-        part = run([node * 2 + (1 - side), 1 - side], p, width, adds)
-        own_swap[p] = swap(part, range(nodes))
-
-    grad_shrink = None
     for step in range(1, last):
         direct.advance(step, lower[0])
-        low_flow.combine(step, lower[0])
-        for p in lower[1:]:
+        for p in lower:
             low_flow.combine(step, p)
-            direct.advance(step, p)
-        up_flow.swap(step + 1)
+        up_flow.swap(step + 2)
         low_flow.swap(step + 2)
         if step == last - 1:
             for p in upper:
                 swap_own(p)
-            own, other = factor_sums(
-                own_first, ones, projection_input, low, slots_each, others, link[0]
-            )
-            link[0] = other
-            grad_shrink = exchange(own, other)
-            for p in lower:
-                swap_own(p)
         for p in upper:
             up_flow.combine(step, p)
-
-    outs = []
-    for p in range(pieces):
+    own, other = factor_sums(
+        own_first, ones, projection_input, low, slots_each, others, link[0]
+    )
+    link[:] = [other]
+    grad_shrink = exchange(own, other)
+    link.append(grad_expand)
+    link += [own_swap[p] for p in upper]
+    for p in lower:
+        link += [a for a in low_flow.arrived[p]]
+    for p in lower:
+        swap_own(p)
+    link.append(grad_shrink)
+
+    outs = {}
+    for p in upper + lower:
         flow = low_flow if p in lower else up_flow
         adds = [(own_swap[p], False)]
         if p in lower:
@@ -422,8 +394,8 @@
             adds.append((arrived[1], False))
         in_piece = piece_rows // row_block
         ids = [tenant_per_block[p * in_piece + i] for i in range(in_piece)]
-        outs.append(run([node * 2 + side, side] + ids, p, width, adds, (low, shrink)))
-    input_gradient = jnp.concatenate(outs, axis=0)
+        outs[p] = run([node * 2 + side, side] + ids, p, width, adds, (low, shrink))
+    input_gradient = jnp.concatenate([outs[p] for p in range(pieces)], axis=0)
     return (input_gradient, grad_shrink, grad_expand)
 
 

time: 335 us -> 309 us (0.922)
  waiting for transfers between devices: 50.2 us -> 122 us
  starting transfers between devices: 97.5 us -> 41.5 us
  Pallas kernels: 144 us -> 102 us
  local copies, waits for them, and re-layouts: 21.3 us -> 8 us
  between operations: 1.71 us -> 14.4 us
    psum x0 -> x1, waiting for transfers between devices: none -> 64.5 us  [per_device(): low_whole = lax.psum(low_part, 'tensor')]
    pallas_call x38 -> x19, Pallas kernels: 132 us -> 87.3 us  [product(): pl.pallas_call(functools.partial(product_kernel, len(adds), block_count),...]
    ppermute x28 -> x11, starting transfers between devices: 68.4 us -> 28.2 us  [along(): return lax.ppermute(x, 'tensor', pairs)]
    ppermute x28 -> x11, waiting for transfers between devices: 35.4 us -> 53.8 us  [along(): return lax.ppermute(x, 'tensor', pairs)]
    ppermute x18 -> x8, starting transfers between devices: 29 us -> 13.3 us  [swap(): return lax.ppermute(x, 'tensor', pairs)]
    unnamed x86 -> x44, local copies, waits for them, and re-layouts: 20.5 us -> 7.35 us
    ppermute x18 -> x8, waiting for transfers between devices: 14.8 us -> 3.8 us  [swap(): return lax.ppermute(x, 'tensor', pairs)]
  transfers between devices with their start and end apart: 48 -> 22, of which waited for: 12 -> 8; matrix products, arithmetic and copies ran while one was open for 4% -> 5% of each run, Pallas kernels for 42% -> 30%
where the time goes in v2:
time: 309 us; the launch traced here: 305 us
  waiting for transfers between devices  122 us (39%)
  Pallas kernels  102 us (33%)
  starting transfers between devices  41.5 us (13%)
  other arithmetic  17.2 us (6%)
  between operations  14.4 us (5%)
  local copies, waits for them, and re-layouts  8 us (3%)
    pallas_call x19, Pallas kernels, product(): pl.pallas_call(functools.partial(product_kernel, len(adds), block_count),...  87.3 us
    psum x1, waiting for transfers between devices, per_device(): low_whole = lax.psum(low_part, 'tensor')  64.5 us
    ppermute x11, waiting for transfers between devices, along(): return lax.ppermute(x, 'tensor', pairs)  53.8 us
    ppermute x11, starting transfers between devices, along(): return lax.ppermute(x, 'tensor', pairs)  28.2 us
    ppermute x8, starting transfers between devices, swap(): return lax.ppermute(x, 'tensor', pairs)  13.3 us
    pallas_call x2, Pallas kernels, factor_sums(): pl.pallas_call(functools.partial(factor_kernel, slots_each, blocks), in_s...  10.3 us
    add x2, other arithmetic, exchange(): total = total + lax.ppermute(theirs, 'dp', pairs).astype(f32)  10.2 us
    unnamed x44, local copies, waits for them, and re-layouts  7.35 us
  transfers between devices with their start and end apart: 22, of which 8 were waited for; matrix products, arithmetic and copies ran while one was open for 5% of the time, Pallas kernels for 30%

profile of v2, /device:TPU:10, one launch (start us, length us, event | category | flops | bytes accessed | tf_op | source)
XLA Modules:
  0.0 304.9 jit_solution(2751603021474286844)
XLA Ops:
  7.3 1.6 copy-done.9
  8.9 6.4 %shard_map.112.refs_3_ = bf16[512,2048]{1,0:T(8,128)(2,1)} custom-call(s32[2]{0:T(128)S(1)} %pad_add_fusion.12.refs_0_, bf16[1024,1024]{1,0:T(8,128)(2,1)S(1)} %copy-done.9, bf16[8192,1024]{1,0:T(8,128)(2,1)} %refs_2_.37), custom_call_target="tpu_custom_call" | custom-call | flops 999999995904 | bytes 1000000000 | tf_op jit(solution)/shard_map/pallas_call | solution.py:86
  16.7 4.1 %shard_map.113.refs_3_ = bf16[512,1024]{1,0:T(8,128)(2,1)} custom-call(s32[2]{0:T(128)S(1)} %get-tuple-element.18.refs_0_, bf16[1024,1024]{1,0:T(8,128)(2,1)S(1)} %copy-done.10, bf16[8192,1024]{1,0:T(8,128)(2,1)} %refs_2_.37, bf16[512,2048]{1,0:T(8,128)(2,1)} %shard_map.112.refs_3_), custom_call_target="tpu_custom_call" | custom-call | flops 999999995904 | bytes 1000000000 | tf_op jit(solution)/shard_map/pallas_call | solution.py:86
  20.8 1.6 collective-permute-start.1
  22.5 4.2 %shard_map.114.refs_3_ = bf16[512,1024]{1,0:T(8,128)(2,1)} custom-call(s32[2]{0:T(128)S(1)} %get-tuple-element.15.refs_0_, bf16[1024,1024]{1,0:T(8,128)(2,1)S(1)} %copy-done.10, bf16[8192,1024]{1,0:T(8,128)(2,1)} %refs_2_.37, bf16[512,1024]{1,0:T(8,128)(2,1)} %shard_map.113.refs_3_), custom_call_target="tpu_custom_call" | custom-call | flops 999999995904 | bytes 1000000000 | tf_op jit(solution)/shard_map/pallas_call | solution.py:86
  26.7 1.7 collective-permute-start.5
  28.3 4.1 %shard_map.115.refs_3_ = bf16[512,1024]{1,0:T(8,128)(2,1)} custom-call(s32[2]{0:T(128)S(1)} %get-tuple-element.16.refs_0_, bf16[1024,1024]{1,0:T(8,128)(2,1)S(1)} %copy-done.10, bf16[8192,1024]{1,0:T(8,128)(2,1)} %refs_2_.37, bf16[512,1024]{1,0:T(8,128)(2,1)} %shard_map.114.refs_3_), custom_call_target="tpu_custom_call" | custom-call | flops 999999995904 | bytes 1000000000 | tf_op jit(solution)/shard_map/pallas_call | solution.py:86
  32.5 1.5 collective-permute-start.3
  34.0 4.1 %shard_map.116.link = bf16[512,1024]{1,0:T(8,128)(2,1)} custom-call(s32[2]{0:T(128)S(1)} %get-tuple-element.17.refs_0_, bf16[1024,1024]{1,0:T(8,128)(2,1)S(1)} %copy-done.10, bf16[8192,1024]{1,0:T(8,128)(2,1)} %refs_2_.37, bf16[512,1024]{1,0:T(8,128)(2,1)} %shard_map.115.refs_3_), custom_call_target="tpu_custom_call" | custom-call | flops 999999995904 | bytes 1000000000 | tf_op jit(solution)/shard_map/pallas_call | solution.py:86
  41.6 2.2 copy-done.6
  43.8 4.2 %shard_map.117.refs_4_ = bf16[1024,128]{1,0:T(8,128)(2,1)} custom-call(s32[8]{0:T(128)S(1)} %copy-done.3, bf16[1024,1024]{1,0:T(8,128)(2,1)S(1)} %copy-done.10, bf16[16,128,1024]{2,1,0:T(8,128)(2,1)S(1)} %copy-done.6, bf16[512,1024]{1,0:T(8,128)(2,1)} %shard_map.116.link), custom_call_target="tpu_custom_call" | custom-call | flops 999999995904 | bytes 1000000000 | tf_op jit(solution)/shard_map/pallas_call | solution.py:110
  50.6 4.3 %shard_map.118.refs_3_ = bf16[512,1024]{1,0:T(8,128)(2,1)} custom-call(s32[2]{0:T(128)S(1)} %get-tuple-element.19.refs_0_, bf16[1024,1024]{1,0:T(8,128)(2,1)S(1)} %copy-done.10, bf16[8192,1024]{1,0:T(8,128)(2,1)} %refs_2_.37, bf16[512,1024]{1,0:T(8,128)(2,1)} %collective-permute-done.1.refs_3_, bf16[1024,128]{1,0:T(8,128)(2,1)} %shard_map.117.refs_4_), custom_call_target="tpu_custom_call" | custom-call | flops 999999995904 | bytes 1000000000 | tf_op jit(solution)/shard_map/pallas_call | solution.py:86
  56.1 3.3 %shard_map.119.refs_3_ = bf16[512,1024]{1,0:T(8,128)(2,1)S(1)} custom-call(s32[2]{0:T(128)S(1)} %get-tuple-element.20.refs_0_, bf16[1024,1024]{1,0:T(8,128)(2,1)S(1)} %copy-done.10, bf16[8192,1024]{1,0:T(8,128)(2,1)} %refs_2_.37, bf16[512,1024]{1,0:T(8,128)(2,1)} %shard_map.118.refs_3_), custom_call_target="tpu_custom_call" | custom-call | flops 999999995904 | bytes 1000000000 | tf_op jit(solution)/shard_map/pallas_call | solution.py:86
  59.5 4.1 %shard_map.120.link = bf16[512,1024]{1,0:T(8,128)(2,1)} custom-call(s32[2]{0:T(128)S(1)} %pad_add_fusion.11.refs_0_, bf16[1024,1024]{1,0:T(8,128)(2,1)S(1)} %copy-done.10, bf16[8192,1024]{1,0:T(8,128)(2,1)} %refs_2_.37, bf16[512,1024]{1,0:T(8,128)(2,1)S(1)} %shard_map.119.refs_3_), custom_call_target="tpu_custom_call" | custom-call | flops 999999995904 | bytes 1000000000 | tf_op jit(solution)/shard_map/pallas_call | solution.py:86
  64.6 4.9 %shard_map.121 = (f32[8,128,1024]{2,1,0:T(8,128)S(1)}, bf16[8,128,1024]{2,1,0:T(8,128)(2,1)}) custom-call(s32[8]{0:T(128)S(1)} %compare_select_fusion.1.slots, f32[8]{0:T(128)S(1)} %copy-done.5, bf16[1024,128]{1,0:T(8,128)(2,1)S(1)} %bitcast_multiply_fusion.1.left, bf16[1024,1024]{1,0:T(8,128)(2,1)S(1)} %copy-done.10, bf16[512,1024]{1,0:T(8,128)(2,1)} %shard_map.120.link), custom_call_target="tpu_custom_call" | custom-call | flops 999999995904 | bytes 1000000000 | tf_op jit(solution)/shard_map/pallas_call | solution.py:155
  69.5 2.0 copy-done
  71.6 64.5 %all-reduce.2.cloned.1.call-done = bf16[1024,128]{1,0:T(8,128)(2,1)} async-done(((bf16[1024,128]{1,0:T(8,128)(2,1)}), bf16[1024,128]{1,0:T(8,128)(2,1)}) %all-reduce.2.cloned.1.call-update) | async-done | bytes 262160 | tf_op jit(solution)/shard_map/psum | solution.py:333
  137.1 3.4 %collective-permute-start.9 = (bf16[512,1024]{1,0:T(8,128)(2,1)}, bf16[512,1024]{1,0:T(8,128)(2,1)}, u32[]{:S(2)}, u32[]{:S(2)}) collective-permute-start(bf16[512,1024]{1,0:T(8,128)(2,1)} %copy-done.11), channel_id=1, source_target_pairs={{0,1},{1,0},{2,3},{3,2},{4,5},{5,4},{8,9},{9,8},{10,11},{11,10},{1... | collective-permute-start | bytes 3145736 | tf_op jit(solution)/shard_map/ppermute | solution.py:219
  140.4 6.6 %shard_map.122.refs_4_ = bf16[512,2048]{1,0:T(8,128)(2,1)} custom-call(s32[2]{0:T(128)S(1)} %pad_add_fusion.13.refs_0_, bf16[1024,1024]{1,0:T(8,128)(2,1)S(1)} %copy-done.10, bf16[8192,1024]{1,0:T(8,128)(2,1)} %refs_2_.37, bf16[512,2048]{1,0:T(8,128)(2,1)} %collective-permute-done.refs_3_, bf16[8,128,1024]{2,1,0:T(8,128)(2,1)} %get-tuple-element.7.refs_4_), custom_call_target="tpu_custom_call" | custom-call | flops 999999995904 | bytes 1000000000 | tf_op jit(solution)/shard_map/pallas_call | solution.py:86
  147.1 2.5 collective-permute-start.7
  149.6 4.3 %shard_map.123.refs_5_ = bf16[512,1024]{1,0:T(8,128)(2,1)} custom-call(s32[2]{0:T(128)S(1)} %pad_add_fusion.3.refs_0_, bf16[1024,1024]{1,0:T(8,128)(2,1)S(1)} %copy-done.10, bf16[8192,1024]{1,0:T(8,128)(2,1)} %refs_2_.37, bf16[512,1024]{1,0:T(8,128)(2,1)} %collective-permute-done.5.refs_3_, bf16[512,2048]{1,0:T(8,128)(2,1)} %shard_map.122.refs_4_), custom_call_target="tpu_custom_call" | custom-call | flops 999999995904 | bytes 1000000000 | tf_op jit(solution)/shard_map/pallas_call | solution.py:86
  153.9 3.2 %collective-permute-start.2 = (bf16[512,2048]{1,0:T(8,128)(2,1)}, bf16[512,2048]{1,0:T(8,128)(2,1)}, u32[]{:S(2)}, u32[]{:S(2)}) collective-permute-start(bf16[512,2048]{1,0:T(8,128)(2,1)} %shard_map.122.refs_4_), channel_id=1, source_target_pairs={{2,4},{3,5},{4,2},{5,3},{10,12},{11,13},{12,10},{13,11},{18,20},{1... | collective-permute-start | bytes 6291464 | tf_op jit(solution)/shard_map/ppermute | solution.py:223
  157.0 4.5 %shard_map.124.refs_4_ = bf16[512,1024]{1,0:T(8,128)(2,1)} custom-call(s32[2]{0:T(128)S(1)} %pad_add_fusion.4.refs_0_, bf16[1024,1024]{1,0:T(8,128)(2,1)S(1)} %copy-done.10, bf16[8192,1024]{1,0:T(8,128)(2,1)} %refs_2_.37, bf16[512,1024]{1,0:T(8,128)(2,1)} %collective-permute-done.3.refs_3_, bf16[512,1024]{1,0:T(8,128)(2,1)} %collective-permute-done.4.refs_4_, ...), custom_call_target="tpu_custom_call" | custom-call | flops 999999995904 | bytes 1000000000 | tf_op jit(solution)/shard_map/pallas_call | solution.py:86
  161.5 1.3 collective-permute-start.12
  162.8 5.9 %convert_add_fusion.1.refs_5_ = f32[8,128,1024]{2,1,0:T(8,128)} fusion(f32[8,128,1024]{2,1,0:T(8,128)} %copy-done, bf16[8,128,1024]{2,1,0:T(8,128)(2,1)} %collective-permute-done.13), kind=kLoop, calls=%fused_computation.1 | loop fusion | flops 2097152 | bytes 10485760 | tf_op jit(solution)/shard_map/add | solution.py:352
  168.8 35.3 %collective-permute-done.2.refs_3_ = bf16[512,2048]{1,0:T(8,128)(2,1)} collective-permute-done((bf16[512,2048]{1,0:T(8,128)(2,1)}, bf16[512,2048]{1,0:T(8,128)(2,1)}, u32[]{:S(2)}, u32[]{:S(2)}) %collective-permute-start.2) | collective-permute-done | bytes 2097184 | tf_op jit(solution)/shard_map/ppermute | solution.py:223
  204.1 3.3 %collective-permute-start.10 = (bf16[512,1024]{1,0:T(8,128)(2,1)}, bf16[512,1024]{1,0:T(8,128)(2,1)}, u32[]{:S(2)}, u32[]{:S(2)}) collective-permute-start(bf16[512,1024]{1,0:T(8,128)(2,1)} %shard_map.124.refs_4_), channel_id=1, source_target_pairs={{0,2},{1,3},{2,4},{3,5},{8,10},{9,11},{10,12},{11,13},{16,18},{17,... | collective-permute-start | bytes 3145736 | tf_op jit(solution)/shard_map/ppermute | solution.py:223
  207.4 6.6 %shard_map.125.refs_5_ = bf16[512,2048]{1,0:T(8,128)(2,1)} custom-call(s32[2]{0:T(128)S(1)} %pad_add_fusion.14.refs_0_, bf16[1024,1024]{1,0:T(8,128)(2,1)S(1)} %copy-done.10, bf16[8192,1024]{1,0:T(8,128)(2,1)} %refs_2_.37, bf16[512,2048]{1,0:T(8,128)(2,1)} %collective-permute-done.2.refs_3_, bf16[512,1024]{1,0:T(8,128)(2,1)} %shard_map.124.refs_4_), custom_call_target="tpu_custom_call" | custom-call | flops 999999995904 | bytes 1000000000 | tf_op jit(solution)/shard_map/pallas_call | solution.py:86
  215.4 5.2 %collective-permute-start.6 = (bf16[512,2048]{1,0:T(8,128)(2,1)}, bf16[512,2048]{1,0:T(8,128)(2,1)}, u32[]{:S(2)}, u32[]{:S(2)}) collective-permute-start(bf16[512,2048]{1,0:T(8,128)(2,1)} %shard_map.125.refs_5_), channel_id=1, source_target_pairs={{4,6},{5,7},{2,0},{3,1},{12,14},{13,15},{10,8},{11,9},{20,22},{21,... | collective-permute-start | bytes 6291464 | tf_op jit(solution)/shard_map/ppermute | solution.py:223
  220.6 4.5 %shard_map.126.refs_3_ = bf16[512,1024]{1,0:T(8,128)(2,1)} custom-call(s32[2]{0:T(128)S(1)} %pad_add_fusion.refs_0_, bf16[1024,1024]{1,0:T(8,128)(2,1)S(1)} %copy-done.10, bf16[8192,1024]{1,0:T(8,128)(2,1)} %refs_2_.37, bf16[512,1024]{1,0:T(8,128)(2,1)} %collective-permute-done.11.refs_3_, bf16[512,1024]{1,0:T(8,128)(2,1)} %collective-permute-done.12.refs_4_, ...), custom_call_target="tpu_custom_call" | custom-call | flops 999999995904 | bytes 1000000000 | tf_op jit(solution)/shard_map/pallas_call | solution.py:86
  225.1 4.2 %shard_map.127.refs_5_ = bf16[512,1024]{1,0:T(8,128)(2,1)} custom-call(s32[2]{0:T(128)S(1)} %pad_add_fusion.17.refs_0_, bf16[1024,1024]{1,0:T(8,128)(2,1)S(1)} %copy-done.10, bf16[8192,1024]{1,0:T(8,128)(2,1)} %refs_2_.37, bf16[512,1024]{1,0:T(8,128)(2,1)} %shard_map.126.refs_3_), custom_call_target="tpu_custom_call" | custom-call | flops 999999995904 | bytes 1000000000 | tf_op jit(solution)/shard_map/pallas_call | solution.py:86
  229.3 3.0 collective-permute-start.15
  232.2 1.6 collective-permute-start.14
  233.8 4.5 %shard_map.128.refs_5_ = bf16[512,1024]{1,0:T(8,128)(2,1)} custom-call(s32[2]{0:T(128)S(1)} %pad_add_fusion.1.refs_0_, bf16[1024,1024]{1,0:T(8,128)(2,1)S(1)} %copy-done.10, bf16[8192,1024]{1,0:T(8,128)(2,1)} %refs_2_.37, bf16[512,1024]{1,0:T(8,128)(2,1)} %collective-permute-done.9.refs_3_, bf16[512,1024]{1,0:T(8,128)(2,1)} %collective-permute-done.10.refs_4_, ...), custom_call_target="tpu_custom_call" | custom-call | flops 999999995904 | bytes 1000000000 | tf_op jit(solution)/shard_map/pallas_call | solution.py:86
  240.8 3.4 %collective-permute-start.18 = (bf16[512,1024]{1,0:T(8,128)(2,1)}, bf16[512,1024]{1,0:T(8,128)(2,1)}, u32[]{:S(2)}, u32[]{:S(2)}) collective-permute-start(bf16[512,1024]{1,0:T(8,128)(2,1)} %shard_map.128.refs_5_), channel_id=1, source_target_pairs={{0,2},{1,3},{2,4},{3,5},{4,6},{5,7},{8,10},{9,11},{10,12},{11,13},... | collective-permute-start | bytes 3145736 | tf_op jit(solution)/shard_map/ppermute | solution.py:223
  244.2 4.5 %shard_map.129.link = bf16[512,1024]{1,0:T(8,128)(2,1)} custom-call(s32[2]{0:T(128)S(1)} %pad_add_fusion.2.refs_0_, bf16[1024,1024]{1,0:T(8,128)(2,1)S(1)} %copy-done.10, bf16[8192,1024]{1,0:T(8,128)(2,1)} %refs_2_.37, bf16[512,1024]{1,0:T(8,128)(2,1)} %collective-permute-done.7.refs_3_, bf16[512,1024]{1,0:T(8,128)(2,1)} %collective-permute-done.8.refs_4_, ...), custom_call_target="tpu_custom_call" | custom-call | flops 999999995904 | bytes 1000000000 | tf_op jit(solution)/shard_map/pallas_call | solution.py:86
  248.7 5.4 %shard_map.130 = (f32[8,1024,128]{2,1,0:T(8,128)S(1)}, bf16[8,1024,128]{2,1,0:T(8,128)(2,1)}) custom-call(s32[8]{0:T(128)S(1)} %compare_select_fusion.1.slots, f32[8]{0:T(128)S(1)} %broadcast_4_scales.2.scales, bf16[1024,1024]{1,0:T(8,128)(2,1)S(1)} %copy-done.8, bf16[1024,128]{1,0:T(8,128)(2,1)S(1)} %fusion.right.refs_6_.refs_7_, ...), custom_call_target="tpu_custom_call" | custom-call | flops 999999995904 | bytes 1000000000 | tf_op jit(solution)/shard_map/pallas_call | solution.py:155
  254.1 2.4 collective-permute-done.14.refs_6_.refs_3_
  256.5 3.8 %collective-permute-start.19 = (bf16[512,1024]{1,0:T(8,128)(2,1)}, bf16[512,1024]{1,0:T(8,128)(2,1)}, u32[]{:S(2)}, u32[]{:S(2)}) collective-permute-start(bf16[512,1024]{1,0:T(8,128)(2,1)} %shard_map.129.link), channel_id=1, source_target_pairs={{2,0},{3,1},{4,2},{5,3},{6,4},{7,5},{10,8},{11,9},{12,10},{13,11},... | collective-permute-start | bytes 3145736 | tf_op jit(solution)/shard_map/ppermute | solution.py:223
  260.4 6.2 %collective-permute-done.16.refs_8_.refs_6_ = bf16[512,1024]{1,0:T(8,128)(2,1)} collective-permute-done((bf16[512,1024]{1,0:T(8,128)(2,1)}, bf16[512,1024]{1,0:T(8,128)(2,1)}, u32[]{:S(2)}, u32[]{:S(2)}) %collective-permute-start.16) | collective-permute-done | bytes 1048608 | tf_op jit(solution)/shard_map/ppermute | solution.py:223
  266.6 4.2 %shard_map.131.refs_11_ = bf16[512,1024]{1,0:T(8,128)(2,1)} custom-call(s32[2]{0:T(128)S(1)} %pad_add_fusion.17.refs_0_, bf16[1024,1024]{1,0:T(8,128)(2,1)S(1)} %copy-done.10, bf16[8192,1024]{1,0:T(8,128)(2,1)} %refs_2_.37, bf16[512,2048]{1,0:T(8,128)(2,1)} %collective-permute-done.6.refs_3_.refs_4_, bf16[8,1024,128]{2,1,0:T(8,128)(2,1)} %get-tuple-element.8.refs_4_, ...), custom_call_target="tpu_custom_call" | custom-call | flops 999999995904 | bytes 1000000000 | tf_op jit(solution)/shard_map/pallas_call | solution.py:86
  271.4 4.2 %convert_add_fusion.refs_12_ = f32[8,1024,128]{2,1,0:T(8,128)} fusion(f32[8,1024,128]{2,1,0:T(8,128)S(1)} %get-tuple-element.10, bf16[8,1024,128]{2,1,0:T(8,128)(2,1)} %collective-permute-done.20), kind=kLoop, calls=%fused_computation | loop fusion | flops 2097152 | bytes 10485760 | tf_op jit(solution)/shard_map/add | solution.py:352
  275.6 2.6 collective-permute-done.18.refs_4_
  278.1 8.5 %collective-permute-done.19.refs_5_ = bf16[512,1024]{1,0:T(8,128)(2,1)} collective-permute-done((bf16[512,1024]{1,0:T(8,128)(2,1)}, bf16[512,1024]{1,0:T(8,128)(2,1)}, u32[]{:S(2)}, u32[]{:S(2)}) %collective-permute-start.19) | collective-permute-done | bytes 1048608 | tf_op jit(solution)/shard_map/ppermute | solution.py:223
  286.6 4.2 %shard_map.132.refs_12_ = bf16[512,1024]{1,0:T(8,128)(2,1)S(1)} custom-call(s32[6]{0:T(128)S(1)} %pad_add_fusion.18.refs_0_, bf16[1024,1024]{1,0:T(8,128)(2,1)S(1)} %copy-done.10, bf16[8192,1024]{1,0:T(8,128)(2,1)} %refs_2_.37, bf16[512,1024]{1,0:T(8,128)(2,1)} %collective-permute-done.14.refs_6_.refs_3_, bf16[512,1024]{1,0:T(8,128)(2,1)} %collective-permute-done.18.refs_4_, ...), custom_call_target="tpu_custom_call" | custom-call | flops 999999995904 | bytes 1000000000 | tf_op jit(solution)/shard_map/pallas_call | solution.py:86
  290.8 1.3 collective-permute-done.17.refs_3_
  292.1 4.5 %shard_map.133 = bf16[512,1024]{1,0:T(8,128)(2,1)S(1)} custom-call(s32[6]{0:T(128)S(1)} %pad_add_fusion.15.refs_0_, bf16[1024,1024]{1,0:T(8,128)(2,1)S(1)} %copy-done.10, bf16[8192,1024]{1,0:T(8,128)(2,1)} %refs_2_.37, bf16[512,1024]{1,0:T(8,128)(2,1)} %collective-permute-done.17.refs_3_, bf16[512,2048]{1,0:T(8,128)(2,1)} %collective-permute-done.6.refs_3_.refs_4_, ...), custom_call_target="tpu_custom_call" | custom-call | flops 999999995904 | bytes 1000000000 | tf_op jit(solution)/shard_map/pallas_call | solution.py:86
  296.6 1.5 pad_maximum_fusion
  (94 shorter events, 15.2 us)
Async XLA Ops:
  7.3 1.6 copy-start.9
  8.8 7.8 %copy-start.10 = (bf16[1024,1024]{1,0:T(8,128)(2,1)S(1)}, bf16[1024,1024]{1,0:T(8,128)(2,1)}, u32[]{:S(2)}) copy-start(bf16[1024,1024]{1,0:T(8,128)(2,1)} %refs_1_.37) | copy-start | bytes 6291460
  15.3 121.8 %collective-permute-start = (bf16[512,2048]{1,0:T(8,128)(2,1)}, bf16[512,2048]{1,0:T(8,128)(2,1)}, u32[]{:S(2)}, u32[]{:S(2)}) collective-permute-start(bf16[512,2048]{1,0:T(8,128)(2,1)} %shard_map.112.refs_3_), channel_id=1, source_target_pairs={{0,2},{1,3},{6,4},{7,5},{8,10},{9,11},{14,12},{15,13},{16,18},{17,... | collective-permute-start | bytes 6291464 | tf_op jit(solution)/shard_map/ppermute | solution.py:223
  20.8 29.8 %collective-permute-start.1 = (bf16[512,1024]{1,0:T(8,128)(2,1)}, bf16[512,1024]{1,0:T(8,128)(2,1)}, u32[]{:S(2)}, u32[]{:S(2)}) collective-permute-start(bf16[512,1024]{1,0:T(8,128)(2,1)} %shard_map.113.refs_3_), channel_id=1, source_target_pairs={{0,1},{1,0},{6,7},{7,6},{8,9},{9,8},{14,15},{15,14},{16,17},{17,16... | collective-permute-start | bytes 3145736 | tf_op jit(solution)/shard_map/ppermute | solution.py:219
  26.7 120.4 %collective-permute-start.5 = (bf16[512,1024]{1,0:T(8,128)(2,1)}, bf16[512,1024]{1,0:T(8,128)(2,1)}, u32[]{:S(2)}, u32[]{:S(2)}) collective-permute-start(bf16[512,1024]{1,0:T(8,128)(2,1)} %shard_map.114.refs_3_), channel_id=1, source_target_pairs={{0,1},{1,0},{6,7},{7,6},{8,9},{9,8},{14,15},{15,14},{16,17},{17,16... | collective-permute-start | bytes 3145736 | tf_op jit(solution)/shard_map/ppermute | solution.py:219
  32.5 121.4 %collective-permute-start.3 = (bf16[512,1024]{1,0:T(8,128)(2,1)}, bf16[512,1024]{1,0:T(8,128)(2,1)}, u32[]{:S(2)}, u32[]{:S(2)}) collective-permute-start(bf16[512,1024]{1,0:T(8,128)(2,1)} %shard_map.115.refs_3_), channel_id=1, source_target_pairs={{0,1},{1,0},{2,3},{3,2},{4,5},{5,4},{6,7},{7,6},{8,9},{9,8},{10,11... | collective-permute-start | bytes 3145736 | tf_op jit(solution)/shard_map/ppermute | solution.py:219
  34.0 5.2 %copy-start.3 = (s32[8]{0:T(128)S(1)}, s32[8]{0:T(128)}, u32[]{:S(2)}) copy-start(s32[8]{0:T(128)} %tenants.1) | copy-start | bytes 100
  34.0 6.1 %copy-start.21 = (s32[16]{0:T(128)S(1)}, s32[16]{0:T(128)}, u32[]{:S(2)}) copy-start(s32[16]{0:T(128)} %param.17) | copy-start | bytes 196
  34.0 6.3 %copy-start.18 = (s32[16]{0:T(128)S(1)}, s32[16]{0:T(128)}, u32[]{:S(2)}) copy-start(s32[16]{0:T(128)} %param.16) | copy-start | bytes 196
  38.1 176.0 %collective-permute-start.11 = (bf16[512,1024]{1,0:T(8,128)(2,1)}, bf16[512,1024]{1,0:T(8,128)(2,1)}, u32[]{:S(2)}, u32[]{:S(2)}) collective-permute-start(bf16[512,1024]{1,0:T(8,128)(2,1)} %shard_map.116.link), channel_id=1, source_target_pairs={{0,1},{1,0},{2,3},{3,2},{4,5},{5,4},{6,7},{7,6},{8,9},{9,8},{10,11... | collective-permute-start | bytes 3145736 | tf_op jit(solution)/shard_map/ppermute | solution.py:219
  41.0 7.0 %copy-start.20 = (s32[8]{0:T(128)}, s32[8]{0:T(128)S(1)}, u32[]{:S(2)}) copy-start(s32[8]{0:T(128)S(1)} %get-tuple-element.11) | copy-start | bytes 100
  41.6 2.2 copy-start.6
  43.8 4.5 %copy-start.16 = (f32[128]{0:T(128)S(1)}, f32[128]{0:T(128)}, u32[]{:S(2)}) copy-start(f32[128]{0:T(128)} %iota_convert_fusion) | copy-start | bytes 1540
  43.8 4.5 %copy-start.17 = (f32[8]{0:T(128)S(1)}, f32[8]{0:T(128)}, u32[]{:S(2)}) copy-start(f32[8]{0:T(128)} %convert_element_type.51) | copy-start | bytes 100
  43.8 4.6 %copy-start.15 = (s32[4]{0:T(128)S(1)}, s32[4]{0:T(128)}, u32[]{:S(2)}) copy-start(s32[4]{0:T(128)} %get-tuple-element.14) | copy-start | bytes 52
  43.8 4.6 %copy-start.12 = (bf16[1024,128]{1,0:T(8,128)(2,1)S(1)}, bf16[1024,128]{1,0:T(8,128)(2,1)}, u32[]{:S(2)}) copy-start(bf16[1024,128]{1,0:T(8,128)(2,1)} %param.11) | copy-start | bytes 786436
  43.8 4.7 %copy-start.14 = (s32[4]{0:T(128)S(1)}, s32[4]{0:T(128)}, u32[]{:S(2)}) copy-start(s32[4]{0:T(128)} %get-tuple-element.13) | copy-start | bytes 52
  43.8 5.6 %copy-start.19 = (s32[8]{0:T(128)S(1)}, s32[8]{0:T(128)}, u32[]{:S(2)}) copy-start(s32[8]{0:T(128)} %get-tuple-element.12) | copy-start | bytes 100
  49.4 0.5 copy-start.4
  54.8 81.2 %all-reduce.2.cloned.1.call-start = ((), (), s32[]{:S(2)}) async-start(), calls=%async_computation | async-start | bytes 524288 | tf_op jit(solution)/shard_map/psum | solution.py:333
  54.8 99.1 %collective-permute-start.4 = (bf16[512,1024]{1,0:T(8,128)(2,1)}, bf16[512,1024]{1,0:T(8,128)(2,1)}, u32[]{:S(2)}, u32[]{:S(2)}) collective-permute-start(bf16[512,1024]{1,0:T(8,128)(2,1)} %shard_map.118.refs_3_), channel_id=1, source_target_pairs={{0,2},{1,3},{6,4},{7,5},{8,10},{9,11},{14,12},{15,13},{16,18},{17,... | collective-permute-start | bytes 3145736 | tf_op jit(solution)/shard_map/ppermute | solution.py:223
  59.5 5.1 %copy-start.5 = (f32[8]{0:T(128)S(1)}, f32[8]{0:T(128)}, u32[]{:S(2)}) copy-start(f32[8]{0:T(128)} %copy-done.4) | copy-start | bytes 100
  63.6 1.0 copy-start.11
  64.6 71.4 %copy-start.13 = (f32[8,128]{1,0:T(8,128)S(1)}, f32[8,128]{1,0:T(8,128)}, u32[]{:S(2)}) copy-start(f32[8,128]{1,0:T(8,128)} %compare_select_fusion) | copy-start | bytes 12292
  69.5 2.0 copy-start
  137.0 111.7 %copy-start.1 = (bf16[1024,128]{1,0:T(8,128)(2,1)}, bf16[1024,128]{1,0:T(8,128)(2,1)S(1)}, u32[]{:S(2)}) copy-start(bf16[1024,128]{1,0:T(8,128)(2,1)S(1)} %fusion.right.refs_6_.refs_7_) | copy-start | bytes 786436
  137.1 92.2 %collective-permute-start.9 = (bf16[512,1024]{1,0:T(8,128)(2,1)}, bf16[512,1024]{1,0:T(8,128)(2,1)}, u32[]{:S(2)}, u32[]{:S(2)}) collective-permute-start(bf16[512,1024]{1,0:T(8,128)(2,1)} %copy-done.11), channel_id=1, source_target_pairs={{0,1},{1,0},{2,3},{3,2},{4,5},{5,4},{8,9},{9,8},{10,11},{11,10},{1... | collective-permute-start | bytes 3145736 | tf_op jit(solution)/shard_map/ppermute | solution.py:219
  147.1 91.2 %collective-permute-start.7 = (bf16[512,1024]{1,0:T(8,128)(2,1)}, bf16[512,1024]{1,0:T(8,128)(2,1)}, u32[]{:S(2)}, u32[]{:S(2)}) collective-permute-start(bf16[512,1024]{1,0:T(8,128)(2,1)} %shard_map.120.link), channel_id=1, source_target_pairs={{2,3},{3,2},{4,5},{5,4},{6,7},{7,6},{10,11},{11,10},{12,13},{13,12... | collective-permute-start | bytes 3145736 | tf_op jit(solution)/shard_map/ppermute | solution.py:219
  153.9 7.7 %collective-permute-start.13 = (bf16[8,128,1024]{2,1,0:T(8,128)(2,1)}, bf16[8,128,1024]{2,1,0:T(8,128)(2,1)}, u32[]{:S(2)}, u32[]{:S(2)}) collective-permute-start(bf16[8,128,1024]{2,1,0:T(8,128)(2,1)} %get-tuple-element.7.refs_4_), channel_id=1, source_target_pairs={{0,8},{8,0},{1,9},{9,1},{2,10},{10,2},{3,11},{11,3},{4,12},{12,4},... | collective-permute-start | bytes 6291464 | tf_op jit(solution)/shard_map/ppermute | solution.py:352
  153.9 50.2 %collective-permute-start.2 = (bf16[512,2048]{1,0:T(8,128)(2,1)}, bf16[512,2048]{1,0:T(8,128)(2,1)}, u32[]{:S(2)}, u32[]{:S(2)}) collective-permute-start(bf16[512,2048]{1,0:T(8,128)(2,1)} %shard_map.122.refs_4_), channel_id=1, source_target_pairs={{2,4},{3,5},{4,2},{5,3},{10,12},{11,13},{12,10},{13,11},{18,20},{1... | collective-permute-start | bytes 6291464 | tf_op jit(solution)/shard_map/ppermute | solution.py:223
  161.5 53.8 %collective-permute-start.12 = (bf16[512,1024]{1,0:T(8,128)(2,1)}, bf16[512,1024]{1,0:T(8,128)(2,1)}, u32[]{:S(2)}, u32[]{:S(2)}) collective-permute-start(bf16[512,1024]{1,0:T(8,128)(2,1)} %shard_map.123.refs_5_), channel_id=1, source_target_pairs={{0,2},{1,3},{6,4},{7,5},{8,10},{9,11},{14,12},{15,13},{16,18},{17,... | collective-permute-start | bytes 3145736 | tf_op jit(solution)/shard_map/ppermute | solution.py:223
  204.1 28.1 %collective-permute-start.10 = (bf16[512,1024]{1,0:T(8,128)(2,1)}, bf16[512,1024]{1,0:T(8,128)(2,1)}, u32[]{:S(2)}, u32[]{:S(2)}) collective-permute-start(bf16[512,1024]{1,0:T(8,128)(2,1)} %shard_map.124.refs_4_), channel_id=1, source_target_pairs={{0,2},{1,3},{2,4},{3,5},{8,10},{9,11},{10,12},{11,13},{16,18},{17,... | collective-permute-start | bytes 3145736 | tf_op jit(solution)/shard_map/ppermute | solution.py:223
  214.1 26.7 %collective-permute-start.8 = (bf16[512,1024]{1,0:T(8,128)(2,1)}, bf16[512,1024]{1,0:T(8,128)(2,1)}, u32[]{:S(2)}, u32[]{:S(2)}) collective-permute-start(bf16[512,1024]{1,0:T(8,128)(2,1)} %shard_map.124.refs_4_), channel_id=1, source_target_pairs={{4,2},{5,3},{6,4},{7,5},{12,10},{13,11},{14,12},{15,13},{20,18},{2... | collective-permute-start | bytes 3145736 | tf_op jit(solution)/shard_map/ppermute | solution.py:223
  215.4 51.2 %collective-permute-start.6 = (bf16[512,2048]{1,0:T(8,128)(2,1)}, bf16[512,2048]{1,0:T(8,128)(2,1)}, u32[]{:S(2)}, u32[]{:S(2)}) collective-permute-start(bf16[512,2048]{1,0:T(8,128)(2,1)} %shard_map.125.refs_5_), channel_id=1, source_target_pairs={{4,6},{5,7},{2,0},{3,1},{12,14},{13,15},{10,8},{11,9},{20,22},{21,... | collective-permute-start | bytes 6291464 | tf_op jit(solution)/shard_map/ppermute | solution.py:223
  229.3 31.1 %collective-permute-start.15 = (bf16[512,1024]{1,0:T(8,128)(2,1)}, bf16[512,1024]{1,0:T(8,128)(2,1)}, u32[]{:S(2)}, u32[]{:S(2)}) collective-permute-start(bf16[512,1024]{1,0:T(8,128)(2,1)} %shard_map.126.refs_3_), channel_id=1, source_target_pairs={{0,2},{1,3},{2,4},{3,5},{8,10},{9,11},{10,12},{11,13},{16,18},{17,... | collective-permute-start | bytes 3145736 | tf_op jit(solution)/shard_map/ppermute | solution.py:223
  232.2 24.3 %collective-permute-start.14 = (bf16[512,1024]{1,0:T(8,128)(2,1)}, bf16[512,1024]{1,0:T(8,128)(2,1)}, u32[]{:S(2)}, u32[]{:S(2)}) collective-permute-start(bf16[512,1024]{1,0:T(8,128)(2,1)} %shard_map.127.refs_5_), channel_id=1, source_target_pairs={{0,1},{1,0},{2,3},{3,2},{4,5},{5,4},{6,7},{7,6},{8,9},{9,8},{10,11... | collective-permute-start | bytes 3145736 | tf_op jit(solution)/shard_map/ppermute | solution.py:219
  238.3 28.3 %collective-permute-start.16 = (bf16[512,1024]{1,0:T(8,128)(2,1)}, bf16[512,1024]{1,0:T(8,128)(2,1)}, u32[]{:S(2)}, u32[]{:S(2)}) collective-permute-start(bf16[512,1024]{1,0:T(8,128)(2,1)} %shard_map.126.refs_3_), channel_id=1, source_target_pairs={{4,2},{5,3},{6,4},{7,5},{12,10},{13,11},{14,12},{15,13},{20,18},{2... | collective-permute-start | bytes 3145736 | tf_op jit(solution)/shard_map/ppermute | solution.py:223
  240.8 37.4 %collective-permute-start.18 = (bf16[512,1024]{1,0:T(8,128)(2,1)}, bf16[512,1024]{1,0:T(8,128)(2,1)}, u32[]{:S(2)}, u32[]{:S(2)}) collective-permute-start(bf16[512,1024]{1,0:T(8,128)(2,1)} %shard_map.128.refs_5_), channel_id=1, source_target_pairs={{0,2},{1,3},{2,4},{3,5},{4,6},{5,7},{8,10},{9,11},{10,12},{11,13},... | collective-permute-start | bytes 3145736 | tf_op jit(solution)/shard_map/ppermute | solution.py:223
  244.2 4.6 %copy-start.8 = (bf16[1024,1024]{1,0:T(8,128)(2,1)S(1)}, bf16[1024,1024]{1,0:T(8,128)(2,1)}, u32[]{:S(2)}) copy-start(bf16[1024,1024]{1,0:T(8,128)(2,1)} %left.1) | copy-start | bytes 6291460
  256.5 30.1 %collective-permute-start.19 = (bf16[512,1024]{1,0:T(8,128)(2,1)}, bf16[512,1024]{1,0:T(8,128)(2,1)}, u32[]{:S(2)}, u32[]{:S(2)}) collective-permute-start(bf16[512,1024]{1,0:T(8,128)(2,1)} %shard_map.129.link), channel_id=1, source_target_pairs={{2,0},{3,1},{4,2},{5,3},{6,4},{7,5},{10,8},{11,9},{12,10},{13,11},... | collective-permute-start | bytes 3145736 | tf_op jit(solution)/shard_map/ppermute | solution.py:223
  260.3 11.0 %collective-permute-start.20 = (bf16[8,1024,128]{2,1,0:T(8,128)(2,1)}, bf16[8,1024,128]{2,1,0:T(8,128)(2,1)}, u32[]{:S(2)}, u32[]{:S(2)}) collective-permute-start(bf16[8,1024,128]{2,1,0:T(8,128)(2,1)} %get-tuple-element.8.refs_4_), channel_id=1, source_target_pairs={{0,8},{8,0},{1,9},{9,1},{2,10},{10,2},{3,11},{11,3},{4,12},{12,4},... | collective-permute-start | bytes 6291464 | tf_op jit(solution)/shard_map/ppermute | solution.py:352
  270.8 15.8 %copy-start.2 = (bf16[1024,128]{1,0:T(8,128)(2,1)S(1)}, bf16[1024,128]{1,0:T(8,128)(2,1)}, u32[]{:S(2)}) copy-start(bf16[1024,128]{1,0:T(8,128)(2,1)} %copy-done.1) | copy-start | bytes 786436
  270.8 15.8 %copy-start.7 = (bf16[16,1024,128]{2,1,0:T(8,128)(2,1)S(1)}, bf16[16,1024,128]{2,1,0:T(8,128)(2,1)}, u32[]{:S(2)}) copy-start(bf16[16,1024,128]{2,1,0:T(8,128)(2,1)} %refs_11_.1) | copy-start | bytes 12582916
  270.8 21.3 %collective-permute-start.17 = (bf16[512,1024]{1,0:T(8,128)(2,1)}, bf16[512,1024]{1,0:T(8,128)(2,1)}, u32[]{:S(2)}, u32[]{:S(2)}) collective-permute-start(bf16[512,1024]{1,0:T(8,128)(2,1)} %shard_map.131.refs_11_), channel_id=1, source_target_pairs={{0,1},{1,0},{2,3},{3,2},{4,5},{5,4},{6,7},{7,6},{8,9},{9,8},{10,11... | collective-permute-start | bytes 3145736 | tf_op jit(solution)/shard_map/ppermute | solution.py:219
Sparse Core Ops, SparseCore 0:
  59.0 76.9 all-reduce.1

commit v3 on v2

--- a/solution.py
+++ b/solution.py
@@ -49,7 +49,7 @@
     refs[-1][...] = total.astype(refs[-1].dtype)
 
 
-def product(scalars, gradient, weights, piece, piece_rows, width, adds, link, adapter=None):
+def product(scalars, gradient, weights, piece, piece_rows, width, adds, link, adapter=None, whole=None):
     depth = gradient.shape[1]
     tile = min(width, 512)
     while width % tile:
@@ -60,13 +60,8 @@
         pl.BlockSpec((tile, depth), lambda j, s: (s[0] * steps + j, 0)),
     ]
     operands = [gradient, weights]
-    for array, shifted in adds:
-        if shifted:
-            in_specs.append(
-                pl.BlockSpec((piece_rows, tile), lambda j, s: (0, s[1] * steps + j))
-            )
-        else:
-            in_specs.append(pl.BlockSpec((piece_rows, tile), lambda j, s: (0, j)))
+    for array in adds:
+        in_specs.append(pl.BlockSpec((piece_rows, tile), lambda j, s: (0, j)))
         operands.append(array)
     block_count = 0
     if adapter is not None:
@@ -77,21 +72,29 @@
         operands.append(low)
         for i in range(block_count):
             in_specs.append(
-                pl.BlockSpec((1, tile, rank), functools.partial(lambda j, s, i: (s[2 + i], j, 0), i=i))
+                pl.BlockSpec((1, tile, rank), functools.partial(lambda j, s, i: (s[1 + i], j, 0), i=i))
             )
             operands.append(shrink)
     for array in link:
         in_specs.append(pl.BlockSpec(memory_space=pl.ANY))
         operands.append(array)
+    out_piece, out_rows, aliases = 0, piece_rows, {}
+    if adapter is not None:
+        out_piece, out_rows = piece, gradient.shape[0]
+        if whole is not None:
+            in_specs.append(pl.BlockSpec(memory_space=pl.ANY))
+            operands.append(whole)
+            aliases = {len(operands): 0}
     return pl.pallas_call(
         functools.partial(product_kernel, len(adds), block_count),
         grid_spec=pltpu.PrefetchScalarGridSpec(
             num_scalar_prefetch=1,
             grid=(steps,),
             in_specs=in_specs,
-            out_specs=pl.BlockSpec((piece_rows, tile), lambda j, s: (0, j)),
+            out_specs=pl.BlockSpec((piece_rows, tile), lambda j, s: (out_piece, j)),
         ),
-        out_shape=jax.ShapeDtypeStruct((piece_rows, width), bf16),
+        out_shape=jax.ShapeDtypeStruct((out_rows, width), bf16),
+        input_output_aliases=aliases,
         compiler_params=params(),
         cost_estimate=declared,
     )(scalars, *operands)
@@ -125,51 +128,64 @@
     )(tenants, gradient, expand, link)
 
 
-def factor_kernel(slots_each, blocks, slots, scales, left, right, link, own, other, other_sum):
-    own[...] = jnp.zeros_like(own)
-    other_sum[...] = jnp.zeros_like(other_sum)
-    for b in range(blocks):
+def scale_kernel(ranks, scales, low, link, out):
+    columns = lax.broadcasted_iota(jnp.int32, (row_block, low.shape[1]), 1)
+    for b in range(low.shape[0] // row_block):
         here = pl.ds(b * row_block, row_block)
-        piece = lax.dot_general(
-            left[here, :], right[here, :], contract_first, preferred_element_type=f32
-        )
-        piece = piece * scales[b]
-        slot = slots[b]
-
-        @pl.when(slot < slots_each)
-        def _():
-            own[slot] += piece
-
-        @pl.when(slot >= slots_each)
-        def _():
-            other_sum[slot - slots_each] += piece
-
-    other[...] = other_sum[...].astype(other.dtype)
-
-
-def factor_sums(slots, scales, left, right, slots_each, others, link):
-    count_of_rows, height = left.shape
-    width = right.shape[1]
-    blocks = count_of_rows // row_block
+        kept = jnp.where(columns < ranks[b], low[here, :].astype(f32) * scales[b], 0.0)
+        out[here, :] = kept.astype(out.dtype)
+
+
+def scaled_low(ranks, scales, low, link):
     whole = pl.BlockSpec(memory_space=pltpu.VMEM)
     return pl.pallas_call(
-        functools.partial(factor_kernel, slots_each, blocks),
+        scale_kernel,
         in_specs=[
             pl.BlockSpec(memory_space=pltpu.SMEM),
             pl.BlockSpec(memory_space=pltpu.SMEM),
             whole,
-            whole,
             pl.BlockSpec(memory_space=pl.ANY),
         ],
-        out_specs=[whole, whole],
-        out_shape=[
-            jax.ShapeDtypeStruct((slots_each, height, width), f32),
-            jax.ShapeDtypeStruct((others, height, width), bf16),
-        ],
-        scratch_shapes=[pltpu.VMEM((others, height, width), f32)],
+        out_specs=whole,
+        out_shape=jax.ShapeDtypeStruct(low.shape, bf16),
         compiler_params=params(),
         cost_estimate=declared,
-    )(slots, scales, left, right, link)
+    )(ranks, scales, low, link)
+
+
+def factor_kernel(slots_each, blocks, sources, slots, scales, *refs):
+    own = refs[-1]
+    own[...] = jnp.zeros_like(own)
+    for source in range(sources):
+        left, right = refs[2 * source], refs[2 * source + 1]
+        for b in range(blocks):
+            entry = source * blocks + b
+            slot = slots[entry]
+
+            @pl.when(slot < slots_each)
+            def _():
+                here = pl.ds(b * row_block, row_block)
+                piece = lax.dot_general(
+                    left[here, :], right[here, :], contract_first, preferred_element_type=f32
+                )
+                own[slot] += piece * scales[entry]
+
+
+def factor_sums(slots, scales, sides, slots_each, link):
+    count_of_rows, height = sides[0].shape
+    width = sides[1].shape[1]
+    blocks = count_of_rows // row_block
+    whole = pl.BlockSpec(memory_space=pltpu.VMEM)
+    return pl.pallas_call(
+        functools.partial(factor_kernel, slots_each, blocks, len(sides) // 2),
+        in_specs=[pl.BlockSpec(memory_space=pltpu.SMEM)] * 2
+        + [whole] * len(sides)
+        + [pl.BlockSpec(memory_space=pl.ANY)] * len(link),
+        out_specs=whole,
+        out_shape=jax.ShapeDtypeStruct((slots_each, height, width), f32),
+        compiler_params=params(),
+        cost_estimate=declared,
+    )(slots, scales, *sides, *link)
 
 
 def per_device(
@@ -204,10 +220,10 @@
 
     link = []
 
-    def run(scalars, piece, columns, adds, adapter=None):
+    def run(scalars, piece, columns, adds, adapter=None, whole=None):
         out = product(
             jnp.stack([jnp.asarray(v, jnp.int32) for v in scalars]),
-            gradient, weights, piece, piece_rows, columns, adds, link, adapter,
+            gradient, weights, piece, piece_rows, columns, adds, link, adapter, whole,
         )
         link[:] = [out]
         return out
@@ -269,7 +285,7 @@
                 return
             for t, (active, dest, _, _) in enumerate(tasks(step, self.lag)):
                 for p in self.piece_ids:
-                    part = run([dest * 2 + (1 - side), 0], p, width, [])
+                    part = run([dest * 2 + (1 - side)], p, width, [])
                     self.swapped[step, t, p] = swap(part, active)
 
         def combine(self, step, p):
@@ -278,9 +294,8 @@
             before = self.arrived[p]
             found = [None, None]
             for t, (active, dest, right_hops, left_hops) in enumerate(tasks(step, self.lag)):
-                adds = [(self.swapped[step, t, p], False)]
-                adds += [(a, False) for a in addends(before, right_hops, left_hops)]
-                part = run([dest * 2 + side, 0], p, width, adds)
+                adds = [self.swapped[step, t, p]] + addends(before, right_hops, left_hops)
+                part = run([dest * 2 + side], p, width, adds)
                 got = forward(part, right_hops, left_hops)
                 if right_hops:
                     found[0] = got[0]
@@ -290,112 +305,126 @@
 
     class DirectFlow:
         def __init__(self):
-            self.arrived = {p: None for p in lower}
-
-        def advance(self, step, p):
+            self.arrived = {(p, part): None for p in lower for part in (0, 1)}
+
+        def advance(self, step, part):
             if step > last - 1:
                 return
             dest = jnp.where(node == step, last, 0)
-            adds = [] if self.arrived[p] is None else [(self.arrived[p], False)]
-            part = run([dest, 0], p, 2 * width, adds)
-            self.arrived[p] = along(part, [(step, step + 1), (last - step, last - step - 1)])
+            column = side if part else 1 - side
+            for p in lower:
+                before = self.arrived[p, part]
+                adds = [] if before is None else [before]
+                out = run([dest * 2 + column], p, width, adds)
+                self.arrived[p, part] = along(
+                    out, [(step, step + 1), (last - step, last - step - 1)]
+                )
 
     low_flow = Flow(lower, 1)
     up_flow = Flow(upper, 0)
     direct = DirectFlow()
 
+    def from_owners(x):
+        found = [x]
+        for hop in range(1, owner_count):
+            pairs = [(i, (i + hop) % owner_count) for i in range(owner_count)]
+            found.append(lax.ppermute(x, "dp", pairs))
+        return found
+
+    block_tenants = jnp.concatenate(from_owners(tenant_per_block))
     tenant_ids = jnp.arange(tenants, dtype=jnp.int32)
-    matches = tenant_per_block[:, None] == tenant_ids[None, :]
-    rank_per_block = jnp.sum(jnp.where(matches, tenant_adapter_rank[None, :], 0), axis=1).astype(f32)
-    scale_per_block = adapter_alpha / rank_per_block
-    block_mask = (jnp.arange(rank_extent).astype(f32)[None, :] < rank_per_block[:, None]).astype(f32)
+    matches = block_tenants[:, None] == tenant_ids[None, :]
+    block_ranks = jnp.sum(jnp.where(matches, tenant_adapter_rank[None, :], 0), axis=1)
+    block_scales = adapter_alpha / block_ranks.astype(f32)
     key = tenant_owner_index * tenants + tenant_ids
     slot_of = jnp.sum((key[None, :] < key[:, None]).astype(jnp.int32), axis=1)
-    block_slot = jnp.sum(jnp.where(matches, slot_of[None, :], 0), axis=1)
     slots_each = tenants // owner_count
-    own_first = lax.rem(block_slot - owner * slots_each + tenants, tenants)
+    slot_here = lax.rem(slot_of - owner * slots_each + tenants, tenants)
+    block_slots = jnp.sum(jnp.where(matches, slot_here[None, :], 0), axis=1)
 
     own_swap = {}
 
     def swap_own(p):
-        adds = [(direct.arrived[p], True)] if p in lower else []
-        part = run([node * 2 + (1 - side), 1 - side], p, width, adds)
+        adds = [direct.arrived[p, 0]] if p in lower else []
+        part = run([node * 2 + (1 - side)], p, width, adds)
         own_swap[p] = swap(part, range(nodes))
 
-    direct.advance(0, lower[0])
+    def adapter_space():
+        part = low_product(tenant_per_block, gradient, expand, link[0])
+        link[:] = [part]
+        return lax.psum(jnp.concatenate(from_owners(part)), "tensor")
+
+    def expand_gradient():
+        ranks = block_ranks[:blocks]
+        kept = jnp.arange(rank_extent, dtype=jnp.int32)[None, :] < ranks[:, None]
+        saved = saved_lowrank.reshape(blocks, row_block, rank_extent)
+        saved = saved * kept[:, None, :].astype(bf16)
+        saved = from_owners(saved.reshape(count_of_rows, rank_extent))
+        sides = [a for pair in zip(saved, from_owners(gradient)) for a in pair]
+        out = factor_sums(block_slots, block_scales, sides, slots_each, link)
+        link[:] = [out]
+        return out
+
+    def shrink_gradient(low):
+        inputs = from_owners(projection_input)
+        lows = [low[i * count_of_rows : (i + 1) * count_of_rows] for i in range(owner_count)]
+        sides = [a for pair in zip(inputs, lows) for a in pair]
+        out = factor_sums(
+            block_slots, jnp.ones_like(block_scales), sides, slots_each, link
+        )
+        link[:] = [out]
+        return out
+
+    direct.advance(0, 0)
     up_flow.swap(0)
+    direct.advance(0, 1)
     low_flow.swap(1)
+    low_whole = adapter_space()
+    direct.advance(1, 0)
+    for p in upper:
+        up_flow.combine(0, p)
     up_flow.swap(1)
     low_flow.swap(2)
-
-    low_part = low_product(tenant_per_block, gradient, expand, link[0])
-    link[:] = [low_part]
-    low_whole = lax.psum(low_part, "tensor")
-    factor = scale_per_block[:, None, None] * block_mask[:, None, :]
-    low = (low_whole.astype(f32).reshape(blocks, row_block, rank_extent) * factor).astype(bf16)
-    low = low.reshape(count_of_rows, rank_extent)
-
-    for p in upper:
-        up_flow.combine(0, p)
-    up_flow.swap(2)
-
-    masked = saved_lowrank.reshape(blocks, row_block, rank_extent) * block_mask[:, None, :].astype(bf16)
-    masked = masked.reshape(count_of_rows, rank_extent)
-    others = slots_each * (owner_count - 1)
-    ones = jnp.ones_like(scale_per_block)
-
-    def exchange(own, other):
-        total = own
-        for hop in range(1, owner_count):
-            theirs = other[(hop - 1) * slots_each : hop * slots_each]
-            pairs = [(i, (i + hop) % owner_count) for i in range(owner_count)]
-            total = total + lax.ppermute(theirs, "dp", pairs).astype(f32)
-        return total
-
-    own, other = factor_sums(
-        own_first, scale_per_block, masked, gradient, slots_each, others, link[0]
-    )
-    link[:] = [other]
-    grad_expand = exchange(own, other)
+    grad_expand = expand_gradient()
+    direct.advance(1, 1)
 
     for step in range(1, last):
-        direct.advance(step, lower[0])
+        direct.advance(step + 1, 0)
         for p in lower:
             low_flow.combine(step, p)
-        up_flow.swap(step + 2)
+        if step == last - 1:
+            for p in lower:
+                swap_own(p)
+        up_flow.swap(step + 1)
+        for p in upper:
+            up_flow.combine(step, p)
+        direct.advance(step + 1, 1)
         low_flow.swap(step + 2)
-        if step == last - 1:
+        if step == last - 2:
             for p in upper:
                 swap_own(p)
-        for p in upper:
-            up_flow.combine(step, p)
-    own, other = factor_sums(
-        own_first, ones, projection_input, low, slots_each, others, link[0]
-    )
-    link[:] = [other]
-    grad_shrink = exchange(own, other)
-    link.append(grad_expand)
+
+    low = scaled_low(block_ranks, block_scales, low_whole, link[0])
+    link[:] = [low] + [direct.arrived[p, 1] for p in lower]
+    link += [a for p in lower for a in low_flow.arrived[p]]
     link += [own_swap[p] for p in upper]
-    for p in lower:
-        link += [a for a in low_flow.arrived[p]]
-    for p in lower:
-        swap_own(p)
-    link.append(grad_shrink)
-
-    outs = {}
-    for p in upper + lower:
+    grad_shrink = shrink_gradient(low)
+
+    input_gradient = None
+    for p in lower + upper:
         flow = low_flow if p in lower else up_flow
-        adds = [(own_swap[p], False)]
+        adds = [own_swap[p]]
         if p in lower:
-            adds.append((direct.arrived[p], True))
+            adds.append(direct.arrived[p, 1])
         arrived = flow.arrived[p]
-        adds.append((arrived[0], False))
+        adds.append(arrived[0])
         if arrived[1] is not arrived[0]:
-            adds.append((arrived[1], False))
+            adds.append(arrived[1])
         in_piece = piece_rows // row_block
         ids = [tenant_per_block[p * in_piece + i] for i in range(in_piece)]
-        outs[p] = run([node * 2 + side, side] + ids, p, width, adds, (low, shrink))
-    input_gradient = jnp.concatenate([outs[p] for p in range(pieces)], axis=0)
+        input_gradient = run(
+            [node * 2 + side] + ids, p, width, adds, (low, shrink), input_gradient
+        )
     return (input_gradient, grad_shrink, grad_expand)
 
 

time: 309 us -> 304 us (0.984); the launches traced: 305 us -> 305 us
  other arithmetic: 17.2 us -> 3.45 us
  starting transfers between devices: 41.5 us -> 53.1 us
  Pallas kernels: 102 us -> 108 us
  waiting for transfers between devices: 122 us -> 118 us
    psum x1, waiting for transfers between devices: 64.5 us -> 0.01 us  [adapter_space(): return lax.psum(jnp.concatenate(from_owners(part)), 'tensor')]
    ppermute x11 -> x14, waiting for transfers between devices: 53.8 us -> 87.4 us  [along(): return lax.ppermute(x, 'tensor', pairs)]
    ppermute x8, waiting for transfers between devices: 3.8 us -> 30.6 us  [swap(): return lax.ppermute(x, 'tensor', pairs)]
    add x2 -> x0, other arithmetic: 10.2 us -> none  [exchange(): total = total + lax.ppermute(theirs, 'dp', pairs).astype(f32)]
    ppermute x11 -> x14, starting transfers between devices: 28.2 us -> 35.4 us  [along(): return lax.ppermute(x, 'tensor', pairs)]
    pallas_call x19 -> x22, Pallas kernels: 87.3 us -> 92 us  [product(): pl.pallas_call(functools.partial(product_kernel, len(adds), block_count),...]
    ppermute x8, starting transfers between devices: 13.3 us -> 16.5 us  [swap(): return lax.ppermute(x, 'tensor', pairs)]
    unnamed x44 -> x27, local copies, waits for them, and re-layouts: 7.35 us -> 6.78 us
  transfers between devices with their start and end apart: 22 -> 28, of which waited for: 8 -> 9; matrix products, arithmetic and copies ran while one was open for 5% -> 2% of each run, Pallas kernels for 30% -> 34%
where the time goes in v3:
time: 304 us; the launch traced here: 305 us
  waiting for transfers between devices  118 us (39%)
  Pallas kernels  108 us (36%)
  starting transfers between devices  53.1 us (17%)
  between operations  14.4 us (5%)
  local copies, waits for them, and re-layouts  7.43 us (2%)
  other arithmetic  3.45 us (1%)
    pallas_call x22, Pallas kernels, product(): pl.pallas_call(functools.partial(product_kernel, len(adds), block_count),...  92 us
    ppermute x14, waiting for transfers between devices, along(): return lax.ppermute(x, 'tensor', pairs)  87.4 us
    ppermute x14, starting transfers between devices, along(): return lax.ppermute(x, 'tensor', pairs)  35.4 us
    ppermute x8, waiting for transfers between devices, swap(): return lax.ppermute(x, 'tensor', pairs)  30.6 us
    ppermute x8, starting transfers between devices, swap(): return lax.ppermute(x, 'tensor', pairs)  16.5 us
    pallas_call x2, Pallas kernels, factor_sums(): pl.pallas_call(functools.partial(factor_kernel, slots_each, blocks, len(s...  10.1 us
    unnamed x27, local copies, waits for them, and re-layouts  6.78 us
  transfers between devices with their start and end apart: 28, of which 9 were waited for; matrix products, arithmetic and copies ran while one was open for 2% of the time, Pallas kernels for 34%

profile of v3, /device:TPU:10, one launch (start us, length us, event | category | flops | bytes accessed | tf_op | source)
XLA Modules:
  0.0 304.8 jit_solution(9972140880344880203)
XLA Ops:
  7.3 3.9 %shard_map.112.refs_3_ = bf16[512,1024]{1,0:T(8,128)(2,1)} custom-call(s32[1]{0:T(128)} %bitcast.6.refs_0_, bf16[1024,1024]{1,0:T(8,128)(2,1)} %refs_1_.45, bf16[8192,1024]{1,0:T(8,128)(2,1)} %refs_2_.43), custom_call_target="tpu_custom_call" | custom-call | flops 999999995904 | bytes 1000000000 | tf_op jit(solution)/shard_map/pallas_call | solution.py:88
  12.5 3.9 %shard_map.113.refs_3_ = bf16[512,1024]{1,0:T(8,128)(2,1)} custom-call(s32[1]{0:T(128)} %bitcast.5.refs_0_, bf16[1024,1024]{1,0:T(8,128)(2,1)} %refs_1_.45, bf16[8192,1024]{1,0:T(8,128)(2,1)} %refs_2_.43, bf16[512,1024]{1,0:T(8,128)(2,1)} %shard_map.112.refs_3_), custom_call_target="tpu_custom_call" | custom-call | flops 999999995904 | bytes 1000000000 | tf_op jit(solution)/shard_map/pallas_call | solution.py:88
  18.1 4.0 %shard_map.114.refs_3_ = bf16[512,1024]{1,0:T(8,128)(2,1)} custom-call(s32[1]{0:T(128)} %bitcast.4.refs_0_, bf16[1024,1024]{1,0:T(8,128)(2,1)} %refs_1_.45, bf16[8192,1024]{1,0:T(8,128)(2,1)} %refs_2_.43, bf16[512,1024]{1,0:T(8,128)(2,1)} %shard_map.113.refs_3_), custom_call_target="tpu_custom_call" | custom-call | flops 999999995904 | bytes 1000000000 | tf_op jit(solution)/shard_map/pallas_call | solution.py:88
  23.4 4.0 %shard_map.115.link = bf16[512,1024]{1,0:T(8,128)(2,1)} custom-call(s32[1]{0:T(128)} %bitcast.12.refs_0_, bf16[1024,1024]{1,0:T(8,128)(2,1)} %refs_1_.45, bf16[8192,1024]{1,0:T(8,128)(2,1)} %refs_2_.43, bf16[512,1024]{1,0:T(8,128)(2,1)} %shard_map.114.refs_3_), custom_call_target="tpu_custom_call" | custom-call | flops 999999995904 | bytes 1000000000 | tf_op jit(solution)/shard_map/pallas_call | solution.py:88
  27.3 1.7 collective-permute-start.9
  30.4 2.2 copy-done.3
  32.6 5.6 %shard_map.116.refs_4_ = bf16[1024,128]{1,0:T(8,128)(2,1)S(1)} custom-call(s32[8]{0:T(128)S(1)} %copy-done.2, bf16[1024,1024]{1,0:T(8,128)(2,1)} %refs_1_.45, bf16[16,128,1024]{2,1,0:T(8,128)(2,1)S(1)} %copy-done.3, bf16[512,1024]{1,0:T(8,128)(2,1)} %shard_map.115.link), custom_call_target="tpu_custom_call" | custom-call | flops 999999995904 | bytes 1000000000 | tf_op jit(solution)/shard_map/pallas_call | solution.py:113
  42.1 4.0 %shard_map.117.refs_4_ = bf16[512,1024]{1,0:T(8,128)(2,1)} custom-call(s32[1]{0:T(128)} %bitcast.11.refs_0_, bf16[1024,1024]{1,0:T(8,128)(2,1)} %refs_1_.45, bf16[8192,1024]{1,0:T(8,128)(2,1)} %refs_2_.43, bf16[512,1024]{1,0:T(8,128)(2,1)} %collective-permute-done.5.refs_3_, bf16[1024,128]{1,0:T(8,128)(2,1)S(1)} %shard_map.116.refs_4_), custom_call_target="tpu_custom_call" | custom-call | flops 999999995904 | bytes 1000000000 | tf_op jit(solution)/shard_map/pallas_call | solution.py:88
  46.2 4.0 %shard_map.118.refs_3_ = bf16[512,1024]{1,0:T(8,128)(2,1)} custom-call(s32[1]{0:T(128)} %bitcast.10.refs_0_, bf16[1024,1024]{1,0:T(8,128)(2,1)} %refs_1_.45, bf16[8192,1024]{1,0:T(8,128)(2,1)} %refs_2_.43, bf16[512,1024]{1,0:T(8,128)(2,1)} %collective-permute-done.4.refs_3_, bf16[512,1024]{1,0:T(8,128)(2,1)} %shard_map.117.refs_4_), custom_call_target="tpu_custom_call" | custom-call | flops 999999995904 | bytes 1000000000 | tf_op jit(solution)/shard_map/pallas_call | solution.py:88
  50.2 3.9 %shard_map.119.refs_3_ = bf16[512,1024]{1,0:T(8,128)(2,1)} custom-call(s32[1]{0:T(128)} %bitcast.9.refs_0_, bf16[1024,1024]{1,0:T(8,128)(2,1)} %refs_1_.45, bf16[8192,1024]{1,0:T(8,128)(2,1)} %refs_2_.43, bf16[512,1024]{1,0:T(8,128)(2,1)} %shard_map.118.refs_3_), custom_call_target="tpu_custom_call" | custom-call | flops 999999995904 | bytes 1000000000 | tf_op jit(solution)/shard_map/pallas_call | solution.py:88
  54.1 3.9 %shard_map.120.refs_4_ = bf16[512,1024]{1,0:T(8,128)(2,1)} custom-call(s32[1]{0:T(128)} %bitcast.8.refs_0_, bf16[1024,1024]{1,0:T(8,128)(2,1)} %refs_1_.45, bf16[8192,1024]{1,0:T(8,128)(2,1)} %refs_2_.43, bf16[512,1024]{1,0:T(8,128)(2,1)} %shard_map.119.refs_3_), custom_call_target="tpu_custom_call" | custom-call | flops 999999995904 | bytes 1000000000 | tf_op jit(solution)/shard_map/pallas_call | solution.py:88
  60.0 5.1 %shard_map.121.refs_4_ = f32[8,128,1024]{2,1,0:T(8,128)} custom-call(s32[16]{0:T(128)S(1)} %get-tuple-element.4.slots, f32[16]{0:T(128)S(1)} %convert_divide_fusion.scales, bf16[1024,128]{1,0:T(8,128)(2,1)} %bitcast_multiply_fusion.refs_0_, bf16[1024,1024]{1,0:T(8,128)(2,1)} %refs_1_.45, bf16[1024,128]{1,0:T(8,128)(2,1)} %collective-permute-done.2.refs_2_, ...), custom_call_target="tpu_custom_call" | custom-call | flops 999999995904 | bytes 1000000000 | tf_op jit(solution)/shard_map/pallas_call | solution.py:179
  65.1 1.9 collective-permute-done.refs_3_
  67.0 3.3 %collective-permute-start.10 = (bf16[512,1024]{1,0:T(8,128)(2,1)}, bf16[512,1024]{1,0:T(8,128)(2,1)}, u32[]{:S(2)}, u32[]{:S(2)}) collective-permute-start(bf16[512,1024]{1,0:T(8,128)(2,1)} %shard_map.117.refs_4_), channel_id=1, source_target_pairs={{2,4},{3,5},{4,2},{5,3},{10,12},{11,13},{12,10},{13,11},{18,20},{1... | collective-permute-start | bytes 3145736 | tf_op jit(solution)/shard_map/ppermute | solution.py:239
  70.4 2.2 copy-done.6
  72.6 4.1 %shard_map.122.refs_4_ = bf16[512,1024]{1,0:T(8,128)(2,1)} custom-call(s32[1]{0:T(128)} %bitcast.3.refs_0_, bf16[1024,1024]{1,0:T(8,128)(2,1)} %refs_1_.45, bf16[8192,1024]{1,0:T(8,128)(2,1)} %refs_2_.43, bf16[512,1024]{1,0:T(8,128)(2,1)} %collective-permute-done.refs_3_, f32[8,128,1024]{2,1,0:T(8,128)S(1)} %copy-done.6), custom_call_target="tpu_custom_call" | custom-call | flops 999999995904 | bytes 1000000000 | tf_op jit(solution)/shard_map/pallas_call | solution.py:88
  76.7 20.4 %collective-permute-done.10.refs_3_ = bf16[512,1024]{1,0:T(8,128)(2,1)} collective-permute-done((bf16[512,1024]{1,0:T(8,128)(2,1)}, bf16[512,1024]{1,0:T(8,128)(2,1)}, u32[]{:S(2)}, u32[]{:S(2)}) %collective-permute-start.10) | collective-permute-done | bytes 1048608 | tf_op jit(solution)/shard_map/ppermute | solution.py:239
  98.4 4.1 %shard_map.123.refs_4_ = bf16[512,1024]{1,0:T(8,128)(2,1)} custom-call(s32[1]{0:T(128)} %bitcast.17.refs_0_, bf16[1024,1024]{1,0:T(8,128)(2,1)} %refs_1_.45, bf16[8192,1024]{1,0:T(8,128)(2,1)} %refs_2_.43, bf16[512,1024]{1,0:T(8,128)(2,1)} %collective-permute-done.10.refs_3_, bf16[512,1024]{1,0:T(8,128)(2,1)} %shard_map.122.refs_4_), custom_call_target="tpu_custom_call" | custom-call | flops 999999995904 | bytes 1000000000 | tf_op jit(solution)/shard_map/pallas_call | solution.py:88
  102.4 3.3 %collective-permute-start.6 = (bf16[512,1024]{1,0:T(8,128)(2,1)}, bf16[512,1024]{1,0:T(8,128)(2,1)}, u32[]{:S(2)}, u32[]{:S(2)}) collective-permute-start(bf16[512,1024]{1,0:T(8,128)(2,1)} %shard_map.122.refs_4_), channel_id=1, source_target_pairs={{2,4},{3,5},{4,2},{5,3},{10,12},{11,13},{12,10},{13,11},{18,20},{1... | collective-permute-start | bytes 3145736 | tf_op jit(solution)/shard_map/ppermute | solution.py:239
  105.7 4.2 %shard_map.124.refs_3_ = bf16[512,1024]{1,0:T(8,128)(2,1)} custom-call(s32[1]{0:T(128)} %bitcast.16.refs_0_, bf16[1024,1024]{1,0:T(8,128)(2,1)} %refs_1_.45, bf16[8192,1024]{1,0:T(8,128)(2,1)} %refs_2_.43, bf16[512,1024]{1,0:T(8,128)(2,1)} %collective-permute-done.9.refs_3_, bf16[512,1024]{1,0:T(8,128)(2,1)} %shard_map.123.refs_4_), custom_call_target="tpu_custom_call" | custom-call | flops 999999995904 | bytes 1000000000 | tf_op jit(solution)/shard_map/pallas_call | solution.py:88
  109.9 3.9 %shard_map.125.refs_3_ = bf16[512,1024]{1,0:T(8,128)(2,1)} custom-call(s32[1]{0:T(128)} %bitcast.15.refs_0_, bf16[1024,1024]{1,0:T(8,128)(2,1)} %refs_1_.45, bf16[8192,1024]{1,0:T(8,128)(2,1)} %refs_2_.43, bf16[512,1024]{1,0:T(8,128)(2,1)} %shard_map.124.refs_3_), custom_call_target="tpu_custom_call" | custom-call | flops 999999995904 | bytes 1000000000 | tf_op jit(solution)/shard_map/pallas_call | solution.py:88
  113.8 3.9 %shard_map.126.refs_5_ = bf16[512,1024]{1,0:T(8,128)(2,1)} custom-call(s32[1]{0:T(128)} %bitcast.14.refs_0_, bf16[1024,1024]{1,0:T(8,128)(2,1)} %refs_1_.45, bf16[8192,1024]{1,0:T(8,128)(2,1)} %refs_2_.43, bf16[512,1024]{1,0:T(8,128)(2,1)} %shard_map.125.refs_3_), custom_call_target="tpu_custom_call" | custom-call | flops 999999995904 | bytes 1000000000 | tf_op jit(solution)/shard_map/pallas_call | solution.py:88
  117.7 12.9 %collective-permute-done.8.refs_4_ = bf16[512,1024]{1,0:T(8,128)(2,1)} collective-permute-done((bf16[512,1024]{1,0:T(8,128)(2,1)}, bf16[512,1024]{1,0:T(8,128)(2,1)}, u32[]{:S(2)}, u32[]{:S(2)}) %collective-permute-start.8) | collective-permute-done | bytes 1048608 | tf_op jit(solution)/shard_map/ppermute | solution.py:239
  130.6 4.4 %shard_map.127.refs_4_ = bf16[512,1024]{1,0:T(8,128)(2,1)} custom-call(s32[1]{0:T(128)} %bitcast.13.refs_0_, bf16[1024,1024]{1,0:T(8,128)(2,1)} %refs_1_.45, bf16[8192,1024]{1,0:T(8,128)(2,1)} %refs_2_.43, bf16[512,1024]{1,0:T(8,128)(2,1)} %collective-permute-done.7.refs_3_, bf16[512,1024]{1,0:T(8,128)(2,1)} %collective-permute-done.8.refs_4_, ...), custom_call_target="tpu_custom_call" | custom-call | flops 999999995904 | bytes 1000000000 | tf_op jit(solution)/shard_map/pallas_call | solution.py:88
  136.3 4.6 %collective-permute-start.13 = (bf16[512,1024]{1,0:T(8,128)(2,1)}, bf16[512,1024]{1,0:T(8,128)(2,1)}, u32[]{:S(2)}, u32[]{:S(2)}) collective-permute-start(bf16[512,1024]{1,0:T(8,128)(2,1)} %shard_map.127.refs_4_), channel_id=1, source_target_pairs={{0,2},{1,3},{2,4},{3,5},{8,10},{9,11},{10,12},{11,13},{16,18},{17,... | collective-permute-start | bytes 3145736 | tf_op jit(solution)/shard_map/ppermute | solution.py:239
  142.2 4.1 %shard_map.128.refs_3_ = bf16[512,1024]{1,0:T(8,128)(2,1)} custom-call(s32[1]{0:T(128)} %bitcast.2.refs_0_, bf16[1024,1024]{1,0:T(8,128)(2,1)} %refs_1_.45, bf16[8192,1024]{1,0:T(8,128)(2,1)} %refs_2_.43, bf16[512,1024]{1,0:T(8,128)(2,1)} %collective-permute-done.6.refs_3_, bf16[512,1024]{1,0:T(8,128)(2,1)} %shard_map.127.refs_4_), custom_call_target="tpu_custom_call" | custom-call | flops 999999995904 | bytes 1000000000 | tf_op jit(solution)/shard_map/pallas_call | solution.py:88
  146.3 3.9 %shard_map.129.refs_5_ = bf16[512,1024]{1,0:T(8,128)(2,1)} custom-call(s32[1]{0:T(128)} %bitcast.1.refs_0_, bf16[1024,1024]{1,0:T(8,128)(2,1)} %refs_1_.45, bf16[8192,1024]{1,0:T(8,128)(2,1)} %refs_2_.43, bf16[512,1024]{1,0:T(8,128)(2,1)} %shard_map.128.refs_3_), custom_call_target="tpu_custom_call" | custom-call | flops 999999995904 | bytes 1000000000 | tf_op jit(solution)/shard_map/pallas_call | solution.py:88
  150.2 3.5 %collective-permute-start.18 = (bf16[512,1024]{1,0:T(8,128)(2,1)}, bf16[512,1024]{1,0:T(8,128)(2,1)}, u32[]{:S(2)}, u32[]{:S(2)}) collective-permute-start(bf16[512,1024]{1,0:T(8,128)(2,1)} %shard_map.126.refs_5_), channel_id=1, source_target_pairs={{2,3},{3,2},{4,5},{5,4},{6,7},{7,6},{10,11},{11,10},{12,13},{13,12... | collective-permute-start | bytes 3145736 | tf_op jit(solution)/shard_map/ppermute | solution.py:235
  153.7 32.1 %collective-permute-done.16.refs_4_ = bf16[512,1024]{1,0:T(8,128)(2,1)} collective-permute-done((bf16[512,1024]{1,0:T(8,128)(2,1)}, bf16[512,1024]{1,0:T(8,128)(2,1)}, u32[]{:S(2)}, u32[]{:S(2)}) %collective-permute-start.16) | collective-permute-done | bytes 1048608 | tf_op jit(solution)/shard_map/ppermute | solution.py:239
  185.8 2.4 collective-permute-start.14
  188.2 4.5 %shard_map.130.refs_4_ = bf16[512,1024]{1,0:T(8,128)(2,1)} custom-call(s32[1]{0:T(128)} %bitcast.19.refs_0_, bf16[1024,1024]{1,0:T(8,128)(2,1)} %refs_1_.45, bf16[8192,1024]{1,0:T(8,128)(2,1)} %refs_2_.43, bf16[512,1024]{1,0:T(8,128)(2,1)} %collective-permute-done.15.refs_3_, bf16[512,1024]{1,0:T(8,128)(2,1)} %collective-permute-done.16.refs_4_, ...), custom_call_target="tpu_custom_call" | custom-call | flops 999999995904 | bytes 1000000000 | tf_op jit(solution)/shard_map/pallas_call | solution.py:88
  192.8 16.3 %collective-permute-done.14.refs_3_ = bf16[512,1024]{1,0:T(8,128)(2,1)} collective-permute-done((bf16[512,1024]{1,0:T(8,128)(2,1)}, bf16[512,1024]{1,0:T(8,128)(2,1)}, u32[]{:S(2)}, u32[]{:S(2)}) %collective-permute-start.14) | collective-permute-done | bytes 1048608 | tf_op jit(solution)/shard_map/ppermute | solution.py:239
  209.1 3.6 %collective-permute-start.12 = (bf16[512,1024]{1,0:T(8,128)(2,1)}, bf16[512,1024]{1,0:T(8,128)(2,1)}, u32[]{:S(2)}, u32[]{:S(2)}) collective-permute-start(bf16[512,1024]{1,0:T(8,128)(2,1)} %shard_map.125.refs_3_), channel_id=1, source_target_pairs={{0,1},{1,0},{2,3},{3,2},{4,5},{5,4},{8,9},{9,8},{10,11},{11,10},{1... | collective-permute-start | bytes 3145736 | tf_op jit(solution)/shard_map/ppermute | solution.py:235
  212.7 4.0 %shard_map.131.refs_5_ = bf16[512,1024]{1,0:T(8,128)(2,1)} custom-call(s32[1]{0:T(128)} %bitcast.1.refs_0_, bf16[1024,1024]{1,0:T(8,128)(2,1)} %refs_1_.45, bf16[8192,1024]{1,0:T(8,128)(2,1)} %refs_2_.43, bf16[512,1024]{1,0:T(8,128)(2,1)} %collective-permute-done.14.refs_3_, bf16[512,1024]{1,0:T(8,128)(2,1)} %shard_map.130.refs_4_), custom_call_target="tpu_custom_call" | custom-call | flops 999999995904 | bytes 1000000000 | tf_op jit(solution)/shard_map/pallas_call | solution.py:88
  218.0 16.4 %collective-permute-done.12.refs_3_ = bf16[512,1024]{1,0:T(8,128)(2,1)} collective-permute-done((bf16[512,1024]{1,0:T(8,128)(2,1)}, bf16[512,1024]{1,0:T(8,128)(2,1)}, u32[]{:S(2)}, u32[]{:S(2)}) %collective-permute-start.12) | collective-permute-done | bytes 1048608 | tf_op jit(solution)/shard_map/ppermute | solution.py:235
  234.4 2.4 collective-permute-start.24
  236.8 4.5 %shard_map.132.refs_5_ = bf16[512,1024]{1,0:T(8,128)(2,1)} custom-call(s32[1]{0:T(128)} %bitcast.18.refs_0_, bf16[1024,1024]{1,0:T(8,128)(2,1)} %refs_1_.45, bf16[8192,1024]{1,0:T(8,128)(2,1)} %refs_2_.43, bf16[512,1024]{1,0:T(8,128)(2,1)} %collective-permute-done.12.refs_3_, bf16[512,1024]{1,0:T(8,128)(2,1)} %collective-permute-done.13.refs_4_, ...), custom_call_target="tpu_custom_call" | custom-call | flops 999999995904 | bytes 1000000000 | tf_op jit(solution)/shard_map/pallas_call | solution.py:88
  242.5 5.9 %collective-permute-start.23 = (bf16[512,1024]{1,0:T(8,128)(2,1)}, bf16[512,1024]{1,0:T(8,128)(2,1)}, u32[]{:S(2)}, u32[]{:S(2)}) collective-permute-start(bf16[512,1024]{1,0:T(8,128)(2,1)} %shard_map.128.refs_3_), channel_id=1, source_target_pairs={{4,6},{5,7},{2,0},{3,1},{12,14},{13,15},{10,8},{11,9},{20,22},{21,... | collective-permute-start | bytes 3145736 | tf_op jit(solution)/shard_map/ppermute | solution.py:239
  248.4 4.4 %shard_map.133.link = bf16[512,1024]{1,0:T(8,128)(2,1)} custom-call(s32[1]{0:T(128)} %bitcast.20.refs_0_, bf16[1024,1024]{1,0:T(8,128)(2,1)} %refs_1_.45, bf16[8192,1024]{1,0:T(8,128)(2,1)} %refs_2_.43, bf16[512,1024]{1,0:T(8,128)(2,1)} %collective-permute-done.18.refs_3_, bf16[512,1024]{1,0:T(8,128)(2,1)} %collective-permute-done.19.refs_4_, ...), custom_call_target="tpu_custom_call" | custom-call | flops 999999995904 | bytes 1000000000 | tf_op jit(solution)/shard_map/pallas_call | solution.py:88
  254.6 1.9 collective-permute-start.20
  256.5 3.9 %collective-permute-start.17 = (bf16[512,1024]{1,0:T(8,128)(2,1)}, bf16[512,1024]{1,0:T(8,128)(2,1)}, u32[]{:S(2)}, u32[]{:S(2)}) collective-permute-start(bf16[512,1024]{1,0:T(8,128)(2,1)} %shard_map.132.refs_5_), channel_id=1, source_target_pairs={{0,2},{1,3},{2,4},{3,5},{4,6},{5,7},{8,10},{9,11},{10,12},{11,13},... | collective-permute-start | bytes 3145736 | tf_op jit(solution)/shard_map/ppermute | solution.py:239
  260.5 2.7 collective-permute-start.22
  263.1 4.5 %collective-permute-done.11.refs_8_.refs_3_ = bf16[512,1024]{1,0:T(8,128)(2,1)} collective-permute-done((bf16[512,1024]{1,0:T(8,128)(2,1)}, bf16[512,1024]{1,0:T(8,128)(2,1)}, u32[]{:S(2)}, u32[]{:S(2)}) %collective-permute-start.11) | collective-permute-done | bytes 1048608 | tf_op jit(solution)/shard_map/ppermute | solution.py:235
  267.6 3.7 %collective-permute-done.23.refs_5_.refs_4_ = bf16[512,1024]{1,0:T(8,128)(2,1)} collective-permute-done((bf16[512,1024]{1,0:T(8,128)(2,1)}, bf16[512,1024]{1,0:T(8,128)(2,1)}, u32[]{:S(2)}, u32[]{:S(2)}) %collective-permute-start.23) | collective-permute-done | bytes 1048608 | tf_op jit(solution)/shard_map/ppermute | solution.py:239
  271.3 5.0 %shard_map.135.refs_12_ = f32[8,1024,128]{2,1,0:T(8,128)} custom-call(s32[16]{0:T(128)S(1)} %get-tuple-element.4.slots, f32[16]{0:T(128)S(1)} %broadcast_3_scales.2.scales, bf16[1024,1024]{1,0:T(8,128)(2,1)} %refs_0_.1, bf16[1024,128]{1,0:T(8,128)(2,1)S(1)} %get-tuple-element.6.refs_1_, bf16[1024,1024]{1,0:T(8,128)(2,1)} %collective-permute-done.26.refs_2_, ...), custom_call_target="tpu_custom_call" | custom-call | flops 999999995904 | bytes 1000000000 | tf_op jit(solution)/shard_map/pallas_call | solution.py:179
  276.3 9.7 %collective-permute-done.22.refs_3_ = bf16[512,1024]{1,0:T(8,128)(2,1)} collective-permute-done((bf16[512,1024]{1,0:T(8,128)(2,1)}, bf16[512,1024]{1,0:T(8,128)(2,1)}, u32[]{:S(2)}, u32[]{:S(2)}) %collective-permute-start.22) | collective-permute-done | bytes 1048608 | tf_op jit(solution)/shard_map/ppermute | solution.py:235
  286.0 5.1 %shard_map.136.refs_11_ = bf16[1024,1024]{1,0:T(8,128)(2,1)S(1)} custom-call(s32[5]{0:T(128)S(1)} %pad_add_fusion.2.refs_0_, bf16[1024,1024]{1,0:T(8,128)(2,1)} %refs_1_.45, bf16[8192,1024]{1,0:T(8,128)(2,1)} %refs_2_.43, bf16[512,1024]{1,0:T(8,128)(2,1)} %collective-permute-done.22.refs_3_, bf16[512,1024]{1,0:T(8,128)(2,1)} %collective-permute-done.23.refs_5_.refs_4_, ...), custom_call_target="tpu_custom_call" | custom-call | flops 999999995904 | bytes 1000000000 | tf_op jit(solution)/shard_map/pallas_call | solution.py:88
  292.5 5.4 %shard_map.137 = bf16[1024,1024]{1,0:T(8,128)(2,1)} custom-call(s32[5]{0:T(128)S(1)} %pad_add_fusion.refs_0_, bf16[1024,1024]{1,0:T(8,128)(2,1)} %refs_1_.45, bf16[8192,1024]{1,0:T(8,128)(2,1)} %refs_2_.43, bf16[512,1024]{1,0:T(8,128)(2,1)} %collective-permute-done.11.refs_8_.refs_3_, ...), custom_call_target="tpu_custom_call", output_to_operand_aliasing={{}: (12, {})} | custom-call | flops 999999995904 | bytes 1000000000 | tf_op jit(solution)/shard_map/pallas_call | solution.py:88
  (76 shorter events, 21.2 us)
Async XLA Ops:
  7.2 245.6 %all-reduce.2.cloned.1.call-start = ((), (), s32[]{:S(2)}) async-start(), calls=%async_computation | async-start | bytes 1048576 | tf_op jit(solution)/shard_map/psum | solution.py:355
  7.2 31.2 %collective-permute-start.1 = (s32[8]{0:T(128)}, s32[8]{0:T(128)}, u32[]{:S(2)}, u32[]{:S(2)}) collective-permute-start(s32[8]{0:T(128)} %tenants.1), channel_id=1, source_target_pairs={{0,8},{8,0},{1,9},{9,1},{2,10},{10,2},{3,11},{11,3},{4,12},{12,4},... | collective-permute-start | bytes 104 | tf_op jit(solution)/shard_map/ppermute | solution.py:331
  11.2 30.4 %collective-permute-start.5 = (bf16[512,1024]{1,0:T(8,128)(2,1)}, bf16[512,1024]{1,0:T(8,128)(2,1)}, u32[]{:S(2)}, u32[]{:S(2)}) collective-permute-start(bf16[512,1024]{1,0:T(8,128)(2,1)} %shard_map.112.refs_3_), channel_id=1, source_target_pairs={{0,2},{1,3},{6,4},{7,5},{8,10},{9,11},{14,12},{15,13},{16,18},{17,... | collective-permute-start | bytes 3145736 | tf_op jit(solution)/shard_map/ppermute | solution.py:239
  16.4 29.7 %collective-permute-start.4 = (bf16[512,1024]{1,0:T(8,128)(2,1)}, bf16[512,1024]{1,0:T(8,128)(2,1)}, u32[]{:S(2)}, u32[]{:S(2)}) collective-permute-start(bf16[512,1024]{1,0:T(8,128)(2,1)} %shard_map.113.refs_3_), channel_id=1, source_target_pairs={{0,1},{1,0},{6,7},{7,6},{8,9},{9,8},{14,15},{15,14},{16,17},{17,16... | collective-permute-start | bytes 3145736 | tf_op jit(solution)/shard_map/ppermute | solution.py:235
  22.0 45.0 %collective-permute-start = (bf16[512,1024]{1,0:T(8,128)(2,1)}, bf16[512,1024]{1,0:T(8,128)(2,1)}, u32[]{:S(2)}, u32[]{:S(2)}) collective-permute-start(bf16[512,1024]{1,0:T(8,128)(2,1)} %shard_map.114.refs_3_), channel_id=1, source_target_pairs={{0,2},{1,3},{6,4},{7,5},{8,10},{9,11},{14,12},{15,13},{16,18},{17,... | collective-permute-start | bytes 3145736 | tf_op jit(solution)/shard_map/ppermute | solution.py:239
  23.3 5.7 %copy-start.2 = (s32[8]{0:T(128)S(1)}, s32[8]{0:T(128)}, u32[]{:S(2)}) copy-start(s32[8]{0:T(128)} %tenants.1) | copy-start | bytes 100
  23.3 6.3 %copy-start.11 = (s32[16]{0:T(128)S(1)}, s32[16]{0:T(128)}, u32[]{:S(2)}) copy-start(s32[16]{0:T(128)} %param.17) | copy-start | bytes 196
  27.3 75.1 %collective-permute-start.9 = (bf16[512,1024]{1,0:T(8,128)(2,1)}, bf16[512,1024]{1,0:T(8,128)(2,1)}, u32[]{:S(2)}, u32[]{:S(2)}) collective-permute-start(bf16[512,1024]{1,0:T(8,128)(2,1)} %shard_map.115.link), channel_id=1, source_target_pairs={{0,1},{1,0},{6,7},{7,6},{8,9},{9,8},{14,15},{15,14},{16,17},{17,16... | collective-permute-start | bytes 3145736 | tf_op jit(solution)/shard_map/ppermute | solution.py:235
  30.4 2.2 copy-start.3
  32.5 5.6 %copy-start.12 = (s32[16]{0:T(128)S(1)}, s32[16]{0:T(128)}, u32[]{:S(2)}) copy-start(s32[16]{0:T(128)} %convert_reduce_fusion) | copy-start | bytes 196
  32.5 5.7 %copy-start.10 = (s32[4]{0:T(128)S(1)}, s32[4]{0:T(128)}, u32[]{:S(2)}) copy-start(s32[4]{0:T(128)} %get-tuple-element.7) | copy-start | bytes 52
  32.5 5.7 %copy-start.9 = (s32[4]{0:T(128)S(1)}, s32[4]{0:T(128)}, u32[]{:S(2)}) copy-start(s32[4]{0:T(128)} %get-tuple-element.8) | copy-start | bytes 52
  32.5 7.0 %copy-start.8 = (s32[16]{0:T(128)S(1)}, s32[16]{0:T(128)}, u32[]{:S(2)}) copy-start(s32[16]{0:T(128)} %param.16) | copy-start | bytes 196
  32.6 7.3 %copy-start.7 = (bf16[1024,128]{1,0:T(8,128)(2,1)S(1)}, bf16[1024,128]{1,0:T(8,128)(2,1)}, u32[]{:S(2)}) copy-start(bf16[1024,128]{1,0:T(8,128)(2,1)} %param.11) | copy-start | bytes 786436
  38.4 2.2 collective-permute-start.21
  39.8 0.8 copy-start
  40.6 18.9 %collective-permute-start.3 = (bf16[1024,1024]{1,0:T(8,128)(2,1)}, bf16[1024,1024]{1,0:T(8,128)(2,1)}, u32[]{:S(2)}, u32[]{:S(2)}) collective-permute-start(bf16[1024,1024]{1,0:T(8,128)(2,1)} %refs_1_.45), channel_id=1, source_target_pairs={{0,8},{8,0},{1,9},{9,1},{2,10},{10,2},{3,11},{11,3},{4,12},{12,4},... | collective-permute-start | bytes 6291464 | tf_op jit(solution)/shard_map/ppermute | solution.py:331
  41.6 213.0 %collective-permute-start.26 = (bf16[1024,1024]{1,0:T(8,128)(2,1)}, bf16[1024,1024]{1,0:T(8,128)(2,1)}, u32[]{:S(2)}, u32[]{:S(2)}) collective-permute-start(bf16[1024,1024]{1,0:T(8,128)(2,1)} %refs_0_.1), channel_id=1, source_target_pairs={{0,8},{8,0},{1,9},{9,1},{2,10},{10,2},{3,11},{11,3},{4,12},{12,4},... | collective-permute-start | bytes 6291464 | tf_op jit(solution)/shard_map/ppermute | solution.py:331
  46.1 11.9 %collective-permute-start.2 = (bf16[1024,128]{1,0:T(8,128)(2,1)}, bf16[1024,128]{1,0:T(8,128)(2,1)}, u32[]{:S(2)}, u32[]{:S(2)}) collective-permute-start(bf16[1024,128]{1,0:T(8,128)(2,1)} %bitcast_multiply_fusion.refs_0_), channel_id=1, source_target_pairs={{0,8},{8,0},{1,9},{9,1},{2,10},{10,2},{3,11},{11,3},{4,12},{12,4},... | collective-permute-start | bytes 786440 | tf_op jit(solution)/shard_map/ppermute | solution.py:331
  58.0 59.7 %collective-permute-start.7 = (bf16[512,1024]{1,0:T(8,128)(2,1)}, bf16[512,1024]{1,0:T(8,128)(2,1)}, u32[]{:S(2)}, u32[]{:S(2)}) collective-permute-start(bf16[512,1024]{1,0:T(8,128)(2,1)} %shard_map.119.refs_3_), channel_id=1, source_target_pairs={{0,1},{1,0},{2,3},{3,2},{4,5},{5,4},{6,7},{7,6},{8,9},{9,8},{10,11... | collective-permute-start | bytes 3145736 | tf_op jit(solution)/shard_map/ppermute | solution.py:235
  59.5 90.6 %collective-permute-start.15 = (bf16[512,1024]{1,0:T(8,128)(2,1)}, bf16[512,1024]{1,0:T(8,128)(2,1)}, u32[]{:S(2)}, u32[]{:S(2)}) collective-permute-start(bf16[512,1024]{1,0:T(8,128)(2,1)} %shard_map.120.refs_4_), channel_id=1, source_target_pairs={{0,1},{1,0},{2,3},{3,2},{4,5},{5,4},{6,7},{7,6},{8,9},{9,8},{10,11... | collective-permute-start | bytes 3145736 | tf_op jit(solution)/shard_map/ppermute | solution.py:235
  67.0 30.0 %collective-permute-start.10 = (bf16[512,1024]{1,0:T(8,128)(2,1)}, bf16[512,1024]{1,0:T(8,128)(2,1)}, u32[]{:S(2)}, u32[]{:S(2)}) collective-permute-start(bf16[512,1024]{1,0:T(8,128)(2,1)} %shard_map.117.refs_4_), channel_id=1, source_target_pairs={{2,4},{3,5},{4,2},{5,3},{10,12},{11,13},{12,10},{13,11},{18,20},{1... | collective-permute-start | bytes 3145736 | tf_op jit(solution)/shard_map/ppermute | solution.py:239
  70.4 2.2 copy-start.6
  97.1 33.5 %collective-permute-start.8 = (bf16[512,1024]{1,0:T(8,128)(2,1)}, bf16[512,1024]{1,0:T(8,128)(2,1)}, u32[]{:S(2)}, u32[]{:S(2)}) collective-permute-start(bf16[512,1024]{1,0:T(8,128)(2,1)} %shard_map.118.refs_3_), channel_id=1, source_target_pairs={{0,2},{1,3},{6,4},{7,5},{8,10},{9,11},{14,12},{15,13},{16,18},{17,... | collective-permute-start | bytes 3145736 | tf_op jit(solution)/shard_map/ppermute | solution.py:239
  102.4 38.4 %collective-permute-start.6 = (bf16[512,1024]{1,0:T(8,128)(2,1)}, bf16[512,1024]{1,0:T(8,128)(2,1)}, u32[]{:S(2)}, u32[]{:S(2)}) collective-permute-start(bf16[512,1024]{1,0:T(8,128)(2,1)} %shard_map.122.refs_4_), channel_id=1, source_target_pairs={{2,4},{3,5},{4,2},{5,3},{10,12},{11,13},{12,10},{13,11},{18,20},{1... | collective-permute-start | bytes 3145736 | tf_op jit(solution)/shard_map/ppermute | solution.py:239
  135.0 106.2 %collective-permute-start.19 = (bf16[512,1024]{1,0:T(8,128)(2,1)}, bf16[512,1024]{1,0:T(8,128)(2,1)}, u32[]{:S(2)}, u32[]{:S(2)}) collective-permute-start(bf16[512,1024]{1,0:T(8,128)(2,1)} %shard_map.127.refs_4_), channel_id=1, source_target_pairs={{4,2},{5,3},{6,4},{7,5},{12,10},{13,11},{14,12},{15,13},{20,18},{2... | collective-permute-start | bytes 3145736 | tf_op jit(solution)/shard_map/ppermute | solution.py:239
  136.3 80.4 %collective-permute-start.13 = (bf16[512,1024]{1,0:T(8,128)(2,1)}, bf16[512,1024]{1,0:T(8,128)(2,1)}, u32[]{:S(2)}, u32[]{:S(2)}) collective-permute-start(bf16[512,1024]{1,0:T(8,128)(2,1)} %shard_map.127.refs_4_), channel_id=1, source_target_pairs={{0,2},{1,3},{2,4},{3,5},{8,10},{9,11},{10,12},{11,13},{16,18},{17,... | collective-permute-start | bytes 3145736 | tf_op jit(solution)/shard_map/ppermute | solution.py:239
  140.9 44.9 %collective-permute-start.16 = (bf16[512,1024]{1,0:T(8,128)(2,1)}, bf16[512,1024]{1,0:T(8,128)(2,1)}, u32[]{:S(2)}, u32[]{:S(2)}) collective-permute-start(bf16[512,1024]{1,0:T(8,128)(2,1)} %shard_map.124.refs_3_), channel_id=1, source_target_pairs={{0,2},{1,3},{6,4},{7,5},{8,10},{9,11},{14,12},{15,13},{16,18},{17,... | collective-permute-start | bytes 3145736 | tf_op jit(solution)/shard_map/ppermute | solution.py:239
  150.2 92.3 %collective-permute-start.18 = (bf16[512,1024]{1,0:T(8,128)(2,1)}, bf16[512,1024]{1,0:T(8,128)(2,1)}, u32[]{:S(2)}, u32[]{:S(2)}) collective-permute-start(bf16[512,1024]{1,0:T(8,128)(2,1)} %shard_map.126.refs_5_), channel_id=1, source_target_pairs={{2,3},{3,2},{4,5},{5,4},{6,7},{7,6},{10,11},{11,10},{12,13},{13,12... | collective-permute-start | bytes 3145736 | tf_op jit(solution)/shard_map/ppermute | solution.py:235
  185.8 23.3 %collective-permute-start.14 = (bf16[512,1024]{1,0:T(8,128)(2,1)}, bf16[512,1024]{1,0:T(8,128)(2,1)}, u32[]{:S(2)}, u32[]{:S(2)}) collective-permute-start(bf16[512,1024]{1,0:T(8,128)(2,1)} %shard_map.123.refs_4_), channel_id=1, source_target_pairs={{4,6},{5,7},{2,0},{3,1},{12,14},{13,15},{10,8},{11,9},{20,22},{21,... | collective-permute-start | bytes 3145736 | tf_op jit(solution)/shard_map/ppermute | solution.py:239
  209.1 25.3 %collective-permute-start.12 = (bf16[512,1024]{1,0:T(8,128)(2,1)}, bf16[512,1024]{1,0:T(8,128)(2,1)}, u32[]{:S(2)}, u32[]{:S(2)}) collective-permute-start(bf16[512,1024]{1,0:T(8,128)(2,1)} %shard_map.125.refs_3_), channel_id=1, source_target_pairs={{0,1},{1,0},{2,3},{3,2},{4,5},{5,4},{8,9},{9,8},{10,11},{11,10},{1... | collective-permute-start | bytes 3145736 | tf_op jit(solution)/shard_map/ppermute | solution.py:235
  216.7 39.8 %collective-permute-start.25 = (bf16[512,1024]{1,0:T(8,128)(2,1)}, bf16[512,1024]{1,0:T(8,128)(2,1)}, u32[]{:S(2)}, u32[]{:S(2)}) collective-permute-start(bf16[512,1024]{1,0:T(8,128)(2,1)} %shard_map.130.refs_4_), channel_id=1, source_target_pairs={{4,2},{5,3},{6,4},{7,5},{12,10},{13,11},{14,12},{15,13},{20,18},{2... | collective-permute-start | bytes 3145736 | tf_op jit(solution)/shard_map/ppermute | solution.py:239
  234.4 26.1 %collective-permute-start.24 = (bf16[512,1024]{1,0:T(8,128)(2,1)}, bf16[512,1024]{1,0:T(8,128)(2,1)}, u32[]{:S(2)}, u32[]{:S(2)}) collective-permute-start(bf16[512,1024]{1,0:T(8,128)(2,1)} %shard_map.130.refs_4_), channel_id=1, source_target_pairs={{0,2},{1,3},{2,4},{3,5},{8,10},{9,11},{10,12},{11,13},{16,18},{17,... | collective-permute-start | bytes 3145736 | tf_op jit(solution)/shard_map/ppermute | solution.py:239
  241.2 26.4 %collective-permute-start.11 = (bf16[512,1024]{1,0:T(8,128)(2,1)}, bf16[512,1024]{1,0:T(8,128)(2,1)}, u32[]{:S(2)}, u32[]{:S(2)}) collective-permute-start(bf16[512,1024]{1,0:T(8,128)(2,1)} %shard_map.129.refs_5_), channel_id=1, source_target_pairs={{0,1},{1,0},{2,3},{3,2},{4,5},{5,4},{6,7},{7,6},{8,9},{9,8},{10,11... | collective-permute-start | bytes 3145736 | tf_op jit(solution)/shard_map/ppermute | solution.py:235
  242.5 28.8 %collective-permute-start.23 = (bf16[512,1024]{1,0:T(8,128)(2,1)}, bf16[512,1024]{1,0:T(8,128)(2,1)}, u32[]{:S(2)}, u32[]{:S(2)}) collective-permute-start(bf16[512,1024]{1,0:T(8,128)(2,1)} %shard_map.128.refs_3_), channel_id=1, source_target_pairs={{4,6},{5,7},{2,0},{3,1},{12,14},{13,15},{10,8},{11,9},{20,22},{21,... | collective-permute-start | bytes 3145736 | tf_op jit(solution)/shard_map/ppermute | solution.py:239
  248.4 4.4 %copy-start.1 = (s32[16]{0:T(128)S(1)}, s32[16]{0:T(128)}, u32[]{:S(2)}) copy-start(s32[16]{0:T(128)} %copy-done) | copy-start | bytes 196
  252.8 1.0 copy-start.5
  254.6 37.9 %collective-permute-start.20 = (bf16[512,1024]{1,0:T(8,128)(2,1)}, bf16[512,1024]{1,0:T(8,128)(2,1)}, u32[]{:S(2)}, u32[]{:S(2)}) collective-permute-start(bf16[512,1024]{1,0:T(8,128)(2,1)} %shard_map.133.link), channel_id=1, source_target_pairs={{2,0},{3,1},{4,2},{5,3},{6,4},{7,5},{10,8},{11,9},{12,10},{13,11},... | collective-permute-start | bytes 3145736 | tf_op jit(solution)/shard_map/ppermute | solution.py:239
  256.5 36.0 %collective-permute-start.17 = (bf16[512,1024]{1,0:T(8,128)(2,1)}, bf16[512,1024]{1,0:T(8,128)(2,1)}, u32[]{:S(2)}, u32[]{:S(2)}) collective-permute-start(bf16[512,1024]{1,0:T(8,128)(2,1)} %shard_map.132.refs_5_), channel_id=1, source_target_pairs={{0,2},{1,3},{2,4},{3,5},{4,6},{5,7},{8,10},{9,11},{10,12},{11,13},... | collective-permute-start | bytes 3145736 | tf_op jit(solution)/shard_map/ppermute | solution.py:239
  260.5 25.6 %collective-permute-start.22 = (bf16[512,1024]{1,0:T(8,128)(2,1)}, bf16[512,1024]{1,0:T(8,128)(2,1)}, u32[]{:S(2)}, u32[]{:S(2)}) collective-permute-start(bf16[512,1024]{1,0:T(8,128)(2,1)} %shard_map.131.refs_5_), channel_id=1, source_target_pairs={{0,1},{1,0},{2,3},{3,2},{4,5},{5,4},{6,7},{7,6},{8,9},{9,8},{10,11... | collective-permute-start | bytes 3145736 | tf_op jit(solution)/shard_map/ppermute | solution.py:235
  271.3 14.7 %copy-start.4 = (bf16[16,1024,128]{2,1,0:T(8,128)(2,1)S(1)}, bf16[16,1024,128]{2,1,0:T(8,128)(2,1)}, u32[]{:S(2)}) copy-start(bf16[16,1024,128]{2,1,0:T(8,128)(2,1)} %refs_10_.3) | copy-start | bytes 12582916
Sparse Core Ops, SparseCore 0:
  41.7 83.5 all-reduce.1

commit v4 on v0

--- a/solution.py
+++ b/solution.py
@@ -1,12 +1,348 @@
+import functools
+
 import jax
 import jax.numpy as jnp
 from jax import lax
+from jax.experimental import pallas as pl
+from jax.experimental.pallas import tpu as pltpu
 from jax.sharding import PartitionSpec as P
 
 adapter_alpha = 32.0
+row_block = 128
+bf16 = jnp.bfloat16
+f32 = jnp.float32
+contract_last = (((1,), (1,)), ((), ()))
+contract_first = (((0,), (0,)), ((), ()))
+vmem_bytes = 40 * 1024 * 1024
+declared = pl.CostEstimate(flops=10**12, bytes_accessed=10**9, transcendentals=0)
+
+
+def params():
+    return pltpu.CompilerParams(vmem_limit_bytes=vmem_bytes)
+
+
+def product_kernel(modes, block_count, *refs):
+    position = 1
+    rows, weights = refs[1], refs[2]
+    position = 3
+    total = lax.dot_general(
+        rows[...], weights[...], contract_last, preferred_element_type=f32
+    )
+    for mode in modes:
+        addend = refs[position][...].astype(f32)
+        if mode:
+            addend = addend * refs[0][1 + mode].astype(f32)
+        total = total + addend
+        position += 1
+    if block_count:
+        low = refs[position]
+        position += 1
+        terms = []
+        for i in range(block_count):
+            terms.append(
+                lax.dot_general(
+                    low[i * row_block : (i + 1) * row_block, :],
+                    refs[position][0],
+                    contract_last,
+                    preferred_element_type=f32,
+                )
+            )
+            position += 1
+        total = total + jnp.concatenate(terms, axis=0)
+    refs[-1][...] = total.astype(refs[-1].dtype)
+
+
+def product(scalars, gradient, weights, piece, piece_rows, width, adds, link, adapter=None, whole=None):
+    depth = gradient.shape[1]
+    tile = min(width, 512)
+    while width % tile:
+        tile //= 2
+    steps = width // tile
+    in_specs = [
+        pl.BlockSpec((piece_rows, depth), lambda j, s: (s[1], 0)),
+        pl.BlockSpec((tile, depth), lambda j, s: (s[0] * steps + j, 0)),
+    ]
+    operands = [gradient, weights]
+    for array, _ in adds:
+        in_specs.append(pl.BlockSpec((piece_rows, tile), lambda j, s: (0, j)))
+        operands.append(array)
+    block_count = 0
+    if adapter is not None:
+        low, shrink = adapter
+        rank = low.shape[1]
+        block_count = piece_rows // row_block
+        in_specs.append(pl.BlockSpec((piece_rows, rank), lambda j, s: (piece, 0)))
+        operands.append(low)
+        for i in range(block_count):
+            in_specs.append(
+                pl.BlockSpec((1, tile, rank), functools.partial(lambda j, s, i: (s[4 + i], j, 0), i=i))
+            )
+            operands.append(shrink)
+    for array in link:
+        in_specs.append(pl.BlockSpec(memory_space=pl.ANY))
+        operands.append(array)
+    out_piece, out_rows, aliases = 0, piece_rows, {}
+    if adapter is not None:
+        out_piece, out_rows = piece, gradient.shape[0]
+        if whole is not None:
+            in_specs.append(pl.BlockSpec(memory_space=pl.ANY))
+            operands.append(whole)
+            aliases = {len(operands): 0}
+    return pl.pallas_call(
+        functools.partial(product_kernel, tuple(mode for _, mode in adds), block_count),
+        grid_spec=pltpu.PrefetchScalarGridSpec(
+            num_scalar_prefetch=1,
+            grid=(steps,),
+            in_specs=in_specs,
+            out_specs=pl.BlockSpec((piece_rows, tile), lambda j, s: (out_piece, j)),
+        ),
+        out_shape=jax.ShapeDtypeStruct((out_rows, width), bf16),
+        input_output_aliases=aliases,
+        compiler_params=params(),
+        cost_estimate=declared,
+    )(scalars, *operands)
+
+
+def low_kernel(tenants, rows, expand, link, out):
+    out[...] = lax.dot_general(
+        rows[...], expand[0], contract_last, preferred_element_type=f32
+    ).astype(out.dtype)
+
+
+def low_product(tenants, gradient, expand, link):
+    count_of_rows, depth = gradient.shape
+    rank = expand.shape[1]
+    return pl.pallas_call(
+        low_kernel,
+        grid_spec=pltpu.PrefetchScalarGridSpec(
+            num_scalar_prefetch=1,
+            grid=(count_of_rows // row_block,),
+            in_specs=[
+                pl.BlockSpec((row_block, depth), lambda b, s: (b, 0)),
+                pl.BlockSpec((1, rank, depth), lambda b, s: (s[b], 0, 0)),
+                pl.BlockSpec(memory_space=pl.ANY),
+            ],
+            out_specs=pl.BlockSpec((row_block, rank), lambda b, s: (b, 0)),
+        ),
+        out_shape=jax.ShapeDtypeStruct((count_of_rows, rank), bf16),
+        compiler_params=params(),
+        cost_estimate=declared,
+    )(tenants, gradient, expand, link)
+
+
+def scale_kernel(ranks, scales, low, link, out):
+    columns = lax.broadcasted_iota(jnp.int32, (row_block, low.shape[1]), 1)
+    for b in range(low.shape[0] // row_block):
+        here = pl.ds(b * row_block, row_block)
+        kept = jnp.where(columns < ranks[b], low[here, :].astype(f32) * scales[b], 0.0)
+        out[here, :] = kept.astype(out.dtype)
+
+
+def scaled_low(ranks, scales, low, link):
+    whole = pl.BlockSpec(memory_space=pltpu.VMEM)
+    return pl.pallas_call(
+        scale_kernel,
+        in_specs=[pl.BlockSpec(memory_space=pltpu.SMEM)] * 2
+        + [whole, pl.BlockSpec(memory_space=pl.ANY)],
+        out_specs=whole,
+        out_shape=jax.ShapeDtypeStruct(low.shape, bf16),
+        compiler_params=params(),
+        cost_estimate=declared,
+    )(ranks, scales, low, link)
+
+
+def factor_kernel(slots_each, slots, scales, left, right, *refs):
+    own = refs[-1]
+    own[...] = jnp.zeros_like(own)
+    for b in range(left.shape[0] // row_block):
+        slot = slots[b]
+
+        @pl.when(slot < slots_each)
+        def _():
+            here = pl.ds(b * row_block, row_block)
+            piece = lax.dot_general(
+                left[here, :], right[here, :], contract_first, preferred_element_type=f32
+            )
+            own[slot] += piece * scales[b]
+
+
+def factor_sums(slots, scales, left, right, slots_each, link):
+    whole = pl.BlockSpec(memory_space=pltpu.VMEM)
+    return pl.pallas_call(
+        functools.partial(factor_kernel, slots_each),
+        in_specs=[pl.BlockSpec(memory_space=pltpu.SMEM)] * 2
+        + [whole] * 2
+        + [pl.BlockSpec(memory_space=pl.ANY)] * len(link),
+        out_specs=whole,
+        out_shape=jax.ShapeDtypeStruct((slots_each, left.shape[1], right.shape[1]), f32),
+        compiler_params=params(),
+        cost_estimate=declared,
+    )(slots, scales, left, right, *link)
 
 
 def per_device(
+    owner_count,
+    gradient,
+    projection_input,
+    saved_lowrank,
+    weights,
+    shrink,
+    expand,
+    tenant_per_block,
+    tenant_adapter_rank,
+    tenant_owner_index,
+):
+    count_of_rows, width = gradient.shape
+    blocks = count_of_rows // row_block
+    tenants = tenant_adapter_rank.shape[0]
+    rank_extent = shrink.shape[2]
+    node = lax.axis_index("tensor") // 2
+    side = lax.axis_index("tensor") % 2
+    owner = lax.axis_index("dp")
+    at_end = (node == 0) | (node == 3)
+    piece_rows = count_of_rows // 2
+    lower, upper = 0, 1
+    link = []
+
+    roles = (at_end, jnp.logical_not(at_end))
+
+    def run(dest, column, piece, adds):
+        scalars = (dest * 2 + column, piece) + roles
+        scalars = jnp.stack([jnp.asarray(v, jnp.int32) for v in scalars])
+        out = product(scalars, gradient, weights, None, piece_rows, width, adds, link)
+        link[:] = [out]
+        return out
+
+    def swap(x, active):
+        pairs = []
+        for z in active:
+            pairs += [(2 * z, 2 * z + 1), (2 * z + 1, 2 * z)]
+        return lax.ppermute(x, "tensor", pairs)
+
+    def along(x, hops):
+        return lax.ppermute(
+            x, "tensor", [(2 * a + y, 2 * b + y) for a, b in hops for y in range(2)]
+        )
+
+    nodes = 4
+    ends, inner, every = (0, 3), (1, 2), (0, 1, 2, 3)
+    from_ends = [(0, 1), (3, 2)]
+    across = [(1, 2), (2, 1)]
+    to_ends = [(1, 0), (2, 3)]
+    first_half = node < 2
+    far = jnp.where(first_half, 3, 0)
+    beyond = jnp.where(first_half, 2, 1)
+    nearer = jnp.where(first_half, 1, 2)
+    near_end = jnp.where(first_half, 0, 3)
+    same, other = side, 1 - side
+
+    def all_owners(x):
+        return lax.all_gather(x, "dp", axis=0, tiled=True)
+
+    block_tenants = jnp.zeros((owner_count * blocks,), jnp.int32)
+    for hop in range(owner_count):
+        pairs = [(i, (i + hop) % owner_count) for i in range(owner_count)]
+        theirs = lax.ppermute(tenant_per_block, "dp", pairs) if hop else tenant_per_block
+        place = lax.rem(owner - hop + owner_count, owner_count) * blocks
+        block_tenants = lax.dynamic_update_slice_in_dim(block_tenants, theirs, place, 0)
+    tenant_ids = jnp.arange(tenants, dtype=jnp.int32)
+    matches = block_tenants[:, None] == tenant_ids[None, :]
+    block_ranks = jnp.sum(jnp.where(matches, tenant_adapter_rank[None, :], 0), axis=1)
+    block_scales = adapter_alpha / block_ranks.astype(f32)
+    key = tenant_owner_index * tenants + tenant_ids
+    slot_of = jnp.sum((key[None, :] < key[:, None]).astype(jnp.int32), axis=1)
+    slots_each = tenants // owner_count
+    slot_here = lax.rem(slot_of - owner * slots_each + tenants, tenants)
+    block_slots = jnp.sum(jnp.where(matches, slot_here[None, :], 0), axis=1)
+
+    own_ranks = lax.dynamic_slice_in_dim(block_ranks, owner * blocks, blocks, 0)
+    own_scales = lax.dynamic_slice_in_dim(block_scales, owner * blocks, blocks, 0)
+
+    def adapter_space():
+        part = low_product(tenant_per_block, gradient, expand, link[0])
+        link[:] = [part]
+        return lax.psum(part, "tensor")
+
+    def scale_low(low):
+        out = scaled_low(own_ranks, own_scales, low, link[0])
+        link[:] = [out]
+        return out
+
+    def expand_gradient():
+        kept = jnp.arange(rank_extent, dtype=jnp.int32)[None, :] < block_ranks[:, None]
+        saved = all_owners(saved_lowrank).reshape(-1, row_block, rank_extent)
+        saved = (saved * kept[:, None, :].astype(bf16)).reshape(-1, rank_extent)
+        out = factor_sums(
+            block_slots, block_scales, saved, all_owners(gradient), slots_each, link
+        )
+        link[:] = [out]
+        return out
+
+    def shrink_gradient(low):
+        out = factor_sums(
+            block_slots, jnp.ones_like(block_scales), all_owners(projection_input), all_owners(low),
+            slots_each, link,
+        )
+        link[:] = [out]
+        return out
+
+    direct_a = along(run(far, other, lower, []), from_ends)
+    low_whole = adapter_space()
+    y1 = swap(run(jnp.where(at_end, far, near_end), other, upper, []), every)
+    direct_b = along(run(far, same, lower, []), from_ends)
+    y2 = swap(run(beyond, other, lower, []), ends)
+    out = run(
+        far,
+        jnp.where(at_end, same, other),
+        jnp.where(at_end, upper, lower),
+        [(y1, 1), (direct_a, 0)],
+    )
+    upper_1, direct_a = along(out, from_ends), along(out, across)
+    y3 = swap(run(jnp.where(at_end, beyond, far), other, upper, []), every)
+    out = run(jnp.where(at_end, beyond, far), same, lower, [(y2, 0), (direct_b, 0)])
+    lower_2, direct_b = along(out, from_ends), along(out, across)
+    y4 = swap(run(jnp.where(at_end, nearer, beyond), other, lower, []), every)
+    out = run(
+        jnp.where(at_end, beyond, near_end),
+        jnp.where(at_end, same, other),
+        jnp.where(at_end, upper, lower),
+        [(y3, 1), (direct_a, 0)],
+    )
+    both_3 = along(out, from_ends + to_ends)
+    y5 = swap(run(jnp.where(at_end, nearer, beyond), other, upper, []), every)
+    upper_far = along(run(far, same, upper, [(y3, 0), (upper_1, 0)]), across)
+    out = run(jnp.where(at_end, nearer, near_end), same, lower, [(y4, 1), (direct_b, 0)])
+    both_4 = along(out, from_ends + to_ends)
+    low = scale_low(low_whole)
+    y6 = swap(run(node, other, upper, []), every)
+    lower_4 = along(run(beyond, same, lower, [(y4, 0), (lower_2, 0)]), across)
+    out = run(
+        jnp.where(at_end, nearer, near_end), same, upper, [(y5, 1), (y1, 2), (upper_far, 0)]
+    )
+    both_5 = along(out, from_ends + to_ends)
+    y7 = swap(run(node, other, lower, [(both_3, 1)]), every)
+    upper_4 = along(run(beyond, same, upper, [(y5, 0), (both_3, 0)]), across)
+    link += [both_4, y6, lower_4]
+    grad_expand = expand_gradient()
+    grad_shrink = shrink_gradient(low)
+
+    input_gradient = None
+    in_piece = piece_rows // row_block
+    for piece, adds in (
+        (lower, [(y7, 0), (both_4, 0), (lower_4, 0)]),
+        (upper, [(y6, 0), (both_5, 0), (upper_4, 0)]),
+    ):
+        scalars = [node * 2 + side, jnp.int32(piece), jnp.int32(0), jnp.int32(0)]
+        scalars += [tenant_per_block[piece * in_piece + i] for i in range(in_piece)]
+        input_gradient = product(
+            jnp.stack(scalars).astype(jnp.int32),
+            gradient, weights, piece, piece_rows, width, adds, link, (low, shrink), input_gradient,
+        )
+        link[:] = [input_gradient]
+    return (input_gradient, grad_shrink, grad_expand)
+
+
+def per_device_any(
     query_cotangent,
     projection_input,
     saved_lowrank,
@@ -25,7 +361,7 @@
         lax.dot_general(
             query_matrix,
             query_cotangent,
-            (((1,), (1,)), ((), ())),
+            contract_last,
             preferred_element_type=jnp.float32,
         ).astype(jnp.bfloat16),
         "tensor",
@@ -101,8 +437,11 @@
         P(),
         P(),
     )
+    body = per_device_any
+    if mesh.shape["tensor"] == 8:
+        body = functools.partial(per_device, mesh.shape["dp"])
     return jax.shard_map(
-        per_device,
+        body,
         mesh=mesh,
         in_specs=placed,
         out_specs=(

time: 430 us -> 216 us (0.50)
  waiting for transfers between devices: 316 us -> 27.1 us
  Pallas kernels: 0 us -> 95.8 us
  starting transfers between devices: 0.35 us -> 53 us
  matrix products: 48.4 us -> 0 us
  local copies, waits for them, and re-layouts: 35 us -> 16.9 us
  other arithmetic: 11.3 us -> 1.81 us
  blocking collectives: 0 us -> 4.46 us
    reduce_scatter x1 -> x0, waiting for transfers between devices: 256 us -> none  [per_device(): lax.psum_scatter(lax.dot_general(query_matrix, query_cotangent, (((1,), (...]
    pallas_call x0 -> x23, Pallas kernels: none -> 95.8 us  [the longest x19 82.5 us: product(): pl.pallas_call(functools.partial(product_kernel, tuple((mode for _, mode...]
    psum x1, waiting for transfers between devices: 60 us -> 0.01 us  [adapter_space(): return lax.psum(part, 'tensor')]
    ppermute x0 -> x20, starting transfers between devices: none -> 52.9 us  [the longest x12 44.5 us: along(): lax.ppermute(x, 'tensor', [(2 * a + y, 2 * b + y) for a, b in hops for y...]
    dot_general x7 -> x0, matrix products: 48.4 us -> none  [the longest x1 26.2 us: per_device(): lax.dot_general(query_matrix, query_cotangent, (((1,), (1,)), ((), ())),...]
    ppermute x0 -> x20, waiting for transfers between devices: none -> 27.1 us  [the longest x12 13.9 us: along(): lax.ppermute(x, 'tensor', [(2 * a + y, 2 * b + y) for a, b in hops for y...]
    gather x2 -> x0, local copies, waits for them, and re-layouts: 7.37 us -> none  [the longest x1 4.19 us: per_device(): expand_per_block = jnp.take(adapter_expand, tenant_per_block, axis=0)]
    convert_element_type x5 -> x1, other arithmetic: 7.04 us -> 0.07 us  [expand_gradient(): saved = (saved * kept[:, None, :].astype(bf16)).reshape(-1, rank_extent)]
  transfers between devices with their start and end apart: 4 -> 23, of which waited for: 2 -> 5; matrix products, arithmetic and copies ran while one was open for 18% -> 3% of each run, Pallas kernels for 0% -> 40%
where the time goes in v4:
time: 216 us; the launch traced here: 215 us
  Pallas kernels  95.8 us (44%)
  starting transfers between devices  53 us (25%)
  waiting for transfers between devices  27.1 us (13%)
  local copies, waits for them, and re-layouts  16.9 us (8%)
  between operations  15.8 us (7%)
  blocking collectives  4.46 us (2%)
    pallas_call x19, Pallas kernels, product(): pl.pallas_call(functools.partial(product_kernel, tuple((mode for _, mode...  82.5 us
    ppermute x12, starting transfers between devices, along(): lax.ppermute(x, 'tensor', [(2 * a + y, 2 * b + y) for a, b in hops for y...  44.5 us
    unnamed x37, local copies, waits for them, and re-layouts  14.2 us
    ppermute x12, waiting for transfers between devices, along(): lax.ppermute(x, 'tensor', [(2 * a + y, 2 * b + y) for a, b in hops for y...  13.9 us
    ppermute x7, waiting for transfers between devices, swap(): return lax.ppermute(x, 'tensor', pairs)  13.2 us
    pallas_call x2, Pallas kernels, factor_sums(): pl.pallas_call(functools.partial(factor_kernel, slots_each), in_specs=[pl...  8.38 us
    ppermute x7, starting transfers between devices, swap(): return lax.ppermute(x, 'tensor', pairs)  8.33 us
    all_gather x2, blocking collectives, all_owners(): return lax.all_gather(x, 'dp', axis=0, tiled=True)  4.46 us
  transfers between devices with their start and end apart: 23, of which 5 were waited for; matrix products, arithmetic and copies ran while one was open for 3% of the time, Pallas kernels for 40%

profile of v4, /device:TPU:10, one launch (start us, length us, event | category | flops | bytes accessed | tf_op | source)
XLA Modules:
  0.0 214.9 jit_solution(6786175199358975267)
XLA Ops:
  8.1 1.6 copy-done
  9.7 4.2 %shard_map.112.link = bf16[512,1024]{1,0:T(8,128)(2,1)} custom-call(s32[4]{0:T(128)S(1)} %fusion.18.refs_0_, bf16[1024,1024]{1,0:T(8,128)(2,1)S(1)} %copy-done, bf16[8192,1024]{1,0:T(8,128)(2,1)} %refs_2_.37), custom_call_target="tpu_custom_call" | custom-call | flops 999999995904 | bytes 1000000000 | tf_op jit(solution)/shard_map/pallas_call | solution.py:91
  15.2 2.2 %copy-done.7 = bf16[16,128,1024]{2,1,0:T(8,128)(2,1)S(1)} copy-done((bf16[16,128,1024]{2,1,0:T(8,128)(2,1)S(1)}, bf16[16,128,1024]{2,1,0:T(8,128)(2,1)}, u32[]{:S(2)}) %copy-start.7) | copy-done | bytes 4194328
  17.4 4.3 %shard_map.113.refs_3_ = bf16[1024,128]{1,0:T(8,128)(2,1)} custom-call(s32[8]{0:T(128)} %tenants.1, bf16[1024,1024]{1,0:T(8,128)(2,1)S(1)} %copy-done.1, bf16[16,128,1024]{2,1,0:T(8,128)(2,1)S(1)} %copy-done.7, bf16[512,1024]{1,0:T(8,128)(2,1)} %shard_map.112.link), custom_call_target="tpu_custom_call" | custom-call | flops 999999995904 | bytes 1000000000 | tf_op jit(solution)/shard_map/pallas_call | solution.py:115
  21.7 4.1 %shard_map.114.refs_3_ = bf16[512,1024]{1,0:T(8,128)(2,1)} custom-call(s32[4]{0:T(128)S(1)} %fusion.6.refs_0_, bf16[1024,1024]{1,0:T(8,128)(2,1)S(1)} %copy-done.1, bf16[8192,1024]{1,0:T(8,128)(2,1)} %refs_2_.37, bf16[1024,128]{1,0:T(8,128)(2,1)} %shard_map.113.refs_3_), custom_call_target="tpu_custom_call" | custom-call | flops 999999995904 | bytes 1000000000 | tf_op jit(solution)/shard_map/pallas_call | solution.py:91
  25.8 1.5 collective-permute-start.3
  27.6 4.1 %shard_map.115.refs_3_ = bf16[512,1024]{1,0:T(8,128)(2,1)} custom-call(s32[4]{0:T(128)S(1)} %fusion.28.refs_0_, bf16[1024,1024]{1,0:T(8,128)(2,1)S(1)} %copy-done.1, bf16[8192,1024]{1,0:T(8,128)(2,1)} %refs_2_.37, bf16[512,1024]{1,0:T(8,128)(2,1)} %shard_map.114.refs_3_), custom_call_target="tpu_custom_call" | custom-call | flops 999999995904 | bytes 1000000000 | tf_op jit(solution)/shard_map/pallas_call | solution.py:91
  33.1 1.6 copy-done.2
  34.7 4.3 %shard_map.116.refs_5_ = bf16[512,1024]{1,0:T(8,128)(2,1)} custom-call(s32[4]{0:T(128)S(1)} %fusion.26.refs_0_, bf16[1024,1024]{1,0:T(8,128)(2,1)S(1)} %copy-done.2, bf16[8192,1024]{1,0:T(8,128)(2,1)} %refs_2_.37, bf16[512,1024]{1,0:T(8,128)(2,1)} %shard_map.115.refs_3_), custom_call_target="tpu_custom_call" | custom-call | flops 999999995904 | bytes 1000000000 | tf_op jit(solution)/shard_map/pallas_call | solution.py:91
  39.0 1.7 collective-permute-start.1
  43.6 2.3 %all_gather.14 = bf16[2048,128]{1,0:T(8,128)(2,1)S(1)} all-gather(bf16[1024,128]{1,0:T(8,128)(2,1)S(1)} %copy-done.15), channel_id=1, replica_groups=mesh['groups'=2,'dp'=2,'tensor'=8] {'dp'}, dimensions={0}, use_global_device_ids=true | all-gather | bytes 786432 | tf_op jit(solution)/shard_map/all_gather | solution.py:240
  47.3 4.8 %collective-permute-done.3.refs_3_.refs_4_ = bf16[512,1024]{1,0:T(8,128)(2,1)} collective-permute-done((bf16[512,1024]{1,0:T(8,128)(2,1)}, bf16[512,1024]{1,0:T(8,128)(2,1)}, u32[]{:S(2)}, u32[]{:S(2)}) %collective-permute-start.3) | collective-permute-done | bytes 1048608 | tf_op jit(solution)/shard_map/ppermute | solution.py:220
  52.1 4.4 %shard_map.117.refs_3_ = bf16[512,1024]{1,0:T(8,128)(2,1)} custom-call(s32[4]{0:T(128)S(1)} %add_add_fusion.refs_0_, bf16[1024,1024]{1,0:T(8,128)(2,1)S(1)} %copy-done.3, bf16[8192,1024]{1,0:T(8,128)(2,1)} %refs_2_.37, bf16[512,1024]{1,0:T(8,128)(2,1)} %collective-permute-done.3.refs_3_.refs_4_, bf16[512,1024]{1,0:T(8,128)(2,1)} %collective-permute-done.4.refs_4_, ...), custom_call_target="tpu_custom_call" | custom-call | flops 999999995904 | bytes 1000000000 | tf_op jit(solution)/shard_map/pallas_call | solution.py:91
  56.5 3.5 %collective-permute-start.9 = (bf16[512,1024]{1,0:T(8,128)(2,1)}, bf16[512,1024]{1,0:T(8,128)(2,1)}, u32[]{:S(2)}, u32[]{:S(2)}) collective-permute-start(bf16[512,1024]{1,0:T(8,128)(2,1)} %shard_map.117.refs_3_), channel_id=1, source_target_pairs={{2,4},{3,5},{4,2},{5,3},{10,12},{11,13},{12,10},{13,11},{18,20},{1... | collective-permute-start | bytes 3145736 | tf_op jit(solution)/shard_map/ppermute | solution.py:223
  60.0 1.3 collective-permute-start.8
  61.3 4.2 %shard_map.118.refs_5_ = bf16[512,1024]{1,0:T(8,128)(2,1)} custom-call(s32[4]{0:T(128)S(1)} %fusion.8.refs_0_, bf16[1024,1024]{1,0:T(8,128)(2,1)S(1)} %copy-done.3, bf16[8192,1024]{1,0:T(8,128)(2,1)} %refs_2_.37, bf16[512,1024]{1,0:T(8,128)(2,1)} %shard_map.117.refs_3_), custom_call_target="tpu_custom_call" | custom-call | flops 999999995904 | bytes 1000000000 | tf_op jit(solution)/shard_map/pallas_call | solution.py:91
  65.5 1.3 collective-permute-start.7
  66.8 1.6 collective-permute-done.2.refs_4_
  68.5 4.4 %shard_map.119.refs_3_ = bf16[512,1024]{1,0:T(8,128)(2,1)} custom-call(s32[4]{0:T(128)S(1)} %fusion.24.refs_0_, bf16[1024,1024]{1,0:T(8,128)(2,1)S(1)} %copy-done.3, bf16[8192,1024]{1,0:T(8,128)(2,1)} %refs_2_.37, bf16[512,1024]{1,0:T(8,128)(2,1)} %collective-permute-done.1.refs_3_, bf16[512,1024]{1,0:T(8,128)(2,1)} %collective-permute-done.2.refs_4_, ...), custom_call_target="tpu_custom_call" | custom-call | flops 999999995904 | bytes 1000000000 | tf_op jit(solution)/shard_map/pallas_call | solution.py:91
  72.9 3.5 %collective-permute-start.6 = (bf16[512,1024]{1,0:T(8,128)(2,1)}, bf16[512,1024]{1,0:T(8,128)(2,1)}, u32[]{:S(2)}, u32[]{:S(2)}) collective-permute-start(bf16[512,1024]{1,0:T(8,128)(2,1)} %shard_map.119.refs_3_), channel_id=1, source_target_pairs={{2,4},{3,5},{4,2},{5,3},{10,12},{11,13},{12,10},{13,11},{18,20},{1... | collective-permute-start | bytes 3145736 | tf_op jit(solution)/shard_map/ppermute | solution.py:223
  77.7 4.1 %shard_map.120.refs_5_ = bf16[512,1024]{1,0:T(8,128)(2,1)} custom-call(s32[4]{0:T(128)S(1)} %fusion.22.refs_0_, bf16[1024,1024]{1,0:T(8,128)(2,1)S(1)} %copy-done.3, bf16[8192,1024]{1,0:T(8,128)(2,1)} %refs_2_.37, bf16[512,1024]{1,0:T(8,128)(2,1)} %shard_map.119.refs_3_), custom_call_target="tpu_custom_call" | custom-call | flops 999999995904 | bytes 1000000000 | tf_op jit(solution)/shard_map/pallas_call | solution.py:91
  81.8 8.4 %collective-permute-done.7.refs_3_ = bf16[512,1024]{1,0:T(8,128)(2,1)} collective-permute-done((bf16[512,1024]{1,0:T(8,128)(2,1)}, bf16[512,1024]{1,0:T(8,128)(2,1)}, u32[]{:S(2)}, u32[]{:S(2)}) %collective-permute-start.7) | collective-permute-done | bytes 1048608 | tf_op jit(solution)/shard_map/ppermute | solution.py:220
  91.4 4.4 %shard_map.121.refs_3_ = bf16[512,1024]{1,0:T(8,128)(2,1)} custom-call(s32[4]{0:T(128)S(1)} %get-tuple-element.10.refs_0_, bf16[1024,1024]{1,0:T(8,128)(2,1)S(1)} %copy-done.3, bf16[8192,1024]{1,0:T(8,128)(2,1)} %refs_2_.37, bf16[512,1024]{1,0:T(8,128)(2,1)} %collective-permute-done.7.refs_3_, bf16[512,1024]{1,0:T(8,128)(2,1)} %collective-permute-done.9.refs_4_, ...), custom_call_target="tpu_custom_call" | custom-call | flops 999999995904 | bytes 1000000000 | tf_op jit(solution)/shard_map/pallas_call | solution.py:91
  95.9 12.3 %collective-permute-start.15 = (bf16[512,1024]{1,0:T(8,128)(2,1)}, bf16[512,1024]{1,0:T(8,128)(2,1)}, u32[]{:S(2)}, u32[]{:S(2)}) collective-permute-start(bf16[512,1024]{1,0:T(8,128)(2,1)} %shard_map.121.refs_3_), channel_id=1, source_target_pairs={{0,2},{1,3},{6,4},{7,5},{2,0},{3,1},{4,6},{5,7},{8,10},{9,11},{14,... | collective-permute-start | bytes 3145736 | tf_op jit(solution)/shard_map/ppermute | solution.py:223
  108.2 4.2 %shard_map.122.refs_5_ = bf16[512,1024]{1,0:T(8,128)(2,1)} custom-call(s32[4]{0:T(128)S(1)} %get-tuple-element.9.refs_0_, bf16[1024,1024]{1,0:T(8,128)(2,1)S(1)} %copy-done.3, bf16[8192,1024]{1,0:T(8,128)(2,1)} %refs_2_.37, bf16[512,1024]{1,0:T(8,128)(2,1)} %shard_map.121.refs_3_), custom_call_target="tpu_custom_call" | custom-call | flops 999999995904 | bytes 1000000000 | tf_op jit(solution)/shard_map/pallas_call | solution.py:91
  112.9 4.4 %shard_map.123.refs_5_ = bf16[512,1024]{1,0:T(8,128)(2,1)} custom-call(s32[4]{0:T(128)S(1)} %fusion.10.refs_0_, bf16[1024,1024]{1,0:T(8,128)(2,1)S(1)} %copy-done.3, bf16[8192,1024]{1,0:T(8,128)(2,1)} %refs_2_.37, bf16[512,1024]{1,0:T(8,128)(2,1)} %collective-permute-done.7.refs_3_, bf16[512,1024]{1,0:T(8,128)(2,1)} %collective-permute-done.8.refs_4_, ...), custom_call_target="tpu_custom_call" | custom-call | flops 999999995904 | bytes 1000000000 | tf_op jit(solution)/shard_map/pallas_call | solution.py:91
  117.3 3.5 %collective-permute-start.12 = (bf16[512,1024]{1,0:T(8,128)(2,1)}, bf16[512,1024]{1,0:T(8,128)(2,1)}, u32[]{:S(2)}, u32[]{:S(2)}) collective-permute-start(bf16[512,1024]{1,0:T(8,128)(2,1)} %shard_map.123.refs_5_), channel_id=1, source_target_pairs={{2,4},{3,5},{4,2},{5,3},{10,12},{11,13},{12,10},{13,11},{18,20},{1... | collective-permute-start | bytes 3145736 | tf_op jit(solution)/shard_map/ppermute | solution.py:223
  120.8 4.5 %shard_map.124.link = bf16[512,1024]{1,0:T(8,128)(2,1)} custom-call(s32[4]{0:T(128)S(1)} %fusion.20.refs_0_, bf16[1024,1024]{1,0:T(8,128)(2,1)S(1)} %copy-done.3, bf16[8192,1024]{1,0:T(8,128)(2,1)} %refs_2_.37, bf16[512,1024]{1,0:T(8,128)(2,1)} %collective-permute-done.5.refs_3_, bf16[512,1024]{1,0:T(8,128)(2,1)} %collective-permute-done.6.refs_4_, ...), custom_call_target="tpu_custom_call" | custom-call | flops 999999995904 | bytes 1000000000 | tf_op jit(solution)/shard_map/pallas_call | solution.py:91
  125.3 9.5 %collective-permute-start.18 = (bf16[512,1024]{1,0:T(8,128)(2,1)}, bf16[512,1024]{1,0:T(8,128)(2,1)}, u32[]{:S(2)}, u32[]{:S(2)}) collective-permute-start(bf16[512,1024]{1,0:T(8,128)(2,1)} %shard_map.124.link), channel_id=1, source_target_pairs={{0,2},{1,3},{6,4},{7,5},{2,0},{3,1},{4,6},{5,7},{8,10},{9,11},{14,... | collective-permute-start | bytes 3145736 | tf_op jit(solution)/shard_map/ppermute | solution.py:223
  136.4 4.1 %shard_map.126.refs_5_ = bf16[512,1024]{1,0:T(8,128)(2,1)} custom-call(s32[4]{0:T(128)S(1)} %fusion.4.refs_0_, bf16[1024,1024]{1,0:T(8,128)(2,1)S(1)} %copy-done.3, bf16[8192,1024]{1,0:T(8,128)(2,1)} %refs_2_.37, bf16[1024,128]{1,0:T(8,128)(2,1)S(1)} %shard_map.125.refs_3_.refs_6_), custom_call_target="tpu_custom_call" | custom-call | flops 999999995904 | bytes 1000000000 | tf_op jit(solution)/shard_map/pallas_call | solution.py:91
  140.5 1.5 collective-permute-start.10
  142.1 4.4 %shard_map.127.refs_6_ = bf16[512,1024]{1,0:T(8,128)(2,1)} custom-call(s32[4]{0:T(128)S(1)} %fusion.30.refs_0_, bf16[1024,1024]{1,0:T(8,128)(2,1)S(1)} %copy-done.3, bf16[8192,1024]{1,0:T(8,128)(2,1)} %refs_2_.37, bf16[512,1024]{1,0:T(8,128)(2,1)} %collective-permute-done.5.refs_3_, bf16[512,1024]{1,0:T(8,128)(2,1)} %collective-permute-done.13.refs_4_, ...), custom_call_target="tpu_custom_call" | custom-call | flops 999999995904 | bytes 1000000000 | tf_op jit(solution)/shard_map/pallas_call | solution.py:91
  146.5 2.2 %all_gather.13.right = bf16[2048,128]{1,0:T(8,128)(2,1)S(1)} all-gather(bf16[1024,128]{1,0:T(8,128)(2,1)S(1)} %copy-done.5), channel_id=1, replica_groups=mesh['groups'=2,'dp'=2,'tensor'=8] {'dp'}, dimensions={0}, use_global_device_ids=true | all-gather | bytes 786432 | tf_op jit(solution)/shard_map/all_gather | solution.py:240
  148.7 3.7 %collective-permute-start.19 = (bf16[512,1024]{1,0:T(8,128)(2,1)}, bf16[512,1024]{1,0:T(8,128)(2,1)}, u32[]{:S(2)}, u32[]{:S(2)}) collective-permute-start(bf16[512,1024]{1,0:T(8,128)(2,1)} %shard_map.127.refs_6_), channel_id=1, source_target_pairs={{2,4},{3,5},{4,2},{5,3},{10,12},{11,13},{12,10},{13,11},{18,20},{1... | collective-permute-start | bytes 3145736 | tf_op jit(solution)/shard_map/ppermute | solution.py:223
  152.4 4.8 %shard_map.128.refs_4_ = bf16[512,1024]{1,0:T(8,128)(2,1)} custom-call(s32[4]{0:T(128)S(1)} %fusion.14.refs_0_, bf16[1024,1024]{1,0:T(8,128)(2,1)S(1)} %copy-done.3, bf16[8192,1024]{1,0:T(8,128)(2,1)} %refs_2_.37, bf16[512,1024]{1,0:T(8,128)(2,1)} %collective-permute-done.11.refs_3_, bf16[512,1024]{1,0:T(8,128)(2,1)} %collective-permute-done.3.refs_3_.refs_4_, ...), custom_call_target="tpu_custom_call" | custom-call | flops 999999995904 | bytes 1000000000 | tf_op jit(solution)/shard_map/pallas_call | solution.py:91
  157.2 4.2 %shard_map.129.refs_5_ = bf16[512,1024]{1,0:T(8,128)(2,1)} custom-call(s32[4]{0:T(128)S(1)} %fusion.32.refs_0_, bf16[1024,1024]{1,0:T(8,128)(2,1)S(1)} %copy-done.3, bf16[8192,1024]{1,0:T(8,128)(2,1)} %refs_2_.37, bf16[512,1024]{1,0:T(8,128)(2,1)} %collective-permute-done.15.refs_3_.refs_4_, bf16[512,1024]{1,0:T(8,128)(2,1)} %shard_map.128.refs_4_), custom_call_target="tpu_custom_call" | custom-call | flops 999999995904 | bytes 1000000000 | tf_op jit(solution)/shard_map/pallas_call | solution.py:91
  161.9 4.5 %shard_map.130.refs_0_ = bf16[512,1024]{1,0:T(8,128)(2,1)} custom-call(s32[4]{0:T(128)S(1)} %fusion.16.refs_0_, bf16[1024,1024]{1,0:T(8,128)(2,1)S(1)} %copy-done.3, bf16[8192,1024]{1,0:T(8,128)(2,1)} %refs_2_.37, bf16[512,1024]{1,0:T(8,128)(2,1)} %collective-permute-done.11.refs_3_, bf16[512,1024]{1,0:T(8,128)(2,1)} %collective-permute-done.15.refs_3_.refs_4_, ...), custom_call_target="tpu_custom_call" | custom-call | flops 999999995904 | bytes 1000000000 | tf_op jit(solution)/shard_map/pallas_call | solution.py:91
  166.4 9.6 %collective-permute-done.19.refs_3_.refs_5_ = bf16[512,1024]{1,0:T(8,128)(2,1)} collective-permute-done((bf16[512,1024]{1,0:T(8,128)(2,1)}, bf16[512,1024]{1,0:T(8,128)(2,1)}, u32[]{:S(2)}, u32[]{:S(2)}) %collective-permute-start.19) | collective-permute-done | bytes 1048608 | tf_op jit(solution)/shard_map/ppermute | solution.py:223
  176.1 3.5 %collective-permute-start.16 = (bf16[512,1024]{1,0:T(8,128)(2,1)}, bf16[512,1024]{1,0:T(8,128)(2,1)}, u32[]{:S(2)}, u32[]{:S(2)}) collective-permute-start(bf16[512,1024]{1,0:T(8,128)(2,1)} %shard_map.130.refs_0_), channel_id=1, source_target_pairs={{2,4},{3,5},{4,2},{5,3},{10,12},{11,13},{12,10},{13,11},{18,20},{1... | collective-permute-start | bytes 3145736 | tf_op jit(solution)/shard_map/ppermute | solution.py:223
  179.6 2.2 %copy-done.9 = bf16[2048,1024]{1,0:T(8,128)(2,1)S(1)} copy-done((bf16[2048,1024]{1,0:T(8,128)(2,1)S(1)}, bf16[2048,1024]{1,0:T(8,128)(2,1)}, u32[]{:S(2)}) %copy-start.9) | copy-done | bytes 4194328
  181.8 4.2 %shard_map.131.refs_0_ = f32[8,128,1024]{2,1,0:T(8,128)} custom-call(s32[16]{0:T(128)S(1)} %get-tuple-element.3.slots, f32[16]{0:T(128)S(1)} %copy-done.14, bf16[2048,128]{1,0:T(8,128)(2,1)S(1)} %bitcast_multiply_fusion.left, bf16[2048,1024]{1,0:T(8,128)(2,1)S(1)} %copy-done.9, bf16[512,1024]{1,0:T(8,128)(2,1)} %shard_map.130.refs_0_, ...), custom_call_target="tpu_custom_call" | custom-call | flops 999999995904 | bytes 1000000000 | tf_op jit(solution)/shard_map/pallas_call | solution.py:171
  186.0 2.2 %copy-done.10 = bf16[2048,1024]{1,0:T(8,128)(2,1)S(1)} copy-done((bf16[2048,1024]{1,0:T(8,128)(2,1)S(1)}, bf16[2048,1024]{1,0:T(8,128)(2,1)}, u32[]{:S(2)}) %copy-start.10) | copy-done | bytes 4194328
  188.2 2.2 %copy-done.12 = f32[8,128,1024]{2,1,0:T(8,128)S(1)} copy-done((f32[8,128,1024]{2,1,0:T(8,128)S(1)}, f32[8,128,1024]{2,1,0:T(8,128)}, u32[]{:S(2)}) %copy-start.12) | copy-done | bytes 4194328
  190.4 4.2 %shard_map.132.refs_11_ = f32[8,1024,128]{2,1,0:T(8,128)} custom-call(s32[16]{0:T(128)S(1)} %get-tuple-element.3.slots, f32[16]{0:T(128)S(1)} %broadcast_6_scales.2.scales, bf16[2048,1024]{1,0:T(8,128)(2,1)S(1)} %copy-done.10, bf16[2048,128]{1,0:T(8,128)(2,1)S(1)} %all_gather.13.right, f32[8,128,1024]{2,1,0:T(8,128)S(1)} %copy-done.12), custom_call_target="tpu_custom_call" | custom-call | flops 999999995904 | bytes 1000000000 | tf_op jit(solution)/shard_map/pallas_call | solution.py:171
  194.6 4.2 %shard_map.133.refs_11_ = bf16[1024,1024]{1,0:T(8,128)(2,1)S(1)} custom-call(s32[8]{0:T(128)S(1)} %get-tuple-element.5.refs_0_, bf16[1024,1024]{1,0:T(8,128)(2,1)S(1)} %copy-done.3, bf16[8192,1024]{1,0:T(8,128)(2,1)} %refs_2_.37, bf16[512,1024]{1,0:T(8,128)(2,1)} %collective-permute-done.17.refs_3_, ...), custom_call_target="tpu_custom_call" | custom-call | flops 999999995904 | bytes 1000000000 | tf_op jit(solution)/shard_map/pallas_call | solution.py:91
  198.8 1.3 copy.16.refs_12_
  200.1 2.6 %collective-permute-done.16.refs_5_ = bf16[512,1024]{1,0:T(8,128)(2,1)} collective-permute-done((bf16[512,1024]{1,0:T(8,128)(2,1)}, bf16[512,1024]{1,0:T(8,128)(2,1)}, u32[]{:S(2)}, u32[]{:S(2)}) %collective-permute-start.16) | collective-permute-done | bytes 1048608 | tf_op jit(solution)/shard_map/ppermute | solution.py:223
  202.7 4.9 %shard_map.134 = bf16[1024,1024]{1,0:T(8,128)(2,1)} custom-call(s32[8]{0:T(128)S(1)} %get-tuple-element.6.refs_0_, bf16[1024,1024]{1,0:T(8,128)(2,1)S(1)} %copy-done.3, bf16[8192,1024]{1,0:T(8,128)(2,1)} %refs_2_.37, bf16[512,1024]{1,0:T(8,128)(2,1)} %collective-permute-done.10.refs_2_.refs_3_, ...), custom_call_target="tpu_custom_call", output_to_operand_aliasing={{}: (12, {})} | custom-call | flops 999999995904 | bytes 1000000000 | tf_op jit(solution)/shard_map/pallas_call | solution.py:91
  (95 shorter events, 12.5 us)
Async XLA Ops:
  8.1 1.6 copy-start
  9.7 5.5 %copy-start.1 = (bf16[1024,1024]{1,0:T(8,128)(2,1)S(1)}, bf16[1024,1024]{1,0:T(8,128)(2,1)}, u32[]{:S(2)}) copy-start(bf16[1024,1024]{1,0:T(8,128)(2,1)} %refs_1_.37) | copy-start | bytes 6291460
  13.9 38.2 %collective-permute-start.4 = (bf16[512,1024]{1,0:T(8,128)(2,1)}, bf16[512,1024]{1,0:T(8,128)(2,1)}, u32[]{:S(2)}, u32[]{:S(2)}) collective-permute-start(bf16[512,1024]{1,0:T(8,128)(2,1)} %shard_map.112.link), channel_id=1, source_target_pairs={{0,2},{1,3},{6,4},{7,5},{8,10},{9,11},{14,12},{15,13},{16,18},{17,... | collective-permute-start | bytes 3145736 | tf_op jit(solution)/shard_map/ppermute | solution.py:223
  15.2 2.2 %copy-start.7 = (bf16[16,128,1024]{2,1,0:T(8,128)(2,1)S(1)}, bf16[16,128,1024]{2,1,0:T(8,128)(2,1)}, u32[]{:S(2)}) copy-start(bf16[16,128,1024]{2,1,0:T(8,128)(2,1)} %expand.1) | copy-start | bytes 12582916
  25.8 109.0 %all-reduce.2.cloned.1.call-start = ((), (), s32[]{:S(2)}) async-start(), calls=%async_computation | async-start | bytes 524288 | tf_op jit(solution)/shard_map/psum | solution.py:264
  25.8 26.3 %collective-permute-start.3 = (bf16[512,1024]{1,0:T(8,128)(2,1)}, bf16[512,1024]{1,0:T(8,128)(2,1)}, u32[]{:S(2)}, u32[]{:S(2)}) collective-permute-start(bf16[512,1024]{1,0:T(8,128)(2,1)} %shard_map.114.refs_3_), channel_id=1, source_target_pairs={{0,1},{1,0},{2,3},{3,2},{4,5},{5,4},{6,7},{7,6},{8,9},{9,8},{10,11... | collective-permute-start | bytes 3145736 | tf_op jit(solution)/shard_map/ppermute | solution.py:220
  27.4 152.3 %all-gather.5.cloned.1.call-start = ((), (), s32[]{:S(2)}) async-start(), calls=%async_computation.2 | async-start | bytes 6291456 | tf_op jit(solution)/shard_map/all_gather | solution.py:240
  27.4 18.5 %collective-permute-start = (s32[8]{0:T(128)}, s32[8]{0:T(128)}, u32[]{:S(2)}, u32[]{:S(2)}) collective-permute-start(s32[8]{0:T(128)} %tenants.1), channel_id=1, source_target_pairs={{0,8},{8,0},{1,9},{9,1},{2,10},{10,2},{3,11},{11,3},{4,12},{12,4},... | collective-permute-start | bytes 104 | tf_op jit(solution)/shard_map/ppermute | solution.py:245
  31.7 36.8 %collective-permute-start.2 = (bf16[512,1024]{1,0:T(8,128)(2,1)}, bf16[512,1024]{1,0:T(8,128)(2,1)}, u32[]{:S(2)}, u32[]{:S(2)}) collective-permute-start(bf16[512,1024]{1,0:T(8,128)(2,1)} %shard_map.115.refs_3_), channel_id=1, source_target_pairs={{0,2},{1,3},{6,4},{7,5},{8,10},{9,11},{14,12},{15,13},{16,18},{17,... | collective-permute-start | bytes 3145736 | tf_op jit(solution)/shard_map/ppermute | solution.py:223
  33.0 153.0 %all-gather.3.cloned.1.call-start = ((), (), s32[]{:S(2)}) async-start(), calls=%async_computation.1 | async-start | bytes 6291456 | tf_op jit(solution)/shard_map/all_gather | solution.py:240
  33.1 1.6 copy-start.2
  34.7 7.7 %copy-start.17 = (s32[16]{0:T(128)S(1)}, s32[16]{0:T(128)}, u32[]{:S(2)}) copy-start(s32[16]{0:T(128)} %param.17) | copy-start | bytes 196
  34.7 8.9 %copy-start.15 = (bf16[1024,128]{1,0:T(8,128)(2,1)S(1)}, bf16[1024,128]{1,0:T(8,128)(2,1)}, u32[]{:S(2)}) copy-start(bf16[1024,128]{1,0:T(8,128)(2,1)} %param.11) | copy-start | bytes 786436
  34.7 12.1 %copy-start.16 = (s32[16]{0:T(128)S(1)}, s32[16]{0:T(128)}, u32[]{:S(2)}) copy-start(s32[16]{0:T(128)} %param.16) | copy-start | bytes 196
  34.7 17.4 %copy-start.3 = (bf16[1024,1024]{1,0:T(8,128)(2,1)S(1)}, bf16[1024,1024]{1,0:T(8,128)(2,1)}, u32[]{:S(2)}) copy-start(bf16[1024,1024]{1,0:T(8,128)(2,1)} %refs_1_.37) | copy-start | bytes 6291460
  39.0 27.8 %collective-permute-start.1 = (bf16[512,1024]{1,0:T(8,128)(2,1)}, bf16[512,1024]{1,0:T(8,128)(2,1)}, u32[]{:S(2)}, u32[]{:S(2)}) collective-permute-start(bf16[512,1024]{1,0:T(8,128)(2,1)} %shard_map.116.refs_5_), channel_id=1, source_target_pairs={{0,1},{1,0},{6,7},{7,6},{8,9},{9,8},{14,15},{15,14},{16,17},{17,16... | collective-permute-start | bytes 3145736 | tf_op jit(solution)/shard_map/ppermute | solution.py:220
  47.1 9.5 %copy-start.13 = (f32[16]{0:T(128)}, f32[16]{0:T(128)S(1)}, u32[]{:S(2)}) copy-start(f32[16]{0:T(128)S(1)} %convert_divide_fusion.scales) | copy-start | bytes 196
  56.5 34.9 %collective-permute-start.9 = (bf16[512,1024]{1,0:T(8,128)(2,1)}, bf16[512,1024]{1,0:T(8,128)(2,1)}, u32[]{:S(2)}, u32[]{:S(2)}) collective-permute-start(bf16[512,1024]{1,0:T(8,128)(2,1)} %shard_map.117.refs_3_), channel_id=1, source_target_pairs={{2,4},{3,5},{4,2},{5,3},{10,12},{11,13},{12,10},{13,11},{18,20},{1... | collective-permute-start | bytes 3145736 | tf_op jit(solution)/shard_map/ppermute | solution.py:223
  60.0 52.3 %collective-permute-start.8 = (bf16[512,1024]{1,0:T(8,128)(2,1)}, bf16[512,1024]{1,0:T(8,128)(2,1)}, u32[]{:S(2)}, u32[]{:S(2)}) collective-permute-start(bf16[512,1024]{1,0:T(8,128)(2,1)} %shard_map.117.refs_3_), channel_id=1, source_target_pairs={{0,2},{1,3},{6,4},{7,5},{8,10},{9,11},{14,12},{15,13},{16,18},{17,... | collective-permute-start | bytes 3145736 | tf_op jit(solution)/shard_map/ppermute | solution.py:223
  65.5 24.7 %collective-permute-start.7 = (bf16[512,1024]{1,0:T(8,128)(2,1)}, bf16[512,1024]{1,0:T(8,128)(2,1)}, u32[]{:S(2)}, u32[]{:S(2)}) collective-permute-start(bf16[512,1024]{1,0:T(8,128)(2,1)} %shard_map.118.refs_5_), channel_id=1, source_target_pairs={{0,1},{1,0},{2,3},{3,2},{4,5},{5,4},{6,7},{7,6},{8,9},{9,8},{10,11... | collective-permute-start | bytes 3145736 | tf_op jit(solution)/shard_map/ppermute | solution.py:220
  72.9 47.9 %collective-permute-start.6 = (bf16[512,1024]{1,0:T(8,128)(2,1)}, bf16[512,1024]{1,0:T(8,128)(2,1)}, u32[]{:S(2)}, u32[]{:S(2)}) collective-permute-start(bf16[512,1024]{1,0:T(8,128)(2,1)} %shard_map.119.refs_3_), channel_id=1, source_target_pairs={{2,4},{3,5},{4,2},{5,3},{10,12},{11,13},{12,10},{13,11},{18,20},{1... | collective-permute-start | bytes 3145736 | tf_op jit(solution)/shard_map/ppermute | solution.py:223
  76.4 64.2 %collective-permute-start.13 = (bf16[512,1024]{1,0:T(8,128)(2,1)}, bf16[512,1024]{1,0:T(8,128)(2,1)}, u32[]{:S(2)}, u32[]{:S(2)}) collective-permute-start(bf16[512,1024]{1,0:T(8,128)(2,1)} %shard_map.119.refs_3_), channel_id=1, source_target_pairs={{0,2},{1,3},{6,4},{7,5},{8,10},{9,11},{14,12},{15,13},{16,18},{17,... | collective-permute-start | bytes 3145736 | tf_op jit(solution)/shard_map/ppermute | solution.py:223
  90.2 27.2 %collective-permute-start.5 = (bf16[512,1024]{1,0:T(8,128)(2,1)}, bf16[512,1024]{1,0:T(8,128)(2,1)}, u32[]{:S(2)}, u32[]{:S(2)}) collective-permute-start(bf16[512,1024]{1,0:T(8,128)(2,1)} %shard_map.120.refs_5_), channel_id=1, source_target_pairs={{0,1},{1,0},{2,3},{3,2},{4,5},{5,4},{6,7},{7,6},{8,9},{9,8},{10,11... | collective-permute-start | bytes 3145736 | tf_op jit(solution)/shard_map/ppermute | solution.py:220
  95.9 61.3 %collective-permute-start.15 = (bf16[512,1024]{1,0:T(8,128)(2,1)}, bf16[512,1024]{1,0:T(8,128)(2,1)}, u32[]{:S(2)}, u32[]{:S(2)}) collective-permute-start(bf16[512,1024]{1,0:T(8,128)(2,1)} %shard_map.121.refs_3_), channel_id=1, source_target_pairs={{0,2},{1,3},{6,4},{7,5},{2,0},{3,1},{4,6},{5,7},{8,10},{9,11},{14,... | collective-permute-start | bytes 3145736 | tf_op jit(solution)/shard_map/ppermute | solution.py:223
  112.4 40.0 %collective-permute-start.11 = (bf16[512,1024]{1,0:T(8,128)(2,1)}, bf16[512,1024]{1,0:T(8,128)(2,1)}, u32[]{:S(2)}, u32[]{:S(2)}) collective-permute-start(bf16[512,1024]{1,0:T(8,128)(2,1)} %shard_map.122.refs_5_), channel_id=1, source_target_pairs={{0,1},{1,0},{2,3},{3,2},{4,5},{5,4},{6,7},{7,6},{8,9},{9,8},{10,11... | collective-permute-start | bytes 3145736 | tf_op jit(solution)/shard_map/ppermute | solution.py:220
  117.3 31.4 %collective-permute-start.12 = (bf16[512,1024]{1,0:T(8,128)(2,1)}, bf16[512,1024]{1,0:T(8,128)(2,1)}, u32[]{:S(2)}, u32[]{:S(2)}) collective-permute-start(bf16[512,1024]{1,0:T(8,128)(2,1)} %shard_map.123.refs_5_), channel_id=1, source_target_pairs={{2,4},{3,5},{4,2},{5,3},{10,12},{11,13},{12,10},{13,11},{18,20},{1... | collective-permute-start | bytes 3145736 | tf_op jit(solution)/shard_map/ppermute | solution.py:223
  125.3 54.3 %collective-permute-start.18 = (bf16[512,1024]{1,0:T(8,128)(2,1)}, bf16[512,1024]{1,0:T(8,128)(2,1)}, u32[]{:S(2)}, u32[]{:S(2)}) collective-permute-start(bf16[512,1024]{1,0:T(8,128)(2,1)} %shard_map.124.link), channel_id=1, source_target_pairs={{0,2},{1,3},{6,4},{7,5},{2,0},{3,1},{4,6},{5,7},{8,10},{9,11},{14,... | collective-permute-start | bytes 3145736 | tf_op jit(solution)/shard_map/ppermute | solution.py:223
  134.8 1.0 copy-start.11
  136.4 4.2 %copy-start.4 = (bf16[1024,128]{1,0:T(8,128)(2,1)}, bf16[1024,128]{1,0:T(8,128)(2,1)S(1)}, u32[]{:S(2)}) copy-start(bf16[1024,128]{1,0:T(8,128)(2,1)S(1)} %shard_map.125.refs_3_.refs_6_) | copy-start | bytes 786436
  140.5 39.0 %collective-permute-start.10 = (bf16[512,1024]{1,0:T(8,128)(2,1)}, bf16[512,1024]{1,0:T(8,128)(2,1)}, u32[]{:S(2)}, u32[]{:S(2)}) collective-permute-start(bf16[512,1024]{1,0:T(8,128)(2,1)} %shard_map.126.refs_5_), channel_id=1, source_target_pairs={{0,1},{1,0},{2,3},{3,2},{4,5},{5,4},{6,7},{7,6},{8,9},{9,8},{10,11... | collective-permute-start | bytes 3145736 | tf_op jit(solution)/shard_map/ppermute | solution.py:220
  142.1 4.4 %copy-start.5 = (bf16[1024,128]{1,0:T(8,128)(2,1)S(1)}, bf16[1024,128]{1,0:T(8,128)(2,1)}, u32[]{:S(2)}) copy-start(bf16[1024,128]{1,0:T(8,128)(2,1)} %copy-done.4) | copy-start | bytes 786436
  148.7 27.4 %collective-permute-start.19 = (bf16[512,1024]{1,0:T(8,128)(2,1)}, bf16[512,1024]{1,0:T(8,128)(2,1)}, u32[]{:S(2)}, u32[]{:S(2)}) collective-permute-start(bf16[512,1024]{1,0:T(8,128)(2,1)} %shard_map.127.refs_6_), channel_id=1, source_target_pairs={{2,4},{3,5},{4,2},{5,3},{10,12},{11,13},{12,10},{13,11},{18,20},{1... | collective-permute-start | bytes 3145736 | tf_op jit(solution)/shard_map/ppermute | solution.py:223
  157.2 45.5 %collective-permute-start.14 = (bf16[512,1024]{1,0:T(8,128)(2,1)}, bf16[512,1024]{1,0:T(8,128)(2,1)}, u32[]{:S(2)}, u32[]{:S(2)}) collective-permute-start(bf16[512,1024]{1,0:T(8,128)(2,1)} %shard_map.128.refs_4_), channel_id=1, source_target_pairs={{0,2},{1,3},{6,4},{7,5},{2,0},{3,1},{4,6},{5,7},{8,10},{9,11},{14,... | collective-permute-start | bytes 3145736 | tf_op jit(solution)/shard_map/ppermute | solution.py:223
  161.4 33.2 %collective-permute-start.17 = (bf16[512,1024]{1,0:T(8,128)(2,1)}, bf16[512,1024]{1,0:T(8,128)(2,1)}, u32[]{:S(2)}, u32[]{:S(2)}) collective-permute-start(bf16[512,1024]{1,0:T(8,128)(2,1)} %shard_map.129.refs_5_), channel_id=1, source_target_pairs={{0,1},{1,0},{2,3},{3,2},{4,5},{5,4},{6,7},{7,6},{8,9},{9,8},{10,11... | collective-permute-start | bytes 3145736 | tf_op jit(solution)/shard_map/ppermute | solution.py:220
  161.9 17.7 %copy-start.14 = (f32[16]{0:T(128)S(1)}, f32[16]{0:T(128)}, u32[]{:S(2)}) copy-start(f32[16]{0:T(128)} %copy-done.13) | copy-start | bytes 196
  176.1 26.6 %collective-permute-start.16 = (bf16[512,1024]{1,0:T(8,128)(2,1)}, bf16[512,1024]{1,0:T(8,128)(2,1)}, u32[]{:S(2)}, u32[]{:S(2)}) collective-permute-start(bf16[512,1024]{1,0:T(8,128)(2,1)} %shard_map.130.refs_0_), channel_id=1, source_target_pairs={{2,4},{3,5},{4,2},{5,3},{10,12},{11,13},{12,10},{13,11},{18,20},{1... | collective-permute-start | bytes 3145736 | tf_op jit(solution)/shard_map/ppermute | solution.py:223
  179.6 2.2 %copy-start.9 = (bf16[2048,1024]{1,0:T(8,128)(2,1)S(1)}, bf16[2048,1024]{1,0:T(8,128)(2,1)}, u32[]{:S(2)}) copy-start(bf16[2048,1024]{1,0:T(8,128)(2,1)} %all-gather.5.cloned.1.call-done.right) | copy-start | bytes 12582916
  186.0 2.2 %copy-start.10 = (bf16[2048,1024]{1,0:T(8,128)(2,1)S(1)}, bf16[2048,1024]{1,0:T(8,128)(2,1)}, u32[]{:S(2)}) copy-start(bf16[2048,1024]{1,0:T(8,128)(2,1)} %all-gather.3.cloned.1.call-done.left) | copy-start | bytes 12582916
  188.2 2.2 %copy-start.12 = (f32[8,128,1024]{2,1,0:T(8,128)S(1)}, f32[8,128,1024]{2,1,0:T(8,128)}, u32[]{:S(2)}) copy-start(f32[8,128,1024]{2,1,0:T(8,128)} %shard_map.131.refs_0_) | copy-start | bytes 12582916
  190.4 4.2 %copy-start.6 = (bf16[1024,128]{1,0:T(8,128)(2,1)S(1)}, bf16[1024,128]{1,0:T(8,128)(2,1)}, u32[]{:S(2)}) copy-start(bf16[1024,128]{1,0:T(8,128)(2,1)} %copy-done.4) | copy-start | bytes 786436
  190.4 4.2 %copy-start.8 = (bf16[16,1024,128]{2,1,0:T(8,128)(2,1)S(1)}, bf16[16,1024,128]{2,1,0:T(8,128)(2,1)}, u32[]{:S(2)}) copy-start(bf16[16,1024,128]{2,1,0:T(8,128)(2,1)} %refs_10_.3) | copy-start | bytes 12582916
Sparse Core Ops, SparseCore 0:
  30.0 75.3 all-reduce.1
Sparse Core Ops, SparseCore 1:
  33.1 17.3 all-gather.4
  51.9 15.0 all-gather.2

commit v5 on v4

--- a/solution.py
+++ b/solution.py
@@ -52,7 +52,7 @@
     refs[-1][...] = total.astype(refs[-1].dtype)
 
 
-def product(scalars, gradient, weights, piece, piece_rows, width, adds, link, adapter=None, whole=None):
+def product(scalars, gradient, weights, piece, piece_rows, width, adds, link, adapter=None):
     depth = gradient.shape[1]
     tile = min(width, 512)
     while width % tile:
@@ -81,26 +81,59 @@
     for array in link:
         in_specs.append(pl.BlockSpec(memory_space=pl.ANY))
         operands.append(array)
-    out_piece, out_rows, aliases = 0, piece_rows, {}
-    if adapter is not None:
-        out_piece, out_rows = piece, gradient.shape[0]
-        if whole is not None:
-            in_specs.append(pl.BlockSpec(memory_space=pl.ANY))
-            operands.append(whole)
-            aliases = {len(operands): 0}
     return pl.pallas_call(
         functools.partial(product_kernel, tuple(mode for _, mode in adds), block_count),
         grid_spec=pltpu.PrefetchScalarGridSpec(
             num_scalar_prefetch=1,
             grid=(steps,),
             in_specs=in_specs,
-            out_specs=pl.BlockSpec((piece_rows, tile), lambda j, s: (out_piece, j)),
+            out_specs=pl.BlockSpec((piece_rows, tile), lambda j, s: (0, j)),
         ),
-        out_shape=jax.ShapeDtypeStruct((out_rows, width), bf16),
-        input_output_aliases=aliases,
+        out_shape=jax.ShapeDtypeStruct((piece_rows, width), f32 if adapter else bf16),
         compiler_params=params(),
         cost_estimate=declared,
     )(scalars, *operands)
+
+
+def finish_kernel(counts, *refs):
+    out = refs[-1]
+    position = 0
+    for piece, count in enumerate(counts):
+
+        @pl.when(pl.program_id(0) == piece)
+        def _():
+            total = refs[position][...].astype(f32)
+            for i in range(1, count):
+                total = total + refs[position + i][...].astype(f32)
+            out[...] = total.astype(out.dtype)
+
+        position += count
+
+
+def finish(groups, link):
+    piece_rows, width = groups[0][0].shape
+    tile = width // 2
+
+    def place(piece):
+        def index(p, j):
+            return (0, jnp.where(p == piece, j, jnp.where(p < piece, 0, 1)))
+
+        return index
+
+    in_specs = [
+        pl.BlockSpec((piece_rows, tile), place(piece))
+        for piece, group in enumerate(groups)
+        for _ in group
+    ]
+    return pl.pallas_call(
+        functools.partial(finish_kernel, tuple(len(group) for group in groups)),
+        grid=(len(groups), 2),
+        in_specs=in_specs + [pl.BlockSpec(memory_space=pl.ANY)] * len(link),
+        out_specs=pl.BlockSpec((piece_rows, tile), lambda p, j: (p, j)),
+        out_shape=jax.ShapeDtypeStruct((len(groups) * piece_rows, width), bf16),
+        compiler_params=params(),
+        cost_estimate=declared,
+    )(*[array for group in groups for array in group], *link)
 
 
 def low_kernel(tenants, rows, expand, link, out):
@@ -286,11 +319,11 @@
         link[:] = [out]
         return out
 
+    y1 = swap(run(jnp.where(at_end, far, near_end), other, upper, []), every)
     direct_a = along(run(far, other, lower, []), from_ends)
     low_whole = adapter_space()
-    y1 = swap(run(jnp.where(at_end, far, near_end), other, upper, []), every)
+    y2 = swap(run(beyond, other, lower, []), ends)
     direct_b = along(run(far, same, lower, []), from_ends)
-    y2 = swap(run(beyond, other, lower, []), ends)
     out = run(
         far,
         jnp.where(at_end, same, other),
@@ -309,6 +342,7 @@
         [(y3, 1), (direct_a, 0)],
     )
     both_3 = along(out, from_ends + to_ends)
+    grad_expand = expand_gradient()
     y5 = swap(run(jnp.where(at_end, nearer, beyond), other, upper, []), every)
     upper_far = along(run(far, same, upper, [(y3, 0), (upper_1, 0)]), across)
     out = run(jnp.where(at_end, nearer, near_end), same, lower, [(y4, 1), (direct_b, 0)])
@@ -322,23 +356,21 @@
     both_5 = along(out, from_ends + to_ends)
     y7 = swap(run(node, other, lower, [(both_3, 1)]), every)
     upper_4 = along(run(beyond, same, upper, [(y5, 0), (both_3, 0)]), across)
-    link += [both_4, y6, lower_4]
-    grad_expand = expand_gradient()
-    grad_shrink = shrink_gradient(low)
-
-    input_gradient = None
-    in_piece = piece_rows // row_block
-    for piece, adds in (
-        (lower, [(y7, 0), (both_4, 0), (lower_4, 0)]),
-        (upper, [(y6, 0), (both_5, 0), (upper_4, 0)]),
-    ):
+    def base(piece, adds):
+        in_piece = piece_rows // row_block
         scalars = [node * 2 + side, jnp.int32(piece), jnp.int32(0), jnp.int32(0)]
         scalars += [tenant_per_block[piece * in_piece + i] for i in range(in_piece)]
-        input_gradient = product(
+        out = product(
             jnp.stack(scalars).astype(jnp.int32),
-            gradient, weights, piece, piece_rows, width, adds, link, (low, shrink), input_gradient,
+            gradient, weights, piece, piece_rows, width, adds, link, (low, shrink),
         )
-        link[:] = [input_gradient]
+        link[:] = [out]
+        return out
+
+    lower_base = base(lower, [(both_4, 0), (lower_4, 0)])
+    upper_base = base(upper, [(y6, 0)])
+    grad_shrink = shrink_gradient(low)
+    input_gradient = finish([[lower_base, y7], [upper_base, both_5, upper_4]], link)
     return (input_gradient, grad_shrink, grad_expand)
 
 

time: 216 us -> 206 us (0.954)
  starting transfers between devices: 53 us -> 33.8 us
  Pallas kernels: 95.8 us -> 103 us
  local copies, waits for them, and re-layouts: 16.9 us -> 21.6 us
  waiting for transfers between devices: 27.1 us -> 24.5 us
    ppermute x12, starting transfers between devices: 44.5 us -> 26.5 us  [along(): lax.ppermute(x, 'tensor', [(2 * a + y, 2 * b + y) for a, b in hops for y...]
    ppermute x7, waiting for transfers between devices: 13.2 us -> 0.02 us  [swap(): return lax.ppermute(x, 'tensor', pairs)]
    ppermute x12, waiting for transfers between devices: 13.9 us -> 23.8 us  [along(): lax.ppermute(x, 'tensor', [(2 * a + y, 2 * b + y) for a, b in hops for y...]
    pallas_call x0 -> x1, Pallas kernels: none -> 4.74 us  [finish(): pl.pallas_call(functools.partial(finish_kernel, tuple((len(group) for gro...]
    unnamed x37 -> x36, local copies, waits for them, and re-layouts: 14.2 us -> 18.9 us
    pallas_call x2, Pallas kernels: 8.38 us -> 11.9 us  [factor_sums(): pl.pallas_call(functools.partial(factor_kernel, slots_each), in_specs=[pl...]
  transfers between devices with their start and end apart: 23 -> 23, of which waited for: 5 -> 5; matrix products, arithmetic and copies ran while one was open for 3% -> 2% of each run, Pallas kernels for 40% -> 48%
where the time goes in v5:
time: 206 us; the launch traced here: 205 us
  Pallas kernels  103 us (50%)
  starting transfers between devices  33.8 us (16%)
  waiting for transfers between devices  24.5 us (12%)
  local copies, waits for them, and re-layouts  21.6 us (10%)
  between operations  15.8 us (8%)
  blocking collectives  4.35 us (2%)
    pallas_call x19, Pallas kernels, product(): pl.pallas_call(functools.partial(product_kernel, tuple((mode for _, mode...  81.9 us
    ppermute x12, starting transfers between devices, along(): lax.ppermute(x, 'tensor', [(2 * a + y, 2 * b + y) for a, b in hops for y...  26.5 us
    ppermute x12, waiting for transfers between devices, along(): lax.ppermute(x, 'tensor', [(2 * a + y, 2 * b + y) for a, b in hops for y...  23.8 us
    unnamed x36, local copies, waits for them, and re-layouts  18.9 us
    pallas_call x2, Pallas kernels, factor_sums(): pl.pallas_call(functools.partial(factor_kernel, slots_each), in_specs=[pl...  11.9 us
    ppermute x7, starting transfers between devices, swap(): return lax.ppermute(x, 'tensor', pairs)  7.17 us
    pallas_call x1, Pallas kernels, finish(): pl.pallas_call(functools.partial(finish_kernel, tuple((len(group) for gro...  4.74 us
    all_gather x2, blocking collectives, all_owners(): return lax.all_gather(x, 'dp', axis=0, tiled=True)  4.35 us
  transfers between devices with their start and end apart: 23, of which 5 were waited for; matrix products, arithmetic and copies ran while one was open for 2% of the time, Pallas kernels for 48%

profile of v5, /device:TPU:10, one launch (start us, length us, event | category | flops | bytes accessed | tf_op | source)
XLA Modules:
  0.0 205.4 jit_solution(1828116390384535279)
XLA Ops:
  8.9 1.6 copy-done
  10.4 4.2 %shard_map.112.refs_3_ = bf16[512,1024]{1,0:T(8,128)(2,1)} custom-call(s32[4]{0:T(128)S(1)} %fusion.4.refs_0_, bf16[1024,1024]{1,0:T(8,128)(2,1)S(1)} %copy-done, bf16[8192,1024]{1,0:T(8,128)(2,1)} %refs_2_.37), custom_call_target="tpu_custom_call" | custom-call | flops 999999995904 | bytes 1000000000 | tf_op jit(solution)/shard_map/pallas_call | solution.py:84
  14.6 1.5 collective-permute-start.2
  16.2 4.2 %shard_map.113.link = bf16[512,1024]{1,0:T(8,128)(2,1)} custom-call(s32[4]{0:T(128)S(1)} %fusion.26.refs_0_, bf16[1024,1024]{1,0:T(8,128)(2,1)S(1)} %copy-done.1, bf16[8192,1024]{1,0:T(8,128)(2,1)} %refs_2_.37, bf16[512,1024]{1,0:T(8,128)(2,1)} %shard_map.112.refs_3_), custom_call_target="tpu_custom_call" | custom-call | flops 999999995904 | bytes 1000000000 | tf_op jit(solution)/shard_map/pallas_call | solution.py:84
  21.8 2.8 %copy-done.2 = bf16[16,128,1024]{2,1,0:T(8,128)(2,1)S(1)} copy-done((bf16[16,128,1024]{2,1,0:T(8,128)(2,1)S(1)}, bf16[16,128,1024]{2,1,0:T(8,128)(2,1)}, u32[]{:S(2)}) %copy-start.2) | copy-done | bytes 4194328
  24.6 4.3 %shard_map.114.refs_3_ = bf16[1024,128]{1,0:T(8,128)(2,1)} custom-call(s32[8]{0:T(128)} %tenants.1, bf16[1024,1024]{1,0:T(8,128)(2,1)S(1)} %copy-done.1, bf16[16,128,1024]{2,1,0:T(8,128)(2,1)S(1)} %copy-done.2, bf16[512,1024]{1,0:T(8,128)(2,1)} %shard_map.113.link), custom_call_target="tpu_custom_call" | custom-call | flops 999999995904 | bytes 1000000000 | tf_op jit(solution)/shard_map/pallas_call | solution.py:148
  29.0 4.1 %shard_map.115.refs_3_ = bf16[512,1024]{1,0:T(8,128)(2,1)} custom-call(s32[4]{0:T(128)S(1)} %fusion.24.refs_0_, bf16[1024,1024]{1,0:T(8,128)(2,1)S(1)} %copy-done.1, bf16[8192,1024]{1,0:T(8,128)(2,1)} %refs_2_.37, bf16[1024,128]{1,0:T(8,128)(2,1)} %shard_map.114.refs_3_), custom_call_target="tpu_custom_call" | custom-call | flops 999999995904 | bytes 1000000000 | tf_op jit(solution)/shard_map/pallas_call | solution.py:84
  33.1 1.6 collective-permute-start
  34.9 4.1 %shard_map.116.refs_5_ = bf16[512,1024]{1,0:T(8,128)(2,1)} custom-call(s32[4]{0:T(128)S(1)} %fusion.28.refs_0_, bf16[1024,1024]{1,0:T(8,128)(2,1)S(1)} %copy-done.1, bf16[8192,1024]{1,0:T(8,128)(2,1)} %refs_2_.37, bf16[512,1024]{1,0:T(8,128)(2,1)} %shard_map.115.refs_3_), custom_call_target="tpu_custom_call" | custom-call | flops 999999995904 | bytes 1000000000 | tf_op jit(solution)/shard_map/pallas_call | solution.py:84
  43.3 2.2 %all_gather.12 = bf16[2048,128]{1,0:T(8,128)(2,1)S(1)} all-gather(bf16[1024,128]{1,0:T(8,128)(2,1)S(1)} %copy-done.15), channel_id=1, replica_groups=mesh['groups'=2,'dp'=2,'tensor'=8] {'dp'}, dimensions={0}, use_global_device_ids=true | all-gather | bytes 786432 | tf_op jit(solution)/shard_map/all_gather | solution.py:273
  47.3 2.6 %collective-permute-done.3.refs_4_ = bf16[512,1024]{1,0:T(8,128)(2,1)} collective-permute-done((bf16[512,1024]{1,0:T(8,128)(2,1)}, bf16[512,1024]{1,0:T(8,128)(2,1)}, u32[]{:S(2)}, u32[]{:S(2)}) %collective-permute-start.3) | collective-permute-done | bytes 1048608 | tf_op jit(solution)/shard_map/ppermute | solution.py:256
  49.9 4.8 %shard_map.117.refs_3_ = bf16[512,1024]{1,0:T(8,128)(2,1)} custom-call(s32[4]{0:T(128)S(1)} %add_add_fusion.refs_0_, bf16[1024,1024]{1,0:T(8,128)(2,1)S(1)} %copy-done.1, bf16[8192,1024]{1,0:T(8,128)(2,1)} %refs_2_.37, bf16[512,1024]{1,0:T(8,128)(2,1)} %collective-permute-done.2.refs_3_.refs_4_, bf16[512,1024]{1,0:T(8,128)(2,1)} %collective-permute-done.3.refs_4_, ...), custom_call_target="tpu_custom_call" | custom-call | flops 999999995904 | bytes 1000000000 | tf_op jit(solution)/shard_map/pallas_call | solution.py:84
  54.8 3.2 %collective-permute-start.9 = (bf16[512,1024]{1,0:T(8,128)(2,1)}, bf16[512,1024]{1,0:T(8,128)(2,1)}, u32[]{:S(2)}, u32[]{:S(2)}) collective-permute-start(bf16[512,1024]{1,0:T(8,128)(2,1)} %shard_map.117.refs_3_), channel_id=1, source_target_pairs={{2,4},{3,5},{4,2},{5,3},{10,12},{11,13},{12,10},{13,11},{18,20},{1... | collective-permute-start | bytes 3145736 | tf_op jit(solution)/shard_map/ppermute | solution.py:256
  59.3 4.1 %shard_map.118.refs_5_ = bf16[512,1024]{1,0:T(8,128)(2,1)} custom-call(s32[4]{0:T(128)S(1)} %fusion.6.refs_0_, bf16[1024,1024]{1,0:T(8,128)(2,1)S(1)} %copy-done.1, bf16[8192,1024]{1,0:T(8,128)(2,1)} %refs_2_.37, bf16[512,1024]{1,0:T(8,128)(2,1)} %shard_map.117.refs_3_), custom_call_target="tpu_custom_call" | custom-call | flops 999999995904 | bytes 1000000000 | tf_op jit(solution)/shard_map/pallas_call | solution.py:84
  63.3 11.7 %collective-permute-done.1.refs_4_ = bf16[512,1024]{1,0:T(8,128)(2,1)} collective-permute-done((bf16[512,1024]{1,0:T(8,128)(2,1)}, bf16[512,1024]{1,0:T(8,128)(2,1)}, u32[]{:S(2)}, u32[]{:S(2)}) %collective-permute-start.1) | collective-permute-done | bytes 1048608 | tf_op jit(solution)/shard_map/ppermute | solution.py:256
  75.1 4.5 %shard_map.119.refs_3_ = bf16[512,1024]{1,0:T(8,128)(2,1)} custom-call(s32[4]{0:T(128)S(1)} %fusion.22.refs_0_, bf16[1024,1024]{1,0:T(8,128)(2,1)S(1)} %copy-done.1, bf16[8192,1024]{1,0:T(8,128)(2,1)} %refs_2_.37, bf16[512,1024]{1,0:T(8,128)(2,1)} %collective-permute-done.refs_3_, bf16[512,1024]{1,0:T(8,128)(2,1)} %collective-permute-done.1.refs_4_, ...), custom_call_target="tpu_custom_call" | custom-call | flops 999999995904 | bytes 1000000000 | tf_op jit(solution)/shard_map/pallas_call | solution.py:84
  79.6 3.5 %collective-permute-start.5 = (bf16[512,1024]{1,0:T(8,128)(2,1)}, bf16[512,1024]{1,0:T(8,128)(2,1)}, u32[]{:S(2)}, u32[]{:S(2)}) collective-permute-start(bf16[512,1024]{1,0:T(8,128)(2,1)} %shard_map.119.refs_3_), channel_id=1, source_target_pairs={{2,4},{3,5},{4,2},{5,3},{10,12},{11,13},{12,10},{13,11},{18,20},{1... | collective-permute-start | bytes 3145736 | tf_op jit(solution)/shard_map/ppermute | solution.py:256
  84.3 4.1 %shard_map.120.refs_5_ = bf16[512,1024]{1,0:T(8,128)(2,1)} custom-call(s32[4]{0:T(128)S(1)} %fusion.20.refs_0_, bf16[1024,1024]{1,0:T(8,128)(2,1)S(1)} %copy-done.1, bf16[8192,1024]{1,0:T(8,128)(2,1)} %refs_2_.37, bf16[512,1024]{1,0:T(8,128)(2,1)} %shard_map.119.refs_3_), custom_call_target="tpu_custom_call" | custom-call | flops 999999995904 | bytes 1000000000 | tf_op jit(solution)/shard_map/pallas_call | solution.py:84
  88.5 4.4 %shard_map.121.refs_0_ = bf16[512,1024]{1,0:T(8,128)(2,1)} custom-call(s32[4]{0:T(128)S(1)} %add_add_fusion.1.refs_0_, bf16[1024,1024]{1,0:T(8,128)(2,1)S(1)} %copy-done.1, bf16[8192,1024]{1,0:T(8,128)(2,1)} %refs_2_.37, bf16[512,1024]{1,0:T(8,128)(2,1)} %collective-permute-done.6.refs_3_, bf16[512,1024]{1,0:T(8,128)(2,1)} %collective-permute-done.9.refs_4_, ...), custom_call_target="tpu_custom_call" | custom-call | flops 999999995904 | bytes 1000000000 | tf_op jit(solution)/shard_map/pallas_call | solution.py:84
  92.9 4.0 %collective-permute-start.14 = (bf16[512,1024]{1,0:T(8,128)(2,1)}, bf16[512,1024]{1,0:T(8,128)(2,1)}, u32[]{:S(2)}, u32[]{:S(2)}) collective-permute-start(bf16[512,1024]{1,0:T(8,128)(2,1)} %shard_map.121.refs_0_), channel_id=1, source_target_pairs={{0,2},{1,3},{6,4},{7,5},{2,0},{3,1},{4,6},{5,7},{8,10},{9,11},{14,... | collective-permute-start | bytes 3145736 | tf_op jit(solution)/shard_map/ppermute | solution.py:256
  97.0 2.2 %copy-done.5 = bf16[2048,1024]{1,0:T(8,128)(2,1)S(1)} copy-done((bf16[2048,1024]{1,0:T(8,128)(2,1)S(1)}, bf16[2048,1024]{1,0:T(8,128)(2,1)}, u32[]{:S(2)}) %copy-start.5) | copy-done | bytes 4194328
  99.2 5.9 %shard_map.122.refs_3_ = f32[8,128,1024]{2,1,0:T(8,128)} custom-call(s32[16]{0:T(128)S(1)} %get-tuple-element.4.slots, f32[16]{0:T(128)S(1)} %copy-done.10, bf16[2048,128]{1,0:T(8,128)(2,1)S(1)} %bitcast_multiply_fusion.left, bf16[2048,1024]{1,0:T(8,128)(2,1)S(1)} %copy-done.5, bf16[512,1024]{1,0:T(8,128)(2,1)} %shard_map.121.refs_0_), custom_call_target="tpu_custom_call" | custom-call | flops 999999995904 | bytes 1000000000 | tf_op jit(solution)/shard_map/pallas_call | solution.py:204
  105.1 2.2 %copy-done.7 = f32[8,128,1024]{2,1,0:T(8,128)S(1)} copy-done((f32[8,128,1024]{2,1,0:T(8,128)S(1)}, f32[8,128,1024]{2,1,0:T(8,128)}, u32[]{:S(2)}) %copy-start.7) | copy-done | bytes 4194328
  107.3 4.1 %shard_map.123.refs_5_ = bf16[512,1024]{1,0:T(8,128)(2,1)} custom-call(s32[4]{0:T(128)S(1)} %fusion.10.refs_0_, bf16[1024,1024]{1,0:T(8,128)(2,1)S(1)} %copy-done.1, bf16[8192,1024]{1,0:T(8,128)(2,1)} %refs_2_.37, f32[8,128,1024]{2,1,0:T(8,128)S(1)} %copy-done.7), custom_call_target="tpu_custom_call" | custom-call | flops 999999995904 | bytes 1000000000 | tf_op jit(solution)/shard_map/pallas_call | solution.py:84
  111.4 1.6 collective-permute-start.13
  113.0 4.4 %shard_map.124.refs_5_ = bf16[512,1024]{1,0:T(8,128)(2,1)} custom-call(s32[4]{0:T(128)S(1)} %fusion.8.refs_0_, bf16[1024,1024]{1,0:T(8,128)(2,1)S(1)} %copy-done.1, bf16[8192,1024]{1,0:T(8,128)(2,1)} %refs_2_.37, bf16[512,1024]{1,0:T(8,128)(2,1)} %collective-permute-done.6.refs_3_, bf16[512,1024]{1,0:T(8,128)(2,1)} %collective-permute-done.7.refs_4_, ...), custom_call_target="tpu_custom_call" | custom-call | flops 999999995904 | bytes 1000000000 | tf_op jit(solution)/shard_map/pallas_call | solution.py:84
  117.5 2.5 %collective-permute-start.15 = (bf16[512,1024]{1,0:T(8,128)(2,1)}, bf16[512,1024]{1,0:T(8,128)(2,1)}, u32[]{:S(2)}, u32[]{:S(2)}) collective-permute-start(bf16[512,1024]{1,0:T(8,128)(2,1)} %shard_map.124.refs_5_), channel_id=1, source_target_pairs={{2,4},{3,5},{4,2},{5,3},{10,12},{11,13},{12,10},{13,11},{18,20},{1... | collective-permute-start | bytes 3145736 | tf_op jit(solution)/shard_map/ppermute | solution.py:256
  120.0 4.5 %shard_map.125.link = bf16[512,1024]{1,0:T(8,128)(2,1)} custom-call(s32[4]{0:T(128)S(1)} %fusion.18.refs_0_, bf16[1024,1024]{1,0:T(8,128)(2,1)S(1)} %copy-done.1, bf16[8192,1024]{1,0:T(8,128)(2,1)} %refs_2_.37, bf16[512,1024]{1,0:T(8,128)(2,1)} %collective-permute-done.4.refs_3_, bf16[512,1024]{1,0:T(8,128)(2,1)} %collective-permute-done.5.refs_4_, ...), custom_call_target="tpu_custom_call" | custom-call | flops 999999995904 | bytes 1000000000 | tf_op jit(solution)/shard_map/pallas_call | solution.py:84
  127.0 4.1 %shard_map.127.refs_5_ = bf16[512,1024]{1,0:T(8,128)(2,1)} custom-call(s32[4]{0:T(128)S(1)} %fusion.12.refs_0_, bf16[1024,1024]{1,0:T(8,128)(2,1)S(1)} %copy-done.1, bf16[8192,1024]{1,0:T(8,128)(2,1)} %refs_2_.37, bf16[1024,128]{1,0:T(8,128)(2,1)S(1)} %shard_map.126.refs_3_.refs_5_.refs_4_), custom_call_target="tpu_custom_call" | custom-call | flops 999999995904 | bytes 1000000000 | tf_op jit(solution)/shard_map/pallas_call | solution.py:84
  131.8 4.5 %shard_map.128.refs_6_ = bf16[512,1024]{1,0:T(8,128)(2,1)} custom-call(s32[4]{0:T(128)S(1)} %fusion.30.refs_0_, bf16[1024,1024]{1,0:T(8,128)(2,1)S(1)} %copy-done.1, bf16[8192,1024]{1,0:T(8,128)(2,1)} %refs_2_.37, bf16[512,1024]{1,0:T(8,128)(2,1)} %collective-permute-done.4.refs_3_, bf16[512,1024]{1,0:T(8,128)(2,1)} %collective-permute-done.11.refs_4_, ...), custom_call_target="tpu_custom_call" | custom-call | flops 999999995904 | bytes 1000000000 | tf_op jit(solution)/shard_map/pallas_call | solution.py:84
  136.3 2.2 %all_gather.15.right = bf16[2048,128]{1,0:T(8,128)(2,1)S(1)} all-gather(bf16[1024,128]{1,0:T(8,128)(2,1)S(1)} %shard_map.126.refs_3_.refs_5_.refs_4_), channel_id=1, replica_groups=mesh['groups'=2,'dp'=2,'tensor'=8] {'dp'}, dimensions={0}, use_global_device_ids=true | all-gather | bytes 786432 | tf_op jit(solution)/shard_map/all_gather | solution.py:273
  138.5 1.4 collective-permute-done.15.refs_5_
  139.9 3.6 %collective-permute-start.12 = (bf16[512,1024]{1,0:T(8,128)(2,1)}, bf16[512,1024]{1,0:T(8,128)(2,1)}, u32[]{:S(2)}, u32[]{:S(2)}) collective-permute-start(bf16[512,1024]{1,0:T(8,128)(2,1)} %shard_map.128.refs_6_), channel_id=1, source_target_pairs={{2,4},{3,5},{4,2},{5,3},{10,12},{11,13},{12,10},{13,11},{18,20},{1... | collective-permute-start | bytes 3145736 | tf_op jit(solution)/shard_map/ppermute | solution.py:256
  143.5 4.8 %shard_map.129.refs_4_ = bf16[512,1024]{1,0:T(8,128)(2,1)} custom-call(s32[4]{0:T(128)S(1)} %fusion.16.refs_0_, bf16[1024,1024]{1,0:T(8,128)(2,1)S(1)} %copy-done.1, bf16[8192,1024]{1,0:T(8,128)(2,1)} %refs_2_.37, bf16[512,1024]{1,0:T(8,128)(2,1)} %collective-permute-done.13.refs_3_, bf16[512,1024]{1,0:T(8,128)(2,1)} %collective-permute-done.2.refs_3_.refs_4_, ...), custom_call_target="tpu_custom_call" | custom-call | flops 999999995904 | bytes 1000000000 | tf_op jit(solution)/shard_map/pallas_call | solution.py:84
  148.3 4.3 %shard_map.130.refs_5_ = bf16[512,1024]{1,0:T(8,128)(2,1)} custom-call(s32[4]{0:T(128)S(1)} %fusion.32.refs_0_, bf16[1024,1024]{1,0:T(8,128)(2,1)S(1)} %copy-done.1, bf16[8192,1024]{1,0:T(8,128)(2,1)} %refs_2_.37, bf16[512,1024]{1,0:T(8,128)(2,1)} %collective-permute-done.14.refs_3_.refs_4_, bf16[512,1024]{1,0:T(8,128)(2,1)} %shard_map.129.refs_4_), custom_call_target="tpu_custom_call" | custom-call | flops 999999995904 | bytes 1000000000 | tf_op jit(solution)/shard_map/pallas_call | solution.py:84
  152.6 1.7 collective-permute-start.16
  154.4 4.7 %shard_map.131.refs_10_ = bf16[512,1024]{1,0:T(8,128)(2,1)} custom-call(s32[4]{0:T(128)S(1)} %fusion.14.refs_0_, bf16[1024,1024]{1,0:T(8,128)(2,1)S(1)} %copy-done.1, bf16[8192,1024]{1,0:T(8,128)(2,1)} %refs_2_.37, bf16[512,1024]{1,0:T(8,128)(2,1)} %collective-permute-done.13.refs_3_, bf16[512,1024]{1,0:T(8,128)(2,1)} %collective-permute-done.14.refs_3_.refs_4_, ...), custom_call_target="tpu_custom_call" | custom-call | flops 999999995904 | bytes 1000000000 | tf_op jit(solution)/shard_map/pallas_call | solution.py:84
  159.1 6.8 %collective-permute-done.12.refs_4_ = bf16[512,1024]{1,0:T(8,128)(2,1)} collective-permute-done((bf16[512,1024]{1,0:T(8,128)(2,1)}, bf16[512,1024]{1,0:T(8,128)(2,1)}, u32[]{:S(2)}, u32[]{:S(2)}) %collective-permute-start.12) | collective-permute-done | bytes 1048608 | tf_op jit(solution)/shard_map/ppermute | solution.py:256
  165.9 3.5 %collective-permute-start.19 = (bf16[512,1024]{1,0:T(8,128)(2,1)}, bf16[512,1024]{1,0:T(8,128)(2,1)}, u32[]{:S(2)}, u32[]{:S(2)}) collective-permute-start(bf16[512,1024]{1,0:T(8,128)(2,1)} %shard_map.131.refs_10_), channel_id=1, source_target_pairs={{2,4},{3,5},{4,2},{5,3},{10,12},{11,13},{12,10},{13,11},{18,20},{1... | collective-permute-start | bytes 3145736 | tf_op jit(solution)/shard_map/ppermute | solution.py:256
  169.4 4.0 %shard_map.132.refs_9_.refs_0_ = f32[512,1024]{1,0:T(8,128)S(1)} custom-call(s32[8]{0:T(128)S(1)} %get-tuple-element.6.refs_0_, bf16[1024,1024]{1,0:T(8,128)(2,1)S(1)} %copy-done.1, bf16[8192,1024]{1,0:T(8,128)(2,1)} %refs_2_.37, bf16[512,1024]{1,0:T(8,128)(2,1)} %collective-permute-done.10.refs_3_, bf16[512,1024]{1,0:T(8,128)(2,1)} %collective-permute-done.12.refs_4_, ...), custom_call_target="tpu_custom_call" | custom-call | flops 999999995904 | bytes 1000000000 | tf_op jit(solution)/shard_map/pallas_call | solution.py:84
  173.5 3.8 %shard_map.133.refs_0_.refs_2_ = f32[512,1024]{1,0:T(8,128)S(1)} custom-call(s32[8]{0:T(128)S(1)} %get-tuple-element.5.refs_0_, bf16[1024,1024]{1,0:T(8,128)(2,1)S(1)} %copy-done.1, bf16[8192,1024]{1,0:T(8,128)(2,1)} %refs_2_.37, bf16[512,1024]{1,0:T(8,128)(2,1)} %collective-permute-done.17.refs_3_, ...), custom_call_target="tpu_custom_call" | custom-call | flops 999999995904 | bytes 1000000000 | tf_op jit(solution)/shard_map/pallas_call | solution.py:84
  177.3 1.3 copy-done.11
  178.6 1.3 copy-done.13
  180.0 2.2 %copy-done.4 = bf16[2048,1024]{1,0:T(8,128)(2,1)S(1)} copy-done((bf16[2048,1024]{1,0:T(8,128)(2,1)S(1)}, bf16[2048,1024]{1,0:T(8,128)(2,1)}, u32[]{:S(2)}) %copy-start.4) | copy-done | bytes 4194328
  182.2 1.6 copy-done.14
  183.7 6.0 %shard_map.134.refs_5_ = f32[8,1024,128]{2,1,0:T(8,128)} custom-call(s32[16]{0:T(128)S(1)} %get-tuple-element.4.slots, f32[16]{0:T(128)S(1)} %broadcast_5_scales.2.scales, bf16[2048,1024]{1,0:T(8,128)(2,1)S(1)} %copy-done.4, bf16[2048,128]{1,0:T(8,128)(2,1)S(1)} %all_gather.15.right, f32[512,1024]{1,0:T(8,128)S(1)} %copy-done.14), custom_call_target="tpu_custom_call" | custom-call | flops 999999995904 | bytes 1000000000 | tf_op jit(solution)/shard_map/pallas_call | solution.py:204
  191.0 2.2 %copy-done.8 = f32[8,1024,128]{2,1,0:T(8,128)S(1)} copy-done((f32[8,1024,128]{2,1,0:T(8,128)S(1)}, f32[8,1024,128]{2,1,0:T(8,128)}, u32[]{:S(2)}) %copy-start.8) | copy-done | bytes 4194328
  193.2 4.7 %shard_map.135 = bf16[1024,1024]{1,0:T(8,128)(2,1)} custom-call(f32[512,1024]{1,0:T(8,128)S(1)} %copy-done.12, bf16[512,1024]{1,0:T(8,128)(2,1)} %collective-permute-done.16.refs_1_, f32[512,1024]{1,0:T(8,128)S(1)} %copy-done.14, bf16[512,1024]{1,0:T(8,128)(2,1)} %collective-permute-done.18.refs_3_, bf16[512,1024]{1,0:T(8,128)(2,1)} %collective-permute-done.19.refs_4_, ...), custom_call_target="tpu_custom_call" | custom-call | flops 999999995904 | bytes 1000000000 | tf_op jit(solution)/shard_map/pallas_call | solution.py:128
  (96 shorter events, 15.6 us)
Async XLA Ops:
  8.0 89.0 %all-gather.3.cloned.1.call-start = ((), (), s32[]{:S(2)}) async-start(), calls=%async_computation | async-start | bytes 6291456 | tf_op jit(solution)/shard_map/all_gather | solution.py:273
  8.9 1.6 copy-start
  10.4 5.8 %copy-start.1 = (bf16[1024,1024]{1,0:T(8,128)(2,1)S(1)}, bf16[1024,1024]{1,0:T(8,128)(2,1)}, u32[]{:S(2)}) copy-start(bf16[1024,1024]{1,0:T(8,128)(2,1)} %refs_1_.37) | copy-start | bytes 6291460
  14.6 35.3 %collective-permute-start.2 = (bf16[512,1024]{1,0:T(8,128)(2,1)}, bf16[512,1024]{1,0:T(8,128)(2,1)}, u32[]{:S(2)}, u32[]{:S(2)}) collective-permute-start(bf16[512,1024]{1,0:T(8,128)(2,1)} %shard_map.112.refs_3_), channel_id=1, source_target_pairs={{0,1},{1,0},{2,3},{3,2},{4,5},{5,4},{6,7},{7,6},{8,9},{9,8},{10,11... | collective-permute-start | bytes 3145736 | tf_op jit(solution)/shard_map/ppermute | solution.py:253
  20.4 29.5 %collective-permute-start.3 = (bf16[512,1024]{1,0:T(8,128)(2,1)}, bf16[512,1024]{1,0:T(8,128)(2,1)}, u32[]{:S(2)}, u32[]{:S(2)}) collective-permute-start(bf16[512,1024]{1,0:T(8,128)(2,1)} %shard_map.113.link), channel_id=1, source_target_pairs={{0,2},{1,3},{6,4},{7,5},{8,10},{9,11},{14,12},{15,13},{16,18},{17,... | collective-permute-start | bytes 3145736 | tf_op jit(solution)/shard_map/ppermute | solution.py:256
  21.7 23.7 %collective-permute-start.8 = (s32[8]{0:T(128)}, s32[8]{0:T(128)}, u32[]{:S(2)}, u32[]{:S(2)}) collective-permute-start(s32[8]{0:T(128)} %tenants.1), channel_id=1, source_target_pairs={{0,8},{8,0},{1,9},{9,1},{2,10},{10,2},{3,11},{11,3},{4,12},{12,4},... | collective-permute-start | bytes 104 | tf_op jit(solution)/shard_map/ppermute | solution.py:278
  21.8 2.8 %copy-start.2 = (bf16[16,128,1024]{2,1,0:T(8,128)(2,1)S(1)}, bf16[16,128,1024]{2,1,0:T(8,128)(2,1)}, u32[]{:S(2)}) copy-start(bf16[16,128,1024]{2,1,0:T(8,128)(2,1)} %expand.1) | copy-start | bytes 12582916
  33.1 92.4 %all-reduce.2.cloned.1.call-start = ((), (), s32[]{:S(2)}) async-start(), calls=%async_computation.1 | async-start | bytes 524288 | tf_op jit(solution)/shard_map/psum | solution.py:297
  33.1 42.0 %collective-permute-start = (bf16[512,1024]{1,0:T(8,128)(2,1)}, bf16[512,1024]{1,0:T(8,128)(2,1)}, u32[]{:S(2)}, u32[]{:S(2)}) collective-permute-start(bf16[512,1024]{1,0:T(8,128)(2,1)} %shard_map.115.refs_3_), channel_id=1, source_target_pairs={{0,1},{1,0},{6,7},{7,6},{8,9},{9,8},{14,15},{15,14},{16,17},{17,16... | collective-permute-start | bytes 3145736 | tf_op jit(solution)/shard_map/ppermute | solution.py:253
  34.7 145.2 %all-gather.5.cloned.1.call-start = ((), (), s32[]{:S(2)}) async-start(), calls=%async_computation.2 | async-start | bytes 6291456 | tf_op jit(solution)/shard_map/all_gather | solution.py:273
  34.9 7.1 %copy-start.17 = (s32[16]{0:T(128)S(1)}, s32[16]{0:T(128)}, u32[]{:S(2)}) copy-start(s32[16]{0:T(128)} %param.17) | copy-start | bytes 196
  34.9 8.4 %copy-start.15 = (bf16[1024,128]{1,0:T(8,128)(2,1)S(1)}, bf16[1024,128]{1,0:T(8,128)(2,1)}, u32[]{:S(2)}) copy-start(bf16[1024,128]{1,0:T(8,128)(2,1)} %param.11) | copy-start | bytes 786436
  34.9 11.5 %copy-start.16 = (s32[16]{0:T(128)S(1)}, s32[16]{0:T(128)}, u32[]{:S(2)}) copy-start(s32[16]{0:T(128)} %param.16) | copy-start | bytes 196
  39.0 36.1 %collective-permute-start.1 = (bf16[512,1024]{1,0:T(8,128)(2,1)}, bf16[512,1024]{1,0:T(8,128)(2,1)}, u32[]{:S(2)}, u32[]{:S(2)}) collective-permute-start(bf16[512,1024]{1,0:T(8,128)(2,1)} %shard_map.116.refs_5_), channel_id=1, source_target_pairs={{0,2},{1,3},{6,4},{7,5},{8,10},{9,11},{14,12},{15,13},{16,18},{17,... | collective-permute-start | bytes 3145736 | tf_op jit(solution)/shard_map/ppermute | solution.py:256
  46.6 0.6 copy-start.9
  54.8 33.7 %collective-permute-start.9 = (bf16[512,1024]{1,0:T(8,128)(2,1)}, bf16[512,1024]{1,0:T(8,128)(2,1)}, u32[]{:S(2)}, u32[]{:S(2)}) collective-permute-start(bf16[512,1024]{1,0:T(8,128)(2,1)} %shard_map.117.refs_3_), channel_id=1, source_target_pairs={{2,4},{3,5},{4,2},{5,3},{10,12},{11,13},{12,10},{13,11},{18,20},{1... | collective-permute-start | bytes 3145736 | tf_op jit(solution)/shard_map/ppermute | solution.py:256
  58.0 53.5 %collective-permute-start.7 = (bf16[512,1024]{1,0:T(8,128)(2,1)}, bf16[512,1024]{1,0:T(8,128)(2,1)}, u32[]{:S(2)}, u32[]{:S(2)}) collective-permute-start(bf16[512,1024]{1,0:T(8,128)(2,1)} %shard_map.117.refs_3_), channel_id=1, source_target_pairs={{0,2},{1,3},{6,4},{7,5},{8,10},{9,11},{14,12},{15,13},{16,18},{17,... | collective-permute-start | bytes 3145736 | tf_op jit(solution)/shard_map/ppermute | solution.py:256
  63.3 25.1 %collective-permute-start.6 = (bf16[512,1024]{1,0:T(8,128)(2,1)}, bf16[512,1024]{1,0:T(8,128)(2,1)}, u32[]{:S(2)}, u32[]{:S(2)}) collective-permute-start(bf16[512,1024]{1,0:T(8,128)(2,1)} %shard_map.118.refs_5_), channel_id=1, source_target_pairs={{0,1},{1,0},{2,3},{3,2},{4,5},{5,4},{6,7},{7,6},{8,9},{9,8},{10,11... | collective-permute-start | bytes 3145736 | tf_op jit(solution)/shard_map/ppermute | solution.py:253
  79.6 40.4 %collective-permute-start.5 = (bf16[512,1024]{1,0:T(8,128)(2,1)}, bf16[512,1024]{1,0:T(8,128)(2,1)}, u32[]{:S(2)}, u32[]{:S(2)}) collective-permute-start(bf16[512,1024]{1,0:T(8,128)(2,1)} %shard_map.119.refs_3_), channel_id=1, source_target_pairs={{2,4},{3,5},{4,2},{5,3},{10,12},{11,13},{12,10},{13,11},{18,20},{1... | collective-permute-start | bytes 3145736 | tf_op jit(solution)/shard_map/ppermute | solution.py:256
  83.0 48.1 %collective-permute-start.11 = (bf16[512,1024]{1,0:T(8,128)(2,1)}, bf16[512,1024]{1,0:T(8,128)(2,1)}, u32[]{:S(2)}, u32[]{:S(2)}) collective-permute-start(bf16[512,1024]{1,0:T(8,128)(2,1)} %shard_map.119.refs_3_), channel_id=1, source_target_pairs={{0,2},{1,3},{6,4},{7,5},{8,10},{9,11},{14,12},{15,13},{16,18},{17,... | collective-permute-start | bytes 3145736 | tf_op jit(solution)/shard_map/ppermute | solution.py:256
  88.5 29.0 %collective-permute-start.4 = (bf16[512,1024]{1,0:T(8,128)(2,1)}, bf16[512,1024]{1,0:T(8,128)(2,1)}, u32[]{:S(2)}, u32[]{:S(2)}) collective-permute-start(bf16[512,1024]{1,0:T(8,128)(2,1)} %shard_map.120.refs_5_), channel_id=1, source_target_pairs={{0,1},{1,0},{2,3},{3,2},{4,5},{5,4},{6,7},{7,6},{8,9},{9,8},{10,11... | collective-permute-start | bytes 3145736 | tf_op jit(solution)/shard_map/ppermute | solution.py:253
  88.5 8.5 %copy-start.10 = (f32[16]{0:T(128)S(1)}, f32[16]{0:T(128)}, u32[]{:S(2)}) copy-start(f32[16]{0:T(128)} %copy-done.9) | copy-start | bytes 196
  92.9 55.4 %collective-permute-start.14 = (bf16[512,1024]{1,0:T(8,128)(2,1)}, bf16[512,1024]{1,0:T(8,128)(2,1)}, u32[]{:S(2)}, u32[]{:S(2)}) collective-permute-start(bf16[512,1024]{1,0:T(8,128)(2,1)} %shard_map.121.refs_0_), channel_id=1, source_target_pairs={{0,2},{1,3},{6,4},{7,5},{2,0},{3,1},{4,6},{5,7},{8,10},{9,11},{14,... | collective-permute-start | bytes 3145736 | tf_op jit(solution)/shard_map/ppermute | solution.py:256
  97.0 2.2 %copy-start.5 = (bf16[2048,1024]{1,0:T(8,128)(2,1)S(1)}, bf16[2048,1024]{1,0:T(8,128)(2,1)}, u32[]{:S(2)}) copy-start(bf16[2048,1024]{1,0:T(8,128)(2,1)} %all-gather.3.cloned.1.call-done.right) | copy-start | bytes 12582916
  105.1 2.2 %copy-start.7 = (f32[8,128,1024]{2,1,0:T(8,128)S(1)}, f32[8,128,1024]{2,1,0:T(8,128)}, u32[]{:S(2)}) copy-start(f32[8,128,1024]{2,1,0:T(8,128)} %shard_map.122.refs_3_) | copy-start | bytes 12582916
  111.4 32.1 %collective-permute-start.13 = (bf16[512,1024]{1,0:T(8,128)(2,1)}, bf16[512,1024]{1,0:T(8,128)(2,1)}, u32[]{:S(2)}, u32[]{:S(2)}) collective-permute-start(bf16[512,1024]{1,0:T(8,128)(2,1)} %shard_map.123.refs_5_), channel_id=1, source_target_pairs={{0,1},{1,0},{2,3},{3,2},{4,5},{5,4},{6,7},{7,6},{8,9},{9,8},{10,11... | collective-permute-start | bytes 3145736 | tf_op jit(solution)/shard_map/ppermute | solution.py:253
  117.5 22.4 %collective-permute-start.15 = (bf16[512,1024]{1,0:T(8,128)(2,1)}, bf16[512,1024]{1,0:T(8,128)(2,1)}, u32[]{:S(2)}, u32[]{:S(2)}) collective-permute-start(bf16[512,1024]{1,0:T(8,128)(2,1)} %shard_map.124.refs_5_), channel_id=1, source_target_pairs={{2,4},{3,5},{4,2},{5,3},{10,12},{11,13},{12,10},{13,11},{18,20},{1... | collective-permute-start | bytes 3145736 | tf_op jit(solution)/shard_map/ppermute | solution.py:256
  124.5 44.9 %collective-permute-start.10 = (bf16[512,1024]{1,0:T(8,128)(2,1)}, bf16[512,1024]{1,0:T(8,128)(2,1)}, u32[]{:S(2)}, u32[]{:S(2)}) collective-permute-start(bf16[512,1024]{1,0:T(8,128)(2,1)} %shard_map.125.link), channel_id=1, source_target_pairs={{0,2},{1,3},{6,4},{7,5},{2,0},{3,1},{4,6},{5,7},{8,10},{9,11},{14,... | collective-permute-start | bytes 3145736 | tf_op jit(solution)/shard_map/ppermute | solution.py:256
  125.5 1.0 copy-start.6
  131.1 42.3 %collective-permute-start.17 = (bf16[512,1024]{1,0:T(8,128)(2,1)}, bf16[512,1024]{1,0:T(8,128)(2,1)}, u32[]{:S(2)}, u32[]{:S(2)}) collective-permute-start(bf16[512,1024]{1,0:T(8,128)(2,1)} %shard_map.127.refs_5_), channel_id=1, source_target_pairs={{0,1},{1,0},{2,3},{3,2},{4,5},{5,4},{6,7},{7,6},{8,9},{9,8},{10,11... | collective-permute-start | bytes 3145736 | tf_op jit(solution)/shard_map/ppermute | solution.py:253
  139.9 26.0 %collective-permute-start.12 = (bf16[512,1024]{1,0:T(8,128)(2,1)}, bf16[512,1024]{1,0:T(8,128)(2,1)}, u32[]{:S(2)}, u32[]{:S(2)}) collective-permute-start(bf16[512,1024]{1,0:T(8,128)(2,1)} %shard_map.128.refs_6_), channel_id=1, source_target_pairs={{2,4},{3,5},{4,2},{5,3},{10,12},{11,13},{12,10},{13,11},{18,20},{1... | collective-permute-start | bytes 3145736 | tf_op jit(solution)/shard_map/ppermute | solution.py:256
  148.3 42.7 %collective-permute-start.18 = (bf16[512,1024]{1,0:T(8,128)(2,1)}, bf16[512,1024]{1,0:T(8,128)(2,1)}, u32[]{:S(2)}, u32[]{:S(2)}) collective-permute-start(bf16[512,1024]{1,0:T(8,128)(2,1)} %shard_map.129.refs_4_), channel_id=1, source_target_pairs={{0,2},{1,3},{6,4},{7,5},{2,0},{3,1},{4,6},{5,7},{8,10},{9,11},{14,... | collective-permute-start | bytes 3145736 | tf_op jit(solution)/shard_map/ppermute | solution.py:256
  152.6 38.4 %collective-permute-start.16 = (bf16[512,1024]{1,0:T(8,128)(2,1)}, bf16[512,1024]{1,0:T(8,128)(2,1)}, u32[]{:S(2)}, u32[]{:S(2)}) collective-permute-start(bf16[512,1024]{1,0:T(8,128)(2,1)} %shard_map.130.refs_5_), channel_id=1, source_target_pairs={{0,1},{1,0},{2,3},{3,2},{4,5},{5,4},{6,7},{7,6},{8,9},{9,8},{10,11... | collective-permute-start | bytes 3145736 | tf_op jit(solution)/shard_map/ppermute | solution.py:253
  154.4 15.1 %copy-start.3 = (bf16[16,1024,128]{2,1,0:T(8,128)(2,1)S(1)}, bf16[16,1024,128]{2,1,0:T(8,128)(2,1)}, u32[]{:S(2)}) copy-start(bf16[16,1024,128]{2,1,0:T(8,128)(2,1)} %refs_8_.3) | copy-start | bytes 12582916
  165.9 25.1 %collective-permute-start.19 = (bf16[512,1024]{1,0:T(8,128)(2,1)}, bf16[512,1024]{1,0:T(8,128)(2,1)}, u32[]{:S(2)}, u32[]{:S(2)}) collective-permute-start(bf16[512,1024]{1,0:T(8,128)(2,1)} %shard_map.131.refs_10_), channel_id=1, source_target_pairs={{2,4},{3,5},{4,2},{5,3},{10,12},{11,13},{12,10},{13,11},{18,20},{1... | collective-permute-start | bytes 3145736 | tf_op jit(solution)/shard_map/ppermute | solution.py:256
  177.3 1.3 copy-start.11
  178.6 1.3 copy-start.13
  180.0 2.2 %copy-start.4 = (bf16[2048,1024]{1,0:T(8,128)(2,1)S(1)}, bf16[2048,1024]{1,0:T(8,128)(2,1)}, u32[]{:S(2)}) copy-start(bf16[2048,1024]{1,0:T(8,128)(2,1)} %all-gather.5.cloned.1.call-done.left) | copy-start | bytes 12582916
  182.2 1.6 copy-start.14
  183.7 7.3 %copy-start.12 = (f32[512,1024]{1,0:T(8,128)S(1)}, f32[512,1024]{1,0:T(8,128)}, u32[]{:S(2)}) copy-start(f32[512,1024]{1,0:T(8,128)} %copy-done.11) | copy-start | bytes 6291460
  191.0 2.2 %copy-start.8 = (f32[8,1024,128]{2,1,0:T(8,128)S(1)}, f32[8,1024,128]{2,1,0:T(8,128)}, u32[]{:S(2)}) copy-start(f32[8,1024,128]{2,1,0:T(8,128)} %shard_map.134.refs_5_) | copy-start | bytes 12582916
Sparse Core Ops, SparseCore 0:
  10.4 15.1 all-gather.2
  40.4 18.1 all-gather.4
Sparse Core Ops, SparseCore 1:
  36.9 73.4 all-reduce.1

commit v6 on v5

--- a/solution.py
+++ b/solution.py
@@ -89,7 +89,7 @@
             in_specs=in_specs,
             out_specs=pl.BlockSpec((piece_rows, tile), lambda j, s: (0, j)),
         ),
-        out_shape=jax.ShapeDtypeStruct((piece_rows, width), f32 if adapter else bf16),
+        out_shape=jax.ShapeDtypeStruct((piece_rows, width), bf16),
         compiler_params=params(),
         cost_estimate=declared,
     )(scalars, *operands)
@@ -250,6 +250,7 @@
         pairs = []
         for z in active:
             pairs += [(2 * z, 2 * z + 1), (2 * z + 1, 2 * z)]
+        pairs += [(2 * z + y, 2 * z + y) for z in every if z not in active for y in range(2)]
         return lax.ppermute(x, "tensor", pairs)
 
     def along(x, hops):
@@ -260,8 +261,10 @@
     nodes = 4
     ends, inner, every = (0, 3), (1, 2), (0, 1, 2, 3)
     from_ends = [(0, 1), (3, 2)]
-    across = [(1, 2), (2, 1)]
+    across_only = [(1, 2), (2, 1)]
     to_ends = [(1, 0), (2, 3)]
+    pairwise = from_ends + to_ends
+    across = across_only + [(0, 0), (3, 3)]
     first_half = node < 2
     far = jnp.where(first_half, 3, 0)
     beyond = jnp.where(first_half, 2, 1)
@@ -320,45 +323,45 @@
         return out
 
     y1 = swap(run(jnp.where(at_end, far, near_end), other, upper, []), every)
-    direct_a = along(run(far, other, lower, []), from_ends)
+    direct_a = along(run(far, other, lower, []), pairwise)
     low_whole = adapter_space()
     y2 = swap(run(beyond, other, lower, []), ends)
-    direct_b = along(run(far, same, lower, []), from_ends)
+    direct_b = along(run(far, same, lower, []), pairwise)
     out = run(
         far,
         jnp.where(at_end, same, other),
         jnp.where(at_end, upper, lower),
-        [(y1, 1), (direct_a, 0)],
-    )
-    upper_1, direct_a = along(out, from_ends), along(out, across)
+        [(y1, 1), (direct_a, 2)],
+    )
+    upper_1, direct_a = along(out, pairwise), along(out, across)
     y3 = swap(run(jnp.where(at_end, beyond, far), other, upper, []), every)
-    out = run(jnp.where(at_end, beyond, far), same, lower, [(y2, 0), (direct_b, 0)])
-    lower_2, direct_b = along(out, from_ends), along(out, across)
+    out = run(jnp.where(at_end, beyond, far), same, lower, [(y2, 1), (direct_b, 2)])
+    lower_2, direct_b = along(out, pairwise), along(out, across)
     y4 = swap(run(jnp.where(at_end, nearer, beyond), other, lower, []), every)
     out = run(
         jnp.where(at_end, beyond, near_end),
         jnp.where(at_end, same, other),
         jnp.where(at_end, upper, lower),
-        [(y3, 1), (direct_a, 0)],
-    )
-    both_3 = along(out, from_ends + to_ends)
+        [(y3, 1), (direct_a, 2)],
+    )
+    both_3 = along(out, pairwise)
     grad_expand = expand_gradient()
     y5 = swap(run(jnp.where(at_end, nearer, beyond), other, upper, []), every)
     upper_far = along(run(far, same, upper, [(y3, 0), (upper_1, 0)]), across)
-    out = run(jnp.where(at_end, nearer, near_end), same, lower, [(y4, 1), (direct_b, 0)])
-    both_4 = along(out, from_ends + to_ends)
+    out = run(jnp.where(at_end, nearer, near_end), same, lower, [(y4, 1), (direct_b, 2)])
+    both_4 = along(out, pairwise)
     low = scale_low(low_whole)
     y6 = swap(run(node, other, upper, []), every)
     lower_4 = along(run(beyond, same, lower, [(y4, 0), (lower_2, 0)]), across)
     out = run(
-        jnp.where(at_end, nearer, near_end), same, upper, [(y5, 1), (y1, 2), (upper_far, 0)]
-    )
-    both_5 = along(out, from_ends + to_ends)
+        jnp.where(at_end, nearer, near_end), same, upper, [(y5, 1), (y1, 2), (upper_far, 2)]
+    )
+    both_5 = along(out, pairwise)
     y7 = swap(run(node, other, lower, [(both_3, 1)]), every)
-    upper_4 = along(run(beyond, same, upper, [(y5, 0), (both_3, 0)]), across)
+    upper_4 = along(run(beyond, same, upper, [(y5, 0), (both_3, 0)]), across_only)
     def base(piece, adds):
         in_piece = piece_rows // row_block
-        scalars = [node * 2 + side, jnp.int32(piece), jnp.int32(0), jnp.int32(0)]
+        scalars = [node * 2 + side, jnp.int32(piece)] + [jnp.asarray(r, jnp.int32) for r in roles]
         scalars += [tenant_per_block[piece * in_piece + i] for i in range(in_piece)]
         out = product(
             jnp.stack(scalars).astype(jnp.int32),
@@ -367,7 +370,7 @@
         link[:] = [out]
         return out
 
-    lower_base = base(lower, [(both_4, 0), (lower_4, 0)])
+    lower_base = base(lower, [(both_4, 0), (lower_4, 2)])
     upper_base = base(upper, [(y6, 0)])
     grad_shrink = shrink_gradient(low)
     input_gradient = finish([[lower_base, y7], [upper_base, both_5, upper_4]], link)

time: 206 us -> 226 us (1.097)
  starting transfers between devices: 33.8 us -> 60.9 us
  waiting for transfers between devices: 24.5 us -> 18.9 us
    ppermute x12, starting transfers between devices: 26.5 us -> 45.6 us  [along(): lax.ppermute(x, 'tensor', [(2 * a + y, 2 * b + y) for a, b in hops for y...]
    ppermute x12, waiting for transfers between devices: 23.8 us -> 10.6 us  [along(): lax.ppermute(x, 'tensor', [(2 * a + y, 2 * b + y) for a, b in hops for y...]
    ppermute x7, starting transfers between devices: 7.17 us -> 15.2 us  [swap(): return lax.ppermute(x, 'tensor', pairs)]
    ppermute x7, waiting for transfers between devices: 0.02 us -> 7.54 us  [swap(): return lax.ppermute(x, 'tensor', pairs)]
    pallas_call x2, Pallas kernels: 11.9 us -> 9.38 us  [factor_sums(): pl.pallas_call(functools.partial(factor_kernel, slots_each), in_specs=[pl...]
  transfers between devices with their start and end apart: 23 -> 23, of which waited for: 5 -> 5; matrix products, arithmetic and copies ran while one was open for 2% -> 2% of each run, Pallas kernels for 48% -> 43%
where the time goes in v6:
time: 226 us; the launch traced here: 223 us
  Pallas kernels  101 us (45%)
  starting transfers between devices  60.9 us (27%)
  local copies, waits for them, and re-layouts  20.6 us (9%)
  waiting for transfers between devices  18.9 us (8%)
  between operations  15.8 us (7%)
  blocking collectives  4.44 us (2%)
    pallas_call x19, Pallas kernels, product(): pl.pallas_call(functools.partial(product_kernel, tuple((mode for _, mode...  81.8 us
    ppermute x12, starting transfers between devices, along(): lax.ppermute(x, 'tensor', [(2 * a + y, 2 * b + y) for a, b in hops for y...  45.6 us
    unnamed x36, local copies, waits for them, and re-layouts  17.8 us
    ppermute x7, starting transfers between devices, swap(): return lax.ppermute(x, 'tensor', pairs)  15.2 us
    ppermute x12, waiting for transfers between devices, along(): lax.ppermute(x, 'tensor', [(2 * a + y, 2 * b + y) for a, b in hops for y...  10.6 us
    pallas_call x2, Pallas kernels, factor_sums(): pl.pallas_call(functools.partial(factor_kernel, slots_each), in_specs=[pl...  9.38 us
    ppermute x7, waiting for transfers between devices, swap(): return lax.ppermute(x, 'tensor', pairs)  7.54 us
    pallas_call x1, Pallas kernels, finish(): pl.pallas_call(functools.partial(finish_kernel, tuple((len(group) for gro...  4.73 us
  transfers between devices with their start and end apart: 23, of which 5 were waited for; matrix products, arithmetic and copies ran while one was open for 2% of the time, Pallas kernels for 43%

profile of v6, /device:TPU:10, one launch (start us, length us, event | category | flops | bytes accessed | tf_op | source)
XLA Modules:
  0.0 223.2 jit_solution(993573604218652635)
XLA Ops:
  8.9 1.6 copy-done
  10.4 4.2 %shard_map.112.refs_3_ = bf16[512,1024]{1,0:T(8,128)(2,1)} custom-call(s32[4]{0:T(128)S(1)} %fusion.2.refs_0_, bf16[1024,1024]{1,0:T(8,128)(2,1)S(1)} %copy-done, bf16[8192,1024]{1,0:T(8,128)(2,1)} %refs_2_.37), custom_call_target="tpu_custom_call" | custom-call | flops 999999995904 | bytes 1000000000 | tf_op jit(solution)/shard_map/pallas_call | solution.py:84
  14.6 1.5 collective-permute-start.2
  16.2 4.2 %shard_map.113.link = bf16[512,1024]{1,0:T(8,128)(2,1)} custom-call(s32[4]{0:T(128)S(1)} %fusion.24.refs_0_, bf16[1024,1024]{1,0:T(8,128)(2,1)S(1)} %copy-done.1, bf16[8192,1024]{1,0:T(8,128)(2,1)} %refs_2_.37, bf16[512,1024]{1,0:T(8,128)(2,1)} %shard_map.112.refs_3_), custom_call_target="tpu_custom_call" | custom-call | flops 999999995904 | bytes 1000000000 | tf_op jit(solution)/shard_map/pallas_call | solution.py:84
  20.9 2.9 %copy-done.2 = bf16[16,128,1024]{2,1,0:T(8,128)(2,1)S(1)} copy-done((bf16[16,128,1024]{2,1,0:T(8,128)(2,1)S(1)}, bf16[16,128,1024]{2,1,0:T(8,128)(2,1)}, u32[]{:S(2)}) %copy-start.2) | copy-done | bytes 4194328
  23.8 4.3 %shard_map.114.refs_3_ = bf16[1024,128]{1,0:T(8,128)(2,1)} custom-call(s32[8]{0:T(128)} %tenants.1, bf16[1024,1024]{1,0:T(8,128)(2,1)S(1)} %copy-done.1, bf16[16,128,1024]{2,1,0:T(8,128)(2,1)S(1)} %copy-done.2, bf16[512,1024]{1,0:T(8,128)(2,1)} %shard_map.113.link), custom_call_target="tpu_custom_call" | custom-call | flops 999999995904 | bytes 1000000000 | tf_op jit(solution)/shard_map/pallas_call | solution.py:148
  28.2 4.1 %shard_map.115.refs_3_ = bf16[512,1024]{1,0:T(8,128)(2,1)} custom-call(s32[4]{0:T(128)S(1)} %fusion.22.refs_0_, bf16[1024,1024]{1,0:T(8,128)(2,1)S(1)} %copy-done.1, bf16[8192,1024]{1,0:T(8,128)(2,1)} %refs_2_.37, bf16[1024,128]{1,0:T(8,128)(2,1)} %shard_map.114.refs_3_), custom_call_target="tpu_custom_call" | custom-call | flops 999999995904 | bytes 1000000000 | tf_op jit(solution)/shard_map/pallas_call | solution.py:84
  32.2 9.5 %collective-permute-start = (bf16[512,1024]{1,0:T(8,128)(2,1)}, bf16[512,1024]{1,0:T(8,128)(2,1)}, u32[]{:S(2)}, u32[]{:S(2)}) collective-permute-start(bf16[512,1024]{1,0:T(8,128)(2,1)} %shard_map.115.refs_3_), channel_id=1, source_target_pairs={{0,1},{1,0},{6,7},{7,6},{2,2},{3,3},{4,4},{5,5},{8,9},{9,8},{14,15... | collective-permute-start | bytes 3145736 | tf_op jit(solution)/shard_map/ppermute | solution.py:254
  41.9 4.1 %shard_map.116.refs_5_ = bf16[512,1024]{1,0:T(8,128)(2,1)} custom-call(s32[4]{0:T(128)S(1)} %fusion.26.refs_0_, bf16[1024,1024]{1,0:T(8,128)(2,1)S(1)} %copy-done.1, bf16[8192,1024]{1,0:T(8,128)(2,1)} %refs_2_.37, bf16[512,1024]{1,0:T(8,128)(2,1)} %shard_map.115.refs_3_), custom_call_target="tpu_custom_call" | custom-call | flops 999999995904 | bytes 1000000000 | tf_op jit(solution)/shard_map/pallas_call | solution.py:84
  49.1 2.3 %all_gather.12 = bf16[2048,128]{1,0:T(8,128)(2,1)S(1)} all-gather(bf16[1024,128]{1,0:T(8,128)(2,1)S(1)} %copy-done.15), channel_id=1, replica_groups=mesh['groups'=2,'dp'=2,'tensor'=8] {'dp'}, dimensions={0}, use_global_device_ids=true | all-gather | bytes 786432 | tf_op jit(solution)/shard_map/all_gather | solution.py:276
  53.1 4.8 %shard_map.117.refs_3_ = bf16[512,1024]{1,0:T(8,128)(2,1)} custom-call(s32[4]{0:T(128)S(1)} %add_add_fusion.refs_0_, bf16[1024,1024]{1,0:T(8,128)(2,1)S(1)} %copy-done.1, bf16[8192,1024]{1,0:T(8,128)(2,1)} %refs_2_.37, bf16[512,1024]{1,0:T(8,128)(2,1)} %collective-permute-done.2.refs_3_.refs_4_, bf16[512,1024]{1,0:T(8,128)(2,1)} %collective-permute-done.3.refs_4_, ...), custom_call_target="tpu_custom_call" | custom-call | flops 999999995904 | bytes 1000000000 | tf_op jit(solution)/shard_map/pallas_call | solution.py:84
  57.9 4.2 %collective-permute-start.9 = (bf16[512,1024]{1,0:T(8,128)(2,1)}, bf16[512,1024]{1,0:T(8,128)(2,1)}, u32[]{:S(2)}, u32[]{:S(2)}) collective-permute-start(bf16[512,1024]{1,0:T(8,128)(2,1)} %shard_map.117.refs_3_), channel_id=1, source_target_pairs={{2,4},{3,5},{4,2},{5,3},{0,0},{1,1},{6,6},{7,7},{10,12},{11,13},{1... | collective-permute-start | bytes 3145736 | tf_op jit(solution)/shard_map/ppermute | solution.py:257
  62.2 7.2 %collective-permute-start.7 = (bf16[512,1024]{1,0:T(8,128)(2,1)}, bf16[512,1024]{1,0:T(8,128)(2,1)}, u32[]{:S(2)}, u32[]{:S(2)}) collective-permute-start(bf16[512,1024]{1,0:T(8,128)(2,1)} %shard_map.117.refs_3_), channel_id=1, source_target_pairs={{0,2},{1,3},{6,4},{7,5},{2,0},{3,1},{4,6},{5,7},{8,10},{9,11},{14,... | collective-permute-start | bytes 3145736 | tf_op jit(solution)/shard_map/ppermute | solution.py:257
  69.4 4.1 %shard_map.118.refs_5_ = bf16[512,1024]{1,0:T(8,128)(2,1)} custom-call(s32[4]{0:T(128)S(1)} %fusion.4.refs_0_, bf16[1024,1024]{1,0:T(8,128)(2,1)S(1)} %copy-done.1, bf16[8192,1024]{1,0:T(8,128)(2,1)} %refs_2_.37, bf16[512,1024]{1,0:T(8,128)(2,1)} %shard_map.117.refs_3_), custom_call_target="tpu_custom_call" | custom-call | flops 999999995904 | bytes 1000000000 | tf_op jit(solution)/shard_map/pallas_call | solution.py:84
  73.6 1.6 collective-permute-done.1.refs_4_
  75.2 4.5 %shard_map.119.refs_3_ = bf16[512,1024]{1,0:T(8,128)(2,1)} custom-call(s32[4]{0:T(128)S(1)} %fusion.20.refs_0_, bf16[1024,1024]{1,0:T(8,128)(2,1)S(1)} %copy-done.1, bf16[8192,1024]{1,0:T(8,128)(2,1)} %refs_2_.37, bf16[512,1024]{1,0:T(8,128)(2,1)} %collective-permute-done.refs_3_, bf16[512,1024]{1,0:T(8,128)(2,1)} %collective-permute-done.1.refs_4_, ...), custom_call_target="tpu_custom_call" | custom-call | flops 999999995904 | bytes 1000000000 | tf_op jit(solution)/shard_map/pallas_call | solution.py:84
  79.7 4.3 %collective-permute-start.5 = (bf16[512,1024]{1,0:T(8,128)(2,1)}, bf16[512,1024]{1,0:T(8,128)(2,1)}, u32[]{:S(2)}, u32[]{:S(2)}) collective-permute-start(bf16[512,1024]{1,0:T(8,128)(2,1)} %shard_map.119.refs_3_), channel_id=1, source_target_pairs={{2,4},{3,5},{4,2},{5,3},{0,0},{1,1},{6,6},{7,7},{10,12},{11,13},{1... | collective-permute-start | bytes 3145736 | tf_op jit(solution)/shard_map/ppermute | solution.py:257
  84.0 6.4 %collective-permute-start.11 = (bf16[512,1024]{1,0:T(8,128)(2,1)}, bf16[512,1024]{1,0:T(8,128)(2,1)}, u32[]{:S(2)}, u32[]{:S(2)}) collective-permute-start(bf16[512,1024]{1,0:T(8,128)(2,1)} %shard_map.119.refs_3_), channel_id=1, source_target_pairs={{0,2},{1,3},{6,4},{7,5},{2,0},{3,1},{4,6},{5,7},{8,10},{9,11},{14,... | collective-permute-start | bytes 3145736 | tf_op jit(solution)/shard_map/ppermute | solution.py:257
  90.4 4.1 %shard_map.120.refs_5_ = bf16[512,1024]{1,0:T(8,128)(2,1)} custom-call(s32[4]{0:T(128)S(1)} %fusion.18.refs_0_, bf16[1024,1024]{1,0:T(8,128)(2,1)S(1)} %copy-done.1, bf16[8192,1024]{1,0:T(8,128)(2,1)} %refs_2_.37, bf16[512,1024]{1,0:T(8,128)(2,1)} %shard_map.119.refs_3_), custom_call_target="tpu_custom_call" | custom-call | flops 999999995904 | bytes 1000000000 | tf_op jit(solution)/shard_map/pallas_call | solution.py:84
  94.5 4.7 %collective-permute-done.6.refs_3_ = bf16[512,1024]{1,0:T(8,128)(2,1)} collective-permute-done((bf16[512,1024]{1,0:T(8,128)(2,1)}, bf16[512,1024]{1,0:T(8,128)(2,1)}, u32[]{:S(2)}, u32[]{:S(2)}) %collective-permute-start.6) | collective-permute-done | bytes 1048608 | tf_op jit(solution)/shard_map/ppermute | solution.py:254
  99.5 4.5 %shard_map.121.refs_0_ = bf16[512,1024]{1,0:T(8,128)(2,1)} custom-call(s32[4]{0:T(128)S(1)} %add_add_fusion.1.refs_0_, bf16[1024,1024]{1,0:T(8,128)(2,1)S(1)} %copy-done.1, bf16[8192,1024]{1,0:T(8,128)(2,1)} %refs_2_.37, bf16[512,1024]{1,0:T(8,128)(2,1)} %collective-permute-done.6.refs_3_, bf16[512,1024]{1,0:T(8,128)(2,1)} %collective-permute-done.9.refs_4_, ...), custom_call_target="tpu_custom_call" | custom-call | flops 999999995904 | bytes 1000000000 | tf_op jit(solution)/shard_map/pallas_call | solution.py:84
  104.3 2.2 copy-done.4
  106.4 4.7 %shard_map.122.refs_3_ = f32[8,128,1024]{2,1,0:T(8,128)} custom-call(s32[16]{0:T(128)S(1)} %get-tuple-element.4.slots, f32[16]{0:T(128)S(1)} %copy-done.10, bf16[2048,128]{1,0:T(8,128)(2,1)S(1)} %bitcast_multiply_fusion.left, bf16[2048,1024]{1,0:T(8,128)(2,1)S(1)} %copy-done.4, bf16[512,1024]{1,0:T(8,128)(2,1)} %shard_map.121.refs_0_), custom_call_target="tpu_custom_call" | custom-call | flops 999999995904 | bytes 1000000000 | tf_op jit(solution)/shard_map/pallas_call | solution.py:204
  111.1 2.2 copy-done.7
  113.3 4.1 %shard_map.123.refs_5_ = bf16[512,1024]{1,0:T(8,128)(2,1)} custom-call(s32[4]{0:T(128)S(1)} %fusion.8.refs_0_, bf16[1024,1024]{1,0:T(8,128)(2,1)S(1)} %copy-done.1, bf16[8192,1024]{1,0:T(8,128)(2,1)} %refs_2_.37, f32[8,128,1024]{2,1,0:T(8,128)S(1)} %copy-done.7), custom_call_target="tpu_custom_call" | custom-call | flops 999999995904 | bytes 1000000000 | tf_op jit(solution)/shard_map/pallas_call | solution.py:84
  117.4 1.7 collective-permute-start.13
  119.2 4.5 %shard_map.124.refs_5_ = bf16[512,1024]{1,0:T(8,128)(2,1)} custom-call(s32[4]{0:T(128)S(1)} %fusion.6.refs_0_, bf16[1024,1024]{1,0:T(8,128)(2,1)S(1)} %copy-done.1, bf16[8192,1024]{1,0:T(8,128)(2,1)} %refs_2_.37, bf16[512,1024]{1,0:T(8,128)(2,1)} %collective-permute-done.6.refs_3_, bf16[512,1024]{1,0:T(8,128)(2,1)} %collective-permute-done.7.refs_4_, ...), custom_call_target="tpu_custom_call" | custom-call | flops 999999995904 | bytes 1000000000 | tf_op jit(solution)/shard_map/pallas_call | solution.py:84
  123.6 2.8 %collective-permute-done.4.refs_3_ = bf16[512,1024]{1,0:T(8,128)(2,1)} collective-permute-done((bf16[512,1024]{1,0:T(8,128)(2,1)}, bf16[512,1024]{1,0:T(8,128)(2,1)}, u32[]{:S(2)}, u32[]{:S(2)}) %collective-permute-start.4) | collective-permute-done | bytes 1048608 | tf_op jit(solution)/shard_map/ppermute | solution.py:254
  126.5 4.1 %collective-permute-start.15 = (bf16[512,1024]{1,0:T(8,128)(2,1)}, bf16[512,1024]{1,0:T(8,128)(2,1)}, u32[]{:S(2)}, u32[]{:S(2)}) collective-permute-start(bf16[512,1024]{1,0:T(8,128)(2,1)} %shard_map.124.refs_5_), channel_id=1, source_target_pairs={{2,4},{3,5},{4,2},{5,3},{0,0},{1,1},{6,6},{7,7},{10,12},{11,13},{1... | collective-permute-start | bytes 3145736 | tf_op jit(solution)/shard_map/ppermute | solution.py:257
  130.6 4.5 %shard_map.125.link = bf16[512,1024]{1,0:T(8,128)(2,1)} custom-call(s32[4]{0:T(128)S(1)} %fusion.16.refs_0_, bf16[1024,1024]{1,0:T(8,128)(2,1)S(1)} %copy-done.1, bf16[8192,1024]{1,0:T(8,128)(2,1)} %refs_2_.37, bf16[512,1024]{1,0:T(8,128)(2,1)} %collective-permute-done.4.refs_3_, bf16[512,1024]{1,0:T(8,128)(2,1)} %collective-permute-done.5.refs_4_, ...), custom_call_target="tpu_custom_call" | custom-call | flops 999999995904 | bytes 1000000000 | tf_op jit(solution)/shard_map/pallas_call | solution.py:84
  135.1 5.6 %collective-permute-start.10 = (bf16[512,1024]{1,0:T(8,128)(2,1)}, bf16[512,1024]{1,0:T(8,128)(2,1)}, u32[]{:S(2)}, u32[]{:S(2)}) collective-permute-start(bf16[512,1024]{1,0:T(8,128)(2,1)} %shard_map.125.link), channel_id=1, source_target_pairs={{0,2},{1,3},{6,4},{7,5},{2,0},{3,1},{4,6},{5,7},{8,10},{9,11},{14,... | collective-permute-start | bytes 3145736 | tf_op jit(solution)/shard_map/ppermute | solution.py:257
  142.2 4.1 %shard_map.127.refs_5_ = bf16[512,1024]{1,0:T(8,128)(2,1)} custom-call(s32[4]{0:T(128)S(1)} %fusion.10.refs_0_, bf16[1024,1024]{1,0:T(8,128)(2,1)S(1)} %copy-done.1, bf16[8192,1024]{1,0:T(8,128)(2,1)} %refs_2_.37, bf16[1024,128]{1,0:T(8,128)(2,1)S(1)} %shard_map.126.refs_3_.refs_5_.refs_4_), custom_call_target="tpu_custom_call" | custom-call | flops 999999995904 | bytes 1000000000 | tf_op jit(solution)/shard_map/pallas_call | solution.py:84
  146.8 4.5 %shard_map.128.refs_6_ = bf16[512,1024]{1,0:T(8,128)(2,1)} custom-call(s32[4]{0:T(128)S(1)} %fusion.28.refs_0_, bf16[1024,1024]{1,0:T(8,128)(2,1)S(1)} %copy-done.1, bf16[8192,1024]{1,0:T(8,128)(2,1)} %refs_2_.37, bf16[512,1024]{1,0:T(8,128)(2,1)} %collective-permute-done.4.refs_3_, bf16[512,1024]{1,0:T(8,128)(2,1)} %collective-permute-done.11.refs_4_, ...), custom_call_target="tpu_custom_call" | custom-call | flops 999999995904 | bytes 1000000000 | tf_op jit(solution)/shard_map/pallas_call | solution.py:84
  151.4 2.2 all_gather.15.right
  153.5 4.7 %collective-permute-start.12 = (bf16[512,1024]{1,0:T(8,128)(2,1)}, bf16[512,1024]{1,0:T(8,128)(2,1)}, u32[]{:S(2)}, u32[]{:S(2)}) collective-permute-start(bf16[512,1024]{1,0:T(8,128)(2,1)} %shard_map.128.refs_6_), channel_id=1, source_target_pairs={{2,4},{3,5},{4,2},{5,3},{0,0},{1,1},{6,6},{7,7},{10,12},{11,13},{1... | collective-permute-start | bytes 3145736 | tf_op jit(solution)/shard_map/ppermute | solution.py:257
  158.2 4.8 %shard_map.129.refs_4_ = bf16[512,1024]{1,0:T(8,128)(2,1)} custom-call(s32[4]{0:T(128)S(1)} %fusion.14.refs_0_, bf16[1024,1024]{1,0:T(8,128)(2,1)S(1)} %copy-done.1, bf16[8192,1024]{1,0:T(8,128)(2,1)} %refs_2_.37, bf16[512,1024]{1,0:T(8,128)(2,1)} %collective-permute-done.13.refs_3_, bf16[512,1024]{1,0:T(8,128)(2,1)} %collective-permute-done.2.refs_3_.refs_4_, ...), custom_call_target="tpu_custom_call" | custom-call | flops 999999995904 | bytes 1000000000 | tf_op jit(solution)/shard_map/pallas_call | solution.py:84
  163.0 4.8 %collective-permute-start.18 = (bf16[512,1024]{1,0:T(8,128)(2,1)}, bf16[512,1024]{1,0:T(8,128)(2,1)}, u32[]{:S(2)}, u32[]{:S(2)}) collective-permute-start(bf16[512,1024]{1,0:T(8,128)(2,1)} %shard_map.129.refs_4_), channel_id=1, source_target_pairs={{0,2},{1,3},{6,4},{7,5},{2,0},{3,1},{4,6},{5,7},{8,10},{9,11},{14,... | collective-permute-start | bytes 3145736 | tf_op jit(solution)/shard_map/ppermute | solution.py:257
  167.8 4.2 %shard_map.130.refs_5_ = bf16[512,1024]{1,0:T(8,128)(2,1)} custom-call(s32[4]{0:T(128)S(1)} %fusion.30.refs_0_, bf16[1024,1024]{1,0:T(8,128)(2,1)S(1)} %copy-done.1, bf16[8192,1024]{1,0:T(8,128)(2,1)} %refs_2_.37, bf16[512,1024]{1,0:T(8,128)(2,1)} %collective-permute-done.14.refs_3_.refs_4_, bf16[512,1024]{1,0:T(8,128)(2,1)} %shard_map.129.refs_4_), custom_call_target="tpu_custom_call" | custom-call | flops 999999995904 | bytes 1000000000 | tf_op jit(solution)/shard_map/pallas_call | solution.py:84
  173.6 4.8 %shard_map.131.refs_10_ = bf16[512,1024]{1,0:T(8,128)(2,1)} custom-call(s32[4]{0:T(128)S(1)} %fusion.12.refs_0_, bf16[1024,1024]{1,0:T(8,128)(2,1)S(1)} %copy-done.1, bf16[8192,1024]{1,0:T(8,128)(2,1)} %refs_2_.37, bf16[512,1024]{1,0:T(8,128)(2,1)} %collective-permute-done.13.refs_3_, bf16[512,1024]{1,0:T(8,128)(2,1)} %collective-permute-done.14.refs_3_.refs_4_, ...), custom_call_target="tpu_custom_call" | custom-call | flops 999999995904 | bytes 1000000000 | tf_op jit(solution)/shard_map/pallas_call | solution.py:84
  178.3 3.6 %collective-permute-done.12.refs_4_ = bf16[512,1024]{1,0:T(8,128)(2,1)} collective-permute-done((bf16[512,1024]{1,0:T(8,128)(2,1)}, bf16[512,1024]{1,0:T(8,128)(2,1)}, u32[]{:S(2)}, u32[]{:S(2)}) %collective-permute-start.12) | collective-permute-done | bytes 1048608 | tf_op jit(solution)/shard_map/ppermute | solution.py:257
  182.0 3.6 %collective-permute-start.19 = (bf16[512,1024]{1,0:T(8,128)(2,1)}, bf16[512,1024]{1,0:T(8,128)(2,1)}, u32[]{:S(2)}, u32[]{:S(2)}) collective-permute-start(bf16[512,1024]{1,0:T(8,128)(2,1)} %shard_map.131.refs_10_), channel_id=1, source_target_pairs={{2,4},{3,5},{4,2},{5,3},{10,12},{11,13},{12,10},{13,11},{18,20},{1... | collective-permute-start | bytes 3145736 | tf_op jit(solution)/shard_map/ppermute | solution.py:257
  185.6 4.0 %shard_map.132.refs_9_.refs_0_ = bf16[512,1024]{1,0:T(8,128)(2,1)S(1)} custom-call(s32[8]{0:T(128)S(1)} %stack.159.refs_0_, bf16[1024,1024]{1,0:T(8,128)(2,1)S(1)} %copy-done.1, bf16[8192,1024]{1,0:T(8,128)(2,1)} %refs_2_.37, bf16[512,1024]{1,0:T(8,128)(2,1)} %collective-permute-done.10.refs_3_, bf16[512,1024]{1,0:T(8,128)(2,1)} %collective-permute-done.12.refs_4_, ...), custom_call_target="tpu_custom_call" | custom-call | flops 999999995904 | bytes 1000000000 | tf_op jit(solution)/shard_map/pallas_call | solution.py:84
  189.6 3.8 %shard_map.133.refs_0_.refs_2_ = bf16[512,1024]{1,0:T(8,128)(2,1)S(1)} custom-call(s32[8]{0:T(128)S(1)} %stack.190.refs_0_, bf16[1024,1024]{1,0:T(8,128)(2,1)S(1)} %copy-done.1, bf16[8192,1024]{1,0:T(8,128)(2,1)} %refs_2_.37, bf16[512,1024]{1,0:T(8,128)(2,1)} %collective-permute-done.17.refs_3_, bf16[1024,128]{1,0:T(8,128)(2,1)S(1)} %shard_map.126.refs_3_.refs_5_.refs_4_, ...), custom_call_target="tpu_custom_call" | custom-call | flops 999999995904 | bytes 1000000000 | tf_op jit(solution)/shard_map/pallas_call | solution.py:84
  195.4 2.2 copy-done.5
  198.8 4.7 %shard_map.134.refs_5_ = f32[8,1024,128]{2,1,0:T(8,128)} custom-call(s32[16]{0:T(128)S(1)} %get-tuple-element.4.slots, f32[16]{0:T(128)S(1)} %broadcast_4_scales.2.scales, bf16[2048,1024]{1,0:T(8,128)(2,1)S(1)} %copy-done.5, bf16[2048,128]{1,0:T(8,128)(2,1)S(1)} %all_gather.15.right, bf16[512,1024]{1,0:T(8,128)(2,1)S(1)} %copy-done.14), custom_call_target="tpu_custom_call" | custom-call | flops 999999995904 | bytes 1000000000 | tf_op jit(solution)/shard_map/pallas_call | solution.py:204
  203.5 5.4 %collective-permute-done.19.refs_4_ = bf16[512,1024]{1,0:T(8,128)(2,1)} collective-permute-done((bf16[512,1024]{1,0:T(8,128)(2,1)}, bf16[512,1024]{1,0:T(8,128)(2,1)}, u32[]{:S(2)}, u32[]{:S(2)}) %collective-permute-start.19) | collective-permute-done | bytes 1048608 | tf_op jit(solution)/shard_map/ppermute | solution.py:257
  208.9 2.2 copy-done.8
  211.1 4.7 %shard_map.135 = bf16[1024,1024]{1,0:T(8,128)(2,1)} custom-call(bf16[512,1024]{1,0:T(8,128)(2,1)S(1)} %copy-done.12, bf16[512,1024]{1,0:T(8,128)(2,1)} %collective-permute-done.16.refs_1_, bf16[512,1024]{1,0:T(8,128)(2,1)S(1)} %copy-done.14, bf16[512,1024]{1,0:T(8,128)(2,1)} %collective-permute-done.18.refs_3_, ...), custom_call_target="tpu_custom_call" | custom-call | flops 999999995904 | bytes 1000000000 | tf_op jit(solution)/shard_map/pallas_call | solution.py:128
  (96 shorter events, 13.9 us)
Async XLA Ops:
  8.0 96.3 %all-gather.3.cloned.1.call-start = ((), (), s32[]{:S(2)}) async-start(), calls=%async_computation | async-start | bytes 6291456 | tf_op jit(solution)/shard_map/all_gather | solution.py:276
  8.9 1.6 copy-start
  10.4 5.8 %copy-start.1 = (bf16[1024,1024]{1,0:T(8,128)(2,1)S(1)}, bf16[1024,1024]{1,0:T(8,128)(2,1)}, u32[]{:S(2)}) copy-start(bf16[1024,1024]{1,0:T(8,128)(2,1)} %refs_1_.37) | copy-start | bytes 6291460
  14.6 38.5 %collective-permute-start.2 = (bf16[512,1024]{1,0:T(8,128)(2,1)}, bf16[512,1024]{1,0:T(8,128)(2,1)}, u32[]{:S(2)}, u32[]{:S(2)}) collective-permute-start(bf16[512,1024]{1,0:T(8,128)(2,1)} %shard_map.112.refs_3_), channel_id=1, source_target_pairs={{0,1},{1,0},{2,3},{3,2},{4,5},{5,4},{6,7},{7,6},{8,9},{9,8},{10,11... | collective-permute-start | bytes 3145736 | tf_op jit(solution)/shard_map/ppermute | solution.py:254
  20.4 32.6 %collective-permute-start.3 = (bf16[512,1024]{1,0:T(8,128)(2,1)}, bf16[512,1024]{1,0:T(8,128)(2,1)}, u32[]{:S(2)}, u32[]{:S(2)}) collective-permute-start(bf16[512,1024]{1,0:T(8,128)(2,1)} %shard_map.113.link), channel_id=1, source_target_pairs={{0,2},{1,3},{6,4},{7,5},{2,0},{3,1},{4,6},{5,7},{8,10},{9,11},{14,... | collective-permute-start | bytes 3145736 | tf_op jit(solution)/shard_map/ppermute | solution.py:257
  20.9 30.5 %collective-permute-start.8 = (s32[8]{0:T(128)}, s32[8]{0:T(128)}, u32[]{:S(2)}, u32[]{:S(2)}) collective-permute-start(s32[8]{0:T(128)} %tenants.1), channel_id=1, source_target_pairs={{0,8},{8,0},{1,9},{9,1},{2,10},{10,2},{3,11},{11,3},{4,12},{12,4},... | collective-permute-start | bytes 104 | tf_op jit(solution)/shard_map/ppermute | solution.py:281
  20.9 2.9 %copy-start.2 = (bf16[16,128,1024]{2,1,0:T(8,128)(2,1)S(1)}, bf16[16,128,1024]{2,1,0:T(8,128)(2,1)}, u32[]{:S(2)}) copy-start(bf16[16,128,1024]{2,1,0:T(8,128)(2,1)} %expand.1) | copy-start | bytes 12582916
  32.2 108.4 %all-reduce.2.cloned.1.call-start = ((), (), s32[]{:S(2)}) async-start(), calls=%async_computation.1 | async-start | bytes 524288 | tf_op jit(solution)/shard_map/psum | solution.py:300
  32.2 43.0 %collective-permute-start = (bf16[512,1024]{1,0:T(8,128)(2,1)}, bf16[512,1024]{1,0:T(8,128)(2,1)}, u32[]{:S(2)}, u32[]{:S(2)}) collective-permute-start(bf16[512,1024]{1,0:T(8,128)(2,1)} %shard_map.115.refs_3_), channel_id=1, source_target_pairs={{0,1},{1,0},{6,7},{7,6},{2,2},{3,3},{4,4},{5,5},{8,9},{9,8},{14,15... | collective-permute-start | bytes 3145736 | tf_op jit(solution)/shard_map/ppermute | solution.py:254
  41.7 153.7 %all-gather.5.cloned.1.call-start = ((), (), s32[]{:S(2)}) async-start(), calls=%async_computation.2 | async-start | bytes 6291456 | tf_op jit(solution)/shard_map/all_gather | solution.py:276
  41.9 5.8 %copy-start.17 = (s32[16]{0:T(128)S(1)}, s32[16]{0:T(128)}, u32[]{:S(2)}) copy-start(s32[16]{0:T(128)} %param.17) | copy-start | bytes 196
  41.9 7.2 %copy-start.15 = (bf16[1024,128]{1,0:T(8,128)(2,1)S(1)}, bf16[1024,128]{1,0:T(8,128)(2,1)}, u32[]{:S(2)}) copy-start(bf16[1024,128]{1,0:T(8,128)(2,1)} %param.11) | copy-start | bytes 786436
  41.9 10.3 %copy-start.16 = (s32[16]{0:T(128)S(1)}, s32[16]{0:T(128)}, u32[]{:S(2)}) copy-start(s32[16]{0:T(128)} %param.16) | copy-start | bytes 196
  46.0 29.3 %collective-permute-start.1 = (bf16[512,1024]{1,0:T(8,128)(2,1)}, bf16[512,1024]{1,0:T(8,128)(2,1)}, u32[]{:S(2)}, u32[]{:S(2)}) collective-permute-start(bf16[512,1024]{1,0:T(8,128)(2,1)} %shard_map.116.refs_5_), channel_id=1, source_target_pairs={{0,2},{1,3},{6,4},{7,5},{2,0},{3,1},{4,6},{5,7},{8,10},{9,11},{14,... | collective-permute-start | bytes 3145736 | tf_op jit(solution)/shard_map/ppermute | solution.py:257
  52.4 0.5 copy-start.9
  57.9 41.6 %collective-permute-start.9 = (bf16[512,1024]{1,0:T(8,128)(2,1)}, bf16[512,1024]{1,0:T(8,128)(2,1)}, u32[]{:S(2)}, u32[]{:S(2)}) collective-permute-start(bf16[512,1024]{1,0:T(8,128)(2,1)} %shard_map.117.refs_3_), channel_id=1, source_target_pairs={{2,4},{3,5},{4,2},{5,3},{0,0},{1,1},{6,6},{7,7},{10,12},{11,13},{1... | collective-permute-start | bytes 3145736 | tf_op jit(solution)/shard_map/ppermute | solution.py:257
  62.2 55.3 %collective-permute-start.7 = (bf16[512,1024]{1,0:T(8,128)(2,1)}, bf16[512,1024]{1,0:T(8,128)(2,1)}, u32[]{:S(2)}, u32[]{:S(2)}) collective-permute-start(bf16[512,1024]{1,0:T(8,128)(2,1)} %shard_map.117.refs_3_), channel_id=1, source_target_pairs={{0,2},{1,3},{6,4},{7,5},{2,0},{3,1},{4,6},{5,7},{8,10},{9,11},{14,... | collective-permute-start | bytes 3145736 | tf_op jit(solution)/shard_map/ppermute | solution.py:257
  73.5 25.8 %collective-permute-start.6 = (bf16[512,1024]{1,0:T(8,128)(2,1)}, bf16[512,1024]{1,0:T(8,128)(2,1)}, u32[]{:S(2)}, u32[]{:S(2)}) collective-permute-start(bf16[512,1024]{1,0:T(8,128)(2,1)} %shard_map.118.refs_5_), channel_id=1, source_target_pairs={{0,1},{1,0},{2,3},{3,2},{4,5},{5,4},{6,7},{7,6},{8,9},{9,8},{10,11... | collective-permute-start | bytes 3145736 | tf_op jit(solution)/shard_map/ppermute | solution.py:254
  79.7 50.9 %collective-permute-start.5 = (bf16[512,1024]{1,0:T(8,128)(2,1)}, bf16[512,1024]{1,0:T(8,128)(2,1)}, u32[]{:S(2)}, u32[]{:S(2)}) collective-permute-start(bf16[512,1024]{1,0:T(8,128)(2,1)} %shard_map.119.refs_3_), channel_id=1, source_target_pairs={{2,4},{3,5},{4,2},{5,3},{0,0},{1,1},{6,6},{7,7},{10,12},{11,13},{1... | collective-permute-start | bytes 3145736 | tf_op jit(solution)/shard_map/ppermute | solution.py:257
  84.0 62.3 %collective-permute-start.11 = (bf16[512,1024]{1,0:T(8,128)(2,1)}, bf16[512,1024]{1,0:T(8,128)(2,1)}, u32[]{:S(2)}, u32[]{:S(2)}) collective-permute-start(bf16[512,1024]{1,0:T(8,128)(2,1)} %shard_map.119.refs_3_), channel_id=1, source_target_pairs={{0,2},{1,3},{6,4},{7,5},{2,0},{3,1},{4,6},{5,7},{8,10},{9,11},{14,... | collective-permute-start | bytes 3145736 | tf_op jit(solution)/shard_map/ppermute | solution.py:257
  99.2 27.2 %collective-permute-start.4 = (bf16[512,1024]{1,0:T(8,128)(2,1)}, bf16[512,1024]{1,0:T(8,128)(2,1)}, u32[]{:S(2)}, u32[]{:S(2)}) collective-permute-start(bf16[512,1024]{1,0:T(8,128)(2,1)} %shard_map.120.refs_5_), channel_id=1, source_target_pairs={{0,1},{1,0},{2,3},{3,2},{4,5},{5,4},{6,7},{7,6},{8,9},{9,8},{10,11... | collective-permute-start | bytes 3145736 | tf_op jit(solution)/shard_map/ppermute | solution.py:254
  99.5 4.7 %copy-start.10 = (f32[16]{0:T(128)S(1)}, f32[16]{0:T(128)}, u32[]{:S(2)}) copy-start(f32[16]{0:T(128)} %copy-done.9) | copy-start | bytes 196
  104.0 63.8 %collective-permute-start.14 = (bf16[512,1024]{1,0:T(8,128)(2,1)}, bf16[512,1024]{1,0:T(8,128)(2,1)}, u32[]{:S(2)}, u32[]{:S(2)}) collective-permute-start(bf16[512,1024]{1,0:T(8,128)(2,1)} %shard_map.121.refs_0_), channel_id=1, source_target_pairs={{0,2},{1,3},{6,4},{7,5},{2,0},{3,1},{4,6},{5,7},{8,10},{9,11},{14,... | collective-permute-start | bytes 3145736 | tf_op jit(solution)/shard_map/ppermute | solution.py:257
  104.3 2.2 copy-start.4
  111.1 2.2 copy-start.7
  117.4 40.8 %collective-permute-start.13 = (bf16[512,1024]{1,0:T(8,128)(2,1)}, bf16[512,1024]{1,0:T(8,128)(2,1)}, u32[]{:S(2)}, u32[]{:S(2)}) collective-permute-start(bf16[512,1024]{1,0:T(8,128)(2,1)} %shard_map.123.refs_5_), channel_id=1, source_target_pairs={{0,1},{1,0},{2,3},{3,2},{4,5},{5,4},{6,7},{7,6},{8,9},{9,8},{10,11... | collective-permute-start | bytes 3145736 | tf_op jit(solution)/shard_map/ppermute | solution.py:254
  126.5 27.1 %collective-permute-start.15 = (bf16[512,1024]{1,0:T(8,128)(2,1)}, bf16[512,1024]{1,0:T(8,128)(2,1)}, u32[]{:S(2)}, u32[]{:S(2)}) collective-permute-start(bf16[512,1024]{1,0:T(8,128)(2,1)} %shard_map.124.refs_5_), channel_id=1, source_target_pairs={{2,4},{3,5},{4,2},{5,3},{0,0},{1,1},{6,6},{7,7},{10,12},{11,13},{1... | collective-permute-start | bytes 3145736 | tf_op jit(solution)/shard_map/ppermute | solution.py:257
  135.1 50.5 %collective-permute-start.10 = (bf16[512,1024]{1,0:T(8,128)(2,1)}, bf16[512,1024]{1,0:T(8,128)(2,1)}, u32[]{:S(2)}, u32[]{:S(2)}) collective-permute-start(bf16[512,1024]{1,0:T(8,128)(2,1)} %shard_map.125.link), channel_id=1, source_target_pairs={{0,2},{1,3},{6,4},{7,5},{2,0},{3,1},{4,6},{5,7},{8,10},{9,11},{14,... | collective-permute-start | bytes 3145736 | tf_op jit(solution)/shard_map/ppermute | solution.py:257
  140.7 1.0 copy-start.6
  146.3 43.3 %collective-permute-start.17 = (bf16[512,1024]{1,0:T(8,128)(2,1)}, bf16[512,1024]{1,0:T(8,128)(2,1)}, u32[]{:S(2)}, u32[]{:S(2)}) collective-permute-start(bf16[512,1024]{1,0:T(8,128)(2,1)} %shard_map.127.refs_5_), channel_id=1, source_target_pairs={{0,1},{1,0},{2,3},{3,2},{4,5},{5,4},{6,7},{7,6},{8,9},{9,8},{10,11... | collective-permute-start | bytes 3145736 | tf_op jit(solution)/shard_map/ppermute | solution.py:254
  153.5 28.4 %collective-permute-start.12 = (bf16[512,1024]{1,0:T(8,128)(2,1)}, bf16[512,1024]{1,0:T(8,128)(2,1)}, u32[]{:S(2)}, u32[]{:S(2)}) collective-permute-start(bf16[512,1024]{1,0:T(8,128)(2,1)} %shard_map.128.refs_6_), channel_id=1, source_target_pairs={{2,4},{3,5},{4,2},{5,3},{0,0},{1,1},{6,6},{7,7},{10,12},{11,13},{1... | collective-permute-start | bytes 3145736 | tf_op jit(solution)/shard_map/ppermute | solution.py:257
  163.0 45.8 %collective-permute-start.18 = (bf16[512,1024]{1,0:T(8,128)(2,1)}, bf16[512,1024]{1,0:T(8,128)(2,1)}, u32[]{:S(2)}, u32[]{:S(2)}) collective-permute-start(bf16[512,1024]{1,0:T(8,128)(2,1)} %shard_map.129.refs_4_), channel_id=1, source_target_pairs={{0,2},{1,3},{6,4},{7,5},{2,0},{3,1},{4,6},{5,7},{8,10},{9,11},{14,... | collective-permute-start | bytes 3145736 | tf_op jit(solution)/shard_map/ppermute | solution.py:257
  172.0 36.8 %collective-permute-start.16 = (bf16[512,1024]{1,0:T(8,128)(2,1)}, bf16[512,1024]{1,0:T(8,128)(2,1)}, u32[]{:S(2)}, u32[]{:S(2)}) collective-permute-start(bf16[512,1024]{1,0:T(8,128)(2,1)} %shard_map.130.refs_5_), channel_id=1, source_target_pairs={{0,1},{1,0},{2,3},{3,2},{4,5},{5,4},{6,7},{7,6},{8,9},{9,8},{10,11... | collective-permute-start | bytes 3145736 | tf_op jit(solution)/shard_map/ppermute | solution.py:254
  173.6 12.1 %copy-start.3 = (bf16[16,1024,128]{2,1,0:T(8,128)(2,1)S(1)}, bf16[16,1024,128]{2,1,0:T(8,128)(2,1)}, u32[]{:S(2)}) copy-start(bf16[16,1024,128]{2,1,0:T(8,128)(2,1)} %refs_8_.3) | copy-start | bytes 12582916
  182.0 26.9 %collective-permute-start.19 = (bf16[512,1024]{1,0:T(8,128)(2,1)}, bf16[512,1024]{1,0:T(8,128)(2,1)}, u32[]{:S(2)}, u32[]{:S(2)}) collective-permute-start(bf16[512,1024]{1,0:T(8,128)(2,1)} %shard_map.131.refs_10_), channel_id=1, source_target_pairs={{2,4},{3,5},{4,2},{5,3},{10,12},{11,13},{12,10},{13,11},{18,20},{1... | collective-permute-start | bytes 3145736 | tf_op jit(solution)/shard_map/ppermute | solution.py:257
  193.4 1.0 copy-start.11
  194.4 1.0 copy-start.13
  195.4 2.2 copy-start.5
  197.6 1.2 copy-start.14
  198.8 10.1 %copy-start.12 = (bf16[512,1024]{1,0:T(8,128)(2,1)S(1)}, bf16[512,1024]{1,0:T(8,128)(2,1)}, u32[]{:S(2)}) copy-start(bf16[512,1024]{1,0:T(8,128)(2,1)} %copy-done.11) | copy-start | bytes 3145732
  208.9 2.2 copy-start.8
Sparse Core Ops, SparseCore 0:
  10.4 15.0 all-gather.2
  46.1 15.5 all-gather.4
Sparse Core Ops, SparseCore 1:
  41.8 72.4 all-reduce.1

commit v7 on v6

--- a/solution.py
+++ b/solution.py
@@ -250,7 +250,6 @@
         pairs = []
         for z in active:
             pairs += [(2 * z, 2 * z + 1), (2 * z + 1, 2 * z)]
-        pairs += [(2 * z + y, 2 * z + y) for z in every if z not in active for y in range(2)]
         return lax.ppermute(x, "tensor", pairs)
 
     def along(x, hops):
@@ -259,12 +258,19 @@
         )
 
     nodes = 4
-    ends, inner, every = (0, 3), (1, 2), (0, 1, 2, 3)
+    every = (0, 1, 2, 3)
     from_ends = [(0, 1), (3, 2)]
-    across_only = [(1, 2), (2, 1)]
+    across = [(1, 2), (2, 1)]
     to_ends = [(1, 0), (2, 3)]
     pairwise = from_ends + to_ends
-    across = across_only + [(0, 0), (3, 3)]
+    def exchange(x):
+        pairs = []
+        for group in range(2):
+            for y in range(2):
+                pairs += [(group * 8 + 2 * a + y, group * 8 + 2 * b + y) for a, b in across]
+                pairs += [(group * 8 + 2 * z + y, (1 - group) * 8 + 2 * z + y) for z in (0, 3)]
+        return lax.ppermute(x, ("groups", "tensor"), pairs)
+
     first_half = node < 2
     far = jnp.where(first_half, 3, 0)
     beyond = jnp.where(first_half, 2, 1)
@@ -325,7 +331,7 @@
     y1 = swap(run(jnp.where(at_end, far, near_end), other, upper, []), every)
     direct_a = along(run(far, other, lower, []), pairwise)
     low_whole = adapter_space()
-    y2 = swap(run(beyond, other, lower, []), ends)
+    y2 = swap(run(beyond, other, lower, []), every)
     direct_b = along(run(far, same, lower, []), pairwise)
     out = run(
         far,
@@ -333,10 +339,10 @@
         jnp.where(at_end, upper, lower),
         [(y1, 1), (direct_a, 2)],
     )
-    upper_1, direct_a = along(out, pairwise), along(out, across)
+    upper_1, direct_a = along(out, pairwise), exchange(out)
     y3 = swap(run(jnp.where(at_end, beyond, far), other, upper, []), every)
     out = run(jnp.where(at_end, beyond, far), same, lower, [(y2, 1), (direct_b, 2)])
-    lower_2, direct_b = along(out, pairwise), along(out, across)
+    lower_2, direct_b = along(out, pairwise), exchange(out)
     y4 = swap(run(jnp.where(at_end, nearer, beyond), other, lower, []), every)
     out = run(
         jnp.where(at_end, beyond, near_end),
@@ -347,18 +353,18 @@
     both_3 = along(out, pairwise)
     grad_expand = expand_gradient()
     y5 = swap(run(jnp.where(at_end, nearer, beyond), other, upper, []), every)
-    upper_far = along(run(far, same, upper, [(y3, 0), (upper_1, 0)]), across)
+    upper_far = exchange(run(far, same, upper, [(y3, 0), (upper_1, 0)]))
     out = run(jnp.where(at_end, nearer, near_end), same, lower, [(y4, 1), (direct_b, 2)])
     both_4 = along(out, pairwise)
     low = scale_low(low_whole)
     y6 = swap(run(node, other, upper, []), every)
-    lower_4 = along(run(beyond, same, lower, [(y4, 0), (lower_2, 0)]), across)
+    lower_4 = exchange(run(beyond, same, lower, [(y4, 0), (lower_2, 0)]))
     out = run(
         jnp.where(at_end, nearer, near_end), same, upper, [(y5, 1), (y1, 2), (upper_far, 2)]
     )
     both_5 = along(out, pairwise)
     y7 = swap(run(node, other, lower, [(both_3, 1)]), every)
-    upper_4 = along(run(beyond, same, upper, [(y5, 0), (both_3, 0)]), across_only)
+    upper_4 = along(run(beyond, same, upper, [(y5, 0), (both_3, 0)]), across)
     def base(piece, adds):
         in_piece = piece_rows // row_block
         scalars = [node * 2 + side, jnp.int32(piece)] + [jnp.asarray(r, jnp.int32) for r in roles]
@@ -473,7 +479,7 @@
         P(),
     )
     body = per_device_any
-    if mesh.shape["tensor"] == 8:
+    if mesh.shape["tensor"] == 8 and mesh.shape["groups"] == 2:
         body = functools.partial(per_device, mesh.shape["dp"])
     return jax.shard_map(
         body,

time: 226 us -> 204 us (0.903)
  starting transfers between devices: 60.9 us -> 17.6 us
  waiting for transfers between devices: 18.9 us -> 38 us
  Pallas kernels: 101 us -> 104 us
    ppermute x12 -> x8, starting transfers between devices: 45.6 us -> 5.96 us  [along(): lax.ppermute(x, 'tensor', [(2 * a + y, 2 * b + y) for a, b in hops for y...]
    ppermute x12 -> x8, waiting for transfers between devices: 10.6 us -> 24.8 us  [along(): lax.ppermute(x, 'tensor', [(2 * a + y, 2 * b + y) for a, b in hops for y...]
    ppermute x7, starting transfers between devices: 15.2 us -> 5.96 us  [swap(): return lax.ppermute(x, 'tensor', pairs)]
    ppermute x0 -> x4, waiting for transfers between devices: none -> 7.54 us  [exchange(): return lax.ppermute(x, ('groups', 'tensor'), pairs)]
    ppermute x0 -> x4, starting transfers between devices: none -> 5.65 us  [exchange(): return lax.ppermute(x, ('groups', 'tensor'), pairs)]
    pallas_call x2, Pallas kernels: 9.38 us -> 12.5 us  [factor_sums(): pl.pallas_call(functools.partial(factor_kernel, slots_each), in_specs=[pl...]
    ppermute x7, waiting for transfers between devices: 7.54 us -> 4.63 us  [swap(): return lax.ppermute(x, 'tensor', pairs)]
  transfers between devices with their start and end apart: 23 -> 23, of which waited for: 5 -> 9; matrix products, arithmetic and copies ran while one was open for 2% -> 2% of each run, Pallas kernels for 43% -> 49%
where the time goes in v7:
time: 204 us; the launch traced here: 202 us
  Pallas kernels  104 us (51%)
  waiting for transfers between devices  38 us (19%)
  local copies, waits for them, and re-layouts  20.7 us (10%)
  starting transfers between devices  17.6 us (9%)
  between operations  15.7 us (8%)
  blocking collectives  4.35 us (2%)
    pallas_call x19, Pallas kernels, product(): pl.pallas_call(functools.partial(product_kernel, tuple((mode for _, mode...  81.9 us
    ppermute x8, waiting for transfers between devices, along(): lax.ppermute(x, 'tensor', [(2 * a + y, 2 * b + y) for a, b in hops for y...  24.8 us
    unnamed x36, local copies, waits for them, and re-layouts  17.9 us
    pallas_call x2, Pallas kernels, factor_sums(): pl.pallas_call(functools.partial(factor_kernel, slots_each), in_specs=[pl...  12.5 us
    ppermute x4, waiting for transfers between devices, exchange(): return lax.ppermute(x, ('groups', 'tensor'), pairs)  7.54 us
    ppermute x7, starting transfers between devices, swap(): return lax.ppermute(x, 'tensor', pairs)  5.96 us
    ppermute x8, starting transfers between devices, along(): lax.ppermute(x, 'tensor', [(2 * a + y, 2 * b + y) for a, b in hops for y...  5.96 us
    ppermute x4, starting transfers between devices, exchange(): return lax.ppermute(x, ('groups', 'tensor'), pairs)  5.65 us
  transfers between devices with their start and end apart: 23, of which 9 were waited for; matrix products, arithmetic and copies ran while one was open for 2% of the time, Pallas kernels for 49%

profile of v7, /device:TPU:10, one launch (start us, length us, event | category | flops | bytes accessed | tf_op | source)
XLA Modules:
  0.0 202.1 jit_solution(5203400041300873597)
XLA Ops:
  8.9 1.6 copy-done
  10.4 4.2 %shard_map.112.refs_3_ = bf16[512,1024]{1,0:T(8,128)(2,1)} custom-call(s32[4]{0:T(128)S(1)} %fusion.2.refs_0_, bf16[1024,1024]{1,0:T(8,128)(2,1)S(1)} %copy-done, bf16[8192,1024]{1,0:T(8,128)(2,1)} %refs_2_.37), custom_call_target="tpu_custom_call" | custom-call | flops 999999995904 | bytes 1000000000 | tf_op jit(solution)/shard_map/pallas_call | solution.py:84
  14.6 1.5 collective-permute-start.2
  16.2 4.2 %shard_map.113.link = bf16[512,1024]{1,0:T(8,128)(2,1)} custom-call(s32[4]{0:T(128)S(1)} %fusion.24.refs_0_, bf16[1024,1024]{1,0:T(8,128)(2,1)S(1)} %copy-done.1, bf16[8192,1024]{1,0:T(8,128)(2,1)} %refs_2_.37, bf16[512,1024]{1,0:T(8,128)(2,1)} %shard_map.112.refs_3_), custom_call_target="tpu_custom_call" | custom-call | flops 999999995904 | bytes 1000000000 | tf_op jit(solution)/shard_map/pallas_call | solution.py:84
  20.9 2.9 %copy-done.2 = bf16[16,128,1024]{2,1,0:T(8,128)(2,1)S(1)} copy-done((bf16[16,128,1024]{2,1,0:T(8,128)(2,1)S(1)}, bf16[16,128,1024]{2,1,0:T(8,128)(2,1)}, u32[]{:S(2)}) %copy-start.2) | copy-done | bytes 4194328
  23.8 4.3 %shard_map.114.refs_3_ = bf16[1024,128]{1,0:T(8,128)(2,1)} custom-call(s32[8]{0:T(128)} %tenants.1, bf16[1024,1024]{1,0:T(8,128)(2,1)S(1)} %copy-done.1, bf16[16,128,1024]{2,1,0:T(8,128)(2,1)S(1)} %copy-done.2, bf16[512,1024]{1,0:T(8,128)(2,1)} %shard_map.113.link), custom_call_target="tpu_custom_call" | custom-call | flops 999999995904 | bytes 1000000000 | tf_op jit(solution)/shard_map/pallas_call | solution.py:148
  28.2 4.1 %shard_map.115.refs_3_ = bf16[512,1024]{1,0:T(8,128)(2,1)} custom-call(s32[4]{0:T(128)S(1)} %fusion.22.refs_0_, bf16[1024,1024]{1,0:T(8,128)(2,1)S(1)} %copy-done.1, bf16[8192,1024]{1,0:T(8,128)(2,1)} %refs_2_.37, bf16[1024,128]{1,0:T(8,128)(2,1)} %shard_map.114.refs_3_), custom_call_target="tpu_custom_call" | custom-call | flops 999999995904 | bytes 1000000000 | tf_op jit(solution)/shard_map/pallas_call | solution.py:84
  32.9 4.1 %shard_map.116.refs_5_ = bf16[512,1024]{1,0:T(8,128)(2,1)} custom-call(s32[4]{0:T(128)S(1)} %fusion.26.refs_0_, bf16[1024,1024]{1,0:T(8,128)(2,1)S(1)} %copy-done.1, bf16[8192,1024]{1,0:T(8,128)(2,1)} %refs_2_.37, bf16[512,1024]{1,0:T(8,128)(2,1)} %shard_map.115.refs_3_), custom_call_target="tpu_custom_call" | custom-call | flops 999999995904 | bytes 1000000000 | tf_op jit(solution)/shard_map/pallas_call | solution.py:84
  37.0 1.4 collective-permute-start.1
  41.5 2.2 %all_gather.12 = bf16[2048,128]{1,0:T(8,128)(2,1)S(1)} all-gather(bf16[1024,128]{1,0:T(8,128)(2,1)S(1)} %copy-done.15), channel_id=1, replica_groups=mesh['groups'=2,'dp'=2,'tensor'=8] {'dp'}, dimensions={0}, use_global_device_ids=true | all-gather | bytes 786432 | tf_op jit(solution)/shard_map/all_gather | solution.py:282
  45.5 2.9 %collective-permute-done.3.refs_4_ = bf16[512,1024]{1,0:T(8,128)(2,1)} collective-permute-done((bf16[512,1024]{1,0:T(8,128)(2,1)}, bf16[512,1024]{1,0:T(8,128)(2,1)}, u32[]{:S(2)}, u32[]{:S(2)}) %collective-permute-start.3) | collective-permute-done | bytes 1048608 | tf_op jit(solution)/shard_map/ppermute | solution.py:256
  48.3 5.0 %shard_map.117.refs_3_ = bf16[512,1024]{1,0:T(8,128)(2,1)} custom-call(s32[4]{0:T(128)S(1)} %add_add_fusion.refs_0_, bf16[1024,1024]{1,0:T(8,128)(2,1)S(1)} %copy-done.1, bf16[8192,1024]{1,0:T(8,128)(2,1)} %refs_2_.37, bf16[512,1024]{1,0:T(8,128)(2,1)} %collective-permute-done.2.refs_3_.refs_4_, bf16[512,1024]{1,0:T(8,128)(2,1)} %collective-permute-done.3.refs_4_, ...), custom_call_target="tpu_custom_call" | custom-call | flops 999999995904 | bytes 1000000000 | tf_op jit(solution)/shard_map/pallas_call | solution.py:84
  54.2 4.1 %shard_map.118.refs_5_ = bf16[512,1024]{1,0:T(8,128)(2,1)} custom-call(s32[4]{0:T(128)S(1)} %fusion.4.refs_0_, bf16[1024,1024]{1,0:T(8,128)(2,1)S(1)} %copy-done.1, bf16[8192,1024]{1,0:T(8,128)(2,1)} %refs_2_.37, bf16[512,1024]{1,0:T(8,128)(2,1)} %shard_map.117.refs_3_), custom_call_target="tpu_custom_call" | custom-call | flops 999999995904 | bytes 1000000000 | tf_op jit(solution)/shard_map/pallas_call | solution.py:84
  58.7 14.5 %collective-permute-done.1.refs_4_ = bf16[512,1024]{1,0:T(8,128)(2,1)} collective-permute-done((bf16[512,1024]{1,0:T(8,128)(2,1)}, bf16[512,1024]{1,0:T(8,128)(2,1)}, u32[]{:S(2)}, u32[]{:S(2)}) %collective-permute-start.1) | collective-permute-done | bytes 1048608 | tf_op jit(solution)/shard_map/ppermute | solution.py:256
  73.2 4.5 %shard_map.119.refs_3_ = bf16[512,1024]{1,0:T(8,128)(2,1)} custom-call(s32[4]{0:T(128)S(1)} %fusion.20.refs_0_, bf16[1024,1024]{1,0:T(8,128)(2,1)S(1)} %copy-done.1, bf16[8192,1024]{1,0:T(8,128)(2,1)} %refs_2_.37, bf16[512,1024]{1,0:T(8,128)(2,1)} %collective-permute-done.refs_3_, bf16[512,1024]{1,0:T(8,128)(2,1)} %collective-permute-done.1.refs_4_, ...), custom_call_target="tpu_custom_call" | custom-call | flops 999999995904 | bytes 1000000000 | tf_op jit(solution)/shard_map/pallas_call | solution.py:84
  77.7 1.6 collective-permute-start.5
  79.2 4.1 %shard_map.120.refs_5_ = bf16[512,1024]{1,0:T(8,128)(2,1)} custom-call(s32[4]{0:T(128)S(1)} %fusion.18.refs_0_, bf16[1024,1024]{1,0:T(8,128)(2,1)S(1)} %copy-done.1, bf16[8192,1024]{1,0:T(8,128)(2,1)} %refs_2_.37, bf16[512,1024]{1,0:T(8,128)(2,1)} %shard_map.119.refs_3_), custom_call_target="tpu_custom_call" | custom-call | flops 999999995904 | bytes 1000000000 | tf_op jit(solution)/shard_map/pallas_call | solution.py:84
  83.3 3.5 %collective-permute-done.6.refs_3_ = bf16[512,1024]{1,0:T(8,128)(2,1)} collective-permute-done((bf16[512,1024]{1,0:T(8,128)(2,1)}, bf16[512,1024]{1,0:T(8,128)(2,1)}, u32[]{:S(2)}, u32[]{:S(2)}) %collective-permute-start.6) | collective-permute-done | bytes 1048608 | tf_op jit(solution)/shard_map/ppermute | solution.py:253
  86.9 1.3 collective-permute-start.4
  88.2 4.4 %shard_map.121.refs_0_ = bf16[512,1024]{1,0:T(8,128)(2,1)} custom-call(s32[4]{0:T(128)S(1)} %add_add_fusion.1.refs_0_, bf16[1024,1024]{1,0:T(8,128)(2,1)S(1)} %copy-done.1, bf16[8192,1024]{1,0:T(8,128)(2,1)} %refs_2_.37, bf16[512,1024]{1,0:T(8,128)(2,1)} %collective-permute-done.6.refs_3_, bf16[512,1024]{1,0:T(8,128)(2,1)} %collective-permute-done.9.refs_4_, ...), custom_call_target="tpu_custom_call" | custom-call | flops 999999995904 | bytes 1000000000 | tf_op jit(solution)/shard_map/pallas_call | solution.py:84
  93.1 2.2 %copy-done.4 = bf16[2048,1024]{1,0:T(8,128)(2,1)S(1)} copy-done((bf16[2048,1024]{1,0:T(8,128)(2,1)S(1)}, bf16[2048,1024]{1,0:T(8,128)(2,1)}, u32[]{:S(2)}) %copy-start.4) | copy-done | bytes 4194328
  95.3 6.3 %shard_map.122.refs_3_ = f32[8,128,1024]{2,1,0:T(8,128)} custom-call(s32[16]{0:T(128)S(1)} %get-tuple-element.4.slots, f32[16]{0:T(128)S(1)} %copy-done.10, bf16[2048,128]{1,0:T(8,128)(2,1)S(1)} %bitcast_multiply_fusion.left, bf16[2048,1024]{1,0:T(8,128)(2,1)S(1)} %copy-done.4, bf16[512,1024]{1,0:T(8,128)(2,1)} %shard_map.121.refs_0_), custom_call_target="tpu_custom_call" | custom-call | flops 999999995904 | bytes 1000000000 | tf_op jit(solution)/shard_map/pallas_call | solution.py:204
  101.5 2.2 %copy-done.7 = f32[8,128,1024]{2,1,0:T(8,128)S(1)} copy-done((f32[8,128,1024]{2,1,0:T(8,128)S(1)}, f32[8,128,1024]{2,1,0:T(8,128)}, u32[]{:S(2)}) %copy-start.7) | copy-done | bytes 4194328
  103.7 4.1 %shard_map.123.refs_5_ = bf16[512,1024]{1,0:T(8,128)(2,1)} custom-call(s32[4]{0:T(128)S(1)} %fusion.8.refs_0_, bf16[1024,1024]{1,0:T(8,128)(2,1)S(1)} %copy-done.1, bf16[8192,1024]{1,0:T(8,128)(2,1)} %refs_2_.37, f32[8,128,1024]{2,1,0:T(8,128)S(1)} %copy-done.7), custom_call_target="tpu_custom_call" | custom-call | flops 999999995904 | bytes 1000000000 | tf_op jit(solution)/shard_map/pallas_call | solution.py:84
  108.6 4.4 %shard_map.124.refs_5_ = bf16[512,1024]{1,0:T(8,128)(2,1)} custom-call(s32[4]{0:T(128)S(1)} %fusion.6.refs_0_, bf16[1024,1024]{1,0:T(8,128)(2,1)S(1)} %copy-done.1, bf16[8192,1024]{1,0:T(8,128)(2,1)} %refs_2_.37, bf16[512,1024]{1,0:T(8,128)(2,1)} %collective-permute-done.6.refs_3_, bf16[512,1024]{1,0:T(8,128)(2,1)} %collective-permute-done.7.refs_4_, ...), custom_call_target="tpu_custom_call" | custom-call | flops 999999995904 | bytes 1000000000 | tf_op jit(solution)/shard_map/pallas_call | solution.py:84
  114.1 1.7 collective-permute-start.15
  115.8 4.5 %shard_map.125.link = bf16[512,1024]{1,0:T(8,128)(2,1)} custom-call(s32[4]{0:T(128)S(1)} %fusion.16.refs_0_, bf16[1024,1024]{1,0:T(8,128)(2,1)S(1)} %copy-done.1, bf16[8192,1024]{1,0:T(8,128)(2,1)} %refs_2_.37, bf16[512,1024]{1,0:T(8,128)(2,1)} %collective-permute-done.4.refs_3_, bf16[512,1024]{1,0:T(8,128)(2,1)} %collective-permute-done.5.refs_4_, ...), custom_call_target="tpu_custom_call" | custom-call | flops 999999995904 | bytes 1000000000 | tf_op jit(solution)/shard_map/pallas_call | solution.py:84
  121.8 4.1 %shard_map.127.refs_5_ = bf16[512,1024]{1,0:T(8,128)(2,1)} custom-call(s32[4]{0:T(128)S(1)} %fusion.10.refs_0_, bf16[1024,1024]{1,0:T(8,128)(2,1)S(1)} %copy-done.1, bf16[8192,1024]{1,0:T(8,128)(2,1)} %refs_2_.37, bf16[1024,128]{1,0:T(8,128)(2,1)S(1)} %shard_map.126.refs_3_.refs_5_.refs_4_), custom_call_target="tpu_custom_call" | custom-call | flops 999999995904 | bytes 1000000000 | tf_op jit(solution)/shard_map/pallas_call | solution.py:84
  125.9 1.4 collective-permute-start.17
  127.4 4.5 %shard_map.128.refs_6_ = bf16[512,1024]{1,0:T(8,128)(2,1)} custom-call(s32[4]{0:T(128)S(1)} %fusion.28.refs_0_, bf16[1024,1024]{1,0:T(8,128)(2,1)S(1)} %copy-done.1, bf16[8192,1024]{1,0:T(8,128)(2,1)} %refs_2_.37, bf16[512,1024]{1,0:T(8,128)(2,1)} %collective-permute-done.4.refs_3_, bf16[512,1024]{1,0:T(8,128)(2,1)} %collective-permute-done.11.refs_4_, ...), custom_call_target="tpu_custom_call" | custom-call | flops 999999995904 | bytes 1000000000 | tf_op jit(solution)/shard_map/pallas_call | solution.py:84
  131.9 2.2 %all_gather.15.right = bf16[2048,128]{1,0:T(8,128)(2,1)S(1)} all-gather(bf16[1024,128]{1,0:T(8,128)(2,1)S(1)} %shard_map.126.refs_3_.refs_5_.refs_4_), channel_id=1, replica_groups=mesh['groups'=2,'dp'=2,'tensor'=8] {'dp'}, dimensions={0}, use_global_device_ids=true | all-gather | bytes 786432 | tf_op jit(solution)/shard_map/all_gather | solution.py:282
  134.1 1.4 collective-permute-done.15.refs_5_
  135.5 1.6 collective-permute-start.12
  137.0 4.8 %shard_map.129.refs_4_ = bf16[512,1024]{1,0:T(8,128)(2,1)} custom-call(s32[4]{0:T(128)S(1)} %fusion.14.refs_0_, bf16[1024,1024]{1,0:T(8,128)(2,1)S(1)} %copy-done.1, bf16[8192,1024]{1,0:T(8,128)(2,1)} %refs_2_.37, bf16[512,1024]{1,0:T(8,128)(2,1)} %collective-permute-done.13.refs_3_, bf16[512,1024]{1,0:T(8,128)(2,1)} %collective-permute-done.2.refs_3_.refs_4_, ...), custom_call_target="tpu_custom_call" | custom-call | flops 999999995904 | bytes 1000000000 | tf_op jit(solution)/shard_map/pallas_call | solution.py:84
  141.8 2.6 %collective-permute-done.14.refs_3_.refs_4_ = bf16[512,1024]{1,0:T(8,128)(2,1)} collective-permute-done((bf16[512,1024]{1,0:T(8,128)(2,1)}, bf16[512,1024]{1,0:T(8,128)(2,1)}, u32[]{:S(2)}, u32[]{:S(2)}) %collective-permute-start.14) | collective-permute-done | bytes 1048608 | tf_op jit(solution)/shard_map/ppermute | solution.py:256
  144.4 4.2 %shard_map.130.refs_5_ = bf16[512,1024]{1,0:T(8,128)(2,1)} custom-call(s32[4]{0:T(128)S(1)} %fusion.30.refs_0_, bf16[1024,1024]{1,0:T(8,128)(2,1)S(1)} %copy-done.1, bf16[8192,1024]{1,0:T(8,128)(2,1)} %refs_2_.37, bf16[512,1024]{1,0:T(8,128)(2,1)} %collective-permute-done.14.refs_3_.refs_4_, bf16[512,1024]{1,0:T(8,128)(2,1)} %shard_map.129.refs_4_), custom_call_target="tpu_custom_call" | custom-call | flops 999999995904 | bytes 1000000000 | tf_op jit(solution)/shard_map/pallas_call | solution.py:84
  149.0 4.8 %shard_map.131.refs_10_ = bf16[512,1024]{1,0:T(8,128)(2,1)} custom-call(s32[4]{0:T(128)S(1)} %fusion.12.refs_0_, bf16[1024,1024]{1,0:T(8,128)(2,1)S(1)} %copy-done.1, bf16[8192,1024]{1,0:T(8,128)(2,1)} %refs_2_.37, bf16[512,1024]{1,0:T(8,128)(2,1)} %collective-permute-done.13.refs_3_, bf16[512,1024]{1,0:T(8,128)(2,1)} %collective-permute-done.14.refs_3_.refs_4_, ...), custom_call_target="tpu_custom_call" | custom-call | flops 999999995904 | bytes 1000000000 | tf_op jit(solution)/shard_map/pallas_call | solution.py:84
  153.8 6.1 %collective-permute-done.12.refs_4_ = bf16[512,1024]{1,0:T(8,128)(2,1)} collective-permute-done((bf16[512,1024]{1,0:T(8,128)(2,1)}, bf16[512,1024]{1,0:T(8,128)(2,1)}, u32[]{:S(2)}, u32[]{:S(2)}) %collective-permute-start.12) | collective-permute-done | bytes 1048608 | tf_op jit(solution)/shard_map/ppermute | solution.py:272
  159.9 3.6 %collective-permute-start.19 = (bf16[512,1024]{1,0:T(8,128)(2,1)}, bf16[512,1024]{1,0:T(8,128)(2,1)}, u32[]{:S(2)}, u32[]{:S(2)}) collective-permute-start(bf16[512,1024]{1,0:T(8,128)(2,1)} %shard_map.131.refs_10_), channel_id=1, source_target_pairs={{2,4},{3,5},{4,2},{5,3},{10,12},{11,13},{12,10},{13,11},{18,20},{1... | collective-permute-start | bytes 3145736 | tf_op jit(solution)/shard_map/ppermute | solution.py:256
  163.6 3.3 %collective-permute-done.10.refs_3_ = bf16[512,1024]{1,0:T(8,128)(2,1)} collective-permute-done((bf16[512,1024]{1,0:T(8,128)(2,1)}, bf16[512,1024]{1,0:T(8,128)(2,1)}, u32[]{:S(2)}, u32[]{:S(2)}) %collective-permute-start.10) | collective-permute-done | bytes 1048608 | tf_op jit(solution)/shard_map/ppermute | solution.py:256
  166.9 4.0 %shard_map.132.refs_9_.refs_0_ = bf16[512,1024]{1,0:T(8,128)(2,1)S(1)} custom-call(s32[8]{0:T(128)S(1)} %stack.159.refs_0_, bf16[1024,1024]{1,0:T(8,128)(2,1)S(1)} %copy-done.1, bf16[8192,1024]{1,0:T(8,128)(2,1)} %refs_2_.37, bf16[512,1024]{1,0:T(8,128)(2,1)} %collective-permute-done.10.refs_3_, bf16[512,1024]{1,0:T(8,128)(2,1)} %collective-permute-done.12.refs_4_, ...), custom_call_target="tpu_custom_call" | custom-call | flops 999999995904 | bytes 1000000000 | tf_op jit(solution)/shard_map/pallas_call | solution.py:84
  170.9 3.8 %shard_map.133.refs_0_.refs_2_ = bf16[512,1024]{1,0:T(8,128)(2,1)S(1)} custom-call(s32[8]{0:T(128)S(1)} %stack.190.refs_0_, bf16[1024,1024]{1,0:T(8,128)(2,1)S(1)} %copy-done.1, bf16[8192,1024]{1,0:T(8,128)(2,1)} %refs_2_.37, bf16[512,1024]{1,0:T(8,128)(2,1)} %collective-permute-done.17.refs_3_, bf16[1024,128]{1,0:T(8,128)(2,1)S(1)} %shard_map.126.refs_3_.refs_5_.refs_4_, ...), custom_call_target="tpu_custom_call" | custom-call | flops 999999995904 | bytes 1000000000 | tf_op jit(solution)/shard_map/pallas_call | solution.py:84
  176.7 2.2 %copy-done.5 = bf16[2048,1024]{1,0:T(8,128)(2,1)S(1)} copy-done((bf16[2048,1024]{1,0:T(8,128)(2,1)S(1)}, bf16[2048,1024]{1,0:T(8,128)(2,1)}, u32[]{:S(2)}) %copy-start.5) | copy-done | bytes 4194328
  178.8 1.2 copy-done.14
  180.1 6.2 %shard_map.134.refs_5_ = f32[8,1024,128]{2,1,0:T(8,128)} custom-call(s32[16]{0:T(128)S(1)} %get-tuple-element.4.slots, f32[16]{0:T(128)S(1)} %broadcast_4_scales.2.scales, bf16[2048,1024]{1,0:T(8,128)(2,1)S(1)} %copy-done.5, bf16[2048,128]{1,0:T(8,128)(2,1)S(1)} %all_gather.15.right, bf16[512,1024]{1,0:T(8,128)(2,1)S(1)} %copy-done.14), custom_call_target="tpu_custom_call" | custom-call | flops 999999995904 | bytes 1000000000 | tf_op jit(solution)/shard_map/pallas_call | solution.py:204
  186.3 1.5 collective-permute-done.18.refs_3_
  187.8 2.2 %copy-done.8 = f32[8,1024,128]{2,1,0:T(8,128)S(1)} copy-done((f32[8,1024,128]{2,1,0:T(8,128)S(1)}, f32[8,1024,128]{2,1,0:T(8,128)}, u32[]{:S(2)}) %copy-start.8) | copy-done | bytes 4194328
  190.0 4.7 %shard_map.135 = bf16[1024,1024]{1,0:T(8,128)(2,1)} custom-call(bf16[512,1024]{1,0:T(8,128)(2,1)S(1)} %copy-done.12, bf16[512,1024]{1,0:T(8,128)(2,1)} %collective-permute-done.16.refs_1_, bf16[512,1024]{1,0:T(8,128)(2,1)S(1)} %copy-done.14, bf16[512,1024]{1,0:T(8,128)(2,1)} %collective-permute-done.18.refs_3_, ...), custom_call_target="tpu_custom_call" | custom-call | flops 999999995904 | bytes 1000000000 | tf_op jit(solution)/shard_map/pallas_call | solution.py:128
  (96 shorter events, 14.2 us)
Async XLA Ops:
  8.0 85.1 %all-gather.3.cloned.1.call-start = ((), (), s32[]{:S(2)}) async-start(), calls=%async_computation | async-start | bytes 6291456 | tf_op jit(solution)/shard_map/all_gather | solution.py:282
  8.9 1.6 copy-start
  10.4 5.8 %copy-start.1 = (bf16[1024,1024]{1,0:T(8,128)(2,1)S(1)}, bf16[1024,1024]{1,0:T(8,128)(2,1)}, u32[]{:S(2)}) copy-start(bf16[1024,1024]{1,0:T(8,128)(2,1)} %refs_1_.37) | copy-start | bytes 6291460
  14.6 33.7 %collective-permute-start.2 = (bf16[512,1024]{1,0:T(8,128)(2,1)}, bf16[512,1024]{1,0:T(8,128)(2,1)}, u32[]{:S(2)}, u32[]{:S(2)}) collective-permute-start(bf16[512,1024]{1,0:T(8,128)(2,1)} %shard_map.112.refs_3_), channel_id=1, source_target_pairs={{0,1},{1,0},{2,3},{3,2},{4,5},{5,4},{6,7},{7,6},{8,9},{9,8},{10,11... | collective-permute-start | bytes 3145736 | tf_op jit(solution)/shard_map/ppermute | solution.py:253
  20.4 27.9 %collective-permute-start.3 = (bf16[512,1024]{1,0:T(8,128)(2,1)}, bf16[512,1024]{1,0:T(8,128)(2,1)}, u32[]{:S(2)}, u32[]{:S(2)}) collective-permute-start(bf16[512,1024]{1,0:T(8,128)(2,1)} %shard_map.113.link), channel_id=1, source_target_pairs={{0,2},{1,3},{6,4},{7,5},{2,0},{3,1},{4,6},{5,7},{8,10},{9,11},{14,... | collective-permute-start | bytes 3145736 | tf_op jit(solution)/shard_map/ppermute | solution.py:256
  20.9 22.9 %collective-permute-start.8 = (s32[8]{0:T(128)}, s32[8]{0:T(128)}, u32[]{:S(2)}, u32[]{:S(2)}) collective-permute-start(s32[8]{0:T(128)} %tenants.1), channel_id=1, source_target_pairs={{0,8},{8,0},{1,9},{9,1},{2,10},{10,2},{3,11},{11,3},{4,12},{12,4},... | collective-permute-start | bytes 104 | tf_op jit(solution)/shard_map/ppermute | solution.py:287
  20.9 2.9 %copy-start.2 = (bf16[16,128,1024]{2,1,0:T(8,128)(2,1)S(1)}, bf16[16,128,1024]{2,1,0:T(8,128)(2,1)}, u32[]{:S(2)}) copy-start(bf16[16,128,1024]{2,1,0:T(8,128)(2,1)} %expand.1) | copy-start | bytes 12582916
  32.2 88.0 %all-reduce.2.cloned.1.call-start = ((), (), s32[]{:S(2)}) async-start(), calls=%async_computation.1 | async-start | bytes 524288 | tf_op jit(solution)/shard_map/psum | solution.py:306
  32.2 40.9 %collective-permute-start = (bf16[512,1024]{1,0:T(8,128)(2,1)}, bf16[512,1024]{1,0:T(8,128)(2,1)}, u32[]{:S(2)}, u32[]{:S(2)}) collective-permute-start(bf16[512,1024]{1,0:T(8,128)(2,1)} %shard_map.115.refs_3_), channel_id=1, source_target_pairs={{0,1},{1,0},{2,3},{3,2},{4,5},{5,4},{6,7},{7,6},{8,9},{9,8},{10,11... | collective-permute-start | bytes 3145736 | tf_op jit(solution)/shard_map/ppermute | solution.py:253
  32.8 143.8 %all-gather.5.cloned.1.call-start = ((), (), s32[]{:S(2)}) async-start(), calls=%async_computation.2 | async-start | bytes 6291456 | tf_op jit(solution)/shard_map/all_gather | solution.py:282
  32.9 7.2 %copy-start.17 = (s32[16]{0:T(128)S(1)}, s32[16]{0:T(128)}, u32[]{:S(2)}) copy-start(s32[16]{0:T(128)} %param.17) | copy-start | bytes 196
  32.9 8.6 %copy-start.15 = (bf16[1024,128]{1,0:T(8,128)(2,1)S(1)}, bf16[1024,128]{1,0:T(8,128)(2,1)}, u32[]{:S(2)}) copy-start(bf16[1024,128]{1,0:T(8,128)(2,1)} %param.11) | copy-start | bytes 786436
  32.9 11.6 %copy-start.16 = (s32[16]{0:T(128)S(1)}, s32[16]{0:T(128)}, u32[]{:S(2)}) copy-start(s32[16]{0:T(128)} %param.16) | copy-start | bytes 196
  37.0 36.1 %collective-permute-start.1 = (bf16[512,1024]{1,0:T(8,128)(2,1)}, bf16[512,1024]{1,0:T(8,128)(2,1)}, u32[]{:S(2)}, u32[]{:S(2)}) collective-permute-start(bf16[512,1024]{1,0:T(8,128)(2,1)} %shard_map.116.refs_5_), channel_id=1, source_target_pairs={{0,2},{1,3},{6,4},{7,5},{2,0},{3,1},{4,6},{5,7},{8,10},{9,11},{14,... | collective-permute-start | bytes 3145736 | tf_op jit(solution)/shard_map/ppermute | solution.py:256
  44.8 0.5 copy-start.9
  53.4 34.8 %collective-permute-start.9 = (bf16[512,1024]{1,0:T(8,128)(2,1)}, bf16[512,1024]{1,0:T(8,128)(2,1)}, u32[]{:S(2)}, u32[]{:S(2)}) collective-permute-start(bf16[512,1024]{1,0:T(8,128)(2,1)} %shard_map.117.refs_3_), channel_id=1, source_target_pairs={{2,4},{4,2},{0,16},{6,22},{3,5},{5,3},{1,17},{7,23},{18,20},{20,18... | collective-permute-start | bytes 3145736 | tf_op jit(solution)/shard_map/ppermute | solution.py:272
  54.2 53.7 %collective-permute-start.7 = (bf16[512,1024]{1,0:T(8,128)(2,1)}, bf16[512,1024]{1,0:T(8,128)(2,1)}, u32[]{:S(2)}, u32[]{:S(2)}) collective-permute-start(bf16[512,1024]{1,0:T(8,128)(2,1)} %shard_map.117.refs_3_), channel_id=1, source_target_pairs={{0,2},{1,3},{6,4},{7,5},{2,0},{3,1},{4,6},{5,7},{8,10},{9,11},{14,... | collective-permute-start | bytes 3145736 | tf_op jit(solution)/shard_map/ppermute | solution.py:256
  58.3 28.6 %collective-permute-start.6 = (bf16[512,1024]{1,0:T(8,128)(2,1)}, bf16[512,1024]{1,0:T(8,128)(2,1)}, u32[]{:S(2)}, u32[]{:S(2)}) collective-permute-start(bf16[512,1024]{1,0:T(8,128)(2,1)} %shard_map.118.refs_5_), channel_id=1, source_target_pairs={{0,1},{1,0},{2,3},{3,2},{4,5},{5,4},{6,7},{7,6},{8,9},{9,8},{10,11... | collective-permute-start | bytes 3145736 | tf_op jit(solution)/shard_map/ppermute | solution.py:253
  77.7 38.1 %collective-permute-start.5 = (bf16[512,1024]{1,0:T(8,128)(2,1)}, bf16[512,1024]{1,0:T(8,128)(2,1)}, u32[]{:S(2)}, u32[]{:S(2)}) collective-permute-start(bf16[512,1024]{1,0:T(8,128)(2,1)} %shard_map.119.refs_3_), channel_id=1, source_target_pairs={{2,4},{4,2},{0,16},{6,22},{3,5},{5,3},{1,17},{7,23},{18,20},{20,18... | collective-permute-start | bytes 3145736 | tf_op jit(solution)/shard_map/ppermute | solution.py:272
  79.2 46.7 %collective-permute-start.11 = (bf16[512,1024]{1,0:T(8,128)(2,1)}, bf16[512,1024]{1,0:T(8,128)(2,1)}, u32[]{:S(2)}, u32[]{:S(2)}) collective-permute-start(bf16[512,1024]{1,0:T(8,128)(2,1)} %shard_map.119.refs_3_), channel_id=1, source_target_pairs={{0,2},{1,3},{6,4},{7,5},{2,0},{3,1},{4,6},{5,7},{8,10},{9,11},{14,... | collective-permute-start | bytes 3145736 | tf_op jit(solution)/shard_map/ppermute | solution.py:256
  86.9 27.2 %collective-permute-start.4 = (bf16[512,1024]{1,0:T(8,128)(2,1)}, bf16[512,1024]{1,0:T(8,128)(2,1)}, u32[]{:S(2)}, u32[]{:S(2)}) collective-permute-start(bf16[512,1024]{1,0:T(8,128)(2,1)} %shard_map.120.refs_5_), channel_id=1, source_target_pairs={{0,1},{1,0},{2,3},{3,2},{4,5},{5,4},{6,7},{7,6},{8,9},{9,8},{10,11... | collective-permute-start | bytes 3145736 | tf_op jit(solution)/shard_map/ppermute | solution.py:253
  88.2 4.9 %copy-start.10 = (f32[16]{0:T(128)S(1)}, f32[16]{0:T(128)}, u32[]{:S(2)}) copy-start(f32[16]{0:T(128)} %copy-done.9) | copy-start | bytes 196
  92.6 51.8 %collective-permute-start.14 = (bf16[512,1024]{1,0:T(8,128)(2,1)}, bf16[512,1024]{1,0:T(8,128)(2,1)}, u32[]{:S(2)}, u32[]{:S(2)}) collective-permute-start(bf16[512,1024]{1,0:T(8,128)(2,1)} %shard_map.121.refs_0_), channel_id=1, source_target_pairs={{0,2},{1,3},{6,4},{7,5},{2,0},{3,1},{4,6},{5,7},{8,10},{9,11},{14,... | collective-permute-start | bytes 3145736 | tf_op jit(solution)/shard_map/ppermute | solution.py:256
  93.1 2.2 %copy-start.4 = (bf16[2048,1024]{1,0:T(8,128)(2,1)S(1)}, bf16[2048,1024]{1,0:T(8,128)(2,1)}, u32[]{:S(2)}) copy-start(bf16[2048,1024]{1,0:T(8,128)(2,1)} %all-gather.3.cloned.1.call-done.right) | copy-start | bytes 12582916
  101.5 2.2 %copy-start.7 = (f32[8,128,1024]{2,1,0:T(8,128)S(1)}, f32[8,128,1024]{2,1,0:T(8,128)}, u32[]{:S(2)}) copy-start(f32[8,128,1024]{2,1,0:T(8,128)} %shard_map.122.refs_3_) | copy-start | bytes 12582916
  107.9 29.2 %collective-permute-start.13 = (bf16[512,1024]{1,0:T(8,128)(2,1)}, bf16[512,1024]{1,0:T(8,128)(2,1)}, u32[]{:S(2)}, u32[]{:S(2)}) collective-permute-start(bf16[512,1024]{1,0:T(8,128)(2,1)} %shard_map.123.refs_5_), channel_id=1, source_target_pairs={{0,1},{1,0},{2,3},{3,2},{4,5},{5,4},{6,7},{7,6},{8,9},{9,8},{10,11... | collective-permute-start | bytes 3145736 | tf_op jit(solution)/shard_map/ppermute | solution.py:253
  114.1 21.4 %collective-permute-start.15 = (bf16[512,1024]{1,0:T(8,128)(2,1)}, bf16[512,1024]{1,0:T(8,128)(2,1)}, u32[]{:S(2)}, u32[]{:S(2)}) collective-permute-start(bf16[512,1024]{1,0:T(8,128)(2,1)} %shard_map.124.refs_5_), channel_id=1, source_target_pairs={{2,4},{4,2},{0,16},{6,22},{3,5},{5,3},{1,17},{7,23},{18,20},{20,18... | collective-permute-start | bytes 3145736 | tf_op jit(solution)/shard_map/ppermute | solution.py:272
  120.2 46.7 %collective-permute-start.10 = (bf16[512,1024]{1,0:T(8,128)(2,1)}, bf16[512,1024]{1,0:T(8,128)(2,1)}, u32[]{:S(2)}, u32[]{:S(2)}) collective-permute-start(bf16[512,1024]{1,0:T(8,128)(2,1)} %shard_map.125.link), channel_id=1, source_target_pairs={{0,2},{1,3},{6,4},{7,5},{2,0},{3,1},{4,6},{5,7},{8,10},{9,11},{14,... | collective-permute-start | bytes 3145736 | tf_op jit(solution)/shard_map/ppermute | solution.py:256
  120.2 1.0 copy-start.6
  125.9 45.0 %collective-permute-start.17 = (bf16[512,1024]{1,0:T(8,128)(2,1)}, bf16[512,1024]{1,0:T(8,128)(2,1)}, u32[]{:S(2)}, u32[]{:S(2)}) collective-permute-start(bf16[512,1024]{1,0:T(8,128)(2,1)} %shard_map.127.refs_5_), channel_id=1, source_target_pairs={{0,1},{1,0},{2,3},{3,2},{4,5},{5,4},{6,7},{7,6},{8,9},{9,8},{10,11... | collective-permute-start | bytes 3145736 | tf_op jit(solution)/shard_map/ppermute | solution.py:253
  135.5 24.5 %collective-permute-start.12 = (bf16[512,1024]{1,0:T(8,128)(2,1)}, bf16[512,1024]{1,0:T(8,128)(2,1)}, u32[]{:S(2)}, u32[]{:S(2)}) collective-permute-start(bf16[512,1024]{1,0:T(8,128)(2,1)} %shard_map.128.refs_6_), channel_id=1, source_target_pairs={{2,4},{4,2},{0,16},{6,22},{3,5},{5,3},{1,17},{7,23},{18,20},{20,18... | collective-permute-start | bytes 3145736 | tf_op jit(solution)/shard_map/ppermute | solution.py:272
  141.8 45.9 %collective-permute-start.18 = (bf16[512,1024]{1,0:T(8,128)(2,1)}, bf16[512,1024]{1,0:T(8,128)(2,1)}, u32[]{:S(2)}, u32[]{:S(2)}) collective-permute-start(bf16[512,1024]{1,0:T(8,128)(2,1)} %shard_map.129.refs_4_), channel_id=1, source_target_pairs={{0,2},{1,3},{6,4},{7,5},{2,0},{3,1},{4,6},{5,7},{8,10},{9,11},{14,... | collective-permute-start | bytes 3145736 | tf_op jit(solution)/shard_map/ppermute | solution.py:256
  148.7 37.6 %collective-permute-start.16 = (bf16[512,1024]{1,0:T(8,128)(2,1)}, bf16[512,1024]{1,0:T(8,128)(2,1)}, u32[]{:S(2)}, u32[]{:S(2)}) collective-permute-start(bf16[512,1024]{1,0:T(8,128)(2,1)} %shard_map.130.refs_5_), channel_id=1, source_target_pairs={{0,1},{1,0},{2,3},{3,2},{4,5},{5,4},{6,7},{7,6},{8,9},{9,8},{10,11... | collective-permute-start | bytes 3145736 | tf_op jit(solution)/shard_map/ppermute | solution.py:253
  149.0 17.9 %copy-start.3 = (bf16[16,1024,128]{2,1,0:T(8,128)(2,1)S(1)}, bf16[16,1024,128]{2,1,0:T(8,128)(2,1)}, u32[]{:S(2)}) copy-start(bf16[16,1024,128]{2,1,0:T(8,128)(2,1)} %refs_8_.3) | copy-start | bytes 12582916
  159.9 26.3 %collective-permute-start.19 = (bf16[512,1024]{1,0:T(8,128)(2,1)}, bf16[512,1024]{1,0:T(8,128)(2,1)}, u32[]{:S(2)}, u32[]{:S(2)}) collective-permute-start(bf16[512,1024]{1,0:T(8,128)(2,1)} %shard_map.131.refs_10_), channel_id=1, source_target_pairs={{2,4},{3,5},{4,2},{5,3},{10,12},{11,13},{12,10},{13,11},{18,20},{1... | collective-permute-start | bytes 3145736 | tf_op jit(solution)/shard_map/ppermute | solution.py:256
  174.7 1.0 copy-start.11
  175.7 1.0 copy-start.13
  176.6 2.2 %copy-start.5 = (bf16[2048,1024]{1,0:T(8,128)(2,1)S(1)}, bf16[2048,1024]{1,0:T(8,128)(2,1)}, u32[]{:S(2)}) copy-start(bf16[2048,1024]{1,0:T(8,128)(2,1)} %all-gather.5.cloned.1.call-done.left) | copy-start | bytes 12582916
  178.8 1.2 copy-start.14
  180.1 7.7 %copy-start.12 = (bf16[512,1024]{1,0:T(8,128)(2,1)S(1)}, bf16[512,1024]{1,0:T(8,128)(2,1)}, u32[]{:S(2)}) copy-start(bf16[512,1024]{1,0:T(8,128)(2,1)} %copy-done.11) | copy-start | bytes 3145732
  187.8 2.2 %copy-start.8 = (f32[8,1024,128]{2,1,0:T(8,128)S(1)}, f32[8,1024,128]{2,1,0:T(8,128)}, u32[]{:S(2)}) copy-start(f32[8,1024,128]{2,1,0:T(8,128)} %shard_map.134.refs_5_) | copy-start | bytes 12582916
Sparse Core Ops, SparseCore 0:
  10.4 15.0 all-gather.2
  38.6 14.8 all-gather.4
Sparse Core Ops, SparseCore 1:
  36.0 72.2 all-reduce.1

commit v8 on v7

--- a/solution.py
+++ b/solution.py
@@ -95,6 +95,44 @@
     )(scalars, *operands)
 
 
+def pair_kernel(scalars, rows, weights, first, second):
+    part = lax.dot_general(
+        rows[...], weights[...], contract_last, preferred_element_type=f32
+    ).astype(bf16)
+
+    @pl.when(pl.program_id(0) == 0)
+    def _():
+        first[...] = part
+
+    @pl.when(pl.program_id(0) == 1)
+    def _():
+        second[...] = part
+
+
+def product_pair(scalars, gradient, weights, piece_rows, width):
+    depth = gradient.shape[1]
+    tile = width // 2
+    piece = jax.ShapeDtypeStruct((piece_rows, width), bf16)
+    return pl.pallas_call(
+        pair_kernel,
+        grid_spec=pltpu.PrefetchScalarGridSpec(
+            num_scalar_prefetch=1,
+            grid=(2, 2),
+            in_specs=[
+                pl.BlockSpec((piece_rows, depth), lambda t, j, s: (s[2 * t + 1], 0)),
+                pl.BlockSpec((tile, depth), lambda t, j, s: (s[2 * t] * 2 + j, 0)),
+            ],
+            out_specs=[
+                pl.BlockSpec((piece_rows, tile), lambda t, j, s: (0, jnp.where(t == 0, j, 1))),
+                pl.BlockSpec((piece_rows, tile), lambda t, j, s: (0, jnp.where(t == 1, j, 0))),
+            ],
+        ),
+        out_shape=[piece, piece],
+        compiler_params=params(),
+        cost_estimate=declared,
+    )(scalars, gradient, weights)
+
+
 def finish_kernel(counts, *refs):
     out = refs[-1]
     position = 0
@@ -328,8 +366,13 @@
         link[:] = [out]
         return out
 
-    y1 = swap(run(jnp.where(at_end, far, near_end), other, upper, []), every)
-    direct_a = along(run(far, other, lower, []), pairwise)
+    firsts = (jnp.where(at_end, far, near_end) * 2 + other, upper, far * 2 + other, lower)
+    out_y, out_z = product_pair(
+        jnp.stack([jnp.asarray(v, jnp.int32) for v in firsts]),
+        gradient, weights, piece_rows, width,
+    )
+    y1, direct_a = swap(out_y, every), along(out_z, pairwise)
+    link[:] = [out_z]
     low_whole = adapter_space()
     y2 = swap(run(beyond, other, lower, []), every)
     direct_b = along(run(far, same, lower, []), pairwise)
@@ -365,6 +408,8 @@
     both_5 = along(out, pairwise)
     y7 = swap(run(node, other, lower, [(both_3, 1)]), every)
     upper_4 = along(run(beyond, same, upper, [(y5, 0), (both_3, 0)]), across)
+    link += [both_4, lower_4]
+    grad_shrink = shrink_gradient(low)
     def base(piece, adds):
         in_piece = piece_rows // row_block
         scalars = [node * 2 + side, jnp.int32(piece)] + [jnp.asarray(r, jnp.int32) for r in roles]
@@ -378,8 +423,7 @@
 
     lower_base = base(lower, [(both_4, 0), (lower_4, 2)])
     upper_base = base(upper, [(y6, 0)])
-    grad_shrink = shrink_gradient(low)
-    input_gradient = finish([[lower_base, y7], [upper_base, both_5, upper_4]], link)
+    input_gradient = finish([[lower_base, y7], [upper_base, both_5, upper_4]], [])
     return (input_gradient, grad_shrink, grad_expand)
 
 

time: 204 us -> 201 us (0.985)
  waiting for transfers between devices: 38 us -> 45.2 us
  Pallas kernels: 104 us -> 97.4 us
  local copies, waits for them, and re-layouts: 20.7 us -> 14.6 us
    ppermute x7, waiting for transfers between devices: 4.63 us -> 14.6 us  [swap(): return lax.ppermute(x, 'tensor', pairs)]
    pallas_call x19 -> x17, Pallas kernels: 81.9 us -> 72.8 us  [product(): pl.pallas_call(functools.partial(product_kernel, tuple((mode for _, mode...]
    pallas_call x0 -> x1, Pallas kernels: none -> 6.9 us  [product_pair(): pl.pallas_call(pair_kernel, grid_spec=pltpu.PrefetchScalarGridSpec(num_sc...]
    unnamed x36 -> x32, local copies, waits for them, and re-layouts: 17.9 us -> 11.8 us
    pallas_call x2, Pallas kernels: 12.5 us -> 8.06 us  [factor_sums(): pl.pallas_call(functools.partial(factor_kernel, slots_each), in_specs=[pl...]
    ppermute x8, waiting for transfers between devices: 24.8 us -> 20.4 us  [along(): lax.ppermute(x, 'tensor', [(2 * a + y, 2 * b + y) for a, b in hops for y...]
  transfers between devices with their start and end apart: 23 -> 23, of which waited for: 9 -> 9; matrix products, arithmetic and copies ran while one was open for 2% -> 2% of each run, Pallas kernels for 49% -> 47%
where the time goes in v8:
time: 201 us; the launch traced here: 199 us
  Pallas kernels  97.4 us (48%)
  waiting for transfers between devices  45.2 us (22%)
  starting transfers between devices  19.6 us (10%)
  between operations  15.7 us (8%)
  local copies, waits for them, and re-layouts  14.6 us (7%)
  blocking collectives  4.35 us (2%)
    pallas_call x17, Pallas kernels, product(): pl.pallas_call(functools.partial(product_kernel, tuple((mode for _, mode...  72.8 us
    ppermute x8, waiting for transfers between devices, along(): lax.ppermute(x, 'tensor', [(2 * a + y, 2 * b + y) for a, b in hops for y...  20.4 us
    ppermute x7, waiting for transfers between devices, swap(): return lax.ppermute(x, 'tensor', pairs)  14.6 us
    unnamed x32, local copies, waits for them, and re-layouts  11.8 us
    ppermute x4, waiting for transfers between devices, exchange(): return lax.ppermute(x, ('groups', 'tensor'), pairs)  9.48 us
    pallas_call x2, Pallas kernels, factor_sums(): pl.pallas_call(functools.partial(factor_kernel, slots_each), in_specs=[pl...  8.06 us
    pallas_call x1, Pallas kernels, product_pair(): pl.pallas_call(pair_kernel, grid_spec=pltpu.PrefetchScalarGridSpec(num_sc...  6.9 us
    ppermute x7, starting transfers between devices, swap(): return lax.ppermute(x, 'tensor', pairs)  6.73 us
  transfers between devices with their start and end apart: 23, of which 9 were waited for; matrix products, arithmetic and copies ran while one was open for 2% of the time, Pallas kernels for 47%

profile of v8, /device:TPU:10, one launch (start us, length us, event | category | flops | bytes accessed | tf_op | source)
XLA Modules:
  0.0 198.5 jit_solution(13403529956689054777)
XLA Ops:
  8.9 1.6 copy-done
  10.5 6.9 %shard_map.112 = (bf16[512,1024]{1,0:T(8,128)(2,1)}, bf16[512,1024]{1,0:T(8,128)(2,1)}) custom-call(s32[4]{0:T(128)S(1)} %get-tuple-element.11.scalars, bf16[1024,1024]{1,0:T(8,128)(2,1)S(1)} %copy-done, bf16[8192,1024]{1,0:T(8,128)(2,1)} %refs_2_.33), custom_call_target="tpu_custom_call" | custom-call | flops 999999995904 | bytes 1000000000 | tf_op jit(solution)/shard_map/pallas_call | solution.py:116
  17.4 1.5 collective-permute-start.2
  19.3 4.3 %shard_map.113.refs_3_ = bf16[1024,128]{1,0:T(8,128)(2,1)} custom-call(s32[8]{0:T(128)} %tenants.1, bf16[1024,1024]{1,0:T(8,128)(2,1)S(1)} %copy-done.1, bf16[16,128,1024]{2,1,0:T(8,128)(2,1)S(1)} %copy-done.4, bf16[512,1024]{1,0:T(8,128)(2,1)} %get-tuple-element.5.link), custom_call_target="tpu_custom_call" | custom-call | flops 999999995904 | bytes 1000000000 | tf_op jit(solution)/shard_map/pallas_call | solution.py:186
  23.6 4.1 %shard_map.114.refs_3_ = bf16[512,1024]{1,0:T(8,128)(2,1)} custom-call(s32[4]{0:T(128)S(1)} %get-tuple-element.12.refs_0_, bf16[1024,1024]{1,0:T(8,128)(2,1)S(1)} %copy-done.1, bf16[8192,1024]{1,0:T(8,128)(2,1)} %refs_2_.33, bf16[1024,128]{1,0:T(8,128)(2,1)} %shard_map.113.refs_3_), custom_call_target="tpu_custom_call" | custom-call | flops 999999995904 | bytes 1000000000 | tf_op jit(solution)/shard_map/pallas_call | solution.py:84
  28.4 4.1 %shard_map.115.refs_5_ = bf16[512,1024]{1,0:T(8,128)(2,1)} custom-call(s32[4]{0:T(128)S(1)} %fusion.24.refs_0_, bf16[1024,1024]{1,0:T(8,128)(2,1)S(1)} %copy-done.1, bf16[8192,1024]{1,0:T(8,128)(2,1)} %refs_2_.33, bf16[512,1024]{1,0:T(8,128)(2,1)} %shard_map.114.refs_3_), custom_call_target="tpu_custom_call" | custom-call | flops 999999995904 | bytes 1000000000 | tf_op jit(solution)/shard_map/pallas_call | solution.py:84
  32.5 1.6 collective-permute-start.1
  37.2 2.2 %all_gather.12 = bf16[2048,128]{1,0:T(8,128)(2,1)S(1)} all-gather(bf16[1024,128]{1,0:T(8,128)(2,1)S(1)} %copy-done.13), channel_id=1, replica_groups=mesh['groups'=2,'dp'=2,'tensor'=8] {'dp'}, dimensions={0}, use_global_device_ids=true | all-gather | bytes 786432 | tf_op jit(solution)/shard_map/all_gather | solution.py:320
  41.1 3.7 %collective-permute-done.2.refs_3_.refs_4_ = bf16[512,1024]{1,0:T(8,128)(2,1)} collective-permute-done((bf16[512,1024]{1,0:T(8,128)(2,1)}, bf16[512,1024]{1,0:T(8,128)(2,1)}, u32[]{:S(2)}, u32[]{:S(2)}) %collective-permute-start.2) | collective-permute-done | bytes 1048608 | tf_op jit(solution)/shard_map/ppermute | solution.py:291
  44.8 3.2 %collective-permute-done.3.refs_4_ = bf16[512,1024]{1,0:T(8,128)(2,1)} collective-permute-done((bf16[512,1024]{1,0:T(8,128)(2,1)}, bf16[512,1024]{1,0:T(8,128)(2,1)}, u32[]{:S(2)}, u32[]{:S(2)}) %collective-permute-start.3) | collective-permute-done | bytes 1048608 | tf_op jit(solution)/shard_map/ppermute | solution.py:294
  48.0 4.4 %shard_map.116.refs_3_ = bf16[512,1024]{1,0:T(8,128)(2,1)} custom-call(s32[4]{0:T(128)S(1)} %add_add_fusion.refs_0_, bf16[1024,1024]{1,0:T(8,128)(2,1)S(1)} %copy-done.1, bf16[8192,1024]{1,0:T(8,128)(2,1)} %refs_2_.33, bf16[512,1024]{1,0:T(8,128)(2,1)} %collective-permute-done.2.refs_3_.refs_4_, bf16[512,1024]{1,0:T(8,128)(2,1)} %collective-permute-done.3.refs_4_, ...), custom_call_target="tpu_custom_call" | custom-call | flops 999999995904 | bytes 1000000000 | tf_op jit(solution)/shard_map/pallas_call | solution.py:84
  52.4 1.8 collective-permute-start.9
  54.2 4.1 %shard_map.117.refs_5_ = bf16[512,1024]{1,0:T(8,128)(2,1)} custom-call(s32[4]{0:T(128)S(1)} %fusion.4.refs_0_, bf16[1024,1024]{1,0:T(8,128)(2,1)S(1)} %copy-done.1, bf16[8192,1024]{1,0:T(8,128)(2,1)} %refs_2_.33, bf16[512,1024]{1,0:T(8,128)(2,1)} %shard_map.116.refs_3_), custom_call_target="tpu_custom_call" | custom-call | flops 999999995904 | bytes 1000000000 | tf_op jit(solution)/shard_map/pallas_call | solution.py:84
  58.4 13.2 %collective-permute-done.1.refs_4_ = bf16[512,1024]{1,0:T(8,128)(2,1)} collective-permute-done((bf16[512,1024]{1,0:T(8,128)(2,1)}, bf16[512,1024]{1,0:T(8,128)(2,1)}, u32[]{:S(2)}, u32[]{:S(2)}) %collective-permute-start.1) | collective-permute-done | bytes 1048608 | tf_op jit(solution)/shard_map/ppermute | solution.py:294
  71.6 4.5 %shard_map.118.refs_3_ = bf16[512,1024]{1,0:T(8,128)(2,1)} custom-call(s32[4]{0:T(128)S(1)} %fusion.20.refs_0_, bf16[1024,1024]{1,0:T(8,128)(2,1)S(1)} %copy-done.1, bf16[8192,1024]{1,0:T(8,128)(2,1)} %refs_2_.33, bf16[512,1024]{1,0:T(8,128)(2,1)} %collective-permute-done.refs_3_, bf16[512,1024]{1,0:T(8,128)(2,1)} %collective-permute-done.1.refs_4_, ...), custom_call_target="tpu_custom_call" | custom-call | flops 999999995904 | bytes 1000000000 | tf_op jit(solution)/shard_map/pallas_call | solution.py:84
  76.1 1.6 collective-permute-start.5
  77.7 4.1 %shard_map.119.refs_5_ = bf16[512,1024]{1,0:T(8,128)(2,1)} custom-call(s32[4]{0:T(128)S(1)} %fusion.18.refs_0_, bf16[1024,1024]{1,0:T(8,128)(2,1)S(1)} %copy-done.1, bf16[8192,1024]{1,0:T(8,128)(2,1)} %refs_2_.33, bf16[512,1024]{1,0:T(8,128)(2,1)} %shard_map.118.refs_3_), custom_call_target="tpu_custom_call" | custom-call | flops 999999995904 | bytes 1000000000 | tf_op jit(solution)/shard_map/pallas_call | solution.py:84
  81.8 7.8 %collective-permute-done.6.refs_3_ = bf16[512,1024]{1,0:T(8,128)(2,1)} collective-permute-done((bf16[512,1024]{1,0:T(8,128)(2,1)}, bf16[512,1024]{1,0:T(8,128)(2,1)}, u32[]{:S(2)}, u32[]{:S(2)}) %collective-permute-start.6) | collective-permute-done | bytes 1048608 | tf_op jit(solution)/shard_map/ppermute | solution.py:291
  89.6 1.3 collective-permute-start.4
  90.9 4.4 %shard_map.120.refs_0_ = bf16[512,1024]{1,0:T(8,128)(2,1)} custom-call(s32[4]{0:T(128)S(1)} %add_add_fusion.1.refs_0_, bf16[1024,1024]{1,0:T(8,128)(2,1)S(1)} %copy-done.1, bf16[8192,1024]{1,0:T(8,128)(2,1)} %refs_2_.33, bf16[512,1024]{1,0:T(8,128)(2,1)} %collective-permute-done.6.refs_3_, bf16[512,1024]{1,0:T(8,128)(2,1)} %collective-permute-done.9.refs_4_, ...), custom_call_target="tpu_custom_call" | custom-call | flops 999999995904 | bytes 1000000000 | tf_op jit(solution)/shard_map/pallas_call | solution.py:84
  95.9 2.2 %copy-done.6 = bf16[2048,1024]{1,0:T(8,128)(2,1)S(1)} copy-done((bf16[2048,1024]{1,0:T(8,128)(2,1)S(1)}, bf16[2048,1024]{1,0:T(8,128)(2,1)}, u32[]{:S(2)}) %copy-start.6) | copy-done | bytes 4194328
  98.0 4.1 %shard_map.121.refs_3_ = f32[8,128,1024]{2,1,0:T(8,128)} custom-call(s32[16]{0:T(128)S(1)} %get-tuple-element.8.slots, f32[16]{0:T(128)S(1)} %copy-done.12, bf16[2048,128]{1,0:T(8,128)(2,1)S(1)} %bitcast_multiply_fusion.left, bf16[2048,1024]{1,0:T(8,128)(2,1)S(1)} %copy-done.6, bf16[512,1024]{1,0:T(8,128)(2,1)} %shard_map.120.refs_0_), custom_call_target="tpu_custom_call" | custom-call | flops 999999995904 | bytes 1000000000 | tf_op jit(solution)/shard_map/pallas_call | solution.py:242
  102.2 2.2 %copy-done.9 = f32[8,128,1024]{2,1,0:T(8,128)S(1)} copy-done((f32[8,128,1024]{2,1,0:T(8,128)S(1)}, f32[8,128,1024]{2,1,0:T(8,128)}, u32[]{:S(2)}) %copy-start.9) | copy-done | bytes 4194328
  104.3 4.1 %shard_map.122.refs_5_ = bf16[512,1024]{1,0:T(8,128)(2,1)} custom-call(s32[4]{0:T(128)S(1)} %fusion.8.refs_0_, bf16[1024,1024]{1,0:T(8,128)(2,1)S(1)} %copy-done.1, bf16[8192,1024]{1,0:T(8,128)(2,1)} %refs_2_.33, f32[8,128,1024]{2,1,0:T(8,128)S(1)} %copy-done.9), custom_call_target="tpu_custom_call" | custom-call | flops 999999995904 | bytes 1000000000 | tf_op jit(solution)/shard_map/pallas_call | solution.py:84
  109.2 4.4 %shard_map.123.refs_5_ = bf16[512,1024]{1,0:T(8,128)(2,1)} custom-call(s32[4]{0:T(128)S(1)} %fusion.6.refs_0_, bf16[1024,1024]{1,0:T(8,128)(2,1)S(1)} %copy-done.1, bf16[8192,1024]{1,0:T(8,128)(2,1)} %refs_2_.33, bf16[512,1024]{1,0:T(8,128)(2,1)} %collective-permute-done.6.refs_3_, bf16[512,1024]{1,0:T(8,128)(2,1)} %collective-permute-done.7.refs_4_, ...), custom_call_target="tpu_custom_call" | custom-call | flops 999999995904 | bytes 1000000000 | tf_op jit(solution)/shard_map/pallas_call | solution.py:84
  113.7 3.1 %collective-permute-done.4.refs_3_ = bf16[512,1024]{1,0:T(8,128)(2,1)} collective-permute-done((bf16[512,1024]{1,0:T(8,128)(2,1)}, bf16[512,1024]{1,0:T(8,128)(2,1)}, u32[]{:S(2)}, u32[]{:S(2)}) %collective-permute-start.4) | collective-permute-done | bytes 1048608 | tf_op jit(solution)/shard_map/ppermute | solution.py:291
  116.7 1.6 collective-permute-start.15
  118.3 4.5 %shard_map.124.link = bf16[512,1024]{1,0:T(8,128)(2,1)} custom-call(s32[4]{0:T(128)S(1)} %fusion.16.refs_0_, bf16[1024,1024]{1,0:T(8,128)(2,1)S(1)} %copy-done.1, bf16[8192,1024]{1,0:T(8,128)(2,1)} %refs_2_.33, bf16[512,1024]{1,0:T(8,128)(2,1)} %collective-permute-done.4.refs_3_, bf16[512,1024]{1,0:T(8,128)(2,1)} %collective-permute-done.5.refs_4_, ...), custom_call_target="tpu_custom_call" | custom-call | flops 999999995904 | bytes 1000000000 | tf_op jit(solution)/shard_map/pallas_call | solution.py:84
  122.8 0.9 copy-done.8
  124.4 4.1 %shard_map.126.refs_5_ = bf16[512,1024]{1,0:T(8,128)(2,1)} custom-call(s32[4]{0:T(128)S(1)} %fusion.10.refs_0_, bf16[1024,1024]{1,0:T(8,128)(2,1)S(1)} %copy-done.1, bf16[8192,1024]{1,0:T(8,128)(2,1)} %refs_2_.33, bf16[1024,128]{1,0:T(8,128)(2,1)S(1)} %shard_map.125.refs_3_.refs_5_.refs_4_), custom_call_target="tpu_custom_call" | custom-call | flops 999999995904 | bytes 1000000000 | tf_op jit(solution)/shard_map/pallas_call | solution.py:84
  128.5 1.3 collective-permute-start.17
  129.7 4.5 %shard_map.127.refs_6_ = bf16[512,1024]{1,0:T(8,128)(2,1)} custom-call(s32[4]{0:T(128)S(1)} %fusion.26.refs_0_, bf16[1024,1024]{1,0:T(8,128)(2,1)S(1)} %copy-done.1, bf16[8192,1024]{1,0:T(8,128)(2,1)} %refs_2_.33, bf16[512,1024]{1,0:T(8,128)(2,1)} %collective-permute-done.4.refs_3_, bf16[512,1024]{1,0:T(8,128)(2,1)} %collective-permute-done.11.refs_4_, ...), custom_call_target="tpu_custom_call" | custom-call | flops 999999995904 | bytes 1000000000 | tf_op jit(solution)/shard_map/pallas_call | solution.py:84
  134.3 2.2 %all_gather.15.right = bf16[2048,128]{1,0:T(8,128)(2,1)S(1)} all-gather(bf16[1024,128]{1,0:T(8,128)(2,1)S(1)} %shard_map.125.refs_3_.refs_5_.refs_4_), channel_id=1, replica_groups=mesh['groups'=2,'dp'=2,'tensor'=8] {'dp'}, dimensions={0}, use_global_device_ids=true | all-gather | bytes 786432 | tf_op jit(solution)/shard_map/all_gather | solution.py:320
  136.4 3.6 %collective-permute-done.15.refs_5_ = bf16[512,1024]{1,0:T(8,128)(2,1)} collective-permute-done((bf16[512,1024]{1,0:T(8,128)(2,1)}, bf16[512,1024]{1,0:T(8,128)(2,1)}, u32[]{:S(2)}, u32[]{:S(2)}) %collective-permute-start.15) | collective-permute-done | bytes 1048608 | tf_op jit(solution)/shard_map/ppermute | solution.py:310
  140.0 1.7 collective-permute-start.12
  141.8 4.8 %shard_map.128.refs_4_ = bf16[512,1024]{1,0:T(8,128)(2,1)} custom-call(s32[4]{0:T(128)S(1)} %fusion.14.refs_0_, bf16[1024,1024]{1,0:T(8,128)(2,1)S(1)} %copy-done.1, bf16[8192,1024]{1,0:T(8,128)(2,1)} %refs_2_.33, bf16[512,1024]{1,0:T(8,128)(2,1)} %collective-permute-done.13.refs_3_, bf16[512,1024]{1,0:T(8,128)(2,1)} %collective-permute-done.2.refs_3_.refs_4_, ...), custom_call_target="tpu_custom_call" | custom-call | flops 999999995904 | bytes 1000000000 | tf_op jit(solution)/shard_map/pallas_call | solution.py:84
  146.6 4.3 %shard_map.129.refs_5_ = bf16[512,1024]{1,0:T(8,128)(2,1)} custom-call(s32[4]{0:T(128)S(1)} %fusion.28.refs_0_, bf16[1024,1024]{1,0:T(8,128)(2,1)S(1)} %copy-done.1, bf16[8192,1024]{1,0:T(8,128)(2,1)} %refs_2_.33, bf16[512,1024]{1,0:T(8,128)(2,1)} %collective-permute-done.14.refs_3_.refs_4_, bf16[512,1024]{1,0:T(8,128)(2,1)} %shard_map.128.refs_4_), custom_call_target="tpu_custom_call" | custom-call | flops 999999995904 | bytes 1000000000 | tf_op jit(solution)/shard_map/pallas_call | solution.py:84
  150.9 1.3 collective-permute-start.16
  152.2 4.5 %shard_map.130.refs_0_ = bf16[512,1024]{1,0:T(8,128)(2,1)} custom-call(s32[4]{0:T(128)S(1)} %fusion.12.refs_0_, bf16[1024,1024]{1,0:T(8,128)(2,1)S(1)} %copy-done.1, bf16[8192,1024]{1,0:T(8,128)(2,1)} %refs_2_.33, bf16[512,1024]{1,0:T(8,128)(2,1)} %collective-permute-done.13.refs_3_, bf16[512,1024]{1,0:T(8,128)(2,1)} %collective-permute-done.14.refs_3_.refs_4_, ...), custom_call_target="tpu_custom_call" | custom-call | flops 999999995904 | bytes 1000000000 | tf_op jit(solution)/shard_map/pallas_call | solution.py:84
  156.7 5.9 %collective-permute-done.12.refs_2_.refs_4_ = bf16[512,1024]{1,0:T(8,128)(2,1)} collective-permute-done((bf16[512,1024]{1,0:T(8,128)(2,1)}, bf16[512,1024]{1,0:T(8,128)(2,1)}, u32[]{:S(2)}, u32[]{:S(2)}) %collective-permute-start.12) | collective-permute-done | bytes 1048608 | tf_op jit(solution)/shard_map/ppermute | solution.py:310
  162.6 3.6 %collective-permute-start.19 = (bf16[512,1024]{1,0:T(8,128)(2,1)}, bf16[512,1024]{1,0:T(8,128)(2,1)}, u32[]{:S(2)}, u32[]{:S(2)}) collective-permute-start(bf16[512,1024]{1,0:T(8,128)(2,1)} %shard_map.130.refs_0_), channel_id=1, source_target_pairs={{2,4},{3,5},{4,2},{5,3},{10,12},{11,13},{12,10},{13,11},{18,20},{1... | collective-permute-start | bytes 3145736 | tf_op jit(solution)/shard_map/ppermute | solution.py:294
  166.3 2.2 %copy-done.7 = bf16[2048,1024]{1,0:T(8,128)(2,1)S(1)} copy-done((bf16[2048,1024]{1,0:T(8,128)(2,1)S(1)}, bf16[2048,1024]{1,0:T(8,128)(2,1)}, u32[]{:S(2)}) %copy-start.7) | copy-done | bytes 4194328
  168.5 4.0 %shard_map.131.refs_10_ = f32[8,1024,128]{2,1,0:T(8,128)} custom-call(s32[16]{0:T(128)S(1)} %get-tuple-element.8.slots, f32[16]{0:T(128)S(1)} %broadcast_4_scales.2.scales, bf16[2048,1024]{1,0:T(8,128)(2,1)S(1)} %copy-done.7, bf16[2048,128]{1,0:T(8,128)(2,1)S(1)} %all_gather.15.right, bf16[512,1024]{1,0:T(8,128)(2,1)} %shard_map.130.refs_0_, ...), custom_call_target="tpu_custom_call" | custom-call | flops 999999995904 | bytes 1000000000 | tf_op jit(solution)/shard_map/pallas_call | solution.py:242
  172.4 2.2 %copy-done.10 = f32[8,1024,128]{2,1,0:T(8,128)S(1)} copy-done((f32[8,1024,128]{2,1,0:T(8,128)S(1)}, f32[8,1024,128]{2,1,0:T(8,128)}, u32[]{:S(2)}) %copy-start.10) | copy-done | bytes 4194328
  174.6 4.0 %shard_map.132.refs_9_.refs_0_ = bf16[512,1024]{1,0:T(8,128)(2,1)S(1)} custom-call(s32[8]{0:T(128)S(1)} %stack.152.refs_0_, bf16[1024,1024]{1,0:T(8,128)(2,1)S(1)} %copy-done.1, bf16[8192,1024]{1,0:T(8,128)(2,1)} %refs_2_.33, bf16[512,1024]{1,0:T(8,128)(2,1)} %collective-permute-done.10.refs_1_.refs_3_, ...), custom_call_target="tpu_custom_call" | custom-call | flops 999999995904 | bytes 1000000000 | tf_op jit(solution)/shard_map/pallas_call | solution.py:84
  178.6 3.8 %shard_map.133.refs_2_ = bf16[512,1024]{1,0:T(8,128)(2,1)S(1)} custom-call(s32[8]{0:T(128)S(1)} %stack.182.refs_0_, bf16[1024,1024]{1,0:T(8,128)(2,1)S(1)} %copy-done.1, bf16[8192,1024]{1,0:T(8,128)(2,1)} %refs_2_.33, bf16[512,1024]{1,0:T(8,128)(2,1)} %collective-permute-done.17.refs_3_, bf16[1024,128]{1,0:T(8,128)(2,1)S(1)} %copy-done.3, ...), custom_call_target="tpu_custom_call" | custom-call | flops 999999995904 | bytes 1000000000 | tf_op jit(solution)/shard_map/pallas_call | solution.py:84
  182.4 3.7 %collective-permute-done.19.refs_4_ = bf16[512,1024]{1,0:T(8,128)(2,1)} collective-permute-done((bf16[512,1024]{1,0:T(8,128)(2,1)}, bf16[512,1024]{1,0:T(8,128)(2,1)}, u32[]{:S(2)}, u32[]{:S(2)}) %collective-permute-start.19) | collective-permute-done | bytes 1048608 | tf_op jit(solution)/shard_map/ppermute | solution.py:294
  186.4 4.7 %shard_map.134 = bf16[1024,1024]{1,0:T(8,128)(2,1)} custom-call(bf16[512,1024]{1,0:T(8,128)(2,1)S(1)} %shard_map.132.refs_9_.refs_0_, bf16[512,1024]{1,0:T(8,128)(2,1)} %collective-permute-done.16.refs_1_, bf16[512,1024]{1,0:T(8,128)(2,1)S(1)} %shard_map.133.refs_2_, bf16[512,1024]{1,0:T(8,128)(2,1)} %collective-permute-done.18.refs_3_, ...), custom_call_target="tpu_custom_call" | custom-call | flops 999999995904 | bytes 1000000000 | tf_op jit(solution)/shard_map/pallas_call | solution.py:166
  (89 shorter events, 9.0 us)
Async XLA Ops:
  8.0 87.9 %all-gather.3.cloned.1.call-start = ((), (), s32[]{:S(2)}) async-start(), calls=%async_computation | async-start | bytes 6291456 | tf_op jit(solution)/shard_map/all_gather | solution.py:320
  8.9 1.6 copy-start
  10.5 8.9 %copy-start.1 = (bf16[1024,1024]{1,0:T(8,128)(2,1)S(1)}, bf16[1024,1024]{1,0:T(8,128)(2,1)}, u32[]{:S(2)}) copy-start(bf16[1024,1024]{1,0:T(8,128)(2,1)} %refs_1_.33) | copy-start | bytes 6291460
  10.5 8.9 %copy-start.4 = (bf16[16,128,1024]{2,1,0:T(8,128)(2,1)S(1)}, bf16[16,128,1024]{2,1,0:T(8,128)(2,1)}, u32[]{:S(2)}) copy-start(bf16[16,128,1024]{2,1,0:T(8,128)(2,1)} %expand.1) | copy-start | bytes 12582916
  17.4 27.4 %collective-permute-start.2 = (bf16[512,1024]{1,0:T(8,128)(2,1)}, bf16[512,1024]{1,0:T(8,128)(2,1)}, u32[]{:S(2)}, u32[]{:S(2)}) collective-permute-start(bf16[512,1024]{1,0:T(8,128)(2,1)} %get-tuple-element.6), channel_id=1, source_target_pairs={{0,1},{1,0},{2,3},{3,2},{4,5},{5,4},{6,7},{7,6},{8,9},{9,8},{10,11... | collective-permute-start | bytes 3145736 | tf_op jit(solution)/shard_map/ppermute | solution.py:291
  18.9 29.1 %collective-permute-start.3 = (bf16[512,1024]{1,0:T(8,128)(2,1)}, bf16[512,1024]{1,0:T(8,128)(2,1)}, u32[]{:S(2)}, u32[]{:S(2)}) collective-permute-start(bf16[512,1024]{1,0:T(8,128)(2,1)} %get-tuple-element.5.link), channel_id=1, source_target_pairs={{0,2},{1,3},{6,4},{7,5},{2,0},{3,1},{4,6},{5,7},{8,10},{9,11},{14,... | collective-permute-start | bytes 3145736 | tf_op jit(solution)/shard_map/ppermute | solution.py:294
  19.3 20.0 %collective-permute-start.8 = (s32[8]{0:T(128)}, s32[8]{0:T(128)}, u32[]{:S(2)}, u32[]{:S(2)}) collective-permute-start(s32[8]{0:T(128)} %tenants.1), channel_id=1, source_target_pairs={{0,8},{8,0},{1,9},{9,1},{2,10},{10,2},{3,11},{11,3},{4,12},{12,4},... | collective-permute-start | bytes 104 | tf_op jit(solution)/shard_map/ppermute | solution.py:325
  27.7 95.1 %all-reduce.2.cloned.1.call-start = ((), (), s32[]{:S(2)}) async-start(), calls=%async_computation.1 | async-start | bytes 524288 | tf_op jit(solution)/shard_map/psum | solution.py:344
  27.7 43.9 %collective-permute-start = (bf16[512,1024]{1,0:T(8,128)(2,1)}, bf16[512,1024]{1,0:T(8,128)(2,1)}, u32[]{:S(2)}, u32[]{:S(2)}) collective-permute-start(bf16[512,1024]{1,0:T(8,128)(2,1)} %shard_map.114.refs_3_), channel_id=1, source_target_pairs={{0,1},{1,0},{2,3},{3,2},{4,5},{5,4},{6,7},{7,6},{8,9},{9,8},{10,11... | collective-permute-start | bytes 3145736 | tf_op jit(solution)/shard_map/ppermute | solution.py:291
  28.3 138.0 %all-gather.5.cloned.1.call-start = ((), (), s32[]{:S(2)}) async-start(), calls=%async_computation.2 | async-start | bytes 6291456 | tf_op jit(solution)/shard_map/all_gather | solution.py:320
  28.4 7.4 %copy-start.15 = (s32[16]{0:T(128)S(1)}, s32[16]{0:T(128)}, u32[]{:S(2)}) copy-start(s32[16]{0:T(128)} %param.17) | copy-start | bytes 196
  28.4 8.8 %copy-start.13 = (bf16[1024,128]{1,0:T(8,128)(2,1)S(1)}, bf16[1024,128]{1,0:T(8,128)(2,1)}, u32[]{:S(2)}) copy-start(bf16[1024,128]{1,0:T(8,128)(2,1)} %param.11) | copy-start | bytes 786436
  28.4 11.8 %copy-start.14 = (s32[16]{0:T(128)S(1)}, s32[16]{0:T(128)}, u32[]{:S(2)}) copy-start(s32[16]{0:T(128)} %param.16) | copy-start | bytes 196
  32.5 39.1 %collective-permute-start.1 = (bf16[512,1024]{1,0:T(8,128)(2,1)}, bf16[512,1024]{1,0:T(8,128)(2,1)}, u32[]{:S(2)}, u32[]{:S(2)}) collective-permute-start(bf16[512,1024]{1,0:T(8,128)(2,1)} %shard_map.115.refs_5_), channel_id=1, source_target_pairs={{0,2},{1,3},{6,4},{7,5},{2,0},{3,1},{4,6},{5,7},{8,10},{9,11},{14,... | collective-permute-start | bytes 3145736 | tf_op jit(solution)/shard_map/ppermute | solution.py:294
  40.5 0.5 copy-start.11
  52.4 38.5 %collective-permute-start.9 = (bf16[512,1024]{1,0:T(8,128)(2,1)}, bf16[512,1024]{1,0:T(8,128)(2,1)}, u32[]{:S(2)}, u32[]{:S(2)}) collective-permute-start(bf16[512,1024]{1,0:T(8,128)(2,1)} %shard_map.116.refs_3_), channel_id=1, source_target_pairs={{2,4},{4,2},{0,16},{6,22},{3,5},{5,3},{1,17},{7,23},{18,20},{20,18... | collective-permute-start | bytes 3145736 | tf_op jit(solution)/shard_map/ppermute | solution.py:310
  54.2 54.3 %collective-permute-start.7 = (bf16[512,1024]{1,0:T(8,128)(2,1)}, bf16[512,1024]{1,0:T(8,128)(2,1)}, u32[]{:S(2)}, u32[]{:S(2)}) collective-permute-start(bf16[512,1024]{1,0:T(8,128)(2,1)} %shard_map.116.refs_3_), channel_id=1, source_target_pairs={{0,2},{1,3},{6,4},{7,5},{2,0},{3,1},{4,6},{5,7},{8,10},{9,11},{14,... | collective-permute-start | bytes 3145736 | tf_op jit(solution)/shard_map/ppermute | solution.py:294
  58.3 31.3 %collective-permute-start.6 = (bf16[512,1024]{1,0:T(8,128)(2,1)}, bf16[512,1024]{1,0:T(8,128)(2,1)}, u32[]{:S(2)}, u32[]{:S(2)}) collective-permute-start(bf16[512,1024]{1,0:T(8,128)(2,1)} %shard_map.117.refs_5_), channel_id=1, source_target_pairs={{0,1},{1,0},{2,3},{3,2},{4,5},{5,4},{6,7},{7,6},{8,9},{9,8},{10,11... | collective-permute-start | bytes 3145736 | tf_op jit(solution)/shard_map/ppermute | solution.py:291
  76.1 42.2 %collective-permute-start.5 = (bf16[512,1024]{1,0:T(8,128)(2,1)}, bf16[512,1024]{1,0:T(8,128)(2,1)}, u32[]{:S(2)}, u32[]{:S(2)}) collective-permute-start(bf16[512,1024]{1,0:T(8,128)(2,1)} %shard_map.118.refs_3_), channel_id=1, source_target_pairs={{2,4},{4,2},{0,16},{6,22},{3,5},{5,3},{1,17},{7,23},{18,20},{20,18... | collective-permute-start | bytes 3145736 | tf_op jit(solution)/shard_map/ppermute | solution.py:310
  77.7 50.8 %collective-permute-start.11 = (bf16[512,1024]{1,0:T(8,128)(2,1)}, bf16[512,1024]{1,0:T(8,128)(2,1)}, u32[]{:S(2)}, u32[]{:S(2)}) collective-permute-start(bf16[512,1024]{1,0:T(8,128)(2,1)} %shard_map.118.refs_3_), channel_id=1, source_target_pairs={{0,2},{1,3},{6,4},{7,5},{2,0},{3,1},{4,6},{5,7},{8,10},{9,11},{14,... | collective-permute-start | bytes 3145736 | tf_op jit(solution)/shard_map/ppermute | solution.py:294
  89.6 27.1 %collective-permute-start.4 = (bf16[512,1024]{1,0:T(8,128)(2,1)}, bf16[512,1024]{1,0:T(8,128)(2,1)}, u32[]{:S(2)}, u32[]{:S(2)}) collective-permute-start(bf16[512,1024]{1,0:T(8,128)(2,1)} %shard_map.119.refs_5_), channel_id=1, source_target_pairs={{0,1},{1,0},{2,3},{3,2},{4,5},{5,4},{6,7},{7,6},{8,9},{9,8},{10,11... | collective-permute-start | bytes 3145736 | tf_op jit(solution)/shard_map/ppermute | solution.py:291
  90.9 4.9 %copy-start.12 = (f32[16]{0:T(128)S(1)}, f32[16]{0:T(128)}, u32[]{:S(2)}) copy-start(f32[16]{0:T(128)} %copy-done.11) | copy-start | bytes 196
  95.4 51.2 %collective-permute-start.14 = (bf16[512,1024]{1,0:T(8,128)(2,1)}, bf16[512,1024]{1,0:T(8,128)(2,1)}, u32[]{:S(2)}, u32[]{:S(2)}) collective-permute-start(bf16[512,1024]{1,0:T(8,128)(2,1)} %shard_map.120.refs_0_), channel_id=1, source_target_pairs={{0,2},{1,3},{6,4},{7,5},{2,0},{3,1},{4,6},{5,7},{8,10},{9,11},{14,... | collective-permute-start | bytes 3145736 | tf_op jit(solution)/shard_map/ppermute | solution.py:294
  95.8 2.2 %copy-start.6 = (bf16[2048,1024]{1,0:T(8,128)(2,1)S(1)}, bf16[2048,1024]{1,0:T(8,128)(2,1)}, u32[]{:S(2)}) copy-start(bf16[2048,1024]{1,0:T(8,128)(2,1)} %all-gather.3.cloned.1.call-done.right) | copy-start | bytes 12582916
  102.2 2.2 %copy-start.9 = (f32[8,128,1024]{2,1,0:T(8,128)S(1)}, f32[8,128,1024]{2,1,0:T(8,128)}, u32[]{:S(2)}) copy-start(f32[8,128,1024]{2,1,0:T(8,128)} %shard_map.121.refs_3_) | copy-start | bytes 12582916
  108.5 33.3 %collective-permute-start.13 = (bf16[512,1024]{1,0:T(8,128)(2,1)}, bf16[512,1024]{1,0:T(8,128)(2,1)}, u32[]{:S(2)}, u32[]{:S(2)}) collective-permute-start(bf16[512,1024]{1,0:T(8,128)(2,1)} %shard_map.122.refs_5_), channel_id=1, source_target_pairs={{0,1},{1,0},{2,3},{3,2},{4,5},{5,4},{6,7},{7,6},{8,9},{9,8},{10,11... | collective-permute-start | bytes 3145736 | tf_op jit(solution)/shard_map/ppermute | solution.py:291
  116.7 23.3 %collective-permute-start.15 = (bf16[512,1024]{1,0:T(8,128)(2,1)}, bf16[512,1024]{1,0:T(8,128)(2,1)}, u32[]{:S(2)}, u32[]{:S(2)}) collective-permute-start(bf16[512,1024]{1,0:T(8,128)(2,1)} %shard_map.123.refs_5_), channel_id=1, source_target_pairs={{2,4},{4,2},{0,16},{6,22},{3,5},{5,3},{1,17},{7,23},{18,20},{20,18... | collective-permute-start | bytes 3145736 | tf_op jit(solution)/shard_map/ppermute | solution.py:310
  122.8 43.5 %collective-permute-start.10 = (bf16[512,1024]{1,0:T(8,128)(2,1)}, bf16[512,1024]{1,0:T(8,128)(2,1)}, u32[]{:S(2)}, u32[]{:S(2)}) collective-permute-start(bf16[512,1024]{1,0:T(8,128)(2,1)} %shard_map.124.link), channel_id=1, source_target_pairs={{0,2},{1,3},{6,4},{7,5},{2,0},{3,1},{4,6},{5,7},{8,10},{9,11},{14,... | collective-permute-start | bytes 3145736 | tf_op jit(solution)/shard_map/ppermute | solution.py:294
  122.8 1.0 copy-start.8
  124.3 9.9 %copy-start.2 = (bf16[1024,128]{1,0:T(8,128)(2,1)}, bf16[1024,128]{1,0:T(8,128)(2,1)S(1)}, u32[]{:S(2)}) copy-start(bf16[1024,128]{1,0:T(8,128)(2,1)S(1)} %shard_map.125.refs_3_.refs_5_.refs_4_) | copy-start | bytes 786436
  128.5 50.1 %collective-permute-start.17 = (bf16[512,1024]{1,0:T(8,128)(2,1)}, bf16[512,1024]{1,0:T(8,128)(2,1)}, u32[]{:S(2)}, u32[]{:S(2)}) collective-permute-start(bf16[512,1024]{1,0:T(8,128)(2,1)} %shard_map.126.refs_5_), channel_id=1, source_target_pairs={{0,1},{1,0},{2,3},{3,2},{4,5},{5,4},{6,7},{7,6},{8,9},{9,8},{10,11... | collective-permute-start | bytes 3145736 | tf_op jit(solution)/shard_map/ppermute | solution.py:291
  140.0 22.5 %collective-permute-start.12 = (bf16[512,1024]{1,0:T(8,128)(2,1)}, bf16[512,1024]{1,0:T(8,128)(2,1)}, u32[]{:S(2)}, u32[]{:S(2)}) collective-permute-start(bf16[512,1024]{1,0:T(8,128)(2,1)} %shard_map.127.refs_6_), channel_id=1, source_target_pairs={{2,4},{4,2},{0,16},{6,22},{3,5},{5,3},{1,17},{7,23},{18,20},{20,18... | collective-permute-start | bytes 3145736 | tf_op jit(solution)/shard_map/ppermute | solution.py:310
  146.6 39.8 %collective-permute-start.18 = (bf16[512,1024]{1,0:T(8,128)(2,1)}, bf16[512,1024]{1,0:T(8,128)(2,1)}, u32[]{:S(2)}, u32[]{:S(2)}) collective-permute-start(bf16[512,1024]{1,0:T(8,128)(2,1)} %shard_map.128.refs_4_), channel_id=1, source_target_pairs={{0,2},{1,3},{6,4},{7,5},{2,0},{3,1},{4,6},{5,7},{8,10},{9,11},{14,... | collective-permute-start | bytes 3145736 | tf_op jit(solution)/shard_map/ppermute | solution.py:294
  150.9 35.2 %collective-permute-start.16 = (bf16[512,1024]{1,0:T(8,128)(2,1)}, bf16[512,1024]{1,0:T(8,128)(2,1)}, u32[]{:S(2)}, u32[]{:S(2)}) collective-permute-start(bf16[512,1024]{1,0:T(8,128)(2,1)} %shard_map.129.refs_5_), channel_id=1, source_target_pairs={{0,1},{1,0},{2,3},{3,2},{4,5},{5,4},{6,7},{7,6},{8,9},{9,8},{10,11... | collective-permute-start | bytes 3145736 | tf_op jit(solution)/shard_map/ppermute | solution.py:291
  162.6 23.5 %collective-permute-start.19 = (bf16[512,1024]{1,0:T(8,128)(2,1)}, bf16[512,1024]{1,0:T(8,128)(2,1)}, u32[]{:S(2)}, u32[]{:S(2)}) collective-permute-start(bf16[512,1024]{1,0:T(8,128)(2,1)} %shard_map.130.refs_0_), channel_id=1, source_target_pairs={{2,4},{3,5},{4,2},{5,3},{10,12},{11,13},{12,10},{13,11},{18,20},{1... | collective-permute-start | bytes 3145736 | tf_op jit(solution)/shard_map/ppermute | solution.py:294
  166.3 2.2 %copy-start.7 = (bf16[2048,1024]{1,0:T(8,128)(2,1)S(1)}, bf16[2048,1024]{1,0:T(8,128)(2,1)}, u32[]{:S(2)}) copy-start(bf16[2048,1024]{1,0:T(8,128)(2,1)} %all-gather.5.cloned.1.call-done.left) | copy-start | bytes 12582916
  168.5 4.0 %copy-start.3 = (bf16[1024,128]{1,0:T(8,128)(2,1)S(1)}, bf16[1024,128]{1,0:T(8,128)(2,1)}, u32[]{:S(2)}) copy-start(bf16[1024,128]{1,0:T(8,128)(2,1)} %copy-done.2) | copy-start | bytes 786436
  168.5 4.0 %copy-start.5 = (bf16[16,1024,128]{2,1,0:T(8,128)(2,1)S(1)}, bf16[16,1024,128]{2,1,0:T(8,128)(2,1)}, u32[]{:S(2)}) copy-start(bf16[16,1024,128]{2,1,0:T(8,128)(2,1)} %refs_8_.3) | copy-start | bytes 12582916
  172.4 2.2 %copy-start.10 = (f32[8,1024,128]{2,1,0:T(8,128)S(1)}, f32[8,1024,128]{2,1,0:T(8,128)}, u32[]{:S(2)}) copy-start(f32[8,1024,128]{2,1,0:T(8,128)} %shard_map.131.refs_10_) | copy-start | bytes 12582916
Sparse Core Ops, SparseCore 0:
  10.4 15.0 all-gather.2
  34.2 15.0 all-gather.4
Sparse Core Ops, SparseCore 1:
  31.5 72.4 all-reduce.1

commit v9 on v8

--- a/solution.py
+++ b/solution.py
@@ -133,45 +133,50 @@
     )(scalars, gradient, weights)
 
 
-def finish_kernel(counts, *refs):
-    out = refs[-1]
+def finish_kernel(counts, inner, *refs):
+    out, staged, done = refs[-3:]
+    rows = refs[0].shape[0]
+    part = rows // 2
+    copies = []
     position = 0
     for piece, count in enumerate(counts):
-
-        @pl.when(pl.program_id(0) == piece)
-        def _():
-            total = refs[position][...].astype(f32)
+        for half in range(2):
+            here = slice(half * part, (half + 1) * part)
+            total = refs[position][here, :].astype(f32)
             for i in range(1, count):
-                total = total + refs[position + i][...].astype(f32)
-            out[...] = total.astype(out.dtype)
-
+                addend = refs[position + i][here, :].astype(f32)
+                if piece and i == count - 1:
+                    addend = addend * inner[0].astype(f32)
+                total = total + addend
+            index = 2 * piece + half
+            staged[index] = total.astype(staged.dtype)
+            copy = pltpu.make_async_copy(
+                staged.at[index], out.at[pl.ds(index * part, part), :], done.at[index]
+            )
+            copy.start()
+            copies.append(copy)
         position += count
-
-
-def finish(groups, link):
-    piece_rows, width = groups[0][0].shape
-    tile = width // 2
-
-    def place(piece):
-        def index(p, j):
-            return (0, jnp.where(p == piece, j, jnp.where(p < piece, 0, 1)))
-
-        return index
-
-    in_specs = [
-        pl.BlockSpec((piece_rows, tile), place(piece))
-        for piece, group in enumerate(groups)
-        for _ in group
-    ]
+    for copy in copies:
+        copy.wait()
+
+
+def finish(inner, groups):
+    rows, width = groups[0][0].shape
+    arrays = [array for group in groups for array in group]
+    parts = 2 * len(groups)
     return pl.pallas_call(
         functools.partial(finish_kernel, tuple(len(group) for group in groups)),
-        grid=(len(groups), 2),
-        in_specs=in_specs + [pl.BlockSpec(memory_space=pl.ANY)] * len(link),
-        out_specs=pl.BlockSpec((piece_rows, tile), lambda p, j: (p, j)),
-        out_shape=jax.ShapeDtypeStruct((len(groups) * piece_rows, width), bf16),
+        in_specs=[pl.BlockSpec(memory_space=pltpu.SMEM)]
+        + [pl.BlockSpec(memory_space=pltpu.VMEM)] * len(arrays),
+        out_specs=pl.BlockSpec(memory_space=pl.ANY),
+        out_shape=jax.ShapeDtypeStruct((len(groups) * rows, width), bf16),
+        scratch_shapes=[
+            pltpu.VMEM((parts, rows // 2, width), bf16),
+            pltpu.SemaphoreType.DMA((parts,)),
+        ],
         compiler_params=params(),
         cost_estimate=declared,
-    )(*[array for group in groups for array in group], *link)
+    )(inner, *arrays)
 
 
 def low_kernel(tenants, rows, expand, link, out):
@@ -407,7 +412,7 @@
     )
     both_5 = along(out, pairwise)
     y7 = swap(run(node, other, lower, [(both_3, 1)]), every)
-    upper_4 = along(run(beyond, same, upper, [(y5, 0), (both_3, 0)]), across)
+    upper_4 = exchange(run(beyond, same, upper, [(y5, 0), (both_3, 0)]))
     link += [both_4, lower_4]
     grad_shrink = shrink_gradient(low)
     def base(piece, adds):
@@ -423,7 +428,8 @@
 
     lower_base = base(lower, [(both_4, 0), (lower_4, 2)])
     upper_base = base(upper, [(y6, 0)])
-    input_gradient = finish([[lower_base, y7], [upper_base, both_5, upper_4]], [])
+    inner = jnp.reshape(roles[1].astype(jnp.int32), (1,))
+    input_gradient = finish(inner, [[lower_base, y7], [upper_base, both_5, upper_4]])
     return (input_gradient, grad_shrink, grad_expand)
 
 

time: 201 us -> 201 us (level)
  waiting for transfers between devices: 45.2 us -> 40.6 us
  Pallas kernels: 97.4 us -> 101 us
    pallas_call x2, Pallas kernels: 8.06 us -> 13.5 us  [factor_sums(): pl.pallas_call(functools.partial(factor_kernel, slots_each), in_specs=[pl...]
    ppermute x7, waiting for transfers between devices: 14.6 us -> 11.8 us  [swap(): return lax.ppermute(x, 'tensor', pairs)]
    ppermute x8 -> x7, starting transfers between devices: 6.13 us -> 3.52 us  [along(): lax.ppermute(x, 'tensor', [(2 * a + y, 2 * b + y) for a, b in hops for y...]
    ppermute x8 -> x7, waiting for transfers between devices: 20.4 us -> 18.1 us  [along(): lax.ppermute(x, 'tensor', [(2 * a + y, 2 * b + y) for a, b in hops for y...]
    ppermute x4 -> x5, starting transfers between devices: 6.67 us -> 8.42 us  [exchange(): return lax.ppermute(x, ('groups', 'tensor'), pairs)]
    ppermute x4 -> x5, waiting for transfers between devices: 9.48 us -> 9.88 us  [exchange(): return lax.ppermute(x, ('groups', 'tensor'), pairs)]
  transfers between devices with their start and end apart: 23 -> 23, of which waited for: 9 -> 10; matrix products, arithmetic and copies ran while one was open for 2% -> 2% of each run, Pallas kernels for 47% -> 50%
where the time goes in v9:
time: 201 us; the launch traced here: 197 us
  Pallas kernels  101 us (50%)
  waiting for transfers between devices  40.6 us (20%)
  starting transfers between devices  18.8 us (9%)
  between operations  15.7 us (8%)
  local copies, waits for them, and re-layouts  14.7 us (7%)
  blocking collectives  4.35 us (2%)
    pallas_call x17, Pallas kernels, product(): pl.pallas_call(functools.partial(product_kernel, tuple((mode for _, mode...  72.8 us
    ppermute x7, waiting for transfers between devices, along(): lax.ppermute(x, 'tensor', [(2 * a + y, 2 * b + y) for a, b in hops for y...  18.1 us
    pallas_call x2, Pallas kernels, factor_sums(): pl.pallas_call(functools.partial(factor_kernel, slots_each), in_specs=[pl...  13.5 us
    unnamed x32, local copies, waits for them, and re-layouts  11.8 us
    ppermute x7, waiting for transfers between devices, swap(): return lax.ppermute(x, 'tensor', pairs)  11.8 us
    ppermute x5, waiting for transfers between devices, exchange(): return lax.ppermute(x, ('groups', 'tensor'), pairs)  9.88 us
    ppermute x5, starting transfers between devices, exchange(): return lax.ppermute(x, ('groups', 'tensor'), pairs)  8.42 us
    pallas_call x1, Pallas kernels, product_pair(): pl.pallas_call(pair_kernel, grid_spec=pltpu.PrefetchScalarGridSpec(num_sc...  6.9 us
  transfers between devices with their start and end apart: 23, of which 10 were waited for; matrix products, arithmetic and copies ran while one was open for 2% of the time, Pallas kernels for 50%

profile of v9, /device:TPU:10, one launch (start us, length us, event | category | flops | bytes accessed | tf_op | source)
XLA Modules:
  0.0 197.2 jit_solution(642575031430731912)
XLA Ops:
  8.9 1.6 copy-done
  10.5 6.9 %shard_map.112 = (bf16[512,1024]{1,0:T(8,128)(2,1)}, bf16[512,1024]{1,0:T(8,128)(2,1)}) custom-call(s32[4]{0:T(128)S(1)} %get-tuple-element.11.scalars, bf16[1024,1024]{1,0:T(8,128)(2,1)S(1)} %copy-done, bf16[8192,1024]{1,0:T(8,128)(2,1)} %refs_2_.33), custom_call_target="tpu_custom_call" | custom-call | flops 999999995904 | bytes 1000000000 | tf_op jit(solution)/shard_map/pallas_call | solution.py:116
  17.4 1.5 collective-permute-start.2
  19.3 4.3 %shard_map.113.refs_3_ = bf16[1024,128]{1,0:T(8,128)(2,1)} custom-call(s32[8]{0:T(128)} %tenants.1, bf16[1024,1024]{1,0:T(8,128)(2,1)S(1)} %copy-done.1, bf16[16,128,1024]{2,1,0:T(8,128)(2,1)S(1)} %copy-done.4, bf16[512,1024]{1,0:T(8,128)(2,1)} %get-tuple-element.5.link), custom_call_target="tpu_custom_call" | custom-call | flops 999999995904 | bytes 1000000000 | tf_op jit(solution)/shard_map/pallas_call | solution.py:191
  23.6 4.1 %shard_map.114.refs_3_ = bf16[512,1024]{1,0:T(8,128)(2,1)} custom-call(s32[4]{0:T(128)S(1)} %get-tuple-element.12.refs_0_, bf16[1024,1024]{1,0:T(8,128)(2,1)S(1)} %copy-done.1, bf16[8192,1024]{1,0:T(8,128)(2,1)} %refs_2_.33, bf16[1024,128]{1,0:T(8,128)(2,1)} %shard_map.113.refs_3_), custom_call_target="tpu_custom_call" | custom-call | flops 999999995904 | bytes 1000000000 | tf_op jit(solution)/shard_map/pallas_call | solution.py:84
  28.4 4.1 %shard_map.115.refs_5_ = bf16[512,1024]{1,0:T(8,128)(2,1)} custom-call(s32[4]{0:T(128)S(1)} %fusion.24.refs_0_, bf16[1024,1024]{1,0:T(8,128)(2,1)S(1)} %copy-done.1, bf16[8192,1024]{1,0:T(8,128)(2,1)} %refs_2_.33, bf16[512,1024]{1,0:T(8,128)(2,1)} %shard_map.114.refs_3_), custom_call_target="tpu_custom_call" | custom-call | flops 999999995904 | bytes 1000000000 | tf_op jit(solution)/shard_map/pallas_call | solution.py:84
  32.5 1.6 collective-permute-start.1
  37.2 2.2 %all_gather.12 = bf16[2048,128]{1,0:T(8,128)(2,1)S(1)} all-gather(bf16[1024,128]{1,0:T(8,128)(2,1)S(1)} %copy-done.13), channel_id=1, replica_groups=mesh['groups'=2,'dp'=2,'tensor'=8] {'dp'}, dimensions={0}, use_global_device_ids=true | all-gather | bytes 786432 | tf_op jit(solution)/shard_map/all_gather | solution.py:325
  41.2 3.6 %collective-permute-done.2.refs_3_.refs_4_ = bf16[512,1024]{1,0:T(8,128)(2,1)} collective-permute-done((bf16[512,1024]{1,0:T(8,128)(2,1)}, bf16[512,1024]{1,0:T(8,128)(2,1)}, u32[]{:S(2)}, u32[]{:S(2)}) %collective-permute-start.2) | collective-permute-done | bytes 1048608 | tf_op jit(solution)/shard_map/ppermute | solution.py:296
  44.8 3.2 %collective-permute-done.3.refs_4_ = bf16[512,1024]{1,0:T(8,128)(2,1)} collective-permute-done((bf16[512,1024]{1,0:T(8,128)(2,1)}, bf16[512,1024]{1,0:T(8,128)(2,1)}, u32[]{:S(2)}, u32[]{:S(2)}) %collective-permute-start.3) | collective-permute-done | bytes 1048608 | tf_op jit(solution)/shard_map/ppermute | solution.py:299
  48.0 4.4 %shard_map.116.refs_3_ = bf16[512,1024]{1,0:T(8,128)(2,1)} custom-call(s32[4]{0:T(128)S(1)} %add_add_fusion.refs_0_, bf16[1024,1024]{1,0:T(8,128)(2,1)S(1)} %copy-done.1, bf16[8192,1024]{1,0:T(8,128)(2,1)} %refs_2_.33, bf16[512,1024]{1,0:T(8,128)(2,1)} %collective-permute-done.2.refs_3_.refs_4_, bf16[512,1024]{1,0:T(8,128)(2,1)} %collective-permute-done.3.refs_4_, ...), custom_call_target="tpu_custom_call" | custom-call | flops 999999995904 | bytes 1000000000 | tf_op jit(solution)/shard_map/pallas_call | solution.py:84
  52.5 1.7 collective-permute-start.9
  54.2 4.1 %shard_map.117.refs_5_ = bf16[512,1024]{1,0:T(8,128)(2,1)} custom-call(s32[4]{0:T(128)S(1)} %fusion.4.refs_0_, bf16[1024,1024]{1,0:T(8,128)(2,1)S(1)} %copy-done.1, bf16[8192,1024]{1,0:T(8,128)(2,1)} %refs_2_.33, bf16[512,1024]{1,0:T(8,128)(2,1)} %shard_map.116.refs_3_), custom_call_target="tpu_custom_call" | custom-call | flops 999999995904 | bytes 1000000000 | tf_op jit(solution)/shard_map/pallas_call | solution.py:84
  58.4 13.2 %collective-permute-done.1.refs_4_ = bf16[512,1024]{1,0:T(8,128)(2,1)} collective-permute-done((bf16[512,1024]{1,0:T(8,128)(2,1)}, bf16[512,1024]{1,0:T(8,128)(2,1)}, u32[]{:S(2)}, u32[]{:S(2)}) %collective-permute-start.1) | collective-permute-done | bytes 1048608 | tf_op jit(solution)/shard_map/ppermute | solution.py:299
  71.6 4.5 %shard_map.118.refs_3_ = bf16[512,1024]{1,0:T(8,128)(2,1)} custom-call(s32[4]{0:T(128)S(1)} %fusion.20.refs_0_, bf16[1024,1024]{1,0:T(8,128)(2,1)S(1)} %copy-done.1, bf16[8192,1024]{1,0:T(8,128)(2,1)} %refs_2_.33, bf16[512,1024]{1,0:T(8,128)(2,1)} %collective-permute-done.refs_3_, bf16[512,1024]{1,0:T(8,128)(2,1)} %collective-permute-done.1.refs_4_, ...), custom_call_target="tpu_custom_call" | custom-call | flops 999999995904 | bytes 1000000000 | tf_op jit(solution)/shard_map/pallas_call | solution.py:84
  76.1 1.6 collective-permute-start.5
  77.7 4.1 %shard_map.119.refs_5_ = bf16[512,1024]{1,0:T(8,128)(2,1)} custom-call(s32[4]{0:T(128)S(1)} %fusion.18.refs_0_, bf16[1024,1024]{1,0:T(8,128)(2,1)S(1)} %copy-done.1, bf16[8192,1024]{1,0:T(8,128)(2,1)} %refs_2_.33, bf16[512,1024]{1,0:T(8,128)(2,1)} %shard_map.118.refs_3_), custom_call_target="tpu_custom_call" | custom-call | flops 999999995904 | bytes 1000000000 | tf_op jit(solution)/shard_map/pallas_call | solution.py:84
  81.8 7.8 %collective-permute-done.6.refs_3_ = bf16[512,1024]{1,0:T(8,128)(2,1)} collective-permute-done((bf16[512,1024]{1,0:T(8,128)(2,1)}, bf16[512,1024]{1,0:T(8,128)(2,1)}, u32[]{:S(2)}, u32[]{:S(2)}) %collective-permute-start.6) | collective-permute-done | bytes 1048608 | tf_op jit(solution)/shard_map/ppermute | solution.py:296
  89.6 1.3 collective-permute-start.4
  90.9 4.4 %shard_map.120.refs_0_ = bf16[512,1024]{1,0:T(8,128)(2,1)} custom-call(s32[4]{0:T(128)S(1)} %add_add_fusion.1.refs_0_, bf16[1024,1024]{1,0:T(8,128)(2,1)S(1)} %copy-done.1, bf16[8192,1024]{1,0:T(8,128)(2,1)} %refs_2_.33, bf16[512,1024]{1,0:T(8,128)(2,1)} %collective-permute-done.6.refs_3_, bf16[512,1024]{1,0:T(8,128)(2,1)} %collective-permute-done.9.refs_4_, ...), custom_call_target="tpu_custom_call" | custom-call | flops 999999995904 | bytes 1000000000 | tf_op jit(solution)/shard_map/pallas_call | solution.py:84
  95.9 2.2 %copy-done.6 = bf16[2048,1024]{1,0:T(8,128)(2,1)S(1)} copy-done((bf16[2048,1024]{1,0:T(8,128)(2,1)S(1)}, bf16[2048,1024]{1,0:T(8,128)(2,1)}, u32[]{:S(2)}) %copy-start.6) | copy-done | bytes 4194328
  98.0 6.8 %shard_map.121.refs_3_ = f32[8,128,1024]{2,1,0:T(8,128)} custom-call(s32[16]{0:T(128)S(1)} %get-tuple-element.8.slots, f32[16]{0:T(128)S(1)} %copy-done.12, bf16[2048,128]{1,0:T(8,128)(2,1)S(1)} %bitcast_multiply_fusion.left, bf16[2048,1024]{1,0:T(8,128)(2,1)S(1)} %copy-done.6, bf16[512,1024]{1,0:T(8,128)(2,1)} %shard_map.120.refs_0_), custom_call_target="tpu_custom_call" | custom-call | flops 999999995904 | bytes 1000000000 | tf_op jit(solution)/shard_map/pallas_call | solution.py:247
  104.8 2.2 %copy-done.9 = f32[8,128,1024]{2,1,0:T(8,128)S(1)} copy-done((f32[8,128,1024]{2,1,0:T(8,128)S(1)}, f32[8,128,1024]{2,1,0:T(8,128)}, u32[]{:S(2)}) %copy-start.9) | copy-done | bytes 4194328
  107.0 4.1 %shard_map.122.refs_5_ = bf16[512,1024]{1,0:T(8,128)(2,1)} custom-call(s32[4]{0:T(128)S(1)} %fusion.8.refs_0_, bf16[1024,1024]{1,0:T(8,128)(2,1)S(1)} %copy-done.1, bf16[8192,1024]{1,0:T(8,128)(2,1)} %refs_2_.33, f32[8,128,1024]{2,1,0:T(8,128)S(1)} %copy-done.9), custom_call_target="tpu_custom_call" | custom-call | flops 999999995904 | bytes 1000000000 | tf_op jit(solution)/shard_map/pallas_call | solution.py:84
  111.9 4.4 %shard_map.123.refs_5_ = bf16[512,1024]{1,0:T(8,128)(2,1)} custom-call(s32[4]{0:T(128)S(1)} %fusion.6.refs_0_, bf16[1024,1024]{1,0:T(8,128)(2,1)S(1)} %copy-done.1, bf16[8192,1024]{1,0:T(8,128)(2,1)} %refs_2_.33, bf16[512,1024]{1,0:T(8,128)(2,1)} %collective-permute-done.6.refs_3_, bf16[512,1024]{1,0:T(8,128)(2,1)} %collective-permute-done.7.refs_4_, ...), custom_call_target="tpu_custom_call" | custom-call | flops 999999995904 | bytes 1000000000 | tf_op jit(solution)/shard_map/pallas_call | solution.py:84
  116.7 2.3 %collective-permute-start.15 = (bf16[512,1024]{1,0:T(8,128)(2,1)}, bf16[512,1024]{1,0:T(8,128)(2,1)}, u32[]{:S(2)}, u32[]{:S(2)}) collective-permute-start(bf16[512,1024]{1,0:T(8,128)(2,1)} %shard_map.123.refs_5_), channel_id=1, source_target_pairs={{2,4},{4,2},{0,16},{6,22},{3,5},{5,3},{1,17},{7,23},{18,20},{20,18... | collective-permute-start | bytes 3145736 | tf_op jit(solution)/shard_map/ppermute | solution.py:315
  119.0 4.5 %shard_map.124.link = bf16[512,1024]{1,0:T(8,128)(2,1)} custom-call(s32[4]{0:T(128)S(1)} %fusion.16.refs_0_, bf16[1024,1024]{1,0:T(8,128)(2,1)S(1)} %copy-done.1, bf16[8192,1024]{1,0:T(8,128)(2,1)} %refs_2_.33, bf16[512,1024]{1,0:T(8,128)(2,1)} %collective-permute-done.4.refs_3_, bf16[512,1024]{1,0:T(8,128)(2,1)} %collective-permute-done.5.refs_4_, ...), custom_call_target="tpu_custom_call" | custom-call | flops 999999995904 | bytes 1000000000 | tf_op jit(solution)/shard_map/pallas_call | solution.py:84
  125.1 4.1 %shard_map.126.refs_5_ = bf16[512,1024]{1,0:T(8,128)(2,1)} custom-call(s32[4]{0:T(128)S(1)} %fusion.10.refs_0_, bf16[1024,1024]{1,0:T(8,128)(2,1)S(1)} %copy-done.1, bf16[8192,1024]{1,0:T(8,128)(2,1)} %refs_2_.33, bf16[1024,128]{1,0:T(8,128)(2,1)S(1)} %shard_map.125.refs_3_.refs_5_.refs_4_), custom_call_target="tpu_custom_call" | custom-call | flops 999999995904 | bytes 1000000000 | tf_op jit(solution)/shard_map/pallas_call | solution.py:84
  129.2 1.3 collective-permute-start.17
  130.5 4.5 %shard_map.127.refs_6_ = bf16[512,1024]{1,0:T(8,128)(2,1)} custom-call(s32[4]{0:T(128)S(1)} %fusion.26.refs_0_, bf16[1024,1024]{1,0:T(8,128)(2,1)S(1)} %copy-done.1, bf16[8192,1024]{1,0:T(8,128)(2,1)} %refs_2_.33, bf16[512,1024]{1,0:T(8,128)(2,1)} %collective-permute-done.4.refs_3_, bf16[512,1024]{1,0:T(8,128)(2,1)} %collective-permute-done.11.refs_4_, ...), custom_call_target="tpu_custom_call" | custom-call | flops 999999995904 | bytes 1000000000 | tf_op jit(solution)/shard_map/pallas_call | solution.py:84
  135.0 2.2 %all_gather.15.right = bf16[2048,128]{1,0:T(8,128)(2,1)S(1)} all-gather(bf16[1024,128]{1,0:T(8,128)(2,1)S(1)} %shard_map.125.refs_3_.refs_5_.refs_4_), channel_id=1, replica_groups=mesh['groups'=2,'dp'=2,'tensor'=8] {'dp'}, dimensions={0}, use_global_device_ids=true | all-gather | bytes 786432 | tf_op jit(solution)/shard_map/all_gather | solution.py:325
  137.2 1.2 collective-permute-done.15.refs_5_
  138.4 1.5 collective-permute-start.12
  139.9 4.8 %shard_map.128.refs_4_ = bf16[512,1024]{1,0:T(8,128)(2,1)} custom-call(s32[4]{0:T(128)S(1)} %fusion.14.refs_0_, bf16[1024,1024]{1,0:T(8,128)(2,1)S(1)} %copy-done.1, bf16[8192,1024]{1,0:T(8,128)(2,1)} %refs_2_.33, bf16[512,1024]{1,0:T(8,128)(2,1)} %collective-permute-done.13.refs_3_, bf16[512,1024]{1,0:T(8,128)(2,1)} %collective-permute-done.2.refs_3_.refs_4_, ...), custom_call_target="tpu_custom_call" | custom-call | flops 999999995904 | bytes 1000000000 | tf_op jit(solution)/shard_map/pallas_call | solution.py:84
  144.7 1.0 collective-permute-start.18
  145.7 4.3 %shard_map.129.refs_5_ = bf16[512,1024]{1,0:T(8,128)(2,1)} custom-call(s32[4]{0:T(128)S(1)} %fusion.28.refs_0_, bf16[1024,1024]{1,0:T(8,128)(2,1)S(1)} %copy-done.1, bf16[8192,1024]{1,0:T(8,128)(2,1)} %refs_2_.33, bf16[512,1024]{1,0:T(8,128)(2,1)} %collective-permute-done.14.refs_3_.refs_4_, bf16[512,1024]{1,0:T(8,128)(2,1)} %shard_map.128.refs_4_), custom_call_target="tpu_custom_call" | custom-call | flops 999999995904 | bytes 1000000000 | tf_op jit(solution)/shard_map/pallas_call | solution.py:84
  150.0 1.3 collective-permute-start.16
  151.3 4.5 %shard_map.130.refs_0_ = bf16[512,1024]{1,0:T(8,128)(2,1)} custom-call(s32[4]{0:T(128)S(1)} %fusion.12.refs_0_, bf16[1024,1024]{1,0:T(8,128)(2,1)S(1)} %copy-done.1, bf16[8192,1024]{1,0:T(8,128)(2,1)} %refs_2_.33, bf16[512,1024]{1,0:T(8,128)(2,1)} %collective-permute-done.13.refs_3_, bf16[512,1024]{1,0:T(8,128)(2,1)} %collective-permute-done.14.refs_3_.refs_4_, ...), custom_call_target="tpu_custom_call" | custom-call | flops 999999995904 | bytes 1000000000 | tf_op jit(solution)/shard_map/pallas_call | solution.py:84
  155.8 6.8 %collective-permute-done.12.refs_2_.refs_4_ = bf16[512,1024]{1,0:T(8,128)(2,1)} collective-permute-done((bf16[512,1024]{1,0:T(8,128)(2,1)}, bf16[512,1024]{1,0:T(8,128)(2,1)}, u32[]{:S(2)}, u32[]{:S(2)}) %collective-permute-start.12) | collective-permute-done | bytes 1048608 | tf_op jit(solution)/shard_map/ppermute | solution.py:315
  162.7 1.3 collective-permute-start.19
  164.0 1.4 collective-permute-done.10.refs_1_.refs_3_
  165.4 2.2 %copy-done.7 = bf16[2048,1024]{1,0:T(8,128)(2,1)S(1)} copy-done((bf16[2048,1024]{1,0:T(8,128)(2,1)S(1)}, bf16[2048,1024]{1,0:T(8,128)(2,1)}, u32[]{:S(2)}) %copy-start.7) | copy-done | bytes 4194328
  167.6 6.7 %shard_map.131.refs_10_ = f32[8,1024,128]{2,1,0:T(8,128)} custom-call(s32[16]{0:T(128)S(1)} %get-tuple-element.8.slots, f32[16]{0:T(128)S(1)} %broadcast_4_scales.2.scales, bf16[2048,1024]{1,0:T(8,128)(2,1)S(1)} %copy-done.7, bf16[2048,128]{1,0:T(8,128)(2,1)S(1)} %all_gather.15.right, bf16[512,1024]{1,0:T(8,128)(2,1)} %shard_map.130.refs_0_, ...), custom_call_target="tpu_custom_call" | custom-call | flops 999999995904 | bytes 1000000000 | tf_op jit(solution)/shard_map/pallas_call | solution.py:247
  174.3 2.2 %copy-done.10 = f32[8,1024,128]{2,1,0:T(8,128)S(1)} copy-done((f32[8,1024,128]{2,1,0:T(8,128)S(1)}, f32[8,1024,128]{2,1,0:T(8,128)}, u32[]{:S(2)}) %copy-start.10) | copy-done | bytes 4194328
  176.5 4.0 %shard_map.132.refs_9_.refs_0_ = bf16[512,1024]{1,0:T(8,128)(2,1)S(1)} custom-call(s32[8]{0:T(128)S(1)} %stack.72.refs_0_, bf16[1024,1024]{1,0:T(8,128)(2,1)S(1)} %copy-done.1, bf16[8192,1024]{1,0:T(8,128)(2,1)} %refs_2_.33, bf16[512,1024]{1,0:T(8,128)(2,1)} %collective-permute-done.10.refs_1_.refs_3_, ...), custom_call_target="tpu_custom_call" | custom-call | flops 999999995904 | bytes 1000000000 | tf_op jit(solution)/shard_map/pallas_call | solution.py:84
  180.4 3.8 %shard_map.133.refs_2_ = bf16[512,1024]{1,0:T(8,128)(2,1)S(1)} custom-call(s32[8]{0:T(128)S(1)} %stack.175.refs_0_, bf16[1024,1024]{1,0:T(8,128)(2,1)S(1)} %copy-done.1, bf16[8192,1024]{1,0:T(8,128)(2,1)} %refs_2_.33, bf16[512,1024]{1,0:T(8,128)(2,1)} %collective-permute-done.17.refs_3_, bf16[1024,128]{1,0:T(8,128)(2,1)S(1)} %copy-done.3, ...), custom_call_target="tpu_custom_call" | custom-call | flops 999999995904 | bytes 1000000000 | tf_op jit(solution)/shard_map/pallas_call | solution.py:84
  184.2 1.8 collective-permute-done.19.refs_4_
  186.4 3.4 %shard_map.134 = bf16[1024,1024]{1,0:T(8,128)(2,1)} custom-call(s32[1]{0:T(128)} %bitcast.inner, bf16[512,1024]{1,0:T(8,128)(2,1)S(1)} %shard_map.132.refs_9_.refs_0_, bf16[512,1024]{1,0:T(8,128)(2,1)} %collective-permute-done.16.refs_1_, bf16[512,1024]{1,0:T(8,128)(2,1)S(1)} %shard_map.133.refs_2_, bf16[512,1024]{1,0:T(8,128)(2,1)} %collective-permute-done.18.refs_3_, ...), custom_call_target="tpu_custom_call" | custom-call | flops 999999995904 | bytes 1000000000 | tf_op jit(solution)/shard_map/pallas_call | solution.py:167
  (89 shorter events, 10.4 us)
Async XLA Ops:
  8.0 87.9 %all-gather.3.cloned.1.call-start = ((), (), s32[]{:S(2)}) async-start(), calls=%async_computation | async-start | bytes 6291456 | tf_op jit(solution)/shard_map/all_gather | solution.py:325
  8.9 1.6 copy-start
  10.5 8.9 %copy-start.1 = (bf16[1024,1024]{1,0:T(8,128)(2,1)S(1)}, bf16[1024,1024]{1,0:T(8,128)(2,1)}, u32[]{:S(2)}) copy-start(bf16[1024,1024]{1,0:T(8,128)(2,1)} %refs_1_.33) | copy-start | bytes 6291460
  10.5 8.9 %copy-start.4 = (bf16[16,128,1024]{2,1,0:T(8,128)(2,1)S(1)}, bf16[16,128,1024]{2,1,0:T(8,128)(2,1)}, u32[]{:S(2)}) copy-start(bf16[16,128,1024]{2,1,0:T(8,128)(2,1)} %expand.1) | copy-start | bytes 12582916
  17.4 27.4 %collective-permute-start.2 = (bf16[512,1024]{1,0:T(8,128)(2,1)}, bf16[512,1024]{1,0:T(8,128)(2,1)}, u32[]{:S(2)}, u32[]{:S(2)}) collective-permute-start(bf16[512,1024]{1,0:T(8,128)(2,1)} %get-tuple-element.6), channel_id=1, source_target_pairs={{0,1},{1,0},{2,3},{3,2},{4,5},{5,4},{6,7},{7,6},{8,9},{9,8},{10,11... | collective-permute-start | bytes 3145736 | tf_op jit(solution)/shard_map/ppermute | solution.py:296
  18.9 29.1 %collective-permute-start.3 = (bf16[512,1024]{1,0:T(8,128)(2,1)}, bf16[512,1024]{1,0:T(8,128)(2,1)}, u32[]{:S(2)}, u32[]{:S(2)}) collective-permute-start(bf16[512,1024]{1,0:T(8,128)(2,1)} %get-tuple-element.5.link), channel_id=1, source_target_pairs={{0,2},{1,3},{6,4},{7,5},{2,0},{3,1},{4,6},{5,7},{8,10},{9,11},{14,... | collective-permute-start | bytes 3145736 | tf_op jit(solution)/shard_map/ppermute | solution.py:299
  19.3 20.0 %collective-permute-start.8 = (s32[8]{0:T(128)}, s32[8]{0:T(128)}, u32[]{:S(2)}, u32[]{:S(2)}) collective-permute-start(s32[8]{0:T(128)} %tenants.1), channel_id=1, source_target_pairs={{0,8},{8,0},{1,9},{9,1},{2,10},{10,2},{3,11},{11,3},{4,12},{12,4},... | collective-permute-start | bytes 104 | tf_op jit(solution)/shard_map/ppermute | solution.py:330
  27.7 95.8 %all-reduce.2.cloned.1.call-start = ((), (), s32[]{:S(2)}) async-start(), calls=%async_computation.1 | async-start | bytes 524288 | tf_op jit(solution)/shard_map/psum | solution.py:349
  27.7 43.9 %collective-permute-start = (bf16[512,1024]{1,0:T(8,128)(2,1)}, bf16[512,1024]{1,0:T(8,128)(2,1)}, u32[]{:S(2)}, u32[]{:S(2)}) collective-permute-start(bf16[512,1024]{1,0:T(8,128)(2,1)} %shard_map.114.refs_3_), channel_id=1, source_target_pairs={{0,1},{1,0},{2,3},{3,2},{4,5},{5,4},{6,7},{7,6},{8,9},{9,8},{10,11... | collective-permute-start | bytes 3145736 | tf_op jit(solution)/shard_map/ppermute | solution.py:296
  28.3 135.7 %all-gather.5.cloned.1.call-start = ((), (), s32[]{:S(2)}) async-start(), calls=%async_computation.2 | async-start | bytes 6291456 | tf_op jit(solution)/shard_map/all_gather | solution.py:325
  28.4 7.4 %copy-start.15 = (s32[16]{0:T(128)S(1)}, s32[16]{0:T(128)}, u32[]{:S(2)}) copy-start(s32[16]{0:T(128)} %param.17) | copy-start | bytes 196
  28.4 8.8 %copy-start.13 = (bf16[1024,128]{1,0:T(8,128)(2,1)S(1)}, bf16[1024,128]{1,0:T(8,128)(2,1)}, u32[]{:S(2)}) copy-start(bf16[1024,128]{1,0:T(8,128)(2,1)} %param.11) | copy-start | bytes 786436
  28.4 11.8 %copy-start.14 = (s32[16]{0:T(128)S(1)}, s32[16]{0:T(128)}, u32[]{:S(2)}) copy-start(s32[16]{0:T(128)} %param.16) | copy-start | bytes 196
  32.5 39.1 %collective-permute-start.1 = (bf16[512,1024]{1,0:T(8,128)(2,1)}, bf16[512,1024]{1,0:T(8,128)(2,1)}, u32[]{:S(2)}, u32[]{:S(2)}) collective-permute-start(bf16[512,1024]{1,0:T(8,128)(2,1)} %shard_map.115.refs_5_), channel_id=1, source_target_pairs={{0,2},{1,3},{6,4},{7,5},{2,0},{3,1},{4,6},{5,7},{8,10},{9,11},{14,... | collective-permute-start | bytes 3145736 | tf_op jit(solution)/shard_map/ppermute | solution.py:299
  40.5 0.6 copy-start.11
  52.5 38.5 %collective-permute-start.9 = (bf16[512,1024]{1,0:T(8,128)(2,1)}, bf16[512,1024]{1,0:T(8,128)(2,1)}, u32[]{:S(2)}, u32[]{:S(2)}) collective-permute-start(bf16[512,1024]{1,0:T(8,128)(2,1)} %shard_map.116.refs_3_), channel_id=1, source_target_pairs={{2,4},{4,2},{0,16},{6,22},{3,5},{5,3},{1,17},{7,23},{18,20},{20,18... | collective-permute-start | bytes 3145736 | tf_op jit(solution)/shard_map/ppermute | solution.py:315
  54.2 56.9 %collective-permute-start.7 = (bf16[512,1024]{1,0:T(8,128)(2,1)}, bf16[512,1024]{1,0:T(8,128)(2,1)}, u32[]{:S(2)}, u32[]{:S(2)}) collective-permute-start(bf16[512,1024]{1,0:T(8,128)(2,1)} %shard_map.116.refs_3_), channel_id=1, source_target_pairs={{0,2},{1,3},{6,4},{7,5},{2,0},{3,1},{4,6},{5,7},{8,10},{9,11},{14,... | collective-permute-start | bytes 3145736 | tf_op jit(solution)/shard_map/ppermute | solution.py:299
  58.3 31.4 %collective-permute-start.6 = (bf16[512,1024]{1,0:T(8,128)(2,1)}, bf16[512,1024]{1,0:T(8,128)(2,1)}, u32[]{:S(2)}, u32[]{:S(2)}) collective-permute-start(bf16[512,1024]{1,0:T(8,128)(2,1)} %shard_map.117.refs_5_), channel_id=1, source_target_pairs={{0,1},{1,0},{2,3},{3,2},{4,5},{5,4},{6,7},{7,6},{8,9},{9,8},{10,11... | collective-permute-start | bytes 3145736 | tf_op jit(solution)/shard_map/ppermute | solution.py:296
  76.1 42.9 %collective-permute-start.5 = (bf16[512,1024]{1,0:T(8,128)(2,1)}, bf16[512,1024]{1,0:T(8,128)(2,1)}, u32[]{:S(2)}, u32[]{:S(2)}) collective-permute-start(bf16[512,1024]{1,0:T(8,128)(2,1)} %shard_map.118.refs_3_), channel_id=1, source_target_pairs={{2,4},{4,2},{0,16},{6,22},{3,5},{5,3},{1,17},{7,23},{18,20},{20,18... | collective-permute-start | bytes 3145736 | tf_op jit(solution)/shard_map/ppermute | solution.py:315
  77.7 51.5 %collective-permute-start.11 = (bf16[512,1024]{1,0:T(8,128)(2,1)}, bf16[512,1024]{1,0:T(8,128)(2,1)}, u32[]{:S(2)}, u32[]{:S(2)}) collective-permute-start(bf16[512,1024]{1,0:T(8,128)(2,1)} %shard_map.118.refs_3_), channel_id=1, source_target_pairs={{0,2},{1,3},{6,4},{7,5},{2,0},{3,1},{4,6},{5,7},{8,10},{9,11},{14,... | collective-permute-start | bytes 3145736 | tf_op jit(solution)/shard_map/ppermute | solution.py:299
  89.6 27.1 %collective-permute-start.4 = (bf16[512,1024]{1,0:T(8,128)(2,1)}, bf16[512,1024]{1,0:T(8,128)(2,1)}, u32[]{:S(2)}, u32[]{:S(2)}) collective-permute-start(bf16[512,1024]{1,0:T(8,128)(2,1)} %shard_map.119.refs_5_), channel_id=1, source_target_pairs={{0,1},{1,0},{2,3},{3,2},{4,5},{5,4},{6,7},{7,6},{8,9},{9,8},{10,11... | collective-permute-start | bytes 3145736 | tf_op jit(solution)/shard_map/ppermute | solution.py:296
  90.9 4.9 %copy-start.12 = (f32[16]{0:T(128)S(1)}, f32[16]{0:T(128)}, u32[]{:S(2)}) copy-start(f32[16]{0:T(128)} %copy-done.11) | copy-start | bytes 196
  95.4 50.4 %collective-permute-start.14 = (bf16[512,1024]{1,0:T(8,128)(2,1)}, bf16[512,1024]{1,0:T(8,128)(2,1)}, u32[]{:S(2)}, u32[]{:S(2)}) collective-permute-start(bf16[512,1024]{1,0:T(8,128)(2,1)} %shard_map.120.refs_0_), channel_id=1, source_target_pairs={{0,2},{1,3},{6,4},{7,5},{2,0},{3,1},{4,6},{5,7},{8,10},{9,11},{14,... | collective-permute-start | bytes 3145736 | tf_op jit(solution)/shard_map/ppermute | solution.py:299
  95.8 2.2 %copy-start.6 = (bf16[2048,1024]{1,0:T(8,128)(2,1)S(1)}, bf16[2048,1024]{1,0:T(8,128)(2,1)}, u32[]{:S(2)}) copy-start(bf16[2048,1024]{1,0:T(8,128)(2,1)} %all-gather.3.cloned.1.call-done.right) | copy-start | bytes 12582916
  104.8 2.2 %copy-start.9 = (f32[8,128,1024]{2,1,0:T(8,128)S(1)}, f32[8,128,1024]{2,1,0:T(8,128)}, u32[]{:S(2)}) copy-start(f32[8,128,1024]{2,1,0:T(8,128)} %shard_map.121.refs_3_) | copy-start | bytes 12582916
  111.1 28.8 %collective-permute-start.13 = (bf16[512,1024]{1,0:T(8,128)(2,1)}, bf16[512,1024]{1,0:T(8,128)(2,1)}, u32[]{:S(2)}, u32[]{:S(2)}) collective-permute-start(bf16[512,1024]{1,0:T(8,128)(2,1)} %shard_map.122.refs_5_), channel_id=1, source_target_pairs={{0,1},{1,0},{2,3},{3,2},{4,5},{5,4},{6,7},{7,6},{8,9},{9,8},{10,11... | collective-permute-start | bytes 3145736 | tf_op jit(solution)/shard_map/ppermute | solution.py:296
  116.7 21.6 %collective-permute-start.15 = (bf16[512,1024]{1,0:T(8,128)(2,1)}, bf16[512,1024]{1,0:T(8,128)(2,1)}, u32[]{:S(2)}, u32[]{:S(2)}) collective-permute-start(bf16[512,1024]{1,0:T(8,128)(2,1)} %shard_map.123.refs_5_), channel_id=1, source_target_pairs={{2,4},{4,2},{0,16},{6,22},{3,5},{5,3},{1,17},{7,23},{18,20},{20,18... | collective-permute-start | bytes 3145736 | tf_op jit(solution)/shard_map/ppermute | solution.py:315
  123.5 41.9 %collective-permute-start.10 = (bf16[512,1024]{1,0:T(8,128)(2,1)}, bf16[512,1024]{1,0:T(8,128)(2,1)}, u32[]{:S(2)}, u32[]{:S(2)}) collective-permute-start(bf16[512,1024]{1,0:T(8,128)(2,1)} %shard_map.124.link), channel_id=1, source_target_pairs={{0,2},{1,3},{6,4},{7,5},{2,0},{3,1},{4,6},{5,7},{8,10},{9,11},{14,... | collective-permute-start | bytes 3145736 | tf_op jit(solution)/shard_map/ppermute | solution.py:299
  123.5 1.0 copy-start.8
  125.1 9.9 %copy-start.2 = (bf16[1024,128]{1,0:T(8,128)(2,1)}, bf16[1024,128]{1,0:T(8,128)(2,1)S(1)}, u32[]{:S(2)}) copy-start(bf16[1024,128]{1,0:T(8,128)(2,1)S(1)} %shard_map.125.refs_3_.refs_5_.refs_4_) | copy-start | bytes 786436
  129.2 51.3 %collective-permute-start.17 = (bf16[512,1024]{1,0:T(8,128)(2,1)}, bf16[512,1024]{1,0:T(8,128)(2,1)}, u32[]{:S(2)}, u32[]{:S(2)}) collective-permute-start(bf16[512,1024]{1,0:T(8,128)(2,1)} %shard_map.126.refs_5_), channel_id=1, source_target_pairs={{0,1},{1,0},{2,3},{3,2},{4,5},{5,4},{6,7},{7,6},{8,9},{9,8},{10,11... | collective-permute-start | bytes 3145736 | tf_op jit(solution)/shard_map/ppermute | solution.py:296
  138.4 24.3 %collective-permute-start.12 = (bf16[512,1024]{1,0:T(8,128)(2,1)}, bf16[512,1024]{1,0:T(8,128)(2,1)}, u32[]{:S(2)}, u32[]{:S(2)}) collective-permute-start(bf16[512,1024]{1,0:T(8,128)(2,1)} %shard_map.127.refs_6_), channel_id=1, source_target_pairs={{2,4},{4,2},{0,16},{6,22},{3,5},{5,3},{1,17},{7,23},{18,20},{20,18... | collective-permute-start | bytes 3145736 | tf_op jit(solution)/shard_map/ppermute | solution.py:315
  144.7 41.7 %collective-permute-start.18 = (bf16[512,1024]{1,0:T(8,128)(2,1)}, bf16[512,1024]{1,0:T(8,128)(2,1)}, u32[]{:S(2)}, u32[]{:S(2)}) collective-permute-start(bf16[512,1024]{1,0:T(8,128)(2,1)} %shard_map.128.refs_4_), channel_id=1, source_target_pairs={{0,2},{1,3},{6,4},{7,5},{2,0},{3,1},{4,6},{5,7},{8,10},{9,11},{14,... | collective-permute-start | bytes 3145736 | tf_op jit(solution)/shard_map/ppermute | solution.py:299
  150.0 36.0 %collective-permute-start.16 = (bf16[512,1024]{1,0:T(8,128)(2,1)}, bf16[512,1024]{1,0:T(8,128)(2,1)}, u32[]{:S(2)}, u32[]{:S(2)}) collective-permute-start(bf16[512,1024]{1,0:T(8,128)(2,1)} %shard_map.129.refs_5_), channel_id=1, source_target_pairs={{0,1},{1,0},{2,3},{3,2},{4,5},{5,4},{6,7},{7,6},{8,9},{9,8},{10,11... | collective-permute-start | bytes 3145736 | tf_op jit(solution)/shard_map/ppermute | solution.py:296
  162.7 23.4 %collective-permute-start.19 = (bf16[512,1024]{1,0:T(8,128)(2,1)}, bf16[512,1024]{1,0:T(8,128)(2,1)}, u32[]{:S(2)}, u32[]{:S(2)}) collective-permute-start(bf16[512,1024]{1,0:T(8,128)(2,1)} %shard_map.130.refs_0_), channel_id=1, source_target_pairs={{2,4},{4,2},{0,16},{6,22},{3,5},{5,3},{1,17},{7,23},{18,20},{20,18... | collective-permute-start | bytes 3145736 | tf_op jit(solution)/shard_map/ppermute | solution.py:315
  165.4 2.2 %copy-start.7 = (bf16[2048,1024]{1,0:T(8,128)(2,1)S(1)}, bf16[2048,1024]{1,0:T(8,128)(2,1)}, u32[]{:S(2)}) copy-start(bf16[2048,1024]{1,0:T(8,128)(2,1)} %all-gather.5.cloned.1.call-done.left) | copy-start | bytes 12582916
  167.6 6.7 %copy-start.3 = (bf16[1024,128]{1,0:T(8,128)(2,1)S(1)}, bf16[1024,128]{1,0:T(8,128)(2,1)}, u32[]{:S(2)}) copy-start(bf16[1024,128]{1,0:T(8,128)(2,1)} %copy-done.2) | copy-start | bytes 786436
  167.6 6.7 %copy-start.5 = (bf16[16,1024,128]{2,1,0:T(8,128)(2,1)S(1)}, bf16[16,1024,128]{2,1,0:T(8,128)(2,1)}, u32[]{:S(2)}) copy-start(bf16[16,1024,128]{2,1,0:T(8,128)(2,1)} %refs_8_.3) | copy-start | bytes 12582916
  174.3 2.2 %copy-start.10 = (f32[8,1024,128]{2,1,0:T(8,128)S(1)}, f32[8,1024,128]{2,1,0:T(8,128)}, u32[]{:S(2)}) copy-start(f32[8,1024,128]{2,1,0:T(8,128)} %shard_map.131.refs_10_) | copy-start | bytes 12582916
Sparse Core Ops, SparseCore 0:
  10.4 15.0 all-gather.2
  34.2 15.0 all-gather.4
Sparse Core Ops, SparseCore 1:
  31.5 72.3 all-reduce.1

commit v10 on v9

--- a/solution.py
+++ b/solution.py
@@ -399,14 +399,14 @@
         [(y3, 1), (direct_a, 2)],
     )
     both_3 = along(out, pairwise)
+    upper_far = exchange(run(far, same, upper, [(y3, 0), (upper_1, 0)]))
     grad_expand = expand_gradient()
     y5 = swap(run(jnp.where(at_end, nearer, beyond), other, upper, []), every)
-    upper_far = exchange(run(far, same, upper, [(y3, 0), (upper_1, 0)]))
     out = run(jnp.where(at_end, nearer, near_end), same, lower, [(y4, 1), (direct_b, 2)])
     both_4 = along(out, pairwise)
+    lower_4 = exchange(run(beyond, same, lower, [(y4, 0), (lower_2, 0)]))
     low = scale_low(low_whole)
     y6 = swap(run(node, other, upper, []), every)
-    lower_4 = exchange(run(beyond, same, lower, [(y4, 0), (lower_2, 0)]))
     out = run(
         jnp.where(at_end, nearer, near_end), same, upper, [(y5, 1), (y1, 2), (upper_far, 2)]
     )

time: 201 us -> 199 us (0.990)
  waiting for transfers between devices: 40.6 us -> 43.9 us
  Pallas kernels: 101 us -> 98.4 us
    ppermute x5, waiting for transfers between devices: 9.88 us -> 0.01 us  [exchange(): return lax.ppermute(x, ('groups', 'tensor'), pairs)]
    ppermute x7, waiting for transfers between devices: 18.1 us -> 26.5 us  [along(): lax.ppermute(x, 'tensor', [(2 * a + y, 2 * b + y) for a, b in hops for y...]
    ppermute x7, waiting for transfers between devices: 11.8 us -> 16.7 us  [swap(): return lax.ppermute(x, 'tensor', pairs)]
    pallas_call x2, Pallas kernels: 13.5 us -> 10.5 us  [factor_sums(): pl.pallas_call(functools.partial(factor_kernel, slots_each), in_specs=[pl...]
  transfers between devices with their start and end apart: 23 -> 23, of which waited for: 10 -> 9; matrix products, arithmetic and copies ran while one was open for 2% -> 2% of each run, Pallas kernels for 50% -> 48%
where the time goes in v10:
time: 199 us; the launch traced here: 197 us
  Pallas kernels  98.4 us (49%)
  waiting for transfers between devices  43.9 us (22%)
  starting transfers between devices  18.5 us (9%)
  between operations  15.7 us (8%)
  local copies, waits for them, and re-layouts  14.6 us (7%)
  blocking collectives  4.35 us (2%)
    pallas_call x17, Pallas kernels, product(): pl.pallas_call(functools.partial(product_kernel, tuple((mode for _, mode...  72.8 us
    ppermute x7, waiting for transfers between devices, along(): lax.ppermute(x, 'tensor', [(2 * a + y, 2 * b + y) for a, b in hops for y...  26.5 us
    ppermute x7, waiting for transfers between devices, swap(): return lax.ppermute(x, 'tensor', pairs)  16.7 us
    unnamed x32, local copies, waits for them, and re-layouts  11.8 us
    pallas_call x2, Pallas kernels, factor_sums(): pl.pallas_call(functools.partial(factor_kernel, slots_each), in_specs=[pl...  10.5 us
    ppermute x5, starting transfers between devices, exchange(): return lax.ppermute(x, ('groups', 'tensor'), pairs)  10.3 us
    pallas_call x1, Pallas kernels, product_pair(): pl.pallas_call(pair_kernel, grid_spec=pltpu.PrefetchScalarGridSpec(num_sc...  6.9 us
    ppermute x7, starting transfers between devices, swap(): return lax.ppermute(x, 'tensor', pairs)  5.56 us
  transfers between devices with their start and end apart: 23, of which 9 were waited for; matrix products, arithmetic and copies ran while one was open for 2% of the time, Pallas kernels for 48%

profile of v10, /device:TPU:10, one launch (start us, length us, event | category | flops | bytes accessed | tf_op | source)
XLA Modules:
  0.0 197.2 jit_solution(15785101804568731030)
XLA Ops:
  8.9 1.6 copy-done
  10.5 6.9 %shard_map.112 = (bf16[512,1024]{1,0:T(8,128)(2,1)}, bf16[512,1024]{1,0:T(8,128)(2,1)}) custom-call(s32[4]{0:T(128)S(1)} %get-tuple-element.11.scalars, bf16[1024,1024]{1,0:T(8,128)(2,1)S(1)} %copy-done, bf16[8192,1024]{1,0:T(8,128)(2,1)} %refs_2_.33), custom_call_target="tpu_custom_call" | custom-call | flops 999999995904 | bytes 1000000000 | tf_op jit(solution)/shard_map/pallas_call | solution.py:116
  17.4 1.5 collective-permute-start.2
  19.3 4.3 %shard_map.113.refs_3_ = bf16[1024,128]{1,0:T(8,128)(2,1)} custom-call(s32[8]{0:T(128)} %tenants.1, bf16[1024,1024]{1,0:T(8,128)(2,1)S(1)} %copy-done.1, bf16[16,128,1024]{2,1,0:T(8,128)(2,1)S(1)} %copy-done.4, bf16[512,1024]{1,0:T(8,128)(2,1)} %get-tuple-element.5.link), custom_call_target="tpu_custom_call" | custom-call | flops 999999995904 | bytes 1000000000 | tf_op jit(solution)/shard_map/pallas_call | solution.py:191
  23.6 4.1 %shard_map.114.refs_3_ = bf16[512,1024]{1,0:T(8,128)(2,1)} custom-call(s32[4]{0:T(128)S(1)} %get-tuple-element.12.refs_0_, bf16[1024,1024]{1,0:T(8,128)(2,1)S(1)} %copy-done.1, bf16[8192,1024]{1,0:T(8,128)(2,1)} %refs_2_.33, bf16[1024,128]{1,0:T(8,128)(2,1)} %shard_map.113.refs_3_), custom_call_target="tpu_custom_call" | custom-call | flops 999999995904 | bytes 1000000000 | tf_op jit(solution)/shard_map/pallas_call | solution.py:84
  28.4 4.1 %shard_map.115.refs_5_ = bf16[512,1024]{1,0:T(8,128)(2,1)} custom-call(s32[4]{0:T(128)S(1)} %fusion.24.refs_0_, bf16[1024,1024]{1,0:T(8,128)(2,1)S(1)} %copy-done.1, bf16[8192,1024]{1,0:T(8,128)(2,1)} %refs_2_.33, bf16[512,1024]{1,0:T(8,128)(2,1)} %shard_map.114.refs_3_), custom_call_target="tpu_custom_call" | custom-call | flops 999999995904 | bytes 1000000000 | tf_op jit(solution)/shard_map/pallas_call | solution.py:84
  32.5 1.6 collective-permute-start.1
  36.1 0.8 dynamic_update_slice.10
  37.1 2.2 %all_gather.12 = bf16[2048,128]{1,0:T(8,128)(2,1)S(1)} all-gather(bf16[1024,128]{1,0:T(8,128)(2,1)S(1)} %copy-done.13), channel_id=1, replica_groups=mesh['groups'=2,'dp'=2,'tensor'=8] {'dp'}, dimensions={0}, use_global_device_ids=true | all-gather | bytes 786432 | tf_op jit(solution)/shard_map/all_gather | solution.py:325
  39.3 0.9 dynamic_update_slice.11
  41.1 3.6 %collective-permute-done.2.refs_3_.refs_4_ = bf16[512,1024]{1,0:T(8,128)(2,1)} collective-permute-done((bf16[512,1024]{1,0:T(8,128)(2,1)}, bf16[512,1024]{1,0:T(8,128)(2,1)}, u32[]{:S(2)}, u32[]{:S(2)}) %collective-permute-start.2) | collective-permute-done | bytes 1048608 | tf_op jit(solution)/shard_map/ppermute | solution.py:296
  44.8 3.2 %collective-permute-done.3.refs_4_ = bf16[512,1024]{1,0:T(8,128)(2,1)} collective-permute-done((bf16[512,1024]{1,0:T(8,128)(2,1)}, bf16[512,1024]{1,0:T(8,128)(2,1)}, u32[]{:S(2)}, u32[]{:S(2)}) %collective-permute-start.3) | collective-permute-done | bytes 1048608 | tf_op jit(solution)/shard_map/ppermute | solution.py:299
  48.0 4.4 %shard_map.116.refs_3_ = bf16[512,1024]{1,0:T(8,128)(2,1)} custom-call(s32[4]{0:T(128)S(1)} %add_add_fusion.refs_0_, bf16[1024,1024]{1,0:T(8,128)(2,1)S(1)} %copy-done.1, bf16[8192,1024]{1,0:T(8,128)(2,1)} %refs_2_.33, bf16[512,1024]{1,0:T(8,128)(2,1)} %collective-permute-done.2.refs_3_.refs_4_, bf16[512,1024]{1,0:T(8,128)(2,1)} %collective-permute-done.3.refs_4_, ...), custom_call_target="tpu_custom_call" | custom-call | flops 999999995904 | bytes 1000000000 | tf_op jit(solution)/shard_map/pallas_call | solution.py:84
  52.4 1.8 collective-permute-start.9
  54.2 4.1 %shard_map.117.refs_5_ = bf16[512,1024]{1,0:T(8,128)(2,1)} custom-call(s32[4]{0:T(128)S(1)} %fusion.4.refs_0_, bf16[1024,1024]{1,0:T(8,128)(2,1)S(1)} %copy-done.1, bf16[8192,1024]{1,0:T(8,128)(2,1)} %refs_2_.33, bf16[512,1024]{1,0:T(8,128)(2,1)} %shard_map.116.refs_3_), custom_call_target="tpu_custom_call" | custom-call | flops 999999995904 | bytes 1000000000 | tf_op jit(solution)/shard_map/pallas_call | solution.py:84
  58.4 13.2 %collective-permute-done.1.refs_4_ = bf16[512,1024]{1,0:T(8,128)(2,1)} collective-permute-done((bf16[512,1024]{1,0:T(8,128)(2,1)}, bf16[512,1024]{1,0:T(8,128)(2,1)}, u32[]{:S(2)}, u32[]{:S(2)}) %collective-permute-start.1) | collective-permute-done | bytes 1048608 | tf_op jit(solution)/shard_map/ppermute | solution.py:299
  71.6 4.5 %shard_map.118.refs_3_ = bf16[512,1024]{1,0:T(8,128)(2,1)} custom-call(s32[4]{0:T(128)S(1)} %fusion.20.refs_0_, bf16[1024,1024]{1,0:T(8,128)(2,1)S(1)} %copy-done.1, bf16[8192,1024]{1,0:T(8,128)(2,1)} %refs_2_.33, bf16[512,1024]{1,0:T(8,128)(2,1)} %collective-permute-done.refs_3_, bf16[512,1024]{1,0:T(8,128)(2,1)} %collective-permute-done.1.refs_4_, ...), custom_call_target="tpu_custom_call" | custom-call | flops 999999995904 | bytes 1000000000 | tf_op jit(solution)/shard_map/pallas_call | solution.py:84
  76.1 1.6 collective-permute-start.5
  77.7 4.1 %shard_map.119.refs_5_ = bf16[512,1024]{1,0:T(8,128)(2,1)} custom-call(s32[4]{0:T(128)S(1)} %fusion.18.refs_0_, bf16[1024,1024]{1,0:T(8,128)(2,1)S(1)} %copy-done.1, bf16[8192,1024]{1,0:T(8,128)(2,1)} %refs_2_.33, bf16[512,1024]{1,0:T(8,128)(2,1)} %shard_map.118.refs_3_), custom_call_target="tpu_custom_call" | custom-call | flops 999999995904 | bytes 1000000000 | tf_op jit(solution)/shard_map/pallas_call | solution.py:84
  81.8 7.8 %collective-permute-done.7.refs_3_ = bf16[512,1024]{1,0:T(8,128)(2,1)} collective-permute-done((bf16[512,1024]{1,0:T(8,128)(2,1)}, bf16[512,1024]{1,0:T(8,128)(2,1)}, u32[]{:S(2)}, u32[]{:S(2)}) %collective-permute-start.7) | collective-permute-done | bytes 1048608 | tf_op jit(solution)/shard_map/ppermute | solution.py:296
  89.6 1.3 collective-permute-start.4
  90.9 4.4 %shard_map.120.refs_5_ = bf16[512,1024]{1,0:T(8,128)(2,1)} custom-call(s32[4]{0:T(128)S(1)} %add_add_fusion.1.refs_0_, bf16[1024,1024]{1,0:T(8,128)(2,1)S(1)} %copy-done.1, bf16[8192,1024]{1,0:T(8,128)(2,1)} %refs_2_.33, bf16[512,1024]{1,0:T(8,128)(2,1)} %collective-permute-done.7.refs_3_, bf16[512,1024]{1,0:T(8,128)(2,1)} %collective-permute-done.9.refs_4_, ...), custom_call_target="tpu_custom_call" | custom-call | flops 999999995904 | bytes 1000000000 | tf_op jit(solution)/shard_map/pallas_call | solution.py:84
  96.2 4.4 %shard_map.121.refs_0_ = bf16[512,1024]{1,0:T(8,128)(2,1)} custom-call(s32[4]{0:T(128)S(1)} %fusion.8.refs_0_, bf16[1024,1024]{1,0:T(8,128)(2,1)S(1)} %copy-done.1, bf16[8192,1024]{1,0:T(8,128)(2,1)} %refs_2_.33, bf16[512,1024]{1,0:T(8,128)(2,1)} %collective-permute-done.7.refs_3_, bf16[512,1024]{1,0:T(8,128)(2,1)} %collective-permute-done.8.refs_4_, ...), custom_call_target="tpu_custom_call" | custom-call | flops 999999995904 | bytes 1000000000 | tf_op jit(solution)/shard_map/pallas_call | solution.py:84
  100.6 2.4 %collective-permute-start.15 = (bf16[512,1024]{1,0:T(8,128)(2,1)}, bf16[512,1024]{1,0:T(8,128)(2,1)}, u32[]{:S(2)}, u32[]{:S(2)}) collective-permute-start(bf16[512,1024]{1,0:T(8,128)(2,1)} %shard_map.121.refs_0_), channel_id=1, source_target_pairs={{2,4},{4,2},{0,16},{6,22},{3,5},{5,3},{1,17},{7,23},{18,20},{20,18... | collective-permute-start | bytes 3145736 | tf_op jit(solution)/shard_map/ppermute | solution.py:315
  103.0 2.2 %copy-done.6 = bf16[2048,1024]{1,0:T(8,128)(2,1)S(1)} copy-done((bf16[2048,1024]{1,0:T(8,128)(2,1)S(1)}, bf16[2048,1024]{1,0:T(8,128)(2,1)}, u32[]{:S(2)}) %copy-start.6) | copy-done | bytes 4194328
  105.2 5.3 %shard_map.122.refs_3_ = f32[8,128,1024]{2,1,0:T(8,128)} custom-call(s32[16]{0:T(128)S(1)} %get-tuple-element.8.slots, f32[16]{0:T(128)S(1)} %copy-done.12, bf16[2048,128]{1,0:T(8,128)(2,1)S(1)} %bitcast_multiply_fusion.left, bf16[2048,1024]{1,0:T(8,128)(2,1)S(1)} %copy-done.6, bf16[512,1024]{1,0:T(8,128)(2,1)} %shard_map.121.refs_0_), custom_call_target="tpu_custom_call" | custom-call | flops 999999995904 | bytes 1000000000 | tf_op jit(solution)/shard_map/pallas_call | solution.py:247
  110.5 2.2 %copy-done.9 = f32[8,128,1024]{2,1,0:T(8,128)S(1)} copy-done((f32[8,128,1024]{2,1,0:T(8,128)S(1)}, f32[8,128,1024]{2,1,0:T(8,128)}, u32[]{:S(2)}) %copy-start.9) | copy-done | bytes 4194328
  112.7 4.1 %shard_map.123.refs_5_ = bf16[512,1024]{1,0:T(8,128)(2,1)} custom-call(s32[4]{0:T(128)S(1)} %fusion.6.refs_0_, bf16[1024,1024]{1,0:T(8,128)(2,1)S(1)} %copy-done.1, bf16[8192,1024]{1,0:T(8,128)(2,1)} %refs_2_.33, f32[8,128,1024]{2,1,0:T(8,128)S(1)} %copy-done.9), custom_call_target="tpu_custom_call" | custom-call | flops 999999995904 | bytes 1000000000 | tf_op jit(solution)/shard_map/pallas_call | solution.py:84
  117.6 4.5 %shard_map.124.refs_5_ = bf16[512,1024]{1,0:T(8,128)(2,1)} custom-call(s32[4]{0:T(128)S(1)} %fusion.16.refs_0_, bf16[1024,1024]{1,0:T(8,128)(2,1)S(1)} %copy-done.1, bf16[8192,1024]{1,0:T(8,128)(2,1)} %refs_2_.33, bf16[512,1024]{1,0:T(8,128)(2,1)} %collective-permute-done.4.refs_3_, bf16[512,1024]{1,0:T(8,128)(2,1)} %collective-permute-done.5.refs_4_, ...), custom_call_target="tpu_custom_call" | custom-call | flops 999999995904 | bytes 1000000000 | tf_op jit(solution)/shard_map/pallas_call | solution.py:84
  122.1 4.5 %shard_map.125.link = bf16[512,1024]{1,0:T(8,128)(2,1)} custom-call(s32[4]{0:T(128)S(1)} %fusion.26.refs_0_, bf16[1024,1024]{1,0:T(8,128)(2,1)S(1)} %copy-done.1, bf16[8192,1024]{1,0:T(8,128)(2,1)} %refs_2_.33, bf16[512,1024]{1,0:T(8,128)(2,1)} %collective-permute-done.4.refs_3_, bf16[512,1024]{1,0:T(8,128)(2,1)} %collective-permute-done.11.refs_4_, ...), custom_call_target="tpu_custom_call" | custom-call | flops 999999995904 | bytes 1000000000 | tf_op jit(solution)/shard_map/pallas_call | solution.py:84
  126.6 1.9 collective-permute-start.12
  128.5 0.9 copy-done.8
  130.1 4.1 %shard_map.127.refs_6_ = bf16[512,1024]{1,0:T(8,128)(2,1)} custom-call(s32[4]{0:T(128)S(1)} %fusion.14.refs_0_, bf16[1024,1024]{1,0:T(8,128)(2,1)S(1)} %copy-done.1, bf16[8192,1024]{1,0:T(8,128)(2,1)} %refs_2_.33, bf16[1024,128]{1,0:T(8,128)(2,1)S(1)} %shard_map.126.refs_3_.refs_5_.refs_4_), custom_call_target="tpu_custom_call" | custom-call | flops 999999995904 | bytes 1000000000 | tf_op jit(solution)/shard_map/pallas_call | solution.py:84
  134.2 2.2 %all_gather.15.right = bf16[2048,128]{1,0:T(8,128)(2,1)S(1)} all-gather(bf16[1024,128]{1,0:T(8,128)(2,1)S(1)} %shard_map.126.refs_3_.refs_5_.refs_4_), channel_id=1, replica_groups=mesh['groups'=2,'dp'=2,'tensor'=8] {'dp'}, dimensions={0}, use_global_device_ids=true | all-gather | bytes 786432 | tf_op jit(solution)/shard_map/all_gather | solution.py:325
  137.1 3.1 %collective-permute-done.13.refs_3_ = bf16[512,1024]{1,0:T(8,128)(2,1)} collective-permute-done((bf16[512,1024]{1,0:T(8,128)(2,1)}, bf16[512,1024]{1,0:T(8,128)(2,1)}, u32[]{:S(2)}, u32[]{:S(2)}) %collective-permute-start.13) | collective-permute-done | bytes 1048608 | tf_op jit(solution)/shard_map/ppermute | solution.py:296
  140.3 4.8 %shard_map.128.refs_4_ = bf16[512,1024]{1,0:T(8,128)(2,1)} custom-call(s32[4]{0:T(128)S(1)} %fusion.12.refs_0_, bf16[1024,1024]{1,0:T(8,128)(2,1)S(1)} %copy-done.1, bf16[8192,1024]{1,0:T(8,128)(2,1)} %refs_2_.33, bf16[512,1024]{1,0:T(8,128)(2,1)} %collective-permute-done.13.refs_3_, bf16[512,1024]{1,0:T(8,128)(2,1)} %collective-permute-done.2.refs_3_.refs_4_, ...), custom_call_target="tpu_custom_call" | custom-call | flops 999999995904 | bytes 1000000000 | tf_op jit(solution)/shard_map/pallas_call | solution.py:84
  145.1 4.3 %shard_map.129.refs_5_ = bf16[512,1024]{1,0:T(8,128)(2,1)} custom-call(s32[4]{0:T(128)S(1)} %fusion.28.refs_0_, bf16[1024,1024]{1,0:T(8,128)(2,1)S(1)} %copy-done.1, bf16[8192,1024]{1,0:T(8,128)(2,1)} %refs_2_.33, bf16[512,1024]{1,0:T(8,128)(2,1)} %collective-permute-done.14.refs_3_.refs_4_, bf16[512,1024]{1,0:T(8,128)(2,1)} %shard_map.128.refs_4_), custom_call_target="tpu_custom_call" | custom-call | flops 999999995904 | bytes 1000000000 | tf_op jit(solution)/shard_map/pallas_call | solution.py:84
  150.0 4.5 %shard_map.130.refs_0_ = bf16[512,1024]{1,0:T(8,128)(2,1)} custom-call(s32[4]{0:T(128)S(1)} %fusion.10.refs_0_, bf16[1024,1024]{1,0:T(8,128)(2,1)S(1)} %copy-done.1, bf16[8192,1024]{1,0:T(8,128)(2,1)} %refs_2_.33, bf16[512,1024]{1,0:T(8,128)(2,1)} %collective-permute-done.13.refs_3_, bf16[512,1024]{1,0:T(8,128)(2,1)} %collective-permute-done.14.refs_3_.refs_4_, ...), custom_call_target="tpu_custom_call" | custom-call | flops 999999995904 | bytes 1000000000 | tf_op jit(solution)/shard_map/pallas_call | solution.py:84
  154.5 2.7 %collective-permute-start.19 = (bf16[512,1024]{1,0:T(8,128)(2,1)}, bf16[512,1024]{1,0:T(8,128)(2,1)}, u32[]{:S(2)}, u32[]{:S(2)}) collective-permute-start(bf16[512,1024]{1,0:T(8,128)(2,1)} %shard_map.130.refs_0_), channel_id=1, source_target_pairs={{2,4},{4,2},{0,16},{6,22},{3,5},{5,3},{1,17},{7,23},{18,20},{20,18... | collective-permute-start | bytes 3145736 | tf_op jit(solution)/shard_map/ppermute | solution.py:315
  157.2 8.2 %collective-permute-done.10.refs_1_.refs_3_ = bf16[512,1024]{1,0:T(8,128)(2,1)} collective-permute-done((bf16[512,1024]{1,0:T(8,128)(2,1)}, bf16[512,1024]{1,0:T(8,128)(2,1)}, u32[]{:S(2)}, u32[]{:S(2)}) %collective-permute-start.10) | collective-permute-done | bytes 1048608 | tf_op jit(solution)/shard_map/ppermute | solution.py:299
  165.4 2.2 %copy-done.7 = bf16[2048,1024]{1,0:T(8,128)(2,1)S(1)} copy-done((bf16[2048,1024]{1,0:T(8,128)(2,1)S(1)}, bf16[2048,1024]{1,0:T(8,128)(2,1)}, u32[]{:S(2)}) %copy-start.7) | copy-done | bytes 4194328
  167.6 5.2 %shard_map.131.refs_10_ = f32[8,1024,128]{2,1,0:T(8,128)} custom-call(s32[16]{0:T(128)S(1)} %get-tuple-element.8.slots, f32[16]{0:T(128)S(1)} %broadcast_4_scales.2.scales, bf16[2048,1024]{1,0:T(8,128)(2,1)S(1)} %copy-done.7, bf16[2048,128]{1,0:T(8,128)(2,1)S(1)} %all_gather.15.right, bf16[512,1024]{1,0:T(8,128)(2,1)} %shard_map.130.refs_0_, ...), custom_call_target="tpu_custom_call" | custom-call | flops 999999995904 | bytes 1000000000 | tf_op jit(solution)/shard_map/pallas_call | solution.py:247
  172.8 2.2 %copy-done.10 = f32[8,1024,128]{2,1,0:T(8,128)S(1)} copy-done((f32[8,1024,128]{2,1,0:T(8,128)S(1)}, f32[8,1024,128]{2,1,0:T(8,128)}, u32[]{:S(2)}) %copy-start.10) | copy-done | bytes 4194328
  174.9 4.0 %shard_map.132.refs_9_.refs_0_ = bf16[512,1024]{1,0:T(8,128)(2,1)S(1)} custom-call(s32[8]{0:T(128)S(1)} %stack.72.refs_0_, bf16[1024,1024]{1,0:T(8,128)(2,1)S(1)} %copy-done.1, bf16[8192,1024]{1,0:T(8,128)(2,1)} %refs_2_.33, bf16[512,1024]{1,0:T(8,128)(2,1)} %collective-permute-done.10.refs_1_.refs_3_, ...), custom_call_target="tpu_custom_call" | custom-call | flops 999999995904 | bytes 1000000000 | tf_op jit(solution)/shard_map/pallas_call | solution.py:84
  178.9 3.8 %shard_map.133.refs_2_ = bf16[512,1024]{1,0:T(8,128)(2,1)S(1)} custom-call(s32[8]{0:T(128)S(1)} %stack.175.refs_0_, bf16[1024,1024]{1,0:T(8,128)(2,1)S(1)} %copy-done.1, bf16[8192,1024]{1,0:T(8,128)(2,1)} %refs_2_.33, bf16[512,1024]{1,0:T(8,128)(2,1)} %collective-permute-done.17.refs_3_, bf16[1024,128]{1,0:T(8,128)(2,1)S(1)} %copy-done.3, ...), custom_call_target="tpu_custom_call" | custom-call | flops 999999995904 | bytes 1000000000 | tf_op jit(solution)/shard_map/pallas_call | solution.py:84
  182.7 2.1 %collective-permute-done.16.refs_1_ = bf16[512,1024]{1,0:T(8,128)(2,1)} collective-permute-done((bf16[512,1024]{1,0:T(8,128)(2,1)}, bf16[512,1024]{1,0:T(8,128)(2,1)}, u32[]{:S(2)}, u32[]{:S(2)}) %collective-permute-start.16) | collective-permute-done | bytes 1048608 | tf_op jit(solution)/shard_map/ppermute | solution.py:296
  184.8 1.6 collective-permute-done.18.refs_3_
  186.4 3.4 %shard_map.134 = bf16[1024,1024]{1,0:T(8,128)(2,1)} custom-call(s32[1]{0:T(128)} %bitcast.inner, bf16[512,1024]{1,0:T(8,128)(2,1)S(1)} %shard_map.132.refs_9_.refs_0_, bf16[512,1024]{1,0:T(8,128)(2,1)} %collective-permute-done.16.refs_1_, bf16[512,1024]{1,0:T(8,128)(2,1)S(1)} %shard_map.133.refs_2_, bf16[512,1024]{1,0:T(8,128)(2,1)} %collective-permute-done.18.refs_3_, ...), custom_call_target="tpu_custom_call" | custom-call | flops 999999995904 | bytes 1000000000 | tf_op jit(solution)/shard_map/pallas_call | solution.py:167
  (89 shorter events, 8.7 us)
Async XLA Ops:
  8.0 95.0 %all-gather.3.cloned.1.call-start = ((), (), s32[]{:S(2)}) async-start(), calls=%async_computation | async-start | bytes 6291456 | tf_op jit(solution)/shard_map/all_gather | solution.py:325
  8.9 1.6 copy-start
  10.5 8.9 %copy-start.1 = (bf16[1024,1024]{1,0:T(8,128)(2,1)S(1)}, bf16[1024,1024]{1,0:T(8,128)(2,1)}, u32[]{:S(2)}) copy-start(bf16[1024,1024]{1,0:T(8,128)(2,1)} %refs_1_.33) | copy-start | bytes 6291460
  10.5 8.9 %copy-start.4 = (bf16[16,128,1024]{2,1,0:T(8,128)(2,1)S(1)}, bf16[16,128,1024]{2,1,0:T(8,128)(2,1)}, u32[]{:S(2)}) copy-start(bf16[16,128,1024]{2,1,0:T(8,128)(2,1)} %expand.1) | copy-start | bytes 12582916
  17.4 27.4 %collective-permute-start.2 = (bf16[512,1024]{1,0:T(8,128)(2,1)}, bf16[512,1024]{1,0:T(8,128)(2,1)}, u32[]{:S(2)}, u32[]{:S(2)}) collective-permute-start(bf16[512,1024]{1,0:T(8,128)(2,1)} %get-tuple-element.6), channel_id=1, source_target_pairs={{0,1},{1,0},{2,3},{3,2},{4,5},{5,4},{6,7},{7,6},{8,9},{9,8},{10,11... | collective-permute-start | bytes 3145736 | tf_op jit(solution)/shard_map/ppermute | solution.py:296
  18.9 29.1 %collective-permute-start.3 = (bf16[512,1024]{1,0:T(8,128)(2,1)}, bf16[512,1024]{1,0:T(8,128)(2,1)}, u32[]{:S(2)}, u32[]{:S(2)}) collective-permute-start(bf16[512,1024]{1,0:T(8,128)(2,1)} %get-tuple-element.5.link), channel_id=1, source_target_pairs={{0,2},{1,3},{6,4},{7,5},{2,0},{3,1},{4,6},{5,7},{8,10},{9,11},{14,... | collective-permute-start | bytes 3145736 | tf_op jit(solution)/shard_map/ppermute | solution.py:299
  19.3 20.0 %collective-permute-start.6 = (s32[8]{0:T(128)}, s32[8]{0:T(128)}, u32[]{:S(2)}, u32[]{:S(2)}) collective-permute-start(s32[8]{0:T(128)} %tenants.1), channel_id=1, source_target_pairs={{0,8},{8,0},{1,9},{9,1},{2,10},{10,2},{3,11},{11,3},{4,12},{12,4},... | collective-permute-start | bytes 104 | tf_op jit(solution)/shard_map/ppermute | solution.py:330
  27.7 100.8 %all-reduce.2.cloned.1.call-start = ((), (), s32[]{:S(2)}) async-start(), calls=%async_computation.1 | async-start | bytes 524288 | tf_op jit(solution)/shard_map/psum | solution.py:349
  27.7 43.9 %collective-permute-start = (bf16[512,1024]{1,0:T(8,128)(2,1)}, bf16[512,1024]{1,0:T(8,128)(2,1)}, u32[]{:S(2)}, u32[]{:S(2)}) collective-permute-start(bf16[512,1024]{1,0:T(8,128)(2,1)} %shard_map.114.refs_3_), channel_id=1, source_target_pairs={{0,1},{1,0},{2,3},{3,2},{4,5},{5,4},{6,7},{7,6},{8,9},{9,8},{10,11... | collective-permute-start | bytes 3145736 | tf_op jit(solution)/shard_map/ppermute | solution.py:296
  28.3 128.9 %all-gather.5.cloned.1.call-start = ((), (), s32[]{:S(2)}) async-start(), calls=%async_computation.2 | async-start | bytes 6291456 | tf_op jit(solution)/shard_map/all_gather | solution.py:325
  28.4 7.4 %copy-start.15 = (s32[16]{0:T(128)S(1)}, s32[16]{0:T(128)}, u32[]{:S(2)}) copy-start(s32[16]{0:T(128)} %param.17) | copy-start | bytes 196
  28.4 8.7 %copy-start.13 = (bf16[1024,128]{1,0:T(8,128)(2,1)S(1)}, bf16[1024,128]{1,0:T(8,128)(2,1)}, u32[]{:S(2)}) copy-start(bf16[1024,128]{1,0:T(8,128)(2,1)} %param.11) | copy-start | bytes 786436
  28.4 11.8 %copy-start.14 = (s32[16]{0:T(128)S(1)}, s32[16]{0:T(128)}, u32[]{:S(2)}) copy-start(s32[16]{0:T(128)} %param.16) | copy-start | bytes 196
  32.5 39.1 %collective-permute-start.1 = (bf16[512,1024]{1,0:T(8,128)(2,1)}, bf16[512,1024]{1,0:T(8,128)(2,1)}, u32[]{:S(2)}, u32[]{:S(2)}) collective-permute-start(bf16[512,1024]{1,0:T(8,128)(2,1)} %shard_map.115.refs_5_), channel_id=1, source_target_pairs={{0,2},{1,3},{6,4},{7,5},{2,0},{3,1},{4,6},{5,7},{8,10},{9,11},{14,... | collective-permute-start | bytes 3145736 | tf_op jit(solution)/shard_map/ppermute | solution.py:299
  40.5 0.6 copy-start.11
  52.4 38.5 %collective-permute-start.9 = (bf16[512,1024]{1,0:T(8,128)(2,1)}, bf16[512,1024]{1,0:T(8,128)(2,1)}, u32[]{:S(2)}, u32[]{:S(2)}) collective-permute-start(bf16[512,1024]{1,0:T(8,128)(2,1)} %shard_map.116.refs_3_), channel_id=1, source_target_pairs={{2,4},{4,2},{0,16},{6,22},{3,5},{5,3},{1,17},{7,23},{18,20},{20,18... | collective-permute-start | bytes 3145736 | tf_op jit(solution)/shard_map/ppermute | solution.py:315
  54.2 41.9 %collective-permute-start.8 = (bf16[512,1024]{1,0:T(8,128)(2,1)}, bf16[512,1024]{1,0:T(8,128)(2,1)}, u32[]{:S(2)}, u32[]{:S(2)}) collective-permute-start(bf16[512,1024]{1,0:T(8,128)(2,1)} %shard_map.116.refs_3_), channel_id=1, source_target_pairs={{0,2},{1,3},{6,4},{7,5},{2,0},{3,1},{4,6},{5,7},{8,10},{9,11},{14,... | collective-permute-start | bytes 3145736 | tf_op jit(solution)/shard_map/ppermute | solution.py:299
  58.3 31.3 %collective-permute-start.7 = (bf16[512,1024]{1,0:T(8,128)(2,1)}, bf16[512,1024]{1,0:T(8,128)(2,1)}, u32[]{:S(2)}, u32[]{:S(2)}) collective-permute-start(bf16[512,1024]{1,0:T(8,128)(2,1)} %shard_map.117.refs_5_), channel_id=1, source_target_pairs={{0,1},{1,0},{2,3},{3,2},{4,5},{5,4},{6,7},{7,6},{8,9},{9,8},{10,11... | collective-permute-start | bytes 3145736 | tf_op jit(solution)/shard_map/ppermute | solution.py:296
  76.1 41.4 %collective-permute-start.5 = (bf16[512,1024]{1,0:T(8,128)(2,1)}, bf16[512,1024]{1,0:T(8,128)(2,1)}, u32[]{:S(2)}, u32[]{:S(2)}) collective-permute-start(bf16[512,1024]{1,0:T(8,128)(2,1)} %shard_map.118.refs_3_), channel_id=1, source_target_pairs={{2,4},{4,2},{0,16},{6,22},{3,5},{5,3},{1,17},{7,23},{18,20},{20,18... | collective-permute-start | bytes 3145736 | tf_op jit(solution)/shard_map/ppermute | solution.py:315
  77.7 44.4 %collective-permute-start.11 = (bf16[512,1024]{1,0:T(8,128)(2,1)}, bf16[512,1024]{1,0:T(8,128)(2,1)}, u32[]{:S(2)}, u32[]{:S(2)}) collective-permute-start(bf16[512,1024]{1,0:T(8,128)(2,1)} %shard_map.118.refs_3_), channel_id=1, source_target_pairs={{0,2},{1,3},{6,4},{7,5},{2,0},{3,1},{4,6},{5,7},{8,10},{9,11},{14,... | collective-permute-start | bytes 3145736 | tf_op jit(solution)/shard_map/ppermute | solution.py:299
  89.6 27.2 %collective-permute-start.4 = (bf16[512,1024]{1,0:T(8,128)(2,1)}, bf16[512,1024]{1,0:T(8,128)(2,1)}, u32[]{:S(2)}, u32[]{:S(2)}) collective-permute-start(bf16[512,1024]{1,0:T(8,128)(2,1)} %shard_map.119.refs_5_), channel_id=1, source_target_pairs={{0,1},{1,0},{2,3},{3,2},{4,5},{5,4},{6,7},{7,6},{8,9},{9,8},{10,11... | collective-permute-start | bytes 3145736 | tf_op jit(solution)/shard_map/ppermute | solution.py:296
  95.4 49.7 %collective-permute-start.14 = (bf16[512,1024]{1,0:T(8,128)(2,1)}, bf16[512,1024]{1,0:T(8,128)(2,1)}, u32[]{:S(2)}, u32[]{:S(2)}) collective-permute-start(bf16[512,1024]{1,0:T(8,128)(2,1)} %shard_map.120.refs_5_), channel_id=1, source_target_pairs={{0,2},{1,3},{6,4},{7,5},{2,0},{3,1},{4,6},{5,7},{8,10},{9,11},{14,... | collective-permute-start | bytes 3145736 | tf_op jit(solution)/shard_map/ppermute | solution.py:299
  96.2 6.8 %copy-start.12 = (f32[16]{0:T(128)S(1)}, f32[16]{0:T(128)}, u32[]{:S(2)}) copy-start(f32[16]{0:T(128)} %copy-done.11) | copy-start | bytes 196
  100.6 35.7 %collective-permute-start.15 = (bf16[512,1024]{1,0:T(8,128)(2,1)}, bf16[512,1024]{1,0:T(8,128)(2,1)}, u32[]{:S(2)}, u32[]{:S(2)}) collective-permute-start(bf16[512,1024]{1,0:T(8,128)(2,1)} %shard_map.121.refs_0_), channel_id=1, source_target_pairs={{2,4},{4,2},{0,16},{6,22},{3,5},{5,3},{1,17},{7,23},{18,20},{20,18... | collective-permute-start | bytes 3145736 | tf_op jit(solution)/shard_map/ppermute | solution.py:315
  103.0 2.2 %copy-start.6 = (bf16[2048,1024]{1,0:T(8,128)(2,1)S(1)}, bf16[2048,1024]{1,0:T(8,128)(2,1)}, u32[]{:S(2)}) copy-start(bf16[2048,1024]{1,0:T(8,128)(2,1)} %all-gather.3.cloned.1.call-done.right) | copy-start | bytes 12582916
  110.5 2.2 %copy-start.9 = (f32[8,128,1024]{2,1,0:T(8,128)S(1)}, f32[8,128,1024]{2,1,0:T(8,128)}, u32[]{:S(2)}) copy-start(f32[8,128,1024]{2,1,0:T(8,128)} %shard_map.122.refs_3_) | copy-start | bytes 12582916
  116.8 23.5 %collective-permute-start.13 = (bf16[512,1024]{1,0:T(8,128)(2,1)}, bf16[512,1024]{1,0:T(8,128)(2,1)}, u32[]{:S(2)}, u32[]{:S(2)}) collective-permute-start(bf16[512,1024]{1,0:T(8,128)(2,1)} %shard_map.123.refs_5_), channel_id=1, source_target_pairs={{0,1},{1,0},{2,3},{3,2},{4,5},{5,4},{6,7},{7,6},{8,9},{9,8},{10,11... | collective-permute-start | bytes 3145736 | tf_op jit(solution)/shard_map/ppermute | solution.py:296
  122.1 43.3 %collective-permute-start.10 = (bf16[512,1024]{1,0:T(8,128)(2,1)}, bf16[512,1024]{1,0:T(8,128)(2,1)}, u32[]{:S(2)}, u32[]{:S(2)}) collective-permute-start(bf16[512,1024]{1,0:T(8,128)(2,1)} %shard_map.124.refs_5_), channel_id=1, source_target_pairs={{0,2},{1,3},{6,4},{7,5},{2,0},{3,1},{4,6},{5,7},{8,10},{9,11},{14,... | collective-permute-start | bytes 3145736 | tf_op jit(solution)/shard_map/ppermute | solution.py:299
  126.6 27.9 %collective-permute-start.12 = (bf16[512,1024]{1,0:T(8,128)(2,1)}, bf16[512,1024]{1,0:T(8,128)(2,1)}, u32[]{:S(2)}, u32[]{:S(2)}) collective-permute-start(bf16[512,1024]{1,0:T(8,128)(2,1)} %shard_map.125.link), channel_id=1, source_target_pairs={{2,4},{4,2},{0,16},{6,22},{3,5},{5,3},{1,17},{7,23},{18,20},{20,18... | collective-permute-start | bytes 3145736 | tf_op jit(solution)/shard_map/ppermute | solution.py:315
  128.5 1.0 copy-start.8
  130.1 4.1 %copy-start.2 = (bf16[1024,128]{1,0:T(8,128)(2,1)}, bf16[1024,128]{1,0:T(8,128)(2,1)S(1)}, u32[]{:S(2)}) copy-start(bf16[1024,128]{1,0:T(8,128)(2,1)S(1)} %shard_map.126.refs_3_.refs_5_.refs_4_) | copy-start | bytes 786436
  136.3 42.6 %collective-permute-start.17 = (bf16[512,1024]{1,0:T(8,128)(2,1)}, bf16[512,1024]{1,0:T(8,128)(2,1)}, u32[]{:S(2)}, u32[]{:S(2)}) collective-permute-start(bf16[512,1024]{1,0:T(8,128)(2,1)} %shard_map.127.refs_6_), channel_id=1, source_target_pairs={{0,1},{1,0},{2,3},{3,2},{4,5},{5,4},{6,7},{7,6},{8,9},{9,8},{10,11... | collective-permute-start | bytes 3145736 | tf_op jit(solution)/shard_map/ppermute | solution.py:296
  145.1 41.2 %collective-permute-start.18 = (bf16[512,1024]{1,0:T(8,128)(2,1)}, bf16[512,1024]{1,0:T(8,128)(2,1)}, u32[]{:S(2)}, u32[]{:S(2)}) collective-permute-start(bf16[512,1024]{1,0:T(8,128)(2,1)} %shard_map.128.refs_4_), channel_id=1, source_target_pairs={{0,2},{1,3},{6,4},{7,5},{2,0},{3,1},{4,6},{5,7},{8,10},{9,11},{14,... | collective-permute-start | bytes 3145736 | tf_op jit(solution)/shard_map/ppermute | solution.py:299
  149.4 35.4 %collective-permute-start.16 = (bf16[512,1024]{1,0:T(8,128)(2,1)}, bf16[512,1024]{1,0:T(8,128)(2,1)}, u32[]{:S(2)}, u32[]{:S(2)}) collective-permute-start(bf16[512,1024]{1,0:T(8,128)(2,1)} %shard_map.129.refs_5_), channel_id=1, source_target_pairs={{0,1},{1,0},{2,3},{3,2},{4,5},{5,4},{6,7},{7,6},{8,9},{9,8},{10,11... | collective-permute-start | bytes 3145736 | tf_op jit(solution)/shard_map/ppermute | solution.py:296
  154.5 28.2 %collective-permute-start.19 = (bf16[512,1024]{1,0:T(8,128)(2,1)}, bf16[512,1024]{1,0:T(8,128)(2,1)}, u32[]{:S(2)}, u32[]{:S(2)}) collective-permute-start(bf16[512,1024]{1,0:T(8,128)(2,1)} %shard_map.130.refs_0_), channel_id=1, source_target_pairs={{2,4},{4,2},{0,16},{6,22},{3,5},{5,3},{1,17},{7,23},{18,20},{20,18... | collective-permute-start | bytes 3145736 | tf_op jit(solution)/shard_map/ppermute | solution.py:315
  165.4 2.2 %copy-start.7 = (bf16[2048,1024]{1,0:T(8,128)(2,1)S(1)}, bf16[2048,1024]{1,0:T(8,128)(2,1)}, u32[]{:S(2)}) copy-start(bf16[2048,1024]{1,0:T(8,128)(2,1)} %all-gather.5.cloned.1.call-done.left) | copy-start | bytes 12582916
  167.6 5.2 %copy-start.3 = (bf16[1024,128]{1,0:T(8,128)(2,1)S(1)}, bf16[1024,128]{1,0:T(8,128)(2,1)}, u32[]{:S(2)}) copy-start(bf16[1024,128]{1,0:T(8,128)(2,1)} %copy-done.2) | copy-start | bytes 786436
  167.6 5.2 %copy-start.5 = (bf16[16,1024,128]{2,1,0:T(8,128)(2,1)S(1)}, bf16[16,1024,128]{2,1,0:T(8,128)(2,1)}, u32[]{:S(2)}) copy-start(bf16[16,1024,128]{2,1,0:T(8,128)(2,1)} %refs_8_.3) | copy-start | bytes 12582916
  172.8 2.2 %copy-start.10 = (f32[8,1024,128]{2,1,0:T(8,128)S(1)}, f32[8,1024,128]{2,1,0:T(8,128)}, u32[]{:S(2)}) copy-start(f32[8,1024,128]{2,1,0:T(8,128)} %shard_map.131.refs_10_) | copy-start | bytes 12582916
Sparse Core Ops, SparseCore 0:
  10.4 15.0 all-gather.2
  34.2 15.0 all-gather.4
Sparse Core Ops, SparseCore 1:
  31.5 72.3 all-reduce.1

commit v11 on v10

--- a/solution.py
+++ b/solution.py
@@ -400,8 +400,8 @@
     )
     both_3 = along(out, pairwise)
     upper_far = exchange(run(far, same, upper, [(y3, 0), (upper_1, 0)]))
+    y5 = swap(run(jnp.where(at_end, nearer, beyond), other, upper, []), every)
     grad_expand = expand_gradient()
-    y5 = swap(run(jnp.where(at_end, nearer, beyond), other, upper, []), every)
     out = run(jnp.where(at_end, nearer, near_end), same, lower, [(y4, 1), (direct_b, 2)])
     both_4 = along(out, pairwise)
     lower_4 = exchange(run(beyond, same, lower, [(y4, 0), (lower_2, 0)]))

time: 199 us -> 199 us (level)
    ppermute x7, starting transfers between devices: 2.49 us -> 4.51 us  [along(): lax.ppermute(x, 'tensor', [(2 * a + y, 2 * b + y) for a, b in hops for y...]
where the time goes in v11:
time: 199 us; the launch traced here: 197 us
  Pallas kernels  97.4 us (49%)
  waiting for transfers between devices  44.3 us (22%)
  starting transfers between devices  19.2 us (10%)
  between operations  15.7 us (8%)
  local copies, waits for them, and re-layouts  14.6 us (7%)
  blocking collectives  4.35 us (2%)
    pallas_call x17, Pallas kernels, product(): pl.pallas_call(functools.partial(product_kernel, tuple((mode for _, mode...  72.8 us
    ppermute x7, waiting for transfers between devices, along(): lax.ppermute(x, 'tensor', [(2 * a + y, 2 * b + y) for a, b in hops for y...  27.7 us
    ppermute x7, waiting for transfers between devices, swap(): return lax.ppermute(x, 'tensor', pairs)  15.8 us
    unnamed x32, local copies, waits for them, and re-layouts  11.8 us
    pallas_call x2, Pallas kernels, factor_sums(): pl.pallas_call(functools.partial(factor_kernel, slots_each), in_specs=[pl...  9.5 us
    ppermute x5, starting transfers between devices, exchange(): return lax.ppermute(x, ('groups', 'tensor'), pairs)  9.08 us
    pallas_call x1, Pallas kernels, product_pair(): pl.pallas_call(pair_kernel, grid_spec=pltpu.PrefetchScalarGridSpec(num_sc...  6.9 us
    ppermute x7, starting transfers between devices, swap(): return lax.ppermute(x, 'tensor', pairs)  5.48 us
  transfers between devices with their start and end apart: 23, of which 9 were waited for; matrix products, arithmetic and copies ran while one was open for 2% of the time, Pallas kernels for 48%

profile of v11, /device:TPU:10, one launch (start us, length us, event | category | flops | bytes accessed | tf_op | source)
XLA Modules:
  0.0 197.2 jit_solution(10296325236011241235)
XLA Ops:
  8.9 1.6 copy-done
  10.5 6.9 %shard_map.112 = (bf16[512,1024]{1,0:T(8,128)(2,1)}, bf16[512,1024]{1,0:T(8,128)(2,1)}) custom-call(s32[4]{0:T(128)S(1)} %get-tuple-element.11.scalars, bf16[1024,1024]{1,0:T(8,128)(2,1)S(1)} %copy-done, bf16[8192,1024]{1,0:T(8,128)(2,1)} %refs_2_.33), custom_call_target="tpu_custom_call" | custom-call | flops 999999995904 | bytes 1000000000 | tf_op jit(solution)/shard_map/pallas_call | solution.py:116
  17.4 1.5 collective-permute-start.2
  19.3 4.3 %shard_map.113.refs_3_ = bf16[1024,128]{1,0:T(8,128)(2,1)} custom-call(s32[8]{0:T(128)} %tenants.1, bf16[1024,1024]{1,0:T(8,128)(2,1)S(1)} %copy-done.1, bf16[16,128,1024]{2,1,0:T(8,128)(2,1)S(1)} %copy-done.4, bf16[512,1024]{1,0:T(8,128)(2,1)} %get-tuple-element.5.link), custom_call_target="tpu_custom_call" | custom-call | flops 999999995904 | bytes 1000000000 | tf_op jit(solution)/shard_map/pallas_call | solution.py:191
  23.6 4.1 %shard_map.114.refs_3_ = bf16[512,1024]{1,0:T(8,128)(2,1)} custom-call(s32[4]{0:T(128)S(1)} %get-tuple-element.12.refs_0_, bf16[1024,1024]{1,0:T(8,128)(2,1)S(1)} %copy-done.1, bf16[8192,1024]{1,0:T(8,128)(2,1)} %refs_2_.33, bf16[1024,128]{1,0:T(8,128)(2,1)} %shard_map.113.refs_3_), custom_call_target="tpu_custom_call" | custom-call | flops 999999995904 | bytes 1000000000 | tf_op jit(solution)/shard_map/pallas_call | solution.py:84
  28.4 4.1 %shard_map.115.refs_5_ = bf16[512,1024]{1,0:T(8,128)(2,1)} custom-call(s32[4]{0:T(128)S(1)} %fusion.24.refs_0_, bf16[1024,1024]{1,0:T(8,128)(2,1)S(1)} %copy-done.1, bf16[8192,1024]{1,0:T(8,128)(2,1)} %refs_2_.33, bf16[512,1024]{1,0:T(8,128)(2,1)} %shard_map.114.refs_3_), custom_call_target="tpu_custom_call" | custom-call | flops 999999995904 | bytes 1000000000 | tf_op jit(solution)/shard_map/pallas_call | solution.py:84
  32.5 1.6 collective-permute-start.1
  37.2 2.2 %all_gather.12 = bf16[2048,128]{1,0:T(8,128)(2,1)S(1)} all-gather(bf16[1024,128]{1,0:T(8,128)(2,1)S(1)} %copy-done.13), channel_id=1, replica_groups=mesh['groups'=2,'dp'=2,'tensor'=8] {'dp'}, dimensions={0}, use_global_device_ids=true | all-gather | bytes 786432 | tf_op jit(solution)/shard_map/all_gather | solution.py:325
  39.4 0.9 dynamic_update_slice.11
  41.1 3.6 %collective-permute-done.2.refs_3_.refs_4_ = bf16[512,1024]{1,0:T(8,128)(2,1)} collective-permute-done((bf16[512,1024]{1,0:T(8,128)(2,1)}, bf16[512,1024]{1,0:T(8,128)(2,1)}, u32[]{:S(2)}, u32[]{:S(2)}) %collective-permute-start.2) | collective-permute-done | bytes 1048608 | tf_op jit(solution)/shard_map/ppermute | solution.py:296
  44.8 3.3 %collective-permute-done.3.refs_4_ = bf16[512,1024]{1,0:T(8,128)(2,1)} collective-permute-done((bf16[512,1024]{1,0:T(8,128)(2,1)}, bf16[512,1024]{1,0:T(8,128)(2,1)}, u32[]{:S(2)}, u32[]{:S(2)}) %collective-permute-start.3) | collective-permute-done | bytes 1048608 | tf_op jit(solution)/shard_map/ppermute | solution.py:299
  48.0 4.4 %shard_map.116.refs_3_ = bf16[512,1024]{1,0:T(8,128)(2,1)} custom-call(s32[4]{0:T(128)S(1)} %add_add_fusion.refs_0_, bf16[1024,1024]{1,0:T(8,128)(2,1)S(1)} %copy-done.1, bf16[8192,1024]{1,0:T(8,128)(2,1)} %refs_2_.33, bf16[512,1024]{1,0:T(8,128)(2,1)} %collective-permute-done.2.refs_3_.refs_4_, bf16[512,1024]{1,0:T(8,128)(2,1)} %collective-permute-done.3.refs_4_, ...), custom_call_target="tpu_custom_call" | custom-call | flops 999999995904 | bytes 1000000000 | tf_op jit(solution)/shard_map/pallas_call | solution.py:84
  52.5 1.7 collective-permute-start.9
  54.2 4.1 %shard_map.117.refs_5_ = bf16[512,1024]{1,0:T(8,128)(2,1)} custom-call(s32[4]{0:T(128)S(1)} %fusion.4.refs_0_, bf16[1024,1024]{1,0:T(8,128)(2,1)S(1)} %copy-done.1, bf16[8192,1024]{1,0:T(8,128)(2,1)} %refs_2_.33, bf16[512,1024]{1,0:T(8,128)(2,1)} %shard_map.116.refs_3_), custom_call_target="tpu_custom_call" | custom-call | flops 999999995904 | bytes 1000000000 | tf_op jit(solution)/shard_map/pallas_call | solution.py:84
  58.4 13.2 %collective-permute-done.1.refs_4_ = bf16[512,1024]{1,0:T(8,128)(2,1)} collective-permute-done((bf16[512,1024]{1,0:T(8,128)(2,1)}, bf16[512,1024]{1,0:T(8,128)(2,1)}, u32[]{:S(2)}, u32[]{:S(2)}) %collective-permute-start.1) | collective-permute-done | bytes 1048608 | tf_op jit(solution)/shard_map/ppermute | solution.py:299
  71.6 4.5 %shard_map.118.refs_3_ = bf16[512,1024]{1,0:T(8,128)(2,1)} custom-call(s32[4]{0:T(128)S(1)} %fusion.20.refs_0_, bf16[1024,1024]{1,0:T(8,128)(2,1)S(1)} %copy-done.1, bf16[8192,1024]{1,0:T(8,128)(2,1)} %refs_2_.33, bf16[512,1024]{1,0:T(8,128)(2,1)} %collective-permute-done.refs_3_, bf16[512,1024]{1,0:T(8,128)(2,1)} %collective-permute-done.1.refs_4_, ...), custom_call_target="tpu_custom_call" | custom-call | flops 999999995904 | bytes 1000000000 | tf_op jit(solution)/shard_map/pallas_call | solution.py:84
  76.1 1.6 collective-permute-start.5
  77.7 4.1 %shard_map.119.refs_5_ = bf16[512,1024]{1,0:T(8,128)(2,1)} custom-call(s32[4]{0:T(128)S(1)} %fusion.18.refs_0_, bf16[1024,1024]{1,0:T(8,128)(2,1)S(1)} %copy-done.1, bf16[8192,1024]{1,0:T(8,128)(2,1)} %refs_2_.33, bf16[512,1024]{1,0:T(8,128)(2,1)} %shard_map.118.refs_3_), custom_call_target="tpu_custom_call" | custom-call | flops 999999995904 | bytes 1000000000 | tf_op jit(solution)/shard_map/pallas_call | solution.py:84
  81.8 7.8 %collective-permute-done.7.refs_3_ = bf16[512,1024]{1,0:T(8,128)(2,1)} collective-permute-done((bf16[512,1024]{1,0:T(8,128)(2,1)}, bf16[512,1024]{1,0:T(8,128)(2,1)}, u32[]{:S(2)}, u32[]{:S(2)}) %collective-permute-start.7) | collective-permute-done | bytes 1048608 | tf_op jit(solution)/shard_map/ppermute | solution.py:296
  89.6 1.3 collective-permute-start.4
  90.9 4.4 %shard_map.120.refs_5_ = bf16[512,1024]{1,0:T(8,128)(2,1)} custom-call(s32[4]{0:T(128)S(1)} %add_add_fusion.1.refs_0_, bf16[1024,1024]{1,0:T(8,128)(2,1)S(1)} %copy-done.1, bf16[8192,1024]{1,0:T(8,128)(2,1)} %refs_2_.33, bf16[512,1024]{1,0:T(8,128)(2,1)} %collective-permute-done.7.refs_3_, bf16[512,1024]{1,0:T(8,128)(2,1)} %collective-permute-done.9.refs_4_, ...), custom_call_target="tpu_custom_call" | custom-call | flops 999999995904 | bytes 1000000000 | tf_op jit(solution)/shard_map/pallas_call | solution.py:84
  96.1 4.5 %shard_map.121.refs_3_ = bf16[512,1024]{1,0:T(8,128)(2,1)} custom-call(s32[4]{0:T(128)S(1)} %fusion.8.refs_0_, bf16[1024,1024]{1,0:T(8,128)(2,1)S(1)} %copy-done.1, bf16[8192,1024]{1,0:T(8,128)(2,1)} %refs_2_.33, bf16[512,1024]{1,0:T(8,128)(2,1)} %collective-permute-done.7.refs_3_, bf16[512,1024]{1,0:T(8,128)(2,1)} %collective-permute-done.8.refs_4_, ...), custom_call_target="tpu_custom_call" | custom-call | flops 999999995904 | bytes 1000000000 | tf_op jit(solution)/shard_map/pallas_call | solution.py:84
  100.6 1.5 collective-permute-start.15
  102.1 4.1 %shard_map.122.refs_0_ = bf16[512,1024]{1,0:T(8,128)(2,1)} custom-call(s32[4]{0:T(128)S(1)} %fusion.6.refs_0_, bf16[1024,1024]{1,0:T(8,128)(2,1)S(1)} %copy-done.1, bf16[8192,1024]{1,0:T(8,128)(2,1)} %refs_2_.33, bf16[512,1024]{1,0:T(8,128)(2,1)} %shard_map.121.refs_3_), custom_call_target="tpu_custom_call" | custom-call | flops 999999995904 | bytes 1000000000 | tf_op jit(solution)/shard_map/pallas_call | solution.py:84
  106.3 2.2 %copy-done.6 = bf16[2048,1024]{1,0:T(8,128)(2,1)S(1)} copy-done((bf16[2048,1024]{1,0:T(8,128)(2,1)S(1)}, bf16[2048,1024]{1,0:T(8,128)(2,1)}, u32[]{:S(2)}) %copy-start.6) | copy-done | bytes 4194328
  108.4 4.8 %shard_map.123.refs_5_ = f32[8,128,1024]{2,1,0:T(8,128)} custom-call(s32[16]{0:T(128)S(1)} %get-tuple-element.8.slots, f32[16]{0:T(128)S(1)} %copy-done.12, bf16[2048,128]{1,0:T(8,128)(2,1)S(1)} %bitcast_multiply_fusion.left, bf16[2048,1024]{1,0:T(8,128)(2,1)S(1)} %copy-done.6, bf16[512,1024]{1,0:T(8,128)(2,1)} %shard_map.122.refs_0_), custom_call_target="tpu_custom_call" | custom-call | flops 999999995904 | bytes 1000000000 | tf_op jit(solution)/shard_map/pallas_call | solution.py:247
  113.2 3.5 %collective-permute-done.4.refs_3_ = bf16[512,1024]{1,0:T(8,128)(2,1)} collective-permute-done((bf16[512,1024]{1,0:T(8,128)(2,1)}, bf16[512,1024]{1,0:T(8,128)(2,1)}, u32[]{:S(2)}, u32[]{:S(2)}) %collective-permute-start.4) | collective-permute-done | bytes 1048608 | tf_op jit(solution)/shard_map/ppermute | solution.py:296
  117.0 2.2 %copy-done.9 = f32[8,128,1024]{2,1,0:T(8,128)S(1)} copy-done((f32[8,128,1024]{2,1,0:T(8,128)S(1)}, f32[8,128,1024]{2,1,0:T(8,128)}, u32[]{:S(2)}) %copy-start.9) | copy-done | bytes 4194328
  119.2 4.5 %shard_map.124.refs_5_ = bf16[512,1024]{1,0:T(8,128)(2,1)} custom-call(s32[4]{0:T(128)S(1)} %fusion.16.refs_0_, bf16[1024,1024]{1,0:T(8,128)(2,1)S(1)} %copy-done.1, bf16[8192,1024]{1,0:T(8,128)(2,1)} %refs_2_.33, bf16[512,1024]{1,0:T(8,128)(2,1)} %collective-permute-done.4.refs_3_, bf16[512,1024]{1,0:T(8,128)(2,1)} %collective-permute-done.5.refs_4_, ...), custom_call_target="tpu_custom_call" | custom-call | flops 999999995904 | bytes 1000000000 | tf_op jit(solution)/shard_map/pallas_call | solution.py:84
  123.7 1.7 collective-permute-start.10
  125.5 4.5 %shard_map.125.link = bf16[512,1024]{1,0:T(8,128)(2,1)} custom-call(s32[4]{0:T(128)S(1)} %fusion.26.refs_0_, bf16[1024,1024]{1,0:T(8,128)(2,1)S(1)} %copy-done.1, bf16[8192,1024]{1,0:T(8,128)(2,1)} %refs_2_.33, bf16[512,1024]{1,0:T(8,128)(2,1)} %collective-permute-done.4.refs_3_, bf16[512,1024]{1,0:T(8,128)(2,1)} %collective-permute-done.11.refs_4_, ...), custom_call_target="tpu_custom_call" | custom-call | flops 999999995904 | bytes 1000000000 | tf_op jit(solution)/shard_map/pallas_call | solution.py:84
  130.0 1.6 collective-permute-start.12
  131.6 0.9 copy-done.8
  133.1 4.2 %shard_map.127.refs_6_ = bf16[512,1024]{1,0:T(8,128)(2,1)} custom-call(s32[4]{0:T(128)S(1)} %fusion.14.refs_0_, bf16[1024,1024]{1,0:T(8,128)(2,1)S(1)} %copy-done.1, bf16[8192,1024]{1,0:T(8,128)(2,1)} %refs_2_.33, bf16[1024,128]{1,0:T(8,128)(2,1)S(1)} %shard_map.126.refs_3_.refs_5_.refs_4_), custom_call_target="tpu_custom_call" | custom-call | flops 999999995904 | bytes 1000000000 | tf_op jit(solution)/shard_map/pallas_call | solution.py:84
  137.3 1.5 collective-permute-start.17
  138.8 4.8 %shard_map.128.refs_4_ = bf16[512,1024]{1,0:T(8,128)(2,1)} custom-call(s32[4]{0:T(128)S(1)} %fusion.12.refs_0_, bf16[1024,1024]{1,0:T(8,128)(2,1)S(1)} %copy-done.1, bf16[8192,1024]{1,0:T(8,128)(2,1)} %refs_2_.33, bf16[512,1024]{1,0:T(8,128)(2,1)} %collective-permute-done.13.refs_3_, bf16[512,1024]{1,0:T(8,128)(2,1)} %collective-permute-done.2.refs_3_.refs_4_, ...), custom_call_target="tpu_custom_call" | custom-call | flops 999999995904 | bytes 1000000000 | tf_op jit(solution)/shard_map/pallas_call | solution.py:84
  144.0 4.3 %shard_map.129.refs_5_ = bf16[512,1024]{1,0:T(8,128)(2,1)} custom-call(s32[4]{0:T(128)S(1)} %fusion.28.refs_0_, bf16[1024,1024]{1,0:T(8,128)(2,1)S(1)} %copy-done.1, bf16[8192,1024]{1,0:T(8,128)(2,1)} %refs_2_.33, bf16[512,1024]{1,0:T(8,128)(2,1)} %collective-permute-done.14.refs_3_.refs_4_, bf16[512,1024]{1,0:T(8,128)(2,1)} %shard_map.128.refs_4_), custom_call_target="tpu_custom_call" | custom-call | flops 999999995904 | bytes 1000000000 | tf_op jit(solution)/shard_map/pallas_call | solution.py:84
  148.8 4.5 %shard_map.130.refs_0_ = bf16[512,1024]{1,0:T(8,128)(2,1)} custom-call(s32[4]{0:T(128)S(1)} %fusion.10.refs_0_, bf16[1024,1024]{1,0:T(8,128)(2,1)S(1)} %copy-done.1, bf16[8192,1024]{1,0:T(8,128)(2,1)} %refs_2_.33, bf16[512,1024]{1,0:T(8,128)(2,1)} %collective-permute-done.13.refs_3_, bf16[512,1024]{1,0:T(8,128)(2,1)} %collective-permute-done.14.refs_3_.refs_4_, ...), custom_call_target="tpu_custom_call" | custom-call | flops 999999995904 | bytes 1000000000 | tf_op jit(solution)/shard_map/pallas_call | solution.py:84
  153.3 2.2 %all_gather.15.right = bf16[2048,128]{1,0:T(8,128)(2,1)S(1)} all-gather(bf16[1024,128]{1,0:T(8,128)(2,1)S(1)} %shard_map.126.refs_3_.refs_5_.refs_4_), channel_id=1, replica_groups=mesh['groups'=2,'dp'=2,'tensor'=8] {'dp'}, dimensions={0}, use_global_device_ids=true | all-gather | bytes 786432 | tf_op jit(solution)/shard_map/all_gather | solution.py:325
  155.5 2.7 %collective-permute-start.19 = (bf16[512,1024]{1,0:T(8,128)(2,1)}, bf16[512,1024]{1,0:T(8,128)(2,1)}, u32[]{:S(2)}, u32[]{:S(2)}) collective-permute-start(bf16[512,1024]{1,0:T(8,128)(2,1)} %shard_map.130.refs_0_), channel_id=1, source_target_pairs={{2,4},{4,2},{0,16},{6,22},{3,5},{5,3},{1,17},{7,23},{18,20},{20,18... | collective-permute-start | bytes 3145736 | tf_op jit(solution)/shard_map/ppermute | solution.py:315
  158.2 7.4 %collective-permute-done.10.refs_1_.refs_3_ = bf16[512,1024]{1,0:T(8,128)(2,1)} collective-permute-done((bf16[512,1024]{1,0:T(8,128)(2,1)}, bf16[512,1024]{1,0:T(8,128)(2,1)}, u32[]{:S(2)}, u32[]{:S(2)}) %collective-permute-start.10) | collective-permute-done | bytes 1048608 | tf_op jit(solution)/shard_map/ppermute | solution.py:299
  165.6 2.2 %copy-done.7 = bf16[2048,1024]{1,0:T(8,128)(2,1)S(1)} copy-done((bf16[2048,1024]{1,0:T(8,128)(2,1)S(1)}, bf16[2048,1024]{1,0:T(8,128)(2,1)}, u32[]{:S(2)}) %copy-start.7) | copy-done | bytes 4194328
  167.8 4.7 %shard_map.131.refs_10_ = f32[8,1024,128]{2,1,0:T(8,128)} custom-call(s32[16]{0:T(128)S(1)} %get-tuple-element.8.slots, f32[16]{0:T(128)S(1)} %broadcast_4_scales.2.scales, bf16[2048,1024]{1,0:T(8,128)(2,1)S(1)} %copy-done.7, bf16[2048,128]{1,0:T(8,128)(2,1)S(1)} %all_gather.15.right, bf16[512,1024]{1,0:T(8,128)(2,1)} %shard_map.130.refs_0_, ...), custom_call_target="tpu_custom_call" | custom-call | flops 999999995904 | bytes 1000000000 | tf_op jit(solution)/shard_map/pallas_call | solution.py:247
  172.5 2.2 %copy-done.10 = f32[8,1024,128]{2,1,0:T(8,128)S(1)} copy-done((f32[8,1024,128]{2,1,0:T(8,128)S(1)}, f32[8,1024,128]{2,1,0:T(8,128)}, u32[]{:S(2)}) %copy-start.10) | copy-done | bytes 4194328
  174.7 4.0 %shard_map.132.refs_9_.refs_0_ = bf16[512,1024]{1,0:T(8,128)(2,1)S(1)} custom-call(s32[8]{0:T(128)S(1)} %stack.72.refs_0_, bf16[1024,1024]{1,0:T(8,128)(2,1)S(1)} %copy-done.1, bf16[8192,1024]{1,0:T(8,128)(2,1)} %refs_2_.33, bf16[512,1024]{1,0:T(8,128)(2,1)} %collective-permute-done.10.refs_1_.refs_3_, ...), custom_call_target="tpu_custom_call" | custom-call | flops 999999995904 | bytes 1000000000 | tf_op jit(solution)/shard_map/pallas_call | solution.py:84
  178.7 3.8 %shard_map.133.refs_2_ = bf16[512,1024]{1,0:T(8,128)(2,1)S(1)} custom-call(s32[8]{0:T(128)S(1)} %stack.175.refs_0_, bf16[1024,1024]{1,0:T(8,128)(2,1)S(1)} %copy-done.1, bf16[8192,1024]{1,0:T(8,128)(2,1)} %refs_2_.33, bf16[512,1024]{1,0:T(8,128)(2,1)} %collective-permute-done.17.refs_3_, bf16[1024,128]{1,0:T(8,128)(2,1)S(1)} %copy-done.3, ...), custom_call_target="tpu_custom_call" | custom-call | flops 999999995904 | bytes 1000000000 | tf_op jit(solution)/shard_map/pallas_call | solution.py:84
  183.3 3.0 %collective-permute-done.18.refs_3_ = bf16[512,1024]{1,0:T(8,128)(2,1)} collective-permute-done((bf16[512,1024]{1,0:T(8,128)(2,1)}, bf16[512,1024]{1,0:T(8,128)(2,1)}, u32[]{:S(2)}, u32[]{:S(2)}) %collective-permute-start.18) | collective-permute-done | bytes 1048608 | tf_op jit(solution)/shard_map/ppermute | solution.py:299
  186.4 3.4 %shard_map.134 = bf16[1024,1024]{1,0:T(8,128)(2,1)} custom-call(s32[1]{0:T(128)} %bitcast.inner, bf16[512,1024]{1,0:T(8,128)(2,1)S(1)} %shard_map.132.refs_9_.refs_0_, bf16[512,1024]{1,0:T(8,128)(2,1)} %collective-permute-done.16.refs_1_, bf16[512,1024]{1,0:T(8,128)(2,1)S(1)} %shard_map.133.refs_2_, bf16[512,1024]{1,0:T(8,128)(2,1)} %collective-permute-done.18.refs_3_, ...), custom_call_target="tpu_custom_call" | custom-call | flops 999999995904 | bytes 1000000000 | tf_op jit(solution)/shard_map/pallas_call | solution.py:167
  (89 shorter events, 9.5 us)
Async XLA Ops:
  8.0 98.3 %all-gather.3.cloned.1.call-start = ((), (), s32[]{:S(2)}) async-start(), calls=%async_computation | async-start | bytes 6291456 | tf_op jit(solution)/shard_map/all_gather | solution.py:325
  8.9 1.6 copy-start
  10.5 8.9 %copy-start.1 = (bf16[1024,1024]{1,0:T(8,128)(2,1)S(1)}, bf16[1024,1024]{1,0:T(8,128)(2,1)}, u32[]{:S(2)}) copy-start(bf16[1024,1024]{1,0:T(8,128)(2,1)} %refs_1_.33) | copy-start | bytes 6291460
  10.5 8.9 %copy-start.4 = (bf16[16,128,1024]{2,1,0:T(8,128)(2,1)S(1)}, bf16[16,128,1024]{2,1,0:T(8,128)(2,1)}, u32[]{:S(2)}) copy-start(bf16[16,128,1024]{2,1,0:T(8,128)(2,1)} %expand.1) | copy-start | bytes 12582916
  17.4 27.4 %collective-permute-start.2 = (bf16[512,1024]{1,0:T(8,128)(2,1)}, bf16[512,1024]{1,0:T(8,128)(2,1)}, u32[]{:S(2)}, u32[]{:S(2)}) collective-permute-start(bf16[512,1024]{1,0:T(8,128)(2,1)} %get-tuple-element.6), channel_id=1, source_target_pairs={{0,1},{1,0},{2,3},{3,2},{4,5},{5,4},{6,7},{7,6},{8,9},{9,8},{10,11... | collective-permute-start | bytes 3145736 | tf_op jit(solution)/shard_map/ppermute | solution.py:296
  18.9 29.2 %collective-permute-start.3 = (bf16[512,1024]{1,0:T(8,128)(2,1)}, bf16[512,1024]{1,0:T(8,128)(2,1)}, u32[]{:S(2)}, u32[]{:S(2)}) collective-permute-start(bf16[512,1024]{1,0:T(8,128)(2,1)} %get-tuple-element.5.link), channel_id=1, source_target_pairs={{0,2},{1,3},{6,4},{7,5},{2,0},{3,1},{4,6},{5,7},{8,10},{9,11},{14,... | collective-permute-start | bytes 3145736 | tf_op jit(solution)/shard_map/ppermute | solution.py:299
  19.3 20.0 %collective-permute-start.6 = (s32[8]{0:T(128)}, s32[8]{0:T(128)}, u32[]{:S(2)}, u32[]{:S(2)}) collective-permute-start(s32[8]{0:T(128)} %tenants.1), channel_id=1, source_target_pairs={{0,8},{8,0},{1,9},{9,1},{2,10},{10,2},{3,11},{11,3},{4,12},{12,4},... | collective-permute-start | bytes 104 | tf_op jit(solution)/shard_map/ppermute | solution.py:330
  27.7 103.8 %all-reduce.2.cloned.1.call-start = ((), (), s32[]{:S(2)}) async-start(), calls=%async_computation.1 | async-start | bytes 524288 | tf_op jit(solution)/shard_map/psum | solution.py:349
  27.7 43.9 %collective-permute-start = (bf16[512,1024]{1,0:T(8,128)(2,1)}, bf16[512,1024]{1,0:T(8,128)(2,1)}, u32[]{:S(2)}, u32[]{:S(2)}) collective-permute-start(bf16[512,1024]{1,0:T(8,128)(2,1)} %shard_map.114.refs_3_), channel_id=1, source_target_pairs={{0,1},{1,0},{2,3},{3,2},{4,5},{5,4},{6,7},{7,6},{8,9},{9,8},{10,11... | collective-permute-start | bytes 3145736 | tf_op jit(solution)/shard_map/ppermute | solution.py:296
  28.3 129.9 %all-gather.5.cloned.1.call-start = ((), (), s32[]{:S(2)}) async-start(), calls=%async_computation.2 | async-start | bytes 6291456 | tf_op jit(solution)/shard_map/all_gather | solution.py:325
  28.4 7.4 %copy-start.15 = (s32[16]{0:T(128)S(1)}, s32[16]{0:T(128)}, u32[]{:S(2)}) copy-start(s32[16]{0:T(128)} %param.17) | copy-start | bytes 196
  28.4 8.8 %copy-start.13 = (bf16[1024,128]{1,0:T(8,128)(2,1)S(1)}, bf16[1024,128]{1,0:T(8,128)(2,1)}, u32[]{:S(2)}) copy-start(bf16[1024,128]{1,0:T(8,128)(2,1)} %param.11) | copy-start | bytes 786436
  28.4 11.8 %copy-start.14 = (s32[16]{0:T(128)S(1)}, s32[16]{0:T(128)}, u32[]{:S(2)}) copy-start(s32[16]{0:T(128)} %param.16) | copy-start | bytes 196
  32.5 39.1 %collective-permute-start.1 = (bf16[512,1024]{1,0:T(8,128)(2,1)}, bf16[512,1024]{1,0:T(8,128)(2,1)}, u32[]{:S(2)}, u32[]{:S(2)}) collective-permute-start(bf16[512,1024]{1,0:T(8,128)(2,1)} %shard_map.115.refs_5_), channel_id=1, source_target_pairs={{0,2},{1,3},{6,4},{7,5},{2,0},{3,1},{4,6},{5,7},{8,10},{9,11},{14,... | collective-permute-start | bytes 3145736 | tf_op jit(solution)/shard_map/ppermute | solution.py:299
  40.5 0.5 copy-start.11
  52.5 38.4 %collective-permute-start.9 = (bf16[512,1024]{1,0:T(8,128)(2,1)}, bf16[512,1024]{1,0:T(8,128)(2,1)}, u32[]{:S(2)}, u32[]{:S(2)}) collective-permute-start(bf16[512,1024]{1,0:T(8,128)(2,1)} %shard_map.116.refs_3_), channel_id=1, source_target_pairs={{2,4},{4,2},{0,16},{6,22},{3,5},{5,3},{1,17},{7,23},{18,20},{20,18... | collective-permute-start | bytes 3145736 | tf_op jit(solution)/shard_map/ppermute | solution.py:315
  54.2 41.9 %collective-permute-start.8 = (bf16[512,1024]{1,0:T(8,128)(2,1)}, bf16[512,1024]{1,0:T(8,128)(2,1)}, u32[]{:S(2)}, u32[]{:S(2)}) collective-permute-start(bf16[512,1024]{1,0:T(8,128)(2,1)} %shard_map.116.refs_3_), channel_id=1, source_target_pairs={{0,2},{1,3},{6,4},{7,5},{2,0},{3,1},{4,6},{5,7},{8,10},{9,11},{14,... | collective-permute-start | bytes 3145736 | tf_op jit(solution)/shard_map/ppermute | solution.py:299
  58.3 31.3 %collective-permute-start.7 = (bf16[512,1024]{1,0:T(8,128)(2,1)}, bf16[512,1024]{1,0:T(8,128)(2,1)}, u32[]{:S(2)}, u32[]{:S(2)}) collective-permute-start(bf16[512,1024]{1,0:T(8,128)(2,1)} %shard_map.117.refs_5_), channel_id=1, source_target_pairs={{0,1},{1,0},{2,3},{3,2},{4,5},{5,4},{6,7},{7,6},{8,9},{9,8},{10,11... | collective-permute-start | bytes 3145736 | tf_op jit(solution)/shard_map/ppermute | solution.py:296
  76.1 40.9 %collective-permute-start.5 = (bf16[512,1024]{1,0:T(8,128)(2,1)}, bf16[512,1024]{1,0:T(8,128)(2,1)}, u32[]{:S(2)}, u32[]{:S(2)}) collective-permute-start(bf16[512,1024]{1,0:T(8,128)(2,1)} %shard_map.118.refs_3_), channel_id=1, source_target_pairs={{2,4},{4,2},{0,16},{6,22},{3,5},{5,3},{1,17},{7,23},{18,20},{20,18... | collective-permute-start | bytes 3145736 | tf_op jit(solution)/shard_map/ppermute | solution.py:315
  77.7 47.8 %collective-permute-start.11 = (bf16[512,1024]{1,0:T(8,128)(2,1)}, bf16[512,1024]{1,0:T(8,128)(2,1)}, u32[]{:S(2)}, u32[]{:S(2)}) collective-permute-start(bf16[512,1024]{1,0:T(8,128)(2,1)} %shard_map.118.refs_3_), channel_id=1, source_target_pairs={{0,2},{1,3},{6,4},{7,5},{2,0},{3,1},{4,6},{5,7},{8,10},{9,11},{14,... | collective-permute-start | bytes 3145736 | tf_op jit(solution)/shard_map/ppermute | solution.py:299
  89.6 27.1 %collective-permute-start.4 = (bf16[512,1024]{1,0:T(8,128)(2,1)}, bf16[512,1024]{1,0:T(8,128)(2,1)}, u32[]{:S(2)}, u32[]{:S(2)}) collective-permute-start(bf16[512,1024]{1,0:T(8,128)(2,1)} %shard_map.119.refs_5_), channel_id=1, source_target_pairs={{0,1},{1,0},{2,3},{3,2},{4,5},{5,4},{6,7},{7,6},{8,9},{9,8},{10,11... | collective-permute-start | bytes 3145736 | tf_op jit(solution)/shard_map/ppermute | solution.py:296
  100.6 38.2 %collective-permute-start.15 = (bf16[512,1024]{1,0:T(8,128)(2,1)}, bf16[512,1024]{1,0:T(8,128)(2,1)}, u32[]{:S(2)}, u32[]{:S(2)}) collective-permute-start(bf16[512,1024]{1,0:T(8,128)(2,1)} %shard_map.121.refs_3_), channel_id=1, source_target_pairs={{2,4},{4,2},{0,16},{6,22},{3,5},{5,3},{1,17},{7,23},{18,20},{20,18... | collective-permute-start | bytes 3145736 | tf_op jit(solution)/shard_map/ppermute | solution.py:315
  102.1 4.2 %copy-start.12 = (f32[16]{0:T(128)S(1)}, f32[16]{0:T(128)}, u32[]{:S(2)}) copy-start(f32[16]{0:T(128)} %copy-done.11) | copy-start | bytes 196
  106.2 31.1 %collective-permute-start.13 = (bf16[512,1024]{1,0:T(8,128)(2,1)}, bf16[512,1024]{1,0:T(8,128)(2,1)}, u32[]{:S(2)}, u32[]{:S(2)}) collective-permute-start(bf16[512,1024]{1,0:T(8,128)(2,1)} %shard_map.122.refs_0_), channel_id=1, source_target_pairs={{0,1},{1,0},{2,3},{3,2},{4,5},{5,4},{6,7},{7,6},{8,9},{9,8},{10,11... | collective-permute-start | bytes 3145736 | tf_op jit(solution)/shard_map/ppermute | solution.py:296
  106.3 2.2 %copy-start.6 = (bf16[2048,1024]{1,0:T(8,128)(2,1)S(1)}, bf16[2048,1024]{1,0:T(8,128)(2,1)}, u32[]{:S(2)}) copy-start(bf16[2048,1024]{1,0:T(8,128)(2,1)} %all-gather.3.cloned.1.call-done.right) | copy-start | bytes 12582916
  116.7 27.3 %collective-permute-start.14 = (bf16[512,1024]{1,0:T(8,128)(2,1)}, bf16[512,1024]{1,0:T(8,128)(2,1)}, u32[]{:S(2)}, u32[]{:S(2)}) collective-permute-start(bf16[512,1024]{1,0:T(8,128)(2,1)} %shard_map.120.refs_5_), channel_id=1, source_target_pairs={{0,2},{1,3},{6,4},{7,5},{2,0},{3,1},{4,6},{5,7},{8,10},{9,11},{14,... | collective-permute-start | bytes 3145736 | tf_op jit(solution)/shard_map/ppermute | solution.py:299
  117.0 2.2 %copy-start.9 = (f32[8,128,1024]{2,1,0:T(8,128)S(1)}, f32[8,128,1024]{2,1,0:T(8,128)}, u32[]{:S(2)}) copy-start(f32[8,128,1024]{2,1,0:T(8,128)} %shard_map.123.refs_5_) | copy-start | bytes 12582916
  123.7 41.9 %collective-permute-start.10 = (bf16[512,1024]{1,0:T(8,128)(2,1)}, bf16[512,1024]{1,0:T(8,128)(2,1)}, u32[]{:S(2)}, u32[]{:S(2)}) collective-permute-start(bf16[512,1024]{1,0:T(8,128)(2,1)} %shard_map.124.refs_5_), channel_id=1, source_target_pairs={{0,2},{1,3},{6,4},{7,5},{2,0},{3,1},{4,6},{5,7},{8,10},{9,11},{14,... | collective-permute-start | bytes 3145736 | tf_op jit(solution)/shard_map/ppermute | solution.py:299
  130.0 25.5 %collective-permute-start.12 = (bf16[512,1024]{1,0:T(8,128)(2,1)}, bf16[512,1024]{1,0:T(8,128)(2,1)}, u32[]{:S(2)}, u32[]{:S(2)}) collective-permute-start(bf16[512,1024]{1,0:T(8,128)(2,1)} %shard_map.125.link), channel_id=1, source_target_pairs={{2,4},{4,2},{0,16},{6,22},{3,5},{5,3},{1,17},{7,23},{18,20},{20,18... | collective-permute-start | bytes 3145736 | tf_op jit(solution)/shard_map/ppermute | solution.py:315
  131.6 1.0 copy-start.8
  133.1 20.2 %copy-start.2 = (bf16[1024,128]{1,0:T(8,128)(2,1)}, bf16[1024,128]{1,0:T(8,128)(2,1)S(1)}, u32[]{:S(2)}) copy-start(bf16[1024,128]{1,0:T(8,128)(2,1)S(1)} %shard_map.126.refs_3_.refs_5_.refs_4_) | copy-start | bytes 786436
  137.3 41.4 %collective-permute-start.17 = (bf16[512,1024]{1,0:T(8,128)(2,1)}, bf16[512,1024]{1,0:T(8,128)(2,1)}, u32[]{:S(2)}, u32[]{:S(2)}) collective-permute-start(bf16[512,1024]{1,0:T(8,128)(2,1)} %shard_map.127.refs_6_), channel_id=1, source_target_pairs={{0,1},{1,0},{2,3},{3,2},{4,5},{5,4},{6,7},{7,6},{8,9},{9,8},{10,11... | collective-permute-start | bytes 3145736 | tf_op jit(solution)/shard_map/ppermute | solution.py:296
  143.6 42.8 %collective-permute-start.18 = (bf16[512,1024]{1,0:T(8,128)(2,1)}, bf16[512,1024]{1,0:T(8,128)(2,1)}, u32[]{:S(2)}, u32[]{:S(2)}) collective-permute-start(bf16[512,1024]{1,0:T(8,128)(2,1)} %shard_map.128.refs_4_), channel_id=1, source_target_pairs={{0,2},{1,3},{6,4},{7,5},{2,0},{3,1},{4,6},{5,7},{8,10},{9,11},{14,... | collective-permute-start | bytes 3145736 | tf_op jit(solution)/shard_map/ppermute | solution.py:299
  148.3 35.0 %collective-permute-start.16 = (bf16[512,1024]{1,0:T(8,128)(2,1)}, bf16[512,1024]{1,0:T(8,128)(2,1)}, u32[]{:S(2)}, u32[]{:S(2)}) collective-permute-start(bf16[512,1024]{1,0:T(8,128)(2,1)} %shard_map.129.refs_5_), channel_id=1, source_target_pairs={{0,1},{1,0},{2,3},{3,2},{4,5},{5,4},{6,7},{7,6},{8,9},{9,8},{10,11... | collective-permute-start | bytes 3145736 | tf_op jit(solution)/shard_map/ppermute | solution.py:296
  155.5 27.0 %collective-permute-start.19 = (bf16[512,1024]{1,0:T(8,128)(2,1)}, bf16[512,1024]{1,0:T(8,128)(2,1)}, u32[]{:S(2)}, u32[]{:S(2)}) collective-permute-start(bf16[512,1024]{1,0:T(8,128)(2,1)} %shard_map.130.refs_0_), channel_id=1, source_target_pairs={{2,4},{4,2},{0,16},{6,22},{3,5},{5,3},{1,17},{7,23},{18,20},{20,18... | collective-permute-start | bytes 3145736 | tf_op jit(solution)/shard_map/ppermute | solution.py:315
  165.6 2.2 %copy-start.7 = (bf16[2048,1024]{1,0:T(8,128)(2,1)S(1)}, bf16[2048,1024]{1,0:T(8,128)(2,1)}, u32[]{:S(2)}) copy-start(bf16[2048,1024]{1,0:T(8,128)(2,1)} %all-gather.5.cloned.1.call-done.left) | copy-start | bytes 12582916
  167.8 4.7 %copy-start.3 = (bf16[1024,128]{1,0:T(8,128)(2,1)S(1)}, bf16[1024,128]{1,0:T(8,128)(2,1)}, u32[]{:S(2)}) copy-start(bf16[1024,128]{1,0:T(8,128)(2,1)} %copy-done.2) | copy-start | bytes 786436
  167.8 4.7 %copy-start.5 = (bf16[16,1024,128]{2,1,0:T(8,128)(2,1)S(1)}, bf16[16,1024,128]{2,1,0:T(8,128)(2,1)}, u32[]{:S(2)}) copy-start(bf16[16,1024,128]{2,1,0:T(8,128)(2,1)} %refs_8_.3) | copy-start | bytes 12582916
  172.5 2.2 %copy-start.10 = (f32[8,1024,128]{2,1,0:T(8,128)S(1)}, f32[8,1024,128]{2,1,0:T(8,128)}, u32[]{:S(2)}) copy-start(f32[8,1024,128]{2,1,0:T(8,128)} %shard_map.131.refs_10_) | copy-start | bytes 12582916
Sparse Core Ops, SparseCore 0:
  10.4 15.0 all-gather.2
  34.2 15.0 all-gather.4
Sparse Core Ops, SparseCore 1:
  31.5 72.3 all-reduce.1

commit v12 on v10

--- a/solution.py
+++ b/solution.py
@@ -13,7 +13,7 @@
 f32 = jnp.float32
 contract_last = (((1,), (1,)), ((), ()))
 contract_first = (((0,), (0,)), ((), ()))
-vmem_bytes = 40 * 1024 * 1024
+vmem_bytes = 58 * 1024 * 1024
 declared = pl.CostEstimate(flops=10**12, bytes_accessed=10**9, transcendentals=0)
 
 

time: 199 us -> 204 us (1.025)
  Pallas kernels: 98.4 us -> 119 us
  waiting for transfers between devices: 43.9 us -> 23.6 us
  other arithmetic: 1.65 us -> 11.3 us
  local copies, waits for them, and re-layouts: 14.6 us -> 6.04 us
    ppermute x7, waiting for transfers between devices: 26.5 us -> 5.6 us  [along(): lax.ppermute(x, 'tensor', [(2 * a + y, 2 * b + y) for a, b in hops for y...]
    pallas_call x17, Pallas kernels: 72.8 us -> 84.8 us  [product(): pl.pallas_call(functools.partial(product_kernel, tuple((mode for _, mode...]
    unnamed x32 -> x10, local copies, waits for them, and re-layouts: 11.8 us -> 0.54 us
    another operation x14, other arithmetic: 1.08 us -> 8.82 us  [run(): scalars = jnp.stack([jnp.asarray(v, jnp.int32) for v in scalars])]
    ppermute x5, starting transfers between devices: 10.3 us -> 5.99 us  [exchange(): return lax.ppermute(x, ('groups', 'tensor'), pairs)]
    pallas_call x2, Pallas kernels: 10.5 us -> 14.1 us  [factor_sums(): pl.pallas_call(functools.partial(factor_kernel, slots_each), in_specs=[pl...]
    pallas_call x1, Pallas kernels: 4.28 us -> 7.4 us  [low_product(): pl.pallas_call(low_kernel, grid_spec=pltpu.PrefetchScalarGridSpec(num_sca...]
    ppermute x7, starting transfers between devices: 5.56 us -> 8.67 us  [swap(): return lax.ppermute(x, 'tensor', pairs)]
  transfers between devices with their start and end apart: 23 -> 23, of which waited for: 9 -> 5; matrix products, arithmetic and copies ran while one was open for 2% -> 8% of each run, Pallas kernels for 48% -> 57%
where the time goes in v12:
time: 204 us; the launch traced here: 201 us
  Pallas kernels  119 us (58%)
  waiting for transfers between devices  23.6 us (12%)
  starting transfers between devices  20.2 us (10%)
  between operations  15.6 us (8%)
  other arithmetic  11.3 us (6%)
  local copies, waits for them, and re-layouts  6.04 us (3%)
  blocking collectives  4.86 us (2%)
    pallas_call x17, Pallas kernels, product(): pl.pallas_call(functools.partial(product_kernel, tuple((mode for _, mode...  84.8 us
    ppermute x7, waiting for transfers between devices, swap(): return lax.ppermute(x, 'tensor', pairs)  16.6 us
    pallas_call x2, Pallas kernels, factor_sums(): pl.pallas_call(functools.partial(factor_kernel, slots_each), in_specs=[pl...  14.1 us
    another operation x14, other arithmetic, run(): scalars = jnp.stack([jnp.asarray(v, jnp.int32) for v in scalars])  8.82 us
    ppermute x7, starting transfers between devices, swap(): return lax.ppermute(x, 'tensor', pairs)  8.67 us
    pallas_call x1, Pallas kernels, low_product(): pl.pallas_call(low_kernel, grid_spec=pltpu.PrefetchScalarGridSpec(num_sca...  7.4 us
    pallas_call x1, Pallas kernels, product_pair(): pl.pallas_call(pair_kernel, grid_spec=pltpu.PrefetchScalarGridSpec(num_sc...  7.39 us
    ppermute x5, starting transfers between devices, exchange(): return lax.ppermute(x, ('groups', 'tensor'), pairs)  5.99 us
  transfers between devices with their start and end apart: 23, of which 5 were waited for; matrix products, arithmetic and copies ran while one was open for 8% of the time, Pallas kernels for 57%

profile of v12, /device:TPU:10, one launch (start us, length us, event | category | flops | bytes accessed | tf_op | source)
XLA Modules:
  0.0 201.1 jit_solution(18200021047340909472)
XLA Ops:
  9.4 7.4 %shard_map.112 = (bf16[512,1024]{1,0:T(8,128)(2,1)}, bf16[512,1024]{1,0:T(8,128)(2,1)}) custom-call(s32[4]{0:T(128)} %get-tuple-element.11.scalars, bf16[1024,1024]{1,0:T(8,128)(2,1)} %refs_1_.33, bf16[8192,1024]{1,0:T(8,128)(2,1)} %refs_2_.33), custom_call_target="tpu_custom_call" | custom-call | flops 999999995904 | bytes 1000000000 | tf_op jit(solution)/shard_map/pallas_call | solution.py:116
  16.8 1.5 collective-permute-start.2
  18.8 7.4 %shard_map.113.refs_3_ = bf16[1024,128]{1,0:T(8,128)(2,1)} custom-call(s32[8]{0:T(128)} %tenants.1, bf16[1024,1024]{1,0:T(8,128)(2,1)} %refs_1_.33, bf16[16,128,1024]{2,1,0:T(8,128)(2,1)} %expand.1, bf16[512,1024]{1,0:T(8,128)(2,1)} %get-tuple-element.5.link), custom_call_target="tpu_custom_call" | custom-call | flops 999999995904 | bytes 1000000000 | tf_op jit(solution)/shard_map/pallas_call | solution.py:191
  26.2 4.5 %shard_map.114.refs_3_ = bf16[512,1024]{1,0:T(8,128)(2,1)} custom-call(s32[4]{0:T(128)} %get-tuple-element.12.refs_0_, bf16[1024,1024]{1,0:T(8,128)(2,1)} %refs_1_.33, bf16[8192,1024]{1,0:T(8,128)(2,1)} %refs_2_.33, bf16[1024,128]{1,0:T(8,128)(2,1)} %shard_map.113.refs_3_), custom_call_target="tpu_custom_call" | custom-call | flops 999999995904 | bytes 1000000000 | tf_op jit(solution)/shard_map/pallas_call | solution.py:84
  32.0 4.7 %shard_map.115.refs_5_ = bf16[512,1024]{1,0:T(8,128)(2,1)} custom-call(s32[4]{0:T(128)} %fusion.24.refs_0_, bf16[1024,1024]{1,0:T(8,128)(2,1)} %refs_1_.33, bf16[8192,1024]{1,0:T(8,128)(2,1)} %refs_2_.33, bf16[512,1024]{1,0:T(8,128)(2,1)} %shard_map.114.refs_3_), custom_call_target="tpu_custom_call" | custom-call | flops 999999995904 | bytes 1000000000 | tf_op jit(solution)/shard_map/pallas_call | solution.py:84
  36.7 1.6 collective-permute-start.1
  44.0 0.8 fusion.30
  48.6 0.8 dynamic_update_slice.10
  49.7 2.6 %all_gather.12 = bf16[2048,128]{1,0:T(8,128)(2,1)S(1)} all-gather(bf16[1024,128]{1,0:T(8,128)(2,1)S(1)} %copy-done), channel_id=1, replica_groups=mesh['groups'=2,'dp'=2,'tensor'=8] {'dp'}, dimensions={0}, use_global_device_ids=true | all-gather | bytes 786432 | tf_op jit(solution)/shard_map/all_gather | solution.py:325
  52.2 0.8 dynamic_update_slice.11
  53.1 0.7 select_reduce_fusion
  55.6 0.8 bitcast_multiply_fusion.left
  56.4 5.1 %shard_map.116.refs_3_ = bf16[512,1024]{1,0:T(8,128)(2,1)} custom-call(s32[4]{0:T(128)} %add_add_fusion.refs_0_, bf16[1024,1024]{1,0:T(8,128)(2,1)} %refs_1_.33, bf16[8192,1024]{1,0:T(8,128)(2,1)} %refs_2_.33, bf16[512,1024]{1,0:T(8,128)(2,1)} %collective-permute-done.2.refs_3_.refs_4_, bf16[512,1024]{1,0:T(8,128)(2,1)} %collective-permute-done.3.refs_4_, ...), custom_call_target="tpu_custom_call" | custom-call | flops 999999995904 | bytes 1000000000 | tf_op jit(solution)/shard_map/pallas_call | solution.py:84
  61.5 1.6 collective-permute-start.9
  63.1 4.5 %shard_map.117.refs_5_ = bf16[512,1024]{1,0:T(8,128)(2,1)} custom-call(s32[4]{0:T(128)} %fusion.4.refs_0_, bf16[1024,1024]{1,0:T(8,128)(2,1)} %refs_1_.33, bf16[8192,1024]{1,0:T(8,128)(2,1)} %refs_2_.33, bf16[512,1024]{1,0:T(8,128)(2,1)} %shard_map.116.refs_3_), custom_call_target="tpu_custom_call" | custom-call | flops 999999995904 | bytes 1000000000 | tf_op jit(solution)/shard_map/pallas_call | solution.py:84
  67.7 1.4 collective-permute-start.7
  69.0 2.0 %collective-permute-done.1.refs_4_ = bf16[512,1024]{1,0:T(8,128)(2,1)} collective-permute-done((bf16[512,1024]{1,0:T(8,128)(2,1)}, bf16[512,1024]{1,0:T(8,128)(2,1)}, u32[]{:S(2)}, u32[]{:S(2)}) %collective-permute-start.1) | collective-permute-done | bytes 1048608 | tf_op jit(solution)/shard_map/ppermute | solution.py:299
  71.1 5.1 %shard_map.118.refs_3_ = bf16[512,1024]{1,0:T(8,128)(2,1)} custom-call(s32[4]{0:T(128)} %fusion.20.refs_0_, bf16[1024,1024]{1,0:T(8,128)(2,1)} %refs_1_.33, bf16[8192,1024]{1,0:T(8,128)(2,1)} %refs_2_.33, bf16[512,1024]{1,0:T(8,128)(2,1)} %collective-permute-done.refs_3_, bf16[512,1024]{1,0:T(8,128)(2,1)} %collective-permute-done.1.refs_4_, ...), custom_call_target="tpu_custom_call" | custom-call | flops 999999995904 | bytes 1000000000 | tf_op jit(solution)/shard_map/pallas_call | solution.py:84
  76.2 1.6 collective-permute-start.5
  77.8 4.6 %shard_map.119.refs_5_ = bf16[512,1024]{1,0:T(8,128)(2,1)} custom-call(s32[4]{0:T(128)} %fusion.18.refs_0_, bf16[1024,1024]{1,0:T(8,128)(2,1)} %refs_1_.33, bf16[8192,1024]{1,0:T(8,128)(2,1)} %refs_2_.33, bf16[512,1024]{1,0:T(8,128)(2,1)} %shard_map.118.refs_3_), custom_call_target="tpu_custom_call" | custom-call | flops 999999995904 | bytes 1000000000 | tf_op jit(solution)/shard_map/pallas_call | solution.py:84
  82.4 11.1 %collective-permute-done.7.refs_3_ = bf16[512,1024]{1,0:T(8,128)(2,1)} collective-permute-done((bf16[512,1024]{1,0:T(8,128)(2,1)}, bf16[512,1024]{1,0:T(8,128)(2,1)}, u32[]{:S(2)}, u32[]{:S(2)}) %collective-permute-start.7) | collective-permute-done | bytes 1048608 | tf_op jit(solution)/shard_map/ppermute | solution.py:296
  93.4 1.4 collective-permute-start.4
  94.8 5.1 %shard_map.120.refs_5_ = bf16[512,1024]{1,0:T(8,128)(2,1)} custom-call(s32[4]{0:T(128)} %add_add_fusion.1.refs_0_, bf16[1024,1024]{1,0:T(8,128)(2,1)} %refs_1_.33, bf16[8192,1024]{1,0:T(8,128)(2,1)} %refs_2_.33, bf16[512,1024]{1,0:T(8,128)(2,1)} %collective-permute-done.7.refs_3_, bf16[512,1024]{1,0:T(8,128)(2,1)} %collective-permute-done.9.refs_4_, ...), custom_call_target="tpu_custom_call" | custom-call | flops 999999995904 | bytes 1000000000 | tf_op jit(solution)/shard_map/pallas_call | solution.py:84
  99.9 1.7 collective-permute-start.14
  101.6 5.1 %shard_map.121.refs_0_ = bf16[512,1024]{1,0:T(8,128)(2,1)} custom-call(s32[4]{0:T(128)} %fusion.8.refs_0_, bf16[1024,1024]{1,0:T(8,128)(2,1)} %refs_1_.33, bf16[8192,1024]{1,0:T(8,128)(2,1)} %refs_2_.33, bf16[512,1024]{1,0:T(8,128)(2,1)} %collective-permute-done.7.refs_3_, bf16[512,1024]{1,0:T(8,128)(2,1)} %collective-permute-done.8.refs_4_, ...), custom_call_target="tpu_custom_call" | custom-call | flops 999999995904 | bytes 1000000000 | tf_op jit(solution)/shard_map/pallas_call | solution.py:84
  107.2 7.2 %shard_map.122.refs_3_ = f32[8,128,1024]{2,1,0:T(8,128)} custom-call(s32[16]{0:T(128)} %get-tuple-element.8.slots, f32[16]{0:T(128)} %copy-done.4, bf16[2048,128]{1,0:T(8,128)(2,1)} %bitcast_multiply_fusion.left, bf16[2048,1024]{1,0:T(8,128)(2,1)} %all-gather.3.cloned.1.call-done.right, bf16[512,1024]{1,0:T(8,128)(2,1)} %shard_map.121.refs_0_), custom_call_target="tpu_custom_call" | custom-call | flops 999999995904 | bytes 1000000000 | tf_op jit(solution)/shard_map/pallas_call | solution.py:247
  114.3 4.6 %shard_map.123.refs_5_ = bf16[512,1024]{1,0:T(8,128)(2,1)} custom-call(s32[4]{0:T(128)} %fusion.6.refs_0_, bf16[1024,1024]{1,0:T(8,128)(2,1)} %refs_1_.33, bf16[8192,1024]{1,0:T(8,128)(2,1)} %refs_2_.33, f32[8,128,1024]{2,1,0:T(8,128)} %shard_map.122.refs_3_), custom_call_target="tpu_custom_call" | custom-call | flops 999999995904 | bytes 1000000000 | tf_op jit(solution)/shard_map/pallas_call | solution.py:84
  118.9 1.2 collective-permute-start.13
  120.1 5.1 %shard_map.124.refs_5_ = bf16[512,1024]{1,0:T(8,128)(2,1)} custom-call(s32[4]{0:T(128)} %fusion.16.refs_0_, bf16[1024,1024]{1,0:T(8,128)(2,1)} %refs_1_.33, bf16[8192,1024]{1,0:T(8,128)(2,1)} %refs_2_.33, bf16[512,1024]{1,0:T(8,128)(2,1)} %collective-permute-done.4.refs_3_, bf16[512,1024]{1,0:T(8,128)(2,1)} %collective-permute-done.5.refs_4_, ...), custom_call_target="tpu_custom_call" | custom-call | flops 999999995904 | bytes 1000000000 | tf_op jit(solution)/shard_map/pallas_call | solution.py:84
  125.3 1.1 collective-permute-start.10
  126.4 5.1 %shard_map.125.link = bf16[512,1024]{1,0:T(8,128)(2,1)} custom-call(s32[4]{0:T(128)} %fusion.26.refs_0_, bf16[1024,1024]{1,0:T(8,128)(2,1)} %refs_1_.33, bf16[8192,1024]{1,0:T(8,128)(2,1)} %refs_2_.33, bf16[512,1024]{1,0:T(8,128)(2,1)} %collective-permute-done.4.refs_3_, bf16[512,1024]{1,0:T(8,128)(2,1)} %collective-permute-done.11.refs_4_, ...), custom_call_target="tpu_custom_call" | custom-call | flops 999999995904 | bytes 1000000000 | tf_op jit(solution)/shard_map/pallas_call | solution.py:84
  131.6 1.4 collective-permute-start.12
  133.0 1.7 shard_map.126.refs_3_.refs_5_.refs_4_
  134.7 4.7 %shard_map.127.refs_6_ = bf16[512,1024]{1,0:T(8,128)(2,1)} custom-call(s32[4]{0:T(128)} %fusion.14.refs_0_, bf16[1024,1024]{1,0:T(8,128)(2,1)} %refs_1_.33, bf16[8192,1024]{1,0:T(8,128)(2,1)} %refs_2_.33, bf16[1024,128]{1,0:T(8,128)(2,1)} %shard_map.126.refs_3_.refs_5_.refs_4_), custom_call_target="tpu_custom_call" | custom-call | flops 999999995904 | bytes 1000000000 | tf_op jit(solution)/shard_map/pallas_call | solution.py:84
  139.4 2.3 %all_gather.15.right = bf16[2048,128]{1,0:T(8,128)(2,1)} all-gather(bf16[1024,128]{1,0:T(8,128)(2,1)S(1)} %copy-done.1), channel_id=1, replica_groups=mesh['groups'=2,'dp'=2,'tensor'=8] {'dp'}, dimensions={0}, use_global_device_ids=true | all-gather | bytes 786432 | tf_op jit(solution)/shard_map/all_gather | solution.py:325
  141.7 1.4 collective-permute-start.17
  143.2 5.4 %shard_map.128.refs_4_ = bf16[512,1024]{1,0:T(8,128)(2,1)} custom-call(s32[4]{0:T(128)} %fusion.12.refs_0_, bf16[1024,1024]{1,0:T(8,128)(2,1)} %refs_1_.33, bf16[8192,1024]{1,0:T(8,128)(2,1)} %refs_2_.33, bf16[512,1024]{1,0:T(8,128)(2,1)} %collective-permute-done.13.refs_3_, bf16[512,1024]{1,0:T(8,128)(2,1)} %collective-permute-done.2.refs_3_.refs_4_, ...), custom_call_target="tpu_custom_call" | custom-call | flops 999999995904 | bytes 1000000000 | tf_op jit(solution)/shard_map/pallas_call | solution.py:84
  149.2 4.8 %shard_map.129.refs_5_ = bf16[512,1024]{1,0:T(8,128)(2,1)} custom-call(s32[4]{0:T(128)} %fusion.28.refs_0_, bf16[1024,1024]{1,0:T(8,128)(2,1)} %refs_1_.33, bf16[8192,1024]{1,0:T(8,128)(2,1)} %refs_2_.33, bf16[512,1024]{1,0:T(8,128)(2,1)} %collective-permute-done.14.refs_3_.refs_4_, bf16[512,1024]{1,0:T(8,128)(2,1)} %shard_map.128.refs_4_), custom_call_target="tpu_custom_call" | custom-call | flops 999999995904 | bytes 1000000000 | tf_op jit(solution)/shard_map/pallas_call | solution.py:84
  154.0 1.2 collective-permute-start.16
  155.2 5.1 %shard_map.130.refs_0_ = bf16[512,1024]{1,0:T(8,128)(2,1)} custom-call(s32[4]{0:T(128)} %fusion.10.refs_0_, bf16[1024,1024]{1,0:T(8,128)(2,1)} %refs_1_.33, bf16[8192,1024]{1,0:T(8,128)(2,1)} %refs_2_.33, bf16[512,1024]{1,0:T(8,128)(2,1)} %collective-permute-done.13.refs_3_, bf16[512,1024]{1,0:T(8,128)(2,1)} %collective-permute-done.14.refs_3_.refs_4_, ...), custom_call_target="tpu_custom_call" | custom-call | flops 999999995904 | bytes 1000000000 | tf_op jit(solution)/shard_map/pallas_call | solution.py:84
  160.3 0.9 collective-permute-start.19
  161.3 3.6 %collective-permute-done.10.refs_1_.refs_3_ = bf16[512,1024]{1,0:T(8,128)(2,1)} collective-permute-done((bf16[512,1024]{1,0:T(8,128)(2,1)}, bf16[512,1024]{1,0:T(8,128)(2,1)}, u32[]{:S(2)}, u32[]{:S(2)}) %collective-permute-start.10) | collective-permute-done | bytes 1048608 | tf_op jit(solution)/shard_map/ppermute | solution.py:299
  165.3 7.0 %shard_map.131.refs_10_ = f32[8,1024,128]{2,1,0:T(8,128)} custom-call(s32[16]{0:T(128)} %get-tuple-element.8.slots, f32[16]{0:T(128)} %broadcast_4_scales.2.scales, bf16[2048,1024]{1,0:T(8,128)(2,1)} %all-gather.5.cloned.1.call-done.left, bf16[2048,128]{1,0:T(8,128)(2,1)} %all_gather.15.right, bf16[512,1024]{1,0:T(8,128)(2,1)} %shard_map.130.refs_0_, ...), custom_call_target="tpu_custom_call" | custom-call | flops 999999995904 | bytes 1000000000 | tf_op jit(solution)/shard_map/pallas_call | solution.py:247
  172.3 5.7 %shard_map.132.refs_9_.refs_0_ = bf16[512,1024]{1,0:T(8,128)(2,1)} custom-call(s32[8]{0:T(128)} %stack.72.refs_0_, bf16[1024,1024]{1,0:T(8,128)(2,1)} %refs_1_.33, bf16[8192,1024]{1,0:T(8,128)(2,1)} %refs_2_.33, bf16[512,1024]{1,0:T(8,128)(2,1)} %collective-permute-done.10.refs_1_.refs_3_, bf16[512,1024]{1,0:T(8,128)(2,1)} %collective-permute-done.12.refs_2_.refs_4_, ...), custom_call_target="tpu_custom_call" | custom-call | flops 999999995904 | bytes 1000000000 | tf_op jit(solution)/shard_map/pallas_call | solution.py:84
  178.0 5.5 %shard_map.133.refs_2_ = bf16[512,1024]{1,0:T(8,128)(2,1)} custom-call(s32[8]{0:T(128)} %stack.175.refs_0_, bf16[1024,1024]{1,0:T(8,128)(2,1)} %refs_1_.33, bf16[8192,1024]{1,0:T(8,128)(2,1)} %refs_2_.33, bf16[512,1024]{1,0:T(8,128)(2,1)} %collective-permute-done.17.refs_3_, bf16[1024,128]{1,0:T(8,128)(2,1)} %shard_map.126.refs_3_.refs_5_.refs_4_, ...), custom_call_target="tpu_custom_call" | custom-call | flops 999999995904 | bytes 1000000000 | tf_op jit(solution)/shard_map/pallas_call | solution.py:84
  183.5 0.7 collective-permute-done.19.refs_4_
  184.2 5.5 %collective-permute-done.16.refs_1_ = bf16[512,1024]{1,0:T(8,128)(2,1)} collective-permute-done((bf16[512,1024]{1,0:T(8,128)(2,1)}, bf16[512,1024]{1,0:T(8,128)(2,1)}, u32[]{:S(2)}, u32[]{:S(2)}) %collective-permute-start.16) | collective-permute-done | bytes 1048608 | tf_op jit(solution)/shard_map/ppermute | solution.py:296
  189.7 4.0 %shard_map.134 = bf16[1024,1024]{1,0:T(8,128)(2,1)} custom-call(s32[1]{0:T(128)} %bitcast.inner, bf16[512,1024]{1,0:T(8,128)(2,1)} %shard_map.132.refs_9_.refs_0_, bf16[512,1024]{1,0:T(8,128)(2,1)} %collective-permute-done.16.refs_1_, bf16[512,1024]{1,0:T(8,128)(2,1)} %shard_map.133.refs_2_, bf16[512,1024]{1,0:T(8,128)(2,1)} %collective-permute-done.18.refs_3_, ...), custom_call_target="tpu_custom_call" | custom-call | flops 999999995904 | bytes 1000000000 | tf_op jit(solution)/shard_map/pallas_call | solution.py:167
  (67 shorter events, 16.2 us)
Async XLA Ops:
  8.0 99.2 %all-gather.3.cloned.1.call-start = ((), (), s32[]{:S(2)}) async-start(), calls=%async_computation | async-start | bytes 6291456 | tf_op jit(solution)/shard_map/all_gather | solution.py:325
  16.8 39.6 %collective-permute-start.2 = (bf16[512,1024]{1,0:T(8,128)(2,1)}, bf16[512,1024]{1,0:T(8,128)(2,1)}, u32[]{:S(2)}, u32[]{:S(2)}) collective-permute-start(bf16[512,1024]{1,0:T(8,128)(2,1)} %get-tuple-element.6), channel_id=1, source_target_pairs={{0,1},{1,0},{2,3},{3,2},{4,5},{5,4},{6,7},{7,6},{8,9},{9,8},{10,11... | collective-permute-start | bytes 3145736 | tf_op jit(solution)/shard_map/ppermute | solution.py:296
  18.3 38.1 %collective-permute-start.3 = (bf16[512,1024]{1,0:T(8,128)(2,1)}, bf16[512,1024]{1,0:T(8,128)(2,1)}, u32[]{:S(2)}, u32[]{:S(2)}) collective-permute-start(bf16[512,1024]{1,0:T(8,128)(2,1)} %get-tuple-element.5.link), channel_id=1, source_target_pairs={{0,2},{1,3},{6,4},{7,5},{2,0},{3,1},{4,6},{5,7},{8,10},{9,11},{14,... | collective-permute-start | bytes 3145736 | tf_op jit(solution)/shard_map/ppermute | solution.py:299
  18.8 33.4 %collective-permute-start.6 = (s32[8]{0:T(128)}, s32[8]{0:T(128)}, u32[]{:S(2)}, u32[]{:S(2)}) collective-permute-start(s32[8]{0:T(128)} %tenants.1), channel_id=1, source_target_pairs={{0,8},{8,0},{1,9},{9,1},{2,10},{10,2},{3,11},{11,3},{4,12},{12,4},... | collective-permute-start | bytes 104 | tf_op jit(solution)/shard_map/ppermute | solution.py:330
  30.7 102.2 %all-reduce.2.cloned.1.call-start = ((), (), s32[]{:S(2)}) async-start(), calls=%async_computation.1 | async-start | bytes 524288 | tf_op jit(solution)/shard_map/psum | solution.py:349
  30.7 40.3 %collective-permute-start = (bf16[512,1024]{1,0:T(8,128)(2,1)}, bf16[512,1024]{1,0:T(8,128)(2,1)}, u32[]{:S(2)}, u32[]{:S(2)}) collective-permute-start(bf16[512,1024]{1,0:T(8,128)(2,1)} %shard_map.114.refs_3_), channel_id=1, source_target_pairs={{0,1},{1,0},{2,3},{3,2},{4,5},{5,4},{6,7},{7,6},{8,9},{9,8},{10,11... | collective-permute-start | bytes 3145736 | tf_op jit(solution)/shard_map/ppermute | solution.py:296
  31.3 130.0 %all-gather.5.cloned.1.call-start = ((), (), s32[]{:S(2)}) async-start(), calls=%async_computation.2 | async-start | bytes 6291456 | tf_op jit(solution)/shard_map/all_gather | solution.py:325
  32.0 14.0 %copy-start.3 = (s32[16]{0:T(128)S(1)}, s32[16]{0:T(128)}, u32[]{:S(2)}) copy-start(s32[16]{0:T(128)} %param.17) | copy-start | bytes 196
  32.0 17.7 %copy-start = (bf16[1024,128]{1,0:T(8,128)(2,1)S(1)}, bf16[1024,128]{1,0:T(8,128)(2,1)}, u32[]{:S(2)}) copy-start(bf16[1024,128]{1,0:T(8,128)(2,1)} %param.11) | copy-start | bytes 786436
  32.0 21.1 %copy-start.2 = (s32[16]{0:T(128)S(1)}, s32[16]{0:T(128)}, u32[]{:S(2)}) copy-start(s32[16]{0:T(128)} %param.16) | copy-start | bytes 196
  36.7 34.4 %collective-permute-start.1 = (bf16[512,1024]{1,0:T(8,128)(2,1)}, bf16[512,1024]{1,0:T(8,128)(2,1)}, u32[]{:S(2)}, u32[]{:S(2)}) collective-permute-start(bf16[512,1024]{1,0:T(8,128)(2,1)} %shard_map.115.refs_5_), channel_id=1, source_target_pairs={{0,2},{1,3},{6,4},{7,5},{2,0},{3,1},{4,6},{5,7},{8,10},{9,11},{14,... | collective-permute-start | bytes 3145736 | tf_op jit(solution)/shard_map/ppermute | solution.py:299
  54.4 0.5 copy-start.4
  61.5 33.3 %collective-permute-start.9 = (bf16[512,1024]{1,0:T(8,128)(2,1)}, bf16[512,1024]{1,0:T(8,128)(2,1)}, u32[]{:S(2)}, u32[]{:S(2)}) collective-permute-start(bf16[512,1024]{1,0:T(8,128)(2,1)} %shard_map.116.refs_3_), channel_id=1, source_target_pairs={{2,4},{4,2},{0,16},{6,22},{3,5},{5,3},{1,17},{7,23},{18,20},{20,18... | collective-permute-start | bytes 3145736 | tf_op jit(solution)/shard_map/ppermute | solution.py:315
  63.1 38.5 %collective-permute-start.8 = (bf16[512,1024]{1,0:T(8,128)(2,1)}, bf16[512,1024]{1,0:T(8,128)(2,1)}, u32[]{:S(2)}, u32[]{:S(2)}) collective-permute-start(bf16[512,1024]{1,0:T(8,128)(2,1)} %shard_map.116.refs_3_), channel_id=1, source_target_pairs={{0,2},{1,3},{6,4},{7,5},{2,0},{3,1},{4,6},{5,7},{8,10},{9,11},{14,... | collective-permute-start | bytes 3145736 | tf_op jit(solution)/shard_map/ppermute | solution.py:299
  67.7 25.8 %collective-permute-start.7 = (bf16[512,1024]{1,0:T(8,128)(2,1)}, bf16[512,1024]{1,0:T(8,128)(2,1)}, u32[]{:S(2)}, u32[]{:S(2)}) collective-permute-start(bf16[512,1024]{1,0:T(8,128)(2,1)} %shard_map.117.refs_5_), channel_id=1, source_target_pairs={{0,1},{1,0},{2,3},{3,2},{4,5},{5,4},{6,7},{7,6},{8,9},{9,8},{10,11... | collective-permute-start | bytes 3145736 | tf_op jit(solution)/shard_map/ppermute | solution.py:296
  76.2 43.9 %collective-permute-start.5 = (bf16[512,1024]{1,0:T(8,128)(2,1)}, bf16[512,1024]{1,0:T(8,128)(2,1)}, u32[]{:S(2)}, u32[]{:S(2)}) collective-permute-start(bf16[512,1024]{1,0:T(8,128)(2,1)} %shard_map.118.refs_3_), channel_id=1, source_target_pairs={{2,4},{4,2},{0,16},{6,22},{3,5},{5,3},{1,17},{7,23},{18,20},{20,18... | collective-permute-start | bytes 3145736 | tf_op jit(solution)/shard_map/ppermute | solution.py:315
  77.8 48.6 %collective-permute-start.11 = (bf16[512,1024]{1,0:T(8,128)(2,1)}, bf16[512,1024]{1,0:T(8,128)(2,1)}, u32[]{:S(2)}, u32[]{:S(2)}) collective-permute-start(bf16[512,1024]{1,0:T(8,128)(2,1)} %shard_map.118.refs_3_), channel_id=1, source_target_pairs={{0,2},{1,3},{6,4},{7,5},{2,0},{3,1},{4,6},{5,7},{8,10},{9,11},{14,... | collective-permute-start | bytes 3145736 | tf_op jit(solution)/shard_map/ppermute | solution.py:299
  93.4 25.5 %collective-permute-start.4 = (bf16[512,1024]{1,0:T(8,128)(2,1)}, bf16[512,1024]{1,0:T(8,128)(2,1)}, u32[]{:S(2)}, u32[]{:S(2)}) collective-permute-start(bf16[512,1024]{1,0:T(8,128)(2,1)} %shard_map.119.refs_5_), channel_id=1, source_target_pairs={{0,1},{1,0},{2,3},{3,2},{4,5},{5,4},{6,7},{7,6},{8,9},{9,8},{10,11... | collective-permute-start | bytes 3145736 | tf_op jit(solution)/shard_map/ppermute | solution.py:296
  99.9 49.3 %collective-permute-start.14 = (bf16[512,1024]{1,0:T(8,128)(2,1)}, bf16[512,1024]{1,0:T(8,128)(2,1)}, u32[]{:S(2)}, u32[]{:S(2)}) collective-permute-start(bf16[512,1024]{1,0:T(8,128)(2,1)} %shard_map.120.refs_5_), channel_id=1, source_target_pairs={{0,2},{1,3},{6,4},{7,5},{2,0},{3,1},{4,6},{5,7},{8,10},{9,11},{14,... | collective-permute-start | bytes 3145736 | tf_op jit(solution)/shard_map/ppermute | solution.py:299
  106.7 35.0 %collective-permute-start.15 = (bf16[512,1024]{1,0:T(8,128)(2,1)}, bf16[512,1024]{1,0:T(8,128)(2,1)}, u32[]{:S(2)}, u32[]{:S(2)}) collective-permute-start(bf16[512,1024]{1,0:T(8,128)(2,1)} %shard_map.121.refs_0_), channel_id=1, source_target_pairs={{2,4},{4,2},{0,16},{6,22},{3,5},{5,3},{1,17},{7,23},{18,20},{20,18... | collective-permute-start | bytes 3145736 | tf_op jit(solution)/shard_map/ppermute | solution.py:315
  118.9 24.2 %collective-permute-start.13 = (bf16[512,1024]{1,0:T(8,128)(2,1)}, bf16[512,1024]{1,0:T(8,128)(2,1)}, u32[]{:S(2)}, u32[]{:S(2)}) collective-permute-start(bf16[512,1024]{1,0:T(8,128)(2,1)} %shard_map.123.refs_5_), channel_id=1, source_target_pairs={{0,1},{1,0},{2,3},{3,2},{4,5},{5,4},{6,7},{7,6},{8,9},{9,8},{10,11... | collective-permute-start | bytes 3145736 | tf_op jit(solution)/shard_map/ppermute | solution.py:296
  125.3 39.6 %collective-permute-start.10 = (bf16[512,1024]{1,0:T(8,128)(2,1)}, bf16[512,1024]{1,0:T(8,128)(2,1)}, u32[]{:S(2)}, u32[]{:S(2)}) collective-permute-start(bf16[512,1024]{1,0:T(8,128)(2,1)} %shard_map.124.refs_5_), channel_id=1, source_target_pairs={{0,2},{1,3},{6,4},{7,5},{2,0},{3,1},{4,6},{5,7},{8,10},{9,11},{14,... | collective-permute-start | bytes 3145736 | tf_op jit(solution)/shard_map/ppermute | solution.py:299
  131.6 28.8 %collective-permute-start.12 = (bf16[512,1024]{1,0:T(8,128)(2,1)}, bf16[512,1024]{1,0:T(8,128)(2,1)}, u32[]{:S(2)}, u32[]{:S(2)}) collective-permute-start(bf16[512,1024]{1,0:T(8,128)(2,1)} %shard_map.125.link), channel_id=1, source_target_pairs={{2,4},{4,2},{0,16},{6,22},{3,5},{5,3},{1,17},{7,23},{18,20},{20,18... | collective-permute-start | bytes 3145736 | tf_op jit(solution)/shard_map/ppermute | solution.py:315
  134.7 4.7 %copy-start.1 = (bf16[1024,128]{1,0:T(8,128)(2,1)S(1)}, bf16[1024,128]{1,0:T(8,128)(2,1)}, u32[]{:S(2)}) copy-start(bf16[1024,128]{1,0:T(8,128)(2,1)} %shard_map.126.refs_3_.refs_5_.refs_4_) | copy-start | bytes 786436
  141.7 36.3 %collective-permute-start.17 = (bf16[512,1024]{1,0:T(8,128)(2,1)}, bf16[512,1024]{1,0:T(8,128)(2,1)}, u32[]{:S(2)}, u32[]{:S(2)}) collective-permute-start(bf16[512,1024]{1,0:T(8,128)(2,1)} %shard_map.127.refs_6_), channel_id=1, source_target_pairs={{0,1},{1,0},{2,3},{3,2},{4,5},{5,4},{6,7},{7,6},{8,9},{9,8},{10,11... | collective-permute-start | bytes 3145736 | tf_op jit(solution)/shard_map/ppermute | solution.py:296
  148.6 41.1 %collective-permute-start.18 = (bf16[512,1024]{1,0:T(8,128)(2,1)}, bf16[512,1024]{1,0:T(8,128)(2,1)}, u32[]{:S(2)}, u32[]{:S(2)}) collective-permute-start(bf16[512,1024]{1,0:T(8,128)(2,1)} %shard_map.128.refs_4_), channel_id=1, source_target_pairs={{0,2},{1,3},{6,4},{7,5},{2,0},{3,1},{4,6},{5,7},{8,10},{9,11},{14,... | collective-permute-start | bytes 3145736 | tf_op jit(solution)/shard_map/ppermute | solution.py:299
  154.0 35.7 %collective-permute-start.16 = (bf16[512,1024]{1,0:T(8,128)(2,1)}, bf16[512,1024]{1,0:T(8,128)(2,1)}, u32[]{:S(2)}, u32[]{:S(2)}) collective-permute-start(bf16[512,1024]{1,0:T(8,128)(2,1)} %shard_map.129.refs_5_), channel_id=1, source_target_pairs={{0,1},{1,0},{2,3},{3,2},{4,5},{5,4},{6,7},{7,6},{8,9},{9,8},{10,11... | collective-permute-start | bytes 3145736 | tf_op jit(solution)/shard_map/ppermute | solution.py:296
  160.3 23.9 %collective-permute-start.19 = (bf16[512,1024]{1,0:T(8,128)(2,1)}, bf16[512,1024]{1,0:T(8,128)(2,1)}, u32[]{:S(2)}, u32[]{:S(2)}) collective-permute-start(bf16[512,1024]{1,0:T(8,128)(2,1)} %shard_map.130.refs_0_), channel_id=1, source_target_pairs={{2,4},{4,2},{0,16},{6,22},{3,5},{5,3},{1,17},{7,23},{18,20},{20,18... | collective-permute-start | bytes 3145736 | tf_op jit(solution)/shard_map/ppermute | solution.py:315
Sparse Core Ops, SparseCore 0:
  10.4 15.0 all-gather.2
  38.4 15.3 all-gather.4
Sparse Core Ops, SparseCore 1:
  34.5 72.2 all-reduce.1
